TPU v7x, 32 devices: a whole 2x2x4 slice. The times are simulated.
32 devices in a mesh: dp: 4 (over x, core), tensor: 8 (over z, y).
Axes of the slice: x: 2, y: 2, z: 4, core: 2. Of those that a mesh axis runs over, the one named last changes fastest.
Arguments:
- inputs: bfloat16 [2, 11776, 1152], P(None, ('dp', 'tensor')), may hold values from -6 to 6
- pad_mask: int32 [2, 16, 736], P(None, 'dp'), may hold values from 0 to 1, as said below
- cotangent: bfloat16 [2, 11776, 1152], P(None, ('dp', 'tensor')), may hold values from -6 to 6
- attn_norm_gain: float32 [1152], replicated, may hold values from 0.5 to 1.5
- attn_norm_shift: float32 [1152], replicated, may hold values from -1.5 to 1.5
- w_query: bfloat16 [1152, 1152], P('dp', 'tensor'), may hold values from -0.1875 to 0.1875
- b_query: float32 [1152], replicated, may hold values from -1.5 to 1.5
- w_key: bfloat16 [1152, 1152], P('dp', 'tensor'), may hold values from -0.1875 to 0.1875
- w_value: bfloat16 [1152, 1152], P('dp', 'tensor'), may hold values from -0.1875 to 0.1875
- b_value: float32 [1152], replicated, may hold values from -1.5 to 1.5
- w_out: bfloat16 [1152, 1152], P('tensor', 'dp'), may hold values from -3 to 3
- b_out: float32 [1152], replicated, may hold values from -1.5 to 1.5
- mlp_norm_gain: float32 [1152], replicated, may hold values from 0.5 to 1.5
- mlp_norm_shift: float32 [1152], replicated, may hold values from -1.5 to 1.5
- w_up: bfloat16 [1152, 4304], P('dp', 'tensor'), may hold values from -0.1875 to 0.1875
- b_up: float32 [4304], replicated, may hold values from -1.5 to 1.5
- w_down: bfloat16 [4304, 1152], P('tensor', 'dp'), may hold values from -0.09375 to 0.09375
- b_down: float32 [1152], replicated, may hold values from -1.5 to 1.5
Outputs:
- layer_out: bfloat16 [2, 11776, 1152], P(None, ('dp', 'tensor'))
- input_grad: float32 [2, 11776, 1152], P(None, ('dp', 'tensor'))
- grad_attn_norm_gain: float32 [1152], replicated
- grad_attn_norm_shift: float32 [1152], replicated
- grad_w_query: float32 [1152, 1152], P('dp', 'tensor')
- grad_b_query: float32 [1152], P('tensor')
- grad_w_key: float32 [1152, 1152], P('dp', 'tensor')
- grad_w_value: float32 [1152, 1152], P('dp', 'tensor')
- grad_b_value: float32 [1152], P('tensor')
- grad_w_out: float32 [1152, 1152], P('tensor', 'dp')
- grad_b_out: float32 [1152], replicated
- grad_mlp_norm_gain: float32 [1152], replicated
- grad_mlp_norm_shift: float32 [1152], replicated
- grad_w_up: float32 [1152, 4304], P('dp', 'tensor')
- grad_b_up: float32 [4304], replicated
- grad_w_down: float32 [4304, 1152], P('tensor', 'dp')
- grad_b_down: float32 [1152], replicated
Inputs may be any that keep to these rules, and one draw needn't show every extreme that they name: `pad_mask`: each slot's ones form a prefix of 368 to 729 positions, so its last 7 positions are 0; numbering slots m * 16 + j, slots 0, 4, 8 and so on have 736 - 7 ones and slots 1, 5, 9 and so on have 736 // 2.
All inputs are finite; a program needn't handle non-finite values.
Results may differ from a plain program's by a relative error of at most 0.015.
Values may be sent and summed in bfloat16 or wider, within the bound.
No kernel may reach another device: no remote copies, remote signals or barrier semaphores. Data moves between devices by JAX's collectives and lax.ppermute only.
A program may use at most 384 MiB of HBM per device.

v0:
```python
from functools import partial

import jax
import jax.numpy as jnp
from jax import lax
from jax.sharding import PartitionSpec as P

HEAD_DIM = 72


norm_eps = 1e-06
masked_score = -1000000000.0


def norm_forward(values, norm_gain, norm_shift):
    row_mean = jnp.mean(values, axis=-1, keepdims=True)
    centred = values - row_mean
    inv_scale = lax.rsqrt(jnp.mean(centred * centred, axis=-1, keepdims=True) + norm_eps)
    unit_rows = centred * inv_scale
    return (unit_rows * norm_gain + norm_shift, unit_rows, inv_scale)


def norm_backward(grad_rows, unit_rows, inv_scale, norm_gain):
    grad_unit = grad_rows * norm_gain
    mean_grad = jnp.mean(grad_unit, axis=-1, keepdims=True)
    mean_along = jnp.mean(grad_unit * unit_rows, axis=-1, keepdims=True)
    grad_values = inv_scale * (grad_unit - mean_grad - unit_rows * mean_along)
    return (grad_values, jnp.sum(grad_rows * unit_rows, axis=0), jnp.sum(grad_rows, axis=0))


def slot_scores(queries, keys_low, key_valid):
    raw_scores = jnp.einsum("lhe,mhe->hlm", queries, keys_low, preferred_element_type=jnp.float32)
    return jnp.where(
        key_valid[None, None, :] > 0, raw_scores * queries.shape[-1] ** (-0.5), masked_score
    )


def attend_slot(members):
    queries, keys_low, values_low, key_valid = members
    scores = slot_scores(queries, keys_low, key_valid)
    row_max = jnp.max(scores, axis=-1, keepdims=True)
    exp_scores = jnp.exp(scores - row_max)
    row_sum = jnp.sum(exp_scores, axis=-1, keepdims=True)
    attn_probs = (exp_scores / row_sum).astype(jnp.bfloat16)
    attended = jnp.einsum(
        "hlm,mhe->lhe", attn_probs, values_low, preferred_element_type=jnp.float32
    )
    return (attended.astype(jnp.bfloat16), row_max + jnp.log(row_sum))


def attend_back(members):
    queries, keys_low, values_low, key_valid, log_total, grad_att = members
    attn_probs = jnp.exp(slot_scores(queries, keys_low, key_valid) - log_total)
    grad_probs = jnp.einsum(
        "lhe,mhe->hlm", grad_att, values_low, preferred_element_type=jnp.float32
    )
    row_dot = jnp.sum(attn_probs * grad_probs, axis=-1, keepdims=True)
    grad_raw = (attn_probs * (grad_probs - row_dot) * queries.shape[-1] ** (-0.5)).astype(
        jnp.bfloat16
    )
    grad_queries = jnp.einsum(
        "hlm,mhe->lhe", grad_raw, keys_low, preferred_element_type=jnp.float32
    )
    grad_keys = jnp.einsum("hlm,lhe->mhe", grad_raw, queries, preferred_element_type=jnp.float32)
    grad_values = jnp.einsum(
        "hlm,lhe->mhe",
        attn_probs.astype(jnp.bfloat16),
        grad_att,
        preferred_element_type=jnp.float32,
    )
    return (
        grad_queries.astype(jnp.bfloat16),
        grad_keys.astype(jnp.bfloat16),
        grad_values.astype(jnp.bfloat16),
    )


def gelu_pullback(pre_act, grad_active):
    outputs_unused, pullback = jax.vjp(partial(jax.nn.gelu, approximate=True), pre_act)
    return pullback(grad_active)[0]


def attention_weights(w_query, w_key, w_value, w_out, again):
    if again:
        pieces = (
            lax.all_gather(w_query, "dp", axis=0, tiled=True),
            lax.all_gather(w_key, "dp", axis=0, tiled=True),
            lax.all_gather(w_value, "dp", axis=0, tiled=True),
            lax.all_gather(w_out, "dp", axis=1, tiled=True),
        )
    else:
        pieces = (
            lax.all_gather(w_query, "dp", axis=0, tiled=True),
            lax.all_gather(w_key, "dp", axis=0, tiled=True),
            lax.all_gather(w_value, "dp", axis=0, tiled=True),
            lax.all_gather(w_out, "dp", axis=1, tiled=True),
        )
    return pieces


def mlp_weights(w_up, w_down, again):
    if again:
        up_rows, down_cols = (
            lax.all_gather(w_up, "dp", axis=0, tiled=True),
            lax.all_gather(w_down, "dp", axis=1, tiled=True),
        )
    else:
        up_rows, down_cols = (
            lax.all_gather(w_up, "dp", axis=0, tiled=True),
            lax.all_gather(w_down, "dp", axis=1, tiled=True),
        )
    return (up_rows, down_cols)


def gather_rows(values):
    return lax.all_gather(values, "tensor", axis=0, tiled=True)


def reduce_rows(values):
    return lax.psum_scatter(values, "tensor", scatter_dimension=0, tiled=True)


def gather_grads(values):
    return lax.all_gather(values, "tensor", axis=0, tiled=True)


def reduce_grads(values):
    return lax.psum_scatter(values, "tensor", scatter_dimension=0, tiled=True)


def attention_grad_owned(terms):
    query_term, key_term, value_term, out_term = terms
    return (
        lax.psum_scatter(
            query_term.astype(jnp.bfloat16), "dp", scatter_dimension=0, tiled=True
        ).astype(jnp.float32),
        lax.psum_scatter(
            key_term.astype(jnp.bfloat16), "dp", scatter_dimension=0, tiled=True
        ).astype(jnp.float32),
        lax.psum_scatter(
            value_term.astype(jnp.bfloat16), "dp", scatter_dimension=0, tiled=True
        ).astype(jnp.float32),
        lax.psum_scatter(
            out_term.astype(jnp.bfloat16), "dp", scatter_dimension=1, tiled=True
        ).astype(jnp.float32),
    )


def mlp_grad_owned(terms):
    up_term, down_term = terms
    return (
        lax.psum_scatter(
            up_term.astype(jnp.bfloat16), "dp", scatter_dimension=0, tiled=True
        ).astype(jnp.float32),
        lax.psum_scatter(
            down_term.astype(jnp.bfloat16), "dp", scatter_dimension=1, tiled=True
        ).astype(jnp.float32),
    )


def add_up(running, terms):
    if running is None:
        return terms
    return jax.tree.map(jnp.add, running, terms)


def shards(
    inputs,
    pad_mask,
    cotangent,
    attn_norm_gain,
    attn_norm_shift,
    w_query,
    b_query,
    w_key,
    w_value,
    b_value,
    w_out,
    b_out,
    mlp_norm_gain,
    mlp_norm_shift,
    w_up,
    b_up,
    w_down,
    b_down,
):
    micro_count = inputs.shape[0]
    slot_count = pad_mask.shape[1]
    seq_len = pad_mask.shape[2]
    model_width = inputs.shape[2]
    head_cols = w_query.shape[1]
    unit_cols = w_up.shape[1]
    tensor_place = lax.axis_index("tensor")
    col_start = tensor_place * head_cols
    unit_start = tensor_place * unit_cols
    head_shape = (slot_count, seq_len, -1, HEAD_DIM)
    stored = []
    layer_parts = []
    for micro_index in range(micro_count):
        x_part = inputs[micro_index].astype(jnp.float32)
        key_valid = pad_mask[micro_index]
        query_full, key_full, value_full, out_full = attention_weights(
            w_query, w_key, w_value, w_out, False
        )
        up_full, down_full = mlp_weights(w_up, w_down, False)
        norm_first, unit_first, scale_first = norm_forward(x_part, attn_norm_gain, attn_norm_shift)
        rows_first = gather_rows(norm_first.astype(jnp.bfloat16))
        query_bias = lax.dynamic_slice_in_dim(b_query, col_start, head_cols)
        value_bias = lax.dynamic_slice_in_dim(b_value, col_start, head_cols)
        queries = (
            jnp.dot(rows_first, query_full, preferred_element_type=jnp.float32) + query_bias
        ).astype(jnp.bfloat16)
        keys_low = jnp.dot(rows_first, key_full, preferred_element_type=jnp.float32).astype(
            jnp.bfloat16
        )
        values_low = (
            jnp.dot(rows_first, value_full, preferred_element_type=jnp.float32) + value_bias
        ).astype(jnp.bfloat16)
        attended, log_total = lax.map(
            attend_slot,
            (
                queries.reshape(head_shape),
                keys_low.reshape(head_shape),
                values_low.reshape(head_shape),
                key_valid,
            ),
        )
        head_rows = attended.reshape(slot_count * seq_len, -1)
        att_rows = head_rows
        out_sum = reduce_rows(jnp.dot(att_rows, out_full, preferred_element_type=jnp.float32))
        middle = x_part + (out_sum + b_out)
        norm_second, unit_second, scale_second = norm_forward(middle, mlp_norm_gain, mlp_norm_shift)
        rows_second = gather_rows(norm_second.astype(jnp.bfloat16))
        up_bias = lax.dynamic_slice_in_dim(b_up, unit_start, unit_cols)
        pre_act = jnp.dot(rows_second, up_full, preferred_element_type=jnp.float32) + up_bias
        active = jax.nn.gelu(pre_act, approximate=True).astype(jnp.bfloat16)
        down_terms = jnp.dot(active, down_full, preferred_element_type=jnp.float32)
        mlp_branch = reduce_rows(down_terms)
        layer_parts.append((middle + (mlp_branch + b_down)).astype(jnp.bfloat16))
        stored.append(
            (
                key_valid,
                unit_first,
                scale_first,
                rows_first,
                queries,
                keys_low,
                values_low,
                log_total,
                att_rows,
                unit_second,
                scale_second,
                rows_second,
                pre_act,
                active,
            )
        )
    attn_running = None
    mlp_running = None
    vector_running = None
    grad_parts = []
    zero_row = jnp.zeros((model_width,), jnp.float32)
    zero_units = jnp.zeros(b_up.shape, jnp.float32)
    for micro_index in range(micro_count):
        (
            key_valid,
            unit_first,
            scale_first,
            rows_first,
            queries,
            keys_low,
            values_low,
            log_total,
            att_rows,
            unit_second,
            scale_second,
            rows_second,
            pre_act,
            active,
        ) = stored[micro_index]
        grad_out = cotangent[micro_index]
        query_full, key_full, value_full, out_full = attention_weights(
            w_query, w_key, w_value, w_out, True
        )
        up_full, down_full = mlp_weights(w_up, w_down, True)
        grad_rows = gather_grads(grad_out)
        grad_active = jnp.einsum(
            "nd,fd->nf", grad_rows, down_full, preferred_element_type=jnp.float32
        )
        grad_pre = gelu_pullback(pre_act, grad_active).astype(jnp.bfloat16)
        mlp_terms = (
            jnp.einsum("nd,nf->df", rows_second, grad_pre, preferred_element_type=jnp.float32),
            jnp.einsum("nf,nd->fd", active, grad_rows, preferred_element_type=jnp.float32),
        )
        up_bias_term = jnp.sum(grad_pre, axis=0, dtype=jnp.float32)
        norm_terms = jnp.einsum("nf,df->nd", grad_pre, up_full, preferred_element_type=jnp.float32)
        up_bias_full = lax.dynamic_update_slice_in_dim(zero_units, up_bias_term, unit_start, 0)
        grad_norm_second = reduce_grads(norm_terms)
        grad_mid_norm, gain_second_term, shift_second_term = norm_backward(
            grad_norm_second, unit_second, scale_second, mlp_norm_gain
        )
        grad_middle = grad_out.astype(jnp.float32) + grad_mid_norm
        grad_branch = grad_middle.astype(jnp.bfloat16)
        branch_rows = gather_grads(grad_branch)
        grad_att = jnp.einsum(
            "nd,cd->nc", branch_rows, out_full, preferred_element_type=jnp.float32
        ).astype(jnp.bfloat16)
        out_term = jnp.einsum(
            "nc,nd->cd", att_rows, branch_rows, preferred_element_type=jnp.float32
        )
        grad_queries, grad_keys, grad_values = lax.map(
            attend_back,
            (
                queries.reshape(head_shape),
                keys_low.reshape(head_shape),
                values_low.reshape(head_shape),
                key_valid,
                log_total,
                grad_att.reshape(head_shape),
            ),
        )
        grad_queries = grad_queries.reshape(slot_count * seq_len, -1)
        grad_keys = grad_keys.reshape(slot_count * seq_len, -1)
        grad_values = grad_values.reshape(slot_count * seq_len, -1)
        attn_terms = (
            jnp.einsum("nd,nc->dc", rows_first, grad_queries, preferred_element_type=jnp.float32),
            jnp.einsum("nd,nc->dc", rows_first, grad_keys, preferred_element_type=jnp.float32),
            jnp.einsum("nd,nc->dc", rows_first, grad_values, preferred_element_type=jnp.float32),
            out_term,
        )
        first_terms = jnp.einsum(
            "nc,dc->nd", grad_queries, query_full, preferred_element_type=jnp.float32
        )
        first_terms = first_terms + jnp.einsum(
            "nc,dc->nd", grad_keys, key_full, preferred_element_type=jnp.float32
        )
        first_terms = first_terms + jnp.einsum(
            "nc,dc->nd", grad_values, value_full, preferred_element_type=jnp.float32
        )
        grad_norm_first = reduce_grads(first_terms)
        query_bias_full = lax.dynamic_update_slice_in_dim(
            zero_row, jnp.sum(grad_queries, axis=0, dtype=jnp.float32), col_start, 0
        )
        value_bias_full = lax.dynamic_update_slice_in_dim(
            zero_row, jnp.sum(grad_values, axis=0, dtype=jnp.float32), col_start, 0
        )
        grad_in_norm, gain_first_term, shift_first_term = norm_backward(
            grad_norm_first, unit_first, scale_first, attn_norm_gain
        )
        grad_parts.append(grad_middle + grad_in_norm)
        vector_terms = (
            gain_first_term,
            shift_first_term,
            query_bias_full,
            value_bias_full,
            jnp.sum(grad_branch, axis=0, dtype=jnp.float32),
            gain_second_term,
            shift_second_term,
            up_bias_full,
            jnp.sum(grad_out, axis=0, dtype=jnp.float32),
        )
        vector_running = add_up(vector_running, vector_terms)
        attn_running = add_up(attn_running, attention_grad_owned(attn_terms))
        mlp_running = add_up(mlp_running, mlp_grad_owned(mlp_terms))
    (
        gain_first_sum,
        shift_first_sum,
        query_bias_sum,
        value_bias_sum,
        out_bias_sum,
        gain_second_sum,
        shift_second_sum,
        up_bias_sum,
        down_bias_sum,
    ) = vector_running
    (
        gain_first_all,
        shift_first_all,
        query_bias_all,
        value_bias_all,
        out_bias_all,
        gain_second_all,
        shift_second_all,
        up_bias_all,
        down_bias_all,
    ) = lax.psum(
        (
            gain_first_sum,
            shift_first_sum,
            query_bias_sum,
            value_bias_sum,
            out_bias_sum,
            gain_second_sum,
            shift_second_sum,
            up_bias_sum,
            down_bias_sum,
        ),
        ("dp", "tensor"),
    )
    grad_b_query = lax.dynamic_slice_in_dim(query_bias_all, col_start, head_cols)
    grad_b_value = lax.dynamic_slice_in_dim(value_bias_all, col_start, head_cols)
    layer_out = jnp.stack(layer_parts, axis=0)
    input_grad = jnp.stack(grad_parts, axis=0)
    return (
        layer_out,
        input_grad,
        gain_first_all,
        shift_first_all,
        attn_running[0],
        grad_b_query,
        attn_running[1],
        attn_running[2],
        grad_b_value,
        attn_running[3],
        out_bias_all,
        gain_second_all,
        shift_second_all,
        mlp_running[0],
        up_bias_all,
        mlp_running[1],
        down_bias_all,
    )


def solution(mesh):
    placed = (
        P(None, ("dp", "tensor"), None),
        P(None, "dp", None),
        P(None, ("dp", "tensor"), None),
        P(),
        P(),
        P("dp", "tensor"),
        P(),
        P("dp", "tensor"),
        P("dp", "tensor"),
        P(),
        P("tensor", "dp"),
        P(),
        P(),
        P(),
        P("dp", "tensor"),
        P(),
        P("tensor", "dp"),
        P(),
    )
    return jax.shard_map(
        shards,
        mesh=mesh,
        in_specs=placed,
        out_specs=(
            P(None, ("dp", "tensor"), None),
            P(None, ("dp", "tensor"), None),
            P(),
            P(),
            P("dp", "tensor"),
            P("tensor"),
            P("dp", "tensor"),
            P("dp", "tensor"),
            P("tensor"),
            P("tensor", "dp"),
            P(),
            P(),
            P(),
            P("dp", "tensor"),
            P(),
            P("tensor", "dp"),
            P(),
        ),
        check_vma=False,
    )
```

profile of v0, /device:TPU:0, one launch (start us, length us, event | category | flops | bytes accessed | tf_op | source)
XLA Modules:
  0.0 3083.0 jit_solution(8633113333988774136)
XLA Ops:
  17.1 8.2 all-gather.3
  26.5 6.8 all-gather.4
  33.8 6.8 all-gather.2
  41.9 6.8 all-gather.5
  49.9 72.8 %all-gather.25.cloned.1.call-done = bf16[2944,1152]{1,0:T(8,128)(2,1)} async-done(((bf16[368,1152]{1,0:T(8,128)(2,1)}), bf16[2944,1152]{1,0:T(8,128)(2,1)}) %all-gather.25.cloned.1.call-update) | async-done | bytes 6782992 | tf_op jit(solution)/shard_map/all_gather | solution.py:116
  140.8 6.0 fusion.192
  153.4 20.2 while.53
  179.3 8.3 fusion.249
  187.7 40.6 %all-gather.17.cloned.1.call-done = bf16[2944,1152]{1,0:T(8,128)(2,1)} async-done(((bf16[368,1152]{1,0:T(8,128)(2,1)}), bf16[2944,1152]{1,0:T(8,128)(2,1)}) %all-gather.17.cloned.1.call-update) | async-done | bytes 6782992 | tf_op jit(solution)/shard_map/all_gather | solution.py:116
  228.2 6.0 fusion.191
  246.1 6.0 convolution_convert_fusion.3
  258.7 20.3 while.52
  285.1 8.3 fusion.247
  294.1 157.4 %reduce-scatter.41.cloned.1.call-done = f32[368,1152]{1,0:T(8,128)} async-done(((f32[2944,1152]{1,0:T(8,128)}), f32[368,1152]{1,0:T(8,128)}) %reduce-scatter.41.cloned.1.call-update) | async-done | bytes 1695760 | tf_op jit(solution)/shard_map/reduce_scatter | solution.py:120
  451.5 224.1 %reduce-scatter.37.cloned.1.call-done = f32[368,1152]{1,0:T(8,128)} async-done(((f32[2944,1152]{1,0:T(8,128)}), f32[368,1152]{1,0:T(8,128)}) %reduce-scatter.37.cloned.1.call-update) | async-done | bytes 1695760 | tf_op jit(solution)/shard_map/reduce_scatter | solution.py:120
  685.5 99.5 %all-gather.27.cloned.1.call-done = bf16[2944,1152]{1,0:T(8,128)(2,1)} async-done(((bf16[368,1152]{1,0:T(8,128)(2,1)}), bf16[2944,1152]{1,0:T(8,128)(2,1)}) %all-gather.27.cloned.1.call-update) | async-done | bytes 6782992 | tf_op jit(solution)/shard_map/all_gather | solution.py:116
  785.1 10.5 fusion.250
  795.6 8.0 all-gather.23.cloned.1.call-done
  803.7 107.0 %all-gather.35.cloned.1.call-done = bf16[1,2944,1152]{2,1,0:T(8,128)(2,1)} async-done(((bf16[1,368,1152]{2,1,0:T(8,128)(2,1)}), bf16[1,2944,1152]{2,1,0:T(8,128)(2,1)}) %all-gather.35.cloned.1.call-update) | async-done | bytes 6782992 | tf_op jit(solution)/shard_map/all_gather | solution.py:124
  910.6 13.4 convert_reduce_fusion
  925.7 8.8 fusion.253
  934.6 81.2 %all-gather.19.cloned.1.call-done = bf16[2944,1152]{1,0:T(8,128)(2,1)} async-done(((bf16[368,1152]{1,0:T(8,128)(2,1)}), bf16[2944,1152]{1,0:T(8,128)(2,1)}) %all-gather.19.cloned.1.call-update) | async-done | bytes 6782992 | tf_op jit(solution)/shard_map/all_gather | solution.py:116
  1015.8 10.2 fusion.248
  1025.9 95.0 %all-gather.33.cloned.1.call-done = bf16[1,2944,1152]{2,1,0:T(8,128)(2,1)} async-done(((bf16[1,368,1152]{2,1,0:T(8,128)(2,1)}), bf16[1,2944,1152]{2,1,0:T(8,128)(2,1)}) %all-gather.33.cloned.1.call-update) | async-done | bytes 6782992 | tf_op jit(solution)/shard_map/all_gather | solution.py:124
  1120.9 13.4 convert_reduce_fusion.1
  1136.0 8.7 fusion.251
  1146.1 12.0 fusion.238
  1158.3 12.5 fusion.239
  1170.8 173.0 %reduce-scatter.49.cloned.1.call-done = f32[368,1152]{1,0:T(8,128)} async-done(((f32[2944,1152]{1,0:T(8,128)}), f32[368,1152]{1,0:T(8,128)}) %reduce-scatter.49.cloned.1.call-update) | async-done | bytes 1695760 | tf_op jit(solution)/shard_map/reduce_scatter | solution.py:128
  1343.8 223.8 %reduce-scatter.45.cloned.1.call-done = f32[368,1152]{1,0:T(8,128)} async-done(((f32[2944,1152]{1,0:T(8,128)}), f32[368,1152]{1,0:T(8,128)}) %reduce-scatter.45.cloned.1.call-update) | async-done | bytes 1695760 | tf_op jit(solution)/shard_map/reduce_scatter | solution.py:128
  1571.5 219.9 %reduce-scatter.39.cloned.1.call-done = f32[368,1152]{1,0:T(8,128)} async-done(((f32[2944,1152]{1,0:T(8,128)}), f32[368,1152]{1,0:T(8,128)}) %reduce-scatter.39.cloned.1.call-update) | async-done | bytes 1695760 | tf_op jit(solution)/shard_map/reduce_scatter | solution.py:120
  1791.4 224.0 %reduce-scatter.43.cloned.1.call-done = f32[368,1152]{1,0:T(8,128)} async-done(((f32[2944,1152]{1,0:T(8,128)}), f32[368,1152]{1,0:T(8,128)}) %reduce-scatter.43.cloned.1.call-update) | async-done | bytes 1695760 | tf_op jit(solution)/shard_map/reduce_scatter | solution.py:120
  2015.4 6.7 convert_reduce_fusion.11
  2022.7 10.7 convolution_convert_fusion.4
  2033.7 9.7 convolution_convert_fusion.5
  2043.5 12.0 fusion.197
  2056.1 12.1 fusion.194
  2068.3 58.3 %all-gather.31.cloned.1.call-done = bf16[2944,1152]{1,0:T(8,128)(2,1)} async-done(((bf16[368,1152]{1,0:T(8,128)(2,1)}), bf16[2944,1152]{1,0:T(8,128)(2,1)}) %all-gather.31.cloned.1.call-update) | async-done | bytes 6782992 | tf_op jit(solution)/shard_map/all_gather | solution.py:124
  2132.2 99.8 %all-gather.29.cloned.1.call-done = bf16[2944,1152]{1,0:T(8,128)(2,1)} async-done(((bf16[368,1152]{1,0:T(8,128)(2,1)}), bf16[2944,1152]{1,0:T(8,128)(2,1)}) %all-gather.29.cloned.1.call-update) | async-done | bytes 6782992 | tf_op jit(solution)/shard_map/all_gather | solution.py:124
  2245.1 105.6 %while.54 = (s32[]{:T(128)}, bf16[4,736,2,72]{1,3,2,0:T(8,128)(2,1)S(1)}, bf16[4,736,2,72]{1,3,2,0:T(8,128)(2,1)}, bf16[4,736,2,72]{1,3,2,0:T(8,128)(2,1)S(1)}, ...) while((s32[]{:T(128)}, ...), condition=%wide.region_25.26_spmd, body=%wide.region_23.25_spmd.sunk | while | flops 795532800 | bytes 68938456 | solution.py:311
  2255.7 8.3 fusion.375
  2264.1 7.5 fusion.374
  2282.2 8.2 fusion.375
  2290.4 7.5 fusion.374
  2308.6 8.2 fusion.375
  2316.8 7.5 fusion.374
  2334.9 8.2 fusion.375
  2343.1 7.5 fusion.374
  2381.1 105.2 %while.55 = (s32[]{:T(128)}, bf16[4,736,2,72]{1,3,2,0:T(8,128)(2,1)S(1)}, bf16[4,736,2,72]{1,3,2,0:T(8,128)(2,1)}, bf16[4,736,2,72]{1,3,2,0:T(8,128)(2,1)S(1)}, ...) while((s32[]{:T(128)}, ...), condition=%wide.region_34.35_spmd, body=%wide.region_32.34_spmd.sunk | while | flops 795532800 | bytes 68938456 | solution.py:311
  2391.6 8.2 fusion.389
  2399.8 7.6 fusion.388
  2417.9 8.3 fusion.389
  2426.3 7.6 fusion.388
  2444.3 8.2 fusion.389
  2452.6 7.5 fusion.388
  2470.6 8.2 fusion.389
  2478.8 7.5 fusion.388
  2517.2 7.1 fusion.254
  2524.3 12.0 convolution_add_fusion.1
  2536.5 12.0 convolution_add_fusion
  2555.6 8.3 convolution_add_fusion.2
  2599.5 200.1 %reduce-scatter.51.cloned.1.call-done = f32[368,1152]{1,0:T(8,128)} async-done(((f32[2944,1152]{1,0:T(8,128)}), f32[368,1152]{1,0:T(8,128)}) %reduce-scatter.51.cloned.1.call-update) | async-done | bytes 1695760 | tf_op jit(solution)/shard_map/reduce_scatter | solution.py:128
  2799.6 224.0 %reduce-scatter.47.cloned.1.call-done = f32[368,1152]{1,0:T(8,128)} async-done(((f32[2944,1152]{1,0:T(8,128)}), f32[368,1152]{1,0:T(8,128)}) %reduce-scatter.47.cloned.1.call-update) | async-done | bytes 1695760 | tf_op jit(solution)/shard_map/reduce_scatter | solution.py:128
  3027.1 41.8 %all-reduce = (f32[1152]{0:T(1024)}, f32[1152]{0:T(1024)}, f32[1152]{0:T(1024)S(1)}, f32[1152]{0:T(1024)S(1)}, f32[1152]{0:T(1024)}, /*index=5*/f32[1152]{0:T(10...) all-reduce(f32[1152]{0:T(1024)S(1)} %add.393, ...), channel_id=1, replica_groups=mesh['dp'=4,'tensor'=8] {'dp','tensor'}, use_global_device_ids=true, to_apply=%region_40.41 | all-reduce | flops 13520 | bytes 108160 | tf_op jit(solution)/shard_map/psum | solution.py:386
  (452 shorter events, 345.2 us)
Async XLA Ops:
  8.0 114.7 %all-gather.25.cloned.1.call-start = ((), (), s32[]{:S(2)}) async-start(), calls=%async_computation.26 | async-start | bytes 7630848 | tf_op jit(solution)/shard_map/all_gather | solution.py:116
  9.9 16.5 copy-start.44
  9.9 16.5 copy-start.46
  9.9 16.5 copy-start.39
  12.0 14.4 copy-start.50
  12.0 14.4 copy-start.51
  12.1 21.8 copy-start.40
  14.7 27.2 copy-start.41
  14.7 213.5 %all-gather.17.cloned.1.call-start = ((), (), s32[]{:S(2)}) async-start(), calls=%async_computation.20 | async-start | bytes 7630848 | tf_op jit(solution)/shard_map/all_gather | solution.py:116
  15.5 34.5 %copy-start.60 = (s32[2,4,736]{2,1,0:T(4,128)S(1)}, s32[2,4,736]{2,1,0:T(4,128)}, u32[]{:S(2)}) copy-start(s32[2,4,736]{2,1,0:T(4,128)} %param.27) | copy-start | bytes 70660
  15.5 436.0 %reduce-scatter.41.cloned.1.call-start = ((), (), s32[]{:S(2)}) async-start(), calls=%async_computation.27 | async-start | bytes 15261696 | tf_op jit(solution)/shard_map/reduce_scatter | solution.py:120
  33.8 94.9 %copy-start.27 = (bf16[1152,144]{0,1:T(8,128)(2,1)}, bf16[1152,144]{0,1:T(8,128)(2,1)S(1)}, u32[]{:S(2)}) copy-start(bf16[1152,144]{0,1:T(8,128)(2,1)S(1)} %reshape.296) | copy-start | bytes 995332
  173.6 13.9 copy-start.23
  173.6 13.9 copy-start.34
  187.6 40.7 %copy-start.30 = (bf16[1152,144]{0,1:T(8,128)(2,1)S(1)}, bf16[1152,144]{0,1:T(8,128)(2,1)}, u32[]{:S(2)}) copy-start(bf16[1152,144]{0,1:T(8,128)(2,1)} %reshape.294) | copy-start | bytes 995332
  187.6 488.0 %reduce-scatter.37.cloned.1.call-start = ((), (), s32[]{:S(2)}) async-start(), calls=%async_computation.21 | async-start | bytes 15261696 | tf_op jit(solution)/shard_map/reduce_scatter | solution.py:120
  279.1 14.3 copy-start.25
  279.1 14.3 copy-start.35
  279.1 14.3 copy-start.37
  293.4 382.2 %copy-start.63 = (f32[1152]{0:T(1024)S(1)}, f32[1152]{0:T(1024)}, u32[]{:S(2)}) copy-start(f32[1152]{0:T(1024)} %param.37) | copy-start | bytes 13828
  293.5 392.1 %all-gather.21.cloned.1.call-start = ((), (), s32[]{:S(2)}) async-start(), calls=%async_computation.23 | async-start | bytes 1843200 | tf_op jit(solution)/shard_map/all_gather | solution.py:109
  294.0 385.3 %copy-start.42 = (f32[1152]{0:T(1024)S(1)}, f32[1152]{0:T(1024)}, u32[]{:S(2)}) copy-start(f32[1152]{0:T(1024)} %param.38) | copy-start | bytes 13828
  294.0 385.3 %copy-start.62 = (f32[1152]{0:T(1024)S(1)}, f32[1152]{0:T(1024)}, u32[]{:S(2)}) copy-start(f32[1152]{0:T(1024)} %param.39) | copy-start | bytes 13828
  294.1 491.0 %all-gather.27.cloned.1.call-start = ((), (), s32[]{:S(2)}) async-start(), calls=%async_computation.28 | async-start | bytes 7630848 | tf_op jit(solution)/shard_map/all_gather | solution.py:116
  681.2 122.5 %all-gather.23.cloned.1.call-start = ((), (), s32[]{:S(2)}) async-start(), calls=%async_computation.24 | async-start | bytes 1843200 | tf_op jit(solution)/shard_map/all_gather | solution.py:110
  681.7 228.9 %all-gather.35.cloned.1.call-start = ((), (), s32[]{:S(2)}) async-start(), calls=%async_computation.41 | async-start | bytes 7630848 | tf_op jit(solution)/shard_map/all_gather | solution.py:124
  683.2 332.6 %all-gather.19.cloned.1.call-start = ((), (), s32[]{:S(2)}) async-start(), calls=%async_computation.22 | async-start | bytes 7630848 | tf_op jit(solution)/shard_map/all_gather | solution.py:116
  684.0 436.9 %all-gather.33.cloned.1.call-start = ((), (), s32[]{:S(2)}) async-start(), calls=%async_computation.40 | async-start | bytes 7630848 | tf_op jit(solution)/shard_map/all_gather | solution.py:124
  684.7 659.1 %reduce-scatter.49.cloned.1.call-start = ((), (), s32[]{:S(2)}) async-start(), calls=%async_computation.33 | async-start | bytes 15261696 | tf_op jit(solution)/shard_map/reduce_scatter | solution.py:128
  795.6 130.1 %copy-start.66 = (bf16[1152,538]{1,0:T(8,128)(2,1)S(1)}, bf16[1152,538]{1,0:T(8,128)(2,1)}, u32[]{:S(2)}) copy-start(bf16[1152,538]{1,0:T(8,128)(2,1)} %all-gather.21.cloned.1.call-done) | copy-start | bytes 3718660
  934.5 633.1 %reduce-scatter.45.cloned.1.call-start = ((), (), s32[]{:S(2)}) async-start(), calls=%async_computation.30 | async-start | bytes 15261696 | tf_op jit(solution)/shard_map/reduce_scatter | solution.py:128
  1144.8 646.6 %reduce-scatter.39.cloned.1.call-start = ((), (), s32[]{:S(2)}) async-start(), calls=%async_computation.25 | async-start | bytes 15261696 | tf_op jit(solution)/shard_map/reduce_scatter | solution.py:120
  1158.2 857.2 %reduce-scatter.43.cloned.1.call-start = ((), (), s32[]{:S(2)}) async-start(), calls=%async_computation.29 | async-start | bytes 15261696 | tf_op jit(solution)/shard_map/reduce_scatter | solution.py:120
  1170.7 396.9 %copy-start.5 = (f32[368,1152]{1,0:T(8,128)S(1)}, f32[368,1152]{1,0:T(8,128)}, u32[]{:S(2)}) copy-start(f32[368,1152]{1,0:T(8,128)} %copy-done.4) | copy-start | bytes 5087236
  1170.7 844.6 %copy-start.61 = (f32[1152]{0:T(1024)S(1)}, f32[1152]{0:T(1024)}, u32[]{:S(2)}) copy-start(f32[1152]{0:T(1024)} %param.43) | copy-start | bytes 13828
  1170.8 955.8 %all-gather.31.cloned.1.call-start = ((), (), s32[]{:S(2)}) async-start(), calls=%async_computation.34 | async-start | bytes 7630848 | tf_op jit(solution)/shard_map/all_gather | solution.py:124
  2022.1 209.8 %all-gather.29.cloned.1.call-start = ((), (), s32[]{:S(2)}) async-start(), calls=%async_computation.31 | async-start | bytes 7630848 | tf_op jit(solution)/shard_map/all_gather | solution.py:124
  2022.7 543.9 %reduce-scatter.55.cloned.1.call-start = ((), (), s32[]{:S(2)}) async-start(), calls=%async_computation.37 | async-start | bytes 1843200 | tf_op jit(solution)/shard_map/reduce_scatter | solution.py:152
  2033.5 533.1 %reduce-scatter.53.cloned.1.call-start = ((), (), s32[]{:S(2)}) async-start(), calls=%async_computation.36 | async-start | bytes 1843200 | tf_op jit(solution)/shard_map/reduce_scatter | solution.py:152
  2043.5 525.2 %reduce-scatter.59.cloned.1.call-start = ((), (), s32[]{:S(2)}) async-start(), calls=%async_computation.39 | async-start | bytes 1843200 | tf_op jit(solution)/shard_map/reduce_scatter | solution.py:155
  2055.6 71.0 %copy-start.11 = (bf16[2944,144]{0,1:T(8,128)(2,1)S(1)}, bf16[2944,144]{0,1:T(8,128)(2,1)}, u32[]{:S(2)}) copy-start(bf16[2944,144]{0,1:T(8,128)(2,1)} %copy-done.10) | copy-start | bytes 2543620
  2055.6 513.1 %reduce-scatter.57.cloned.1.call-start = ((), (), s32[]{:S(2)}) async-start(), calls=%async_computation.38 | async-start | bytes 1843200 | tf_op jit(solution)/shard_map/reduce_scatter | solution.py:155
  2068.2 511.8 %reduce-scatter.75.cloned.1.call-start = ((), (), s32[]{:S(2)}) async-start(), calls=%async_computation.49 | async-start | bytes 737280
  2068.2 163.7 %copy-start.32 = (bf16[1152,144]{0,1:T(8,128)(2,1)S(1)}, bf16[1152,144]{0,1:T(8,128)(2,1)}, u32[]{:S(2)}) copy-start(bf16[1152,144]{0,1:T(8,128)(2,1)} %reshape.298) | copy-start | bytes 995332
  2132.1 106.3 %copy-start.13 = (bf16[2944,144]{0,1:T(8,128)(2,1)S(1)}, bf16[2944,144]{0,1:T(8,128)(2,1)}, u32[]{:S(2)}) copy-start(bf16[2944,144]{0,1:T(8,128)(2,1)} %copy-done.12) | copy-start | bytes 2543620
  2132.1 449.1 %reduce-scatter.73.cloned.1.call-start = ((), (), s32[]{:S(2)}) async-start(), calls=%async_computation.48 | async-start | bytes 737280
  2243.7 339.1 %reduce-scatter.61.cloned.1.call-start = ((), (), s32[]{:S(2)}) async-start(), calls=%async_computation.42 | async-start | bytes 737280
  2350.7 22.1 copy-start.19
  2359.3 225.2 %reduce-scatter.65.cloned.1.call-start = ((), (), s32[]{:S(2)}) async-start(), calls=%async_computation.44 | async-start | bytes 737280
  2366.3 219.9 %reduce-scatter.69.cloned.1.call-start = ((), (), s32[]{:S(2)}) async-start(), calls=%async_computation.46 | async-start | bytes 737280
  2379.7 208.2 %reduce-scatter.63.cloned.1.call-start = ((), (), s32[]{:S(2)}) async-start(), calls=%async_computation.43 | async-start | bytes 737280
  2505.7 83.8 %reduce-scatter.67.cloned.1.call-start = ((), (), s32[]{:S(2)}) async-start(), calls=%async_computation.45 | async-start | bytes 737280
  2524.3 66.9 %reduce-scatter.71.cloned.1.call-start = ((), (), s32[]{:S(2)}) async-start(), calls=%async_computation.47 | async-start | bytes 737280
  2536.4 263.2 %reduce-scatter.51.cloned.1.call-start = ((), (), s32[]{:S(2)}) async-start(), calls=%async_computation.35 | async-start | bytes 15261696 | tf_op jit(solution)/shard_map/reduce_scatter | solution.py:128
  2548.5 475.2 %reduce-scatter.47.cloned.1.call-start = ((), (), s32[]{:S(2)}) async-start(), calls=%async_computation.32 | async-start | bytes 15261696 | tf_op jit(solution)/shard_map/reduce_scatter | solution.py:128
  2575.3 448.3 %copy-start.3 = (bf16[2,368,1152]{2,1,0:T(8,128)(2,1)S(1)}, bf16[2,368,1152]{2,1,0:T(8,128)(2,1)}, u32[]{:S(2)}) copy-start(bf16[2,368,1152]{2,1,0:T(8,128)(2,1)} %param.26) | copy-start | bytes 5087236
  2575.3 448.3 %copy-start.43 = (f32[1152]{0:T(1024)S(1)}, f32[1152]{0:T(1024)}, u32[]{:S(2)}) copy-start(f32[1152]{0:T(1024)} %param.29) | copy-start | bytes 13828
  2575.3 448.3 %copy-start.45 = (f32[368]{0:T(512)S(1)}, f32[368]{0:T(512)}, u32[]{:S(2)}) copy-start(f32[368]{0:T(512)} %copy-done.44) | copy-start | bytes 4420
  2575.3 448.3 %copy-start.47 = (f32[368]{0:T(512)S(1)}, f32[368]{0:T(512)}, u32[]{:S(2)}) copy-start(f32[368]{0:T(512)} %copy-done.46) | copy-start | bytes 4420
  2580.0 490.2 %copy-start.21 = (f32[368,1152]{1,0:T(8,128)S(1)}, f32[368,1152]{1,0:T(8,128)}, u32[]{:S(2)}) copy-start(f32[368,1152]{1,0:T(8,128)} %get-tuple-element.419) | copy-start | bytes 5087236
  2594.5 432.6 %copy-start.56 = (f32[1152]{0:T(1024)S(1)}, f32[1152]{0:T(1024)}, u32[]{:S(2)}) copy-start(f32[1152]{0:T(1024)} %add.407) | copy-start | bytes 13828
  2594.5 432.6 %copy-start.57 = (f32[1152]{0:T(1024)S(1)}, f32[1152]{0:T(1024)}, u32[]{:S(2)}) copy-start(f32[1152]{0:T(1024)} %add.402) | copy-start | bytes 13828
  2594.5 432.6 %copy-start.58 = (f32[1152]{0:T(1024)S(1)}, f32[1152]{0:T(1024)}, u32[]{:S(2)}) copy-start(f32[1152]{0:T(1024)} %add.401) | copy-start | bytes 13828
  2594.5 432.7 %copy-start.59 = (f32[1152]{0:T(1024)S(1)}, f32[1152]{0:T(1024)}, u32[]{:S(2)}) copy-start(f32[1152]{0:T(1024)} %add.403) | copy-start | bytes 13828
  (43 other events, 227.3 us)
Sparse Core Ops, SparseCore 0:
  14.8 107.8 all-gather.24
  124.9 103.2 all-gather.16
  231.8 219.6 reduce-scatter.40
  455.0 220.6 reduce-scatter.36
  2022.2 104.2 all-gather.30
  2128.6 103.2 all-gather.28
Sparse Core Ops, SparseCore 1:
  295.5 17.6 all-gather.20
  681.3 103.8 all-gather.26
  786.5 17.1 all-gather.22
  805.9 104.7 all-gather.34
  912.8 102.9 all-gather.18
  1018.0 102.9 all-gather.32
  1124.4 219.4 reduce-scatter.48
  1347.2 220.3 reduce-scatter.44
  1571.0 220.3 reduce-scatter.38
  1795.0 220.3 reduce-scatter.42
  2033.6 26.6 reduce-scatter.54
  2063.6 27.5 reduce-scatter.52
  2093.5 27.4 reduce-scatter.58
  2123.8 27.4 reduce-scatter.56
  2153.8 21.9 reduce-scatter.74
  2243.8 20.1 reduce-scatter.72
  2359.3 20.0 reduce-scatter.60
  2382.0 22.0 reduce-scatter.64
  2406.3 22.0 reduce-scatter.68
  2505.8 20.3 reduce-scatter.62
  2528.5 22.0 reduce-scatter.66
  2552.9 22.0 reduce-scatter.70
  2578.4 221.2 reduce-scatter.50
  2803.3 220.3 reduce-scatter.46
where the time goes:
time: 3090 us; the launch traced here: 3080 us
  waiting for transfers between devices  2310 us (75%)
  matrix products  493 us (16%)
  local copies, waits for them, and re-layouts  121 us (4%)
  blocking collectives  70.5 us (2%)
  other arithmetic  65 us (2%)
    reduce_scatter x4, waiting for transfers between devices, reduce_rows(): return lax.psum_scatter(values, 'tensor', scatter_dimension=0, tiled=True)  825 us
    reduce_scatter x4, waiting for transfers between devices, reduce_grads(): return lax.psum_scatter(values, 'tensor', scatter_dimension=0, tiled=True)  821 us
    all_gather x4, waiting for transfers between devices, gather_grads(): return lax.all_gather(values, 'tensor', axis=0, tiled=True)  360 us
    all_gather x4, waiting for transfers between devices, gather_rows(): return lax.all_gather(values, 'tensor', axis=0, tiled=True)  294 us
    dot_general x8, matrix products, attend_back(): jnp.einsum('hlm,lhe->mhe', grad_raw, queries, preferred_element_type=jnp....  66 us
  transfers between devices with their start and end apart: 30, of which 17 were waited for; matrix products, arithmetic and copies ran while one was open for 20% of the time, Pallas kernels for 0%

commit v1 on v0

v1 whole, which is shorter than its diff:
```python
from functools import partial

import jax
import jax.numpy as jnp
from jax import lax
from jax.experimental import pallas as pl
from jax.experimental.pallas import tpu as pltpu
from jax.sharding import PartitionSpec as P

HEAD_DIM = 72
norm_eps = 1e-06
masked_score = -1000000000.0
low = jnp.bfloat16
wide = jnp.float32
score_scale = HEAD_DIM**-0.5
log2_e = 1.4426950408889634
gelu_scale = 0.7978845608028654
gelu_cube = 0.044715
everyone = ("dp", "tensor")


def product(left, right, left_dim, right_dim):
    return lax.dot_general(
        left, right, (((left_dim,), (right_dim,)), ((), ())), preferred_element_type=wide
    )


def norm_stats(values):
    row_mean = jnp.mean(values, axis=-1, keepdims=True)
    centred = values - row_mean
    inv_scale = lax.rsqrt(jnp.mean(centred * centred, axis=-1, keepdims=True) + norm_eps)
    return centred * inv_scale, inv_scale


def norm_backward(grad_rows, unit_rows, inv_scale, norm_gain):
    grad_unit = grad_rows * norm_gain
    mean_grad = jnp.mean(grad_unit, axis=-1, keepdims=True)
    mean_along = jnp.mean(grad_unit * unit_rows, axis=-1, keepdims=True)
    grad_values = inv_scale * (grad_unit - mean_grad - unit_rows * mean_along)
    return (grad_values, jnp.sum(grad_rows * unit_rows, axis=0), jnp.sum(grad_rows, axis=0))


def attend_kernel(heads, query_ref, key_ref, value_ref, bias_ref, out_ref, total_ref):
    for head in range(heads):
        rows = slice(head * HEAD_DIM, (head + 1) * HEAD_DIM)
        scores = product(key_ref[rows, :], query_ref[rows, :], 0, 0) * (score_scale * log2_e)
        scores = scores + bias_ref[...]
        top = jnp.max(scores, axis=0, keepdims=True)
        weights = jnp.exp2(scores - top)
        total = jnp.sum(weights, axis=0, keepdims=True)
        mixed = product(value_ref[rows, :], weights.astype(low), 1, 0)
        out_ref[rows, :] = (mixed * (1.0 / total)).astype(low)
        total_ref[head] = top + jnp.log2(total)


def attend_back_kernel(
    heads,
    query_ref,
    key_ref,
    value_ref,
    bias_ref,
    out_ref,
    total_ref,
    grad_ref,
    grad_query_ref,
    grad_key_ref,
    grad_value_ref,
):
    for head in range(heads):
        rows = slice(head * HEAD_DIM, (head + 1) * HEAD_DIM)
        query, key, value, grad = (
            query_ref[rows, :],
            key_ref[rows, :],
            value_ref[rows, :],
            grad_ref[rows, :],
        )
        scores = product(key, query, 0, 0) * (score_scale * log2_e) + bias_ref[...]
        probs = jnp.exp2(scores - total_ref[head])
        grad_probs = product(value, grad, 0, 0)
        along = jnp.sum(
            grad.astype(wide) * out_ref[rows, :].astype(wide), axis=0, keepdims=True
        )
        grad_raw = (probs * (grad_probs - along)).astype(low)
        grad_value_ref[rows, :] = product(grad, probs.astype(low), 1, 1).astype(low)
        grad_query_ref[rows, :] = (product(key, grad_raw, 1, 0) * score_scale).astype(low)
        grad_key_ref[rows, :] = (product(query, grad_raw, 1, 1) * score_scale).astype(low)


def attend(projected, bias, heads, step_heads):
    tokens = projected.shape[1]
    steps = heads // step_heads
    part = lambda place: pl.BlockSpec(
        (HEAD_DIM * step_heads, tokens), lambda i, place=place: (place * steps + i, 0)
    )
    return pl.pallas_call(
        partial(attend_kernel, step_heads),
        grid=(steps,),
        in_specs=[part(0), part(1), part(2), pl.BlockSpec((tokens, 1), lambda i: (0, 0))],
        out_specs=[part(0), pl.BlockSpec((step_heads, 1, tokens), lambda i: (i, 0, 0))],
        out_shape=[
            jax.ShapeDtypeStruct((heads * HEAD_DIM, tokens), low),
            jax.ShapeDtypeStruct((heads, 1, tokens), wide),
        ],
        compiler_params=pltpu.CompilerParams(vmem_limit_bytes=48 * 2**20),
        cost_estimate=pl.CostEstimate(
            flops=heads * tokens * tokens * 1024, bytes_accessed=16 * 2**20, transcendentals=0
        ),
        name="attend",
    )(projected, projected, projected, bias)


def attend_back(projected, bias, attended, total, grad, heads, step_heads):
    tokens = projected.shape[1]
    steps = heads // step_heads
    part = lambda place: pl.BlockSpec(
        (HEAD_DIM * step_heads, tokens), lambda i, place=place: (place * steps + i, 0)
    )
    return pl.pallas_call(
        partial(attend_back_kernel, step_heads),
        grid=(steps,),
        in_specs=[
            part(0),
            part(1),
            part(2),
            pl.BlockSpec((tokens, 1), lambda i: (0, 0)),
            part(0),
            pl.BlockSpec((step_heads, 1, tokens), lambda i: (i, 0, 0)),
            part(0),
        ],
        out_specs=[part(0)] * 3,
        out_shape=[jax.ShapeDtypeStruct((heads * HEAD_DIM, tokens), low)] * 3,
        compiler_params=pltpu.CompilerParams(vmem_limit_bytes=48 * 2**20),
        cost_estimate=pl.CostEstimate(
            flops=heads * tokens * tokens * 2048, bytes_accessed=16 * 2**20, transcendentals=0
        ),
        name="attend_back",
    )(projected, projected, projected, bias, attended, total, grad)


def mlp_kernel(
    normed_ref,
    grad_ref,
    up_ref,
    down_ref,
    bias_ref,
    out_ref,
    grad_normed_ref,
    grad_up_ref,
    grad_down_ref,
    grad_bias_ref,
):
    step = pl.program_id(0)
    normed, grad = normed_ref[...], grad_ref[...]
    up, down = up_ref[...], down_ref[...]
    pre_act = product(up, normed, 1, 1) + bias_ref[...]
    square = pre_act * pre_act
    bent = jnp.tanh(gelu_scale * (pre_act + gelu_cube * square * pre_act))
    half = 0.5 * (1.0 + bent)
    active = (pre_act * half).astype(low)
    slope = half + 0.5 * pre_act * (1.0 - bent * bent) * (
        gelu_scale * (1.0 + 3.0 * gelu_cube * square)
    )
    grad_wide = product(down, grad, 1, 1) * slope
    grad_pre = grad_wide.astype(low)
    grad_bias_ref[...] = jnp.sum(grad_wide, axis=1, keepdims=True)
    grad_down_ref[...] = product(active, grad, 1, 0).astype(low)
    grad_up_ref[...] = product(grad_pre, normed, 1, 0).astype(low)
    out_term = product(active, down, 0, 0)
    normed_term = product(grad_pre, up, 0, 0)

    @pl.when(step == 0)
    def first():
        out_ref[...] = out_term
        grad_normed_ref[...] = normed_term

    @pl.when(step > 0)
    def later():
        out_ref[...] += out_term
        grad_normed_ref[...] += normed_term


def mlp(normed, grad, up, down, bias, block):
    tokens, width = normed.shape
    units = up.shape[0]
    whole = pl.BlockSpec((tokens, width), lambda i: (0, 0))
    rows = pl.BlockSpec((block, width), lambda i: (i, 0))
    column = pl.BlockSpec((block, 1), lambda i: (i, 0))
    return pl.pallas_call(
        mlp_kernel,
        grid=(units // block,),
        in_specs=[whole, whole, rows, rows, column],
        out_specs=[whole, whole, rows, rows, column],
        out_shape=[
            jax.ShapeDtypeStruct((tokens, width), wide),
            jax.ShapeDtypeStruct((tokens, width), wide),
            jax.ShapeDtypeStruct((units, width), low),
            jax.ShapeDtypeStruct((units, width), low),
            jax.ShapeDtypeStruct((units, 1), wide),
        ],
        compiler_params=pltpu.CompilerParams(vmem_limit_bytes=60 * 2**20),
        cost_estimate=pl.CostEstimate(
            flops=16 * tokens * width * units, bytes_accessed=64 * 2**20, transcendentals=0
        ),
        name="mlp",
    )(normed, grad, up, down, bias)


def gather_slab(pieces, dp_count):
    rows, part = pieces.shape
    owned = lax.all_to_all(
        pieces.reshape(dp_count, rows // dp_count, part), "dp", 0, 2, tiled=True
    )
    return lax.all_gather(owned[0], everyone, axis=0, tiled=True)


def scatter_slab(terms, dp_count):
    owned = lax.psum_scatter(terms, everyone, scatter_dimension=0, tiled=True)
    rows, width = owned.shape
    back = lax.all_to_all(owned[None], "dp", 2, 0, tiled=True)
    return back.reshape(dp_count * rows, width // dp_count).astype(wide)


def shards(
    dp_count,
    tensor_count,
    inputs,
    pad_mask,
    cotangent,
    attn_norm_gain,
    attn_norm_shift,
    w_query,
    b_query,
    w_key,
    w_value,
    b_value,
    w_out,
    b_out,
    mlp_norm_gain,
    mlp_norm_shift,
    w_up,
    b_up,
    w_down,
    b_down,
):
    half_rows, width = inputs.shape[1:]
    head_cols = w_query.shape[1]
    unit_cols = w_up.shape[1]
    heads = head_cols * tensor_count // HEAD_DIM
    quantum = 8 * dp_count
    slab_units = -(-unit_cols // quantum) * quantum
    tensor_place = lax.axis_index("tensor")
    col_start = tensor_place * head_cols
    side = tensor_place % 2
    pairs = [(place, place ^ 1) for place in range(tensor_count)]

    def swap(values):
        return lax.ppermute(values, "tensor", pairs)

    def one_slot(values):
        kept = lax.dynamic_index_in_dim(values, side, 0, keepdims=False)
        sent = lax.dynamic_index_in_dim(values, 1 - side, 0, keepdims=False)
        return jnp.concatenate([kept, swap(sent)], axis=0)

    def both_micros(values):
        kept = values[:half_rows]
        other = swap(values[half_rows:].astype(low)).astype(values.dtype)
        return jnp.where(side == 0, jnp.stack([kept, other]), jnp.stack([other, kept]))

    def slab_order(values):
        padded = jnp.pad(
            values.reshape(tensor_count, unit_cols), ((0, 0), (0, slab_units - unit_cols))
        )
        return padded.reshape(tensor_count, dp_count, -1).transpose(1, 0, 2).reshape(-1)

    def unit_order(values):
        slabs = values.reshape(dp_count, tensor_count, -1).transpose(1, 0, 2)
        return slabs.reshape(tensor_count, slab_units)[:, :unit_cols].reshape(-1)

    x_slot = one_slot(inputs).astype(wide)
    grad_out = one_slot(cotangent)
    mask_row = lax.dynamic_slice(
        pad_mask, (side, tensor_place // 2, 0), (1, 1, 2 * half_rows)
    ).reshape(2, half_rows)
    mask_row = jnp.where(side == 0, mask_row, mask_row[::-1]).reshape(2 * half_rows, 1)
    bias_col = jnp.where(mask_row > 0, 0.0, masked_score).astype(wide)

    attn_rows = gather_slab(
        jnp.concatenate([w_query.T, w_key.T, w_value.T, w_out], axis=0), dp_count
    )
    kinds = attn_rows.reshape(4, dp_count // 4, tensor_count, -1, width)
    kinds = kinds.transpose(0, 2, 1, 3, 4).reshape(4, -1, width)
    qkv_rows = kinds[:3].reshape(-1, width)
    out_rows = kinds[3]
    unit_pad = ((0, slab_units - unit_cols), (0, 0))
    up_rows = gather_slab(jnp.pad(w_up.T, unit_pad), dp_count)
    down_rows = gather_slab(jnp.pad(w_down, unit_pad), dp_count)

    unit_first, scale_first = norm_stats(x_slot)
    normed_first = (unit_first * attn_norm_gain + attn_norm_shift).astype(low)
    qkv_bias = jnp.concatenate([b_query, jnp.zeros_like(b_query), b_value])
    projected = (product(qkv_rows, normed_first, 1, 1) + qkv_bias[:, None]).astype(low)
    attended, total = attend(projected, bias_col, heads, 4)
    middle = x_slot + (product(attended, out_rows, 0, 0) + b_out)
    unit_second, scale_second = norm_stats(middle)
    normed_second = (unit_second * mlp_norm_gain + mlp_norm_shift).astype(low)
    down_out, grad_normed_second, grad_up, grad_down, grad_up_bias = mlp(
        normed_second,
        grad_out,
        up_rows,
        down_rows,
        slab_order(b_up)[:, None],
        8 * (slab_units // 8),
    )
    layer_out = both_micros((middle + (down_out + b_down)).astype(low))
    grad_w_up = scatter_slab(grad_up, dp_count)[:unit_cols].T
    grad_w_down = scatter_slab(grad_down, dp_count)[:unit_cols]

    grad_mid_norm, gain_second, shift_second = norm_backward(
        grad_normed_second, unit_second, scale_second, mlp_norm_gain
    )
    grad_wide = grad_out.astype(wide)
    grad_middle = grad_wide + grad_mid_norm
    grad_branch = grad_middle.astype(low)
    grad_attended = product(out_rows, grad_branch, 1, 1).astype(low)
    grad_out_rows = product(attended, grad_branch, 1, 0).astype(low)
    grad_query, grad_key, grad_value = attend_back(
        projected, bias_col, attended, total, grad_attended, heads, 4
    )
    grad_projected = jnp.concatenate([grad_query, grad_key, grad_value], axis=0)
    grad_qkv_rows = product(grad_projected, normed_first, 1, 0).astype(low)
    grad_normed_first = product(grad_projected, qkv_rows, 0, 0)
    grad_in_norm, gain_first, shift_first = norm_backward(
        grad_normed_first, unit_first, scale_first, attn_norm_gain
    )
    input_grad = both_micros(grad_middle + grad_in_norm)
    grad_kinds = jnp.concatenate([grad_qkv_rows, grad_out_rows], axis=0)
    grad_kinds = grad_kinds.reshape(4, tensor_count, dp_count // 4, -1, width)
    grad_kinds = grad_kinds.transpose(0, 2, 1, 3, 4).reshape(-1, width)
    attn_owned = scatter_slab(grad_kinds, dp_count).reshape(4, head_cols, -1)

    vectors = [
        gain_first,
        shift_first,
        jnp.sum(grad_query, axis=1, dtype=wide),
        jnp.sum(grad_value, axis=1, dtype=wide),
        jnp.sum(grad_branch, axis=0, dtype=wide),
        gain_second,
        shift_second,
        jnp.sum(grad_wide, axis=0),
        grad_up_bias[:, 0],
    ]
    summed = lax.psum(jnp.concatenate(vectors), everyone)
    small = [summed[i * width : (i + 1) * width] for i in range(8)]
    return (
        layer_out,
        input_grad,
        small[0],
        small[1],
        attn_owned[0].T,
        lax.dynamic_slice_in_dim(small[2], col_start, head_cols),
        attn_owned[1].T,
        attn_owned[2].T,
        lax.dynamic_slice_in_dim(small[3], col_start, head_cols),
        attn_owned[3],
        small[4],
        small[5],
        small[6],
        grad_w_up,
        unit_order(summed[8 * width :]),
        grad_w_down,
        small[7],
    )


def solution(mesh):
    tokens = P(None, ("dp", "tensor"), None)
    columns = P("dp", "tensor")
    rows = P("tensor", "dp")
    return jax.shard_map(
        partial(shards, mesh.shape["dp"], mesh.shape["tensor"]),
        mesh=mesh,
        in_specs=(
            tokens,
            P(None, "dp", None),
            tokens,
            P(),
            P(),
            columns,
            P(),
            columns,
            columns,
            P(),
            rows,
            P(),
            P(),
            P(),
            columns,
            P(),
            rows,
            P(),
        ),
        out_specs=(
            tokens,
            tokens,
            P(),
            P(),
            columns,
            P("tensor"),
            columns,
            columns,
            P("tensor"),
            rows,
            P(),
            P(),
            P(),
            columns,
            P(),
            rows,
            P(),
        ),
        check_vma=False,
    )
```

time: 3090 us -> 825 us (0.27)
  waiting for transfers between devices: 2310 us -> 417 us
  matrix products: 493 us -> 48.6 us
  Pallas kernels: 0 us -> 114 us
  local copies, waits for them, and re-layouts: 121 us -> 71.2 us
    reduce_scatter x12 -> x1, waiting for transfers between devices: 1650 us -> 120 us  [scatter_slab(): owned = lax.psum_scatter(terms, everyone, scatter_dimension=0, tiled=True)]
    all_gather x10 -> x3, waiting for transfers between devices: 662 us -> 154 us  [gather_slab(): return lax.all_gather(owned[0], everyone, axis=0, tiled=True)]
    dot_general x92 -> x6, matrix products: 493 us -> 48.6 us  [product(): lax.dot_general(left, right, (((left_dim,), (right_dim,)), ((), ())), pre...]
    pallas_call x0 -> x3, Pallas kernels: none -> 114 us  [the longest x1 73.5 us: mlp(): pl.pallas_call(mlp_kernel, grid=(units // block,), in_specs=[whole, whole...]
    unnamed x38 -> x8, waiting for transfers between devices: 4.1 us -> 86.8 us
    ppermute x0 -> x4, waiting for transfers between devices: none -> 50.5 us  [swap(): return lax.ppermute(values, 'tensor', pairs)]
    while x32 -> x0, local copies, waits for them, and re-layouts: 36.5 us -> none
    all_to_all x0 -> x3, blocking collectives: none -> 32.2 us  [gather_slab(): lax.all_to_all(pieces.reshape(dp_count, rows // dp_count, part), 'dp', 0,...]
  transfers between devices with their start and end apart: 30 -> 13, of which waited for: 17 -> 9; matrix products, arithmetic and copies ran while one was open for 20% -> 20% of each run, Pallas kernels for 0% -> 5%
where the time goes in v1:
time: 825 us; the launch traced here: 821 us
  waiting for transfers between devices  417 us (51%)
  Pallas kernels  114 us (14%)
  blocking collectives  72.1 us (9%)
  local copies, waits for them, and re-layouts  71.2 us (9%)
  other arithmetic  65.5 us (8%)
  matrix products  48.6 us (6%)
  starting transfers between devices  17.2 us (2%)
  between operations  15.1 us (2%)
    all_gather x3, waiting for transfers between devices, gather_slab(): return lax.all_gather(owned[0], everyone, axis=0, tiled=True)  154 us
    reduce_scatter x1, waiting for transfers between devices, scatter_slab(): owned = lax.psum_scatter(terms, everyone, scatter_dimension=0, tiled=True)  120 us
    unnamed x8, waiting for transfers between devices  86.8 us
    pallas_call x1, Pallas kernels, mlp(): pl.pallas_call(mlp_kernel, grid=(units // block,), in_specs=[whole, whole...  73.5 us
    ppermute x4, waiting for transfers between devices, swap(): return lax.ppermute(values, 'tensor', pairs)  50.5 us
    dot_general x6, matrix products, product(): lax.dot_general(left, right, (((left_dim,), (right_dim,)), ((), ())), pre...  48.6 us
    psum x1, blocking collectives, shards(): summed = lax.psum(jnp.concatenate(vectors), everyone)  39.8 us
    unnamed x97, local copies, waits for them, and re-layouts  33.8 us
  transfers between devices with their start and end apart: 13, of which 9 were waited for; matrix products, arithmetic and copies ran while one was open for 20% of the time, Pallas kernels for 5%

profile of v1, /device:TPU:0, one launch (start us, length us, event | category | flops | bytes accessed | tf_op | source)
XLA Modules:
  0.0 821.2 jit_solution(2420541282668029594)
XLA Ops:
  8.4 12.0 %all_to_all.72 = bf16[4,144,288]{2,1,0:T(8,128)(2,1)S(1)} all-to-all(bf16[4,144,288]{2,1,0:T(8,128)(2,1)S(1)} %bitcast.79), channel_id=1, replica_groups=mesh['dp'=4,'tensor'=8] {'dp'}, dimensions={0} | all-to-all | bytes 663552 | tf_op jit(solution)/shard_map/all_to_all | solution.py:210
  22.0 10.2 %all_to_all.73 = bf16[4,136,288]{2,1,0:T(8,128)(2,1)S(1)} all-to-all(bf16[4,136,288]{2,1,0:T(8,128)(2,1)S(1)} %bitcast.83), channel_id=1, replica_groups=mesh['dp'=4,'tensor'=8] {'dp'}, dimensions={0} | all-to-all | bytes 626688 | tf_op jit(solution)/shard_map/all_to_all | solution.py:210
  33.8 10.1 %all_to_all.74 = bf16[4,136,288]{2,1,0:T(8,128)(2,1)S(1)} all-to-all(bf16[4,136,288]{2,1,0:T(8,128)(2,1)S(1)} %bitcast.82), channel_id=1, replica_groups=mesh['dp'=4,'tensor'=8] {'dp'}, dimensions={0} | all-to-all | bytes 626688 | tf_op jit(solution)/shard_map/all_to_all | solution.py:210
  46.4 1.6 collective-permute-start
  47.9 2.4 dynamic-slice_bitcast_fusion.1
  51.5 2.1 broadcast_in_dim_reshape.4.bias_ref
  53.6 19.5 %collective-permute-done = bf16[368,1152]{1,0:T(8,128)(2,1)S(1)} collective-permute-done((bf16[368,1152]{1,0:T(8,128)(2,1)}, bf16[368,1152]{1,0:T(8,128)(2,1)S(1)}, u32[]{:S(2)}, u32[]{:S(2)}) %collective-permute-start) | collective-permute-done | bytes 847904 | tf_op jit(solution)/shard_map/ppermute | solution.py:257
  73.9 31.0 %collective-permute-done.1 = bf16[368,1152]{1,0:T(8,128)(2,1)} collective-permute-done((bf16[368,1152]{1,0:T(8,128)(2,1)}, bf16[368,1152]{1,0:T(8,128)(2,1)}, u32[]{:S(2)}, u32[]{:S(2)}) %collective-permute-start.1) | collective-permute-done | bytes 847904 | tf_op jit(solution)/shard_map/ppermute | solution.py:257
  104.9 2.5 pad_maximum_fusion.2.grad_ref
  107.5 17.3 %all-gather.4.cloned.1.call-done = bf16[4608,1152]{1,0:T(8,128)(2,1)} async-done(((bf16[144,1152]{1,0:T(8,128)(2,1)}), bf16[4608,1152]{1,0:T(8,128)(2,1)}) %all-gather.4.cloned.1.call-update) | async-done | bytes 10616848 | tf_op jit(solution)/shard_map/all_gather | solution.py:213
  124.8 11.6 %add_convert_fusion.query_ref.key_ref.value_ref = bf16[3456,736]{1,0:T(8,128)(2,1)} fusion(bf16[4608,1152]{1,0:T(8,128)(2,1)} %all-gather.4.cloned.1.call-done, f32[3456]{0:T(1024)S(1)} %pad_maximum_fusion.4, f32[1152]{0:T(1024)S(1)} %copy-done.36, f32[1152]{0:T(1024)S(1)} %copy-done.32, f32[736]{0:T(1024)S(1)} %add_rsqrt_fusion.1, ...), kind=kOutput, calls=%fused_computation.2 | convolution fusion | flops 5873209344 | bytes 14774528 | tf_op jit(solution)/shard_map/dot_general | solution.py:23
  136.4 15.3 %attend.1 = (bf16[1152,736]{1,0:T(8,128)(2,1)S(1)}, f32[16,1,736]{2,1,0:T(1,128)S(1)}) custom-call(bf16[3456,736]{1,0:T(8,128)(2,1)} %add_convert_fusion.query_ref.key_ref.value_ref, bf16[3456,736]{1,0:T(8,128)(2,1)} %add_convert_fusion.query_ref.key_ref.value_ref, bf16[3456,736]{1,0:T(8,128)(2,1)} %add_convert_fusion.query_ref.key_ref.value_ref, ...), custom_call_target="tpu_custom_call" | custom-call | flops 8875147264 | bytes 16777216 | tf_op jit(solution)/shard_map/attend/pallas_call | solution.py:95
  151.7 5.9 fusion.27
  158.4 1.8 add_convert_fusion.2.normed_ref
  160.1 50.7 %all-gather.6.cloned.1.call-done.up_ref = bf16[4352,1152]{1,0:T(8,128)(2,1)} async-done(((bf16[136,1152]{1,0:T(8,128)(2,1)}), bf16[4352,1152]{1,0:T(8,128)(2,1)}) %all-gather.6.cloned.1.call-update) | async-done | bytes 10027024 | tf_op jit(solution)/shard_map/all_gather | solution.py:213
  210.8 85.9 %all-gather.8.cloned.1.call-done.down_ref = bf16[4352,1152]{1,0:T(8,128)(2,1)} async-done(((bf16[136,1152]{1,0:T(8,128)(2,1)}), bf16[4352,1152]{1,0:T(8,128)(2,1)}) %all-gather.8.cloned.1.call-update) | async-done | bytes 10027024 | tf_op jit(solution)/shard_map/all_gather | solution.py:213
  296.8 73.5 %mlp.1 = (f32[736,1152]{1,0:T(8,128)}, f32[736,1152]{1,0:T(8,128)}, bf16[4352,1152]{1,0:T(8,128)(2,1)}, bf16[4352,1152]{1,0:T(8,128)(2,1)}, f32[4352,1]{1,0:T(8,128)}) custom-call(bf16[736,1152]{1,0:T(8,128)(2,1)} %add_convert_fusion.2.normed_ref, bf16[736,1152]{1,0:T(8,128)(2,1)} %pad_maximum_fusion.2.grad_ref, ...), custom_call_target="tpu_custom_call" | custom-call | flops 59039023104 | bytes 67108864 | tf_op jit(solution)/shard_map/mlp/pallas_call | solution.py:188
  371.3 4.0 multiply_reduce_fusion
  375.4 5.5 convert_reduce_fusion.4
  380.9 1.7 copy-done.8
  382.6 4.5 convolution_convert_fusion.2
  387.1 2.3 copy.127.grad_ref
  391.2 25.6 %attend_back.1 = (bf16[1152,736]{1,0:T(8,128)(2,1)S(1)}, bf16[1152,736]{1,0:T(8,128)(2,1)S(1)}, bf16[1152,736]{1,0:T(8,128)(2,1)S(1)}) custom-call(bf16[3456,736]{1,0:T(8,128)(2,1)} %add_convert_fusion.query_ref.key_ref.value_ref, bf16[3456,736]{1,0:T(8,128)(2,1)} %add_convert_fusion.query_ref.key_ref.value_ref, ...), custom_call_target="tpu_custom_call" | custom-call | flops 17750294528 | bytes 16777216 | tf_op jit(solution)/shard_map/attend_back/pallas_call | solution.py:118
  416.8 1.4 constant_dynamic-update-slice_fusion.2
  418.2 1.3 constant_dynamic-update-slice_fusion.1
  419.5 1.3 constant_dynamic-update-slice_fusion
  421.9 2.5 convolution_convert_fusion.1
  424.5 9.6 %convolution_convert_fusion = bf16[3456,1152]{1,0:T(8,128)(2,1)S(1)} fusion(bf16[3456,736]{1,0:T(8,128)(2,1)} %constant_dynamic-update-slice_fusion, f32[1152]{0:T(1024)S(1)} %copy-done.37, f32[1152]{0:T(1024)S(1)} %copy-done.33, f32[736]{0:T(1024)S(1)} %add_rsqrt_fusion.1, f32[736]{0:T(1024)S(1)} %broadcast_multiply_fusion.5, ...), kind=kOutput, calls=%fused_computation | convolution fusion | flops 5872103424 | bytes 14760704 | tf_op jit(solution)/shard_map/dot_general | solution.py:23
  434.1 15.5 %pad_maximum_fusion = bf16[4608,1152]{1,0:T(8,128)(2,1)} fusion(bf16[1152,1152]{1,0:T(8,128)(2,1)S(1)} %convolution_convert_fusion.1, bf16[3456,1152]{1,0:T(8,128)(2,1)S(1)} %convolution_convert_fusion), kind=kLoop, calls=%fused_computation.1 | loop fusion | flops 21233664 | bytes 21233664 | tf_op jit(solution)/shard_map/concatenate | solution.py:336
  449.7 14.5 %fusion.18 = (f32[1152]{0:T(1024)}, f32[736]{0:T(1024)S(1)}, f32[736]{0:T(1024)S(1)}, f32[1152]{0:T(1024)}, f32[736,1152]{1,0:T(8,128)S(1)}) fusion(f32[736]{0:T(1024)S(1)} %add_rsqrt_fusion.1, f32[736]{0:T(1024)S(1)} %broadcast_multiply_fusion.5, bf16[368,1152]{1,0:T(8,128)(2,1)} %copy-done.15, bf16[368,1152]{1,0:T(8,128)(2,1)} %copy-done.12, ...), kind=kOutput, calls=%fused_computation.28 | convolution fusion | flops 5871510528 | bytes 18387456 | tf_op jit(solution)/shard_map/dot_general | solution.py:23
  464.3 3.2 fusion.17
  467.5 2.5 slice.158
  470.0 1.5 collective-permute-start.3
  471.5 2.9 reduce.1
  474.3 1.4 constant_dynamic-update-slice_fusion.3
  475.8 1.3 constant_dynamic-update-slice_fusion.5
  480.4 1.3 constant_dynamic-update-slice_fusion.10
  481.7 1.3 constant_dynamic-update-slice_fusion.9
  484.3 1.3 constant_dynamic-update-slice_fusion.7
  486.5 39.8 %psum.7 = f32[13568]{0:T(1024)S(1)} all-reduce(f32[13568]{0:T(1024)S(1)} %constant_dynamic-update-slice_fusion.6), channel_id=1, replica_groups=mesh['dp'=4,'tensor'=8] {'dp','tensor'}, use_global_device_ids=true, to_apply=%region_16.17 | all-reduce | flops 13568 | bytes 108544 | tf_op jit(solution)/shard_map/psum | solution.py:352
  529.1 2.3 collective-permute-start.2
  531.4 1.6 slice_bitcast_fusion
  534.4 2.0 maximum_select_fusion
  536.3 3.3 copy.130
  540.1 6.8 reduce.4
  547.0 1.9 reshape.183
  548.9 3.7 all-to-all-start.4
  552.6 2.9 maximum_select_fusion.1
  555.5 86.2 %reduce-scatter.12.cloned.1.call-done = bf16[136,1152]{1,0:T(8,128)(2,1)} async-done(((bf16[4352,1152]{1,0:T(8,128)(2,1)}), bf16[136,1152]{1,0:T(8,128)(2,1)}) %reduce-scatter.12.cloned.1.call-update) | async-done | bytes 313360
  641.7 3.3 copy.134
  645.0 6.8 reduce.5
  651.8 1.9 reshape.185
  653.7 3.5 all-to-all-start.5
  657.1 2.1 reshape.184
  659.2 2.4 copy.131
  663.7 2.1 reshape.186
  665.8 2.4 copy.135
  668.6 120.1 %reduce-scatter.8.cloned.1.call-done = bf16[144,1152]{1,0:T(8,128)(2,1)} async-done(((bf16[4608,1152]{1,0:T(8,128)(2,1)}), bf16[144,1152]{1,0:T(8,128)(2,1)}) %reduce-scatter.8.cloned.1.call-update) | async-done | bytes 331792 | tf_op jit(solution)/shard_map/reduce_scatter | solution.py:217
  788.6 3.3 copy.128
  791.9 6.8 reduce.3
  798.7 1.6 reshape.181
  800.4 3.5 all-to-all-start.3
  805.1 5.5 all-to-all-done.3
  810.6 1.9 reshape.182
  (154 shorter events, 28.8 us)
Async XLA Ops:
  7.2 43.7 %copy-start = (s32[2,4,736]{2,1,0:T(4,128)S(1)}, s32[2,4,736]{2,1,0:T(4,128)}, u32[]{:S(2)}) copy-start(s32[2,4,736]{2,1,0:T(4,128)} %param.19) | copy-start | bytes 70660
  7.2 14.5 %copy-start.22 = (bf16[288,538]{1,0:T(8,128)(2,1)S(1)}, bf16[288,538]{1,0:T(8,128)(2,1)}, u32[]{:S(2)}) copy-start(bf16[288,538]{1,0:T(8,128)(2,1)} %param.32) | copy-start | bytes 929668
  7.2 117.6 %all-gather.4.cloned.1.call-start = ((), (), s32[]{:S(2)}) async-start(), calls=%async_computation.9 | async-start | bytes 10948608 | tf_op jit(solution)/shard_map/all_gather | solution.py:213
  20.4 13.1 %copy-start.23 = (bf16[538,288]{0,1:T(8,128)(2,1)S(1)}, bf16[538,288]{0,1:T(8,128)(2,1)}, u32[]{:S(2)}) copy-start(bf16[538,288]{0,1:T(8,128)(2,1)} %param.34) | copy-start | bytes 929668
  21.6 189.2 %all-gather.6.cloned.1.call-start = ((), (), s32[]{:S(2)}) async-start(), calls=%async_computation.10 | async-start | bytes 10340352 | tf_op jit(solution)/shard_map/all_gather | solution.py:213
  22.0 23.3 %copy-start.21 = (bf16[2,368,1152]{2,1,0:T(8,128)(2,1)S(1)}, bf16[2,368,1152]{2,1,0:T(8,128)(2,1)}, u32[]{:S(2)}) copy-start(bf16[2,368,1152]{2,1,0:T(8,128)(2,1)} %param.18) | copy-start | bytes 5087236
  33.4 263.3 %all-gather.8.cloned.1.call-start = ((), (), s32[]{:S(2)}) async-start(), calls=%async_computation.11 | async-start | bytes 10340352 | tf_op jit(solution)/shard_map/all_gather | solution.py:213
  45.1 491.3 %reduce-scatter.10.cloned.1.call-start = ((), (), s32[]{:S(2)}) async-start(), calls=%async_computation.13 | async-start | bytes 10340352
  45.3 5.9 copy-start.27
  46.4 90.0 %copy-start.12 = (bf16[368,1152]{1,0:T(8,128)(2,1)}, bf16[368,1152]{1,0:T(8,128)(2,1)S(1)}, u32[]{:S(2)}) copy-start(bf16[368,1152]{1,0:T(8,128)(2,1)S(1)} %get-tuple-element.138) | copy-start | bytes 2543620
  46.4 7.2 copy-start.30
  46.4 7.2 copy-start.31
  46.4 26.7 %collective-permute-start = (bf16[368,1152]{1,0:T(8,128)(2,1)}, bf16[368,1152]{1,0:T(8,128)(2,1)S(1)}, u32[]{:S(2)}, u32[]{:S(2)}) collective-permute-start(bf16[368,1152]{1,0:T(8,128)(2,1)} %get-tuple-element.139), channel_id=1, source_target_pairs={{0,1},{1,0},{2,3},{3,2},{4,5},{5,4},{6,7},{7,6},{8,9},{9,8},{10,11... | collective-permute-start | bytes 2543624 | tf_op jit(solution)/shard_map/ppermute | solution.py:257
  50.4 57.1 %copy-start.18 = (bf16[368,1152]{1,0:T(8,128)(2,1)}, bf16[368,1152]{1,0:T(8,128)(2,1)S(1)}, u32[]{:S(2)}) copy-start(bf16[368,1152]{1,0:T(8,128)(2,1)S(1)} %get-tuple-element.136) | copy-start | bytes 2543620
  50.4 54.6 %collective-permute-start.1 = (bf16[368,1152]{1,0:T(8,128)(2,1)}, bf16[368,1152]{1,0:T(8,128)(2,1)}, u32[]{:S(2)}, u32[]{:S(2)}) collective-permute-start(bf16[368,1152]{1,0:T(8,128)(2,1)} %get-tuple-element.137), channel_id=1, source_target_pairs={{0,1},{1,0},{2,3},{3,2},{4,5},{5,4},{6,7},{7,6},{8,9},{9,8},{10,11... | collective-permute-start | bytes 2543624 | tf_op jit(solution)/shard_map/ppermute | solution.py:257
  51.3 85.1 %copy-start.2 = (f32[736,1]{1,0:T(8,128)}, f32[736,1]{1,0:T(8,128)S(1)}, u32[]{:S(2)}) copy-start(f32[736,1]{1,0:T(8,128)S(1)} %select_n.69.bias_ref) | copy-start | bytes 8836
  73.0 63.3 %copy-start.15 = (bf16[368,1152]{1,0:T(8,128)(2,1)}, bf16[368,1152]{1,0:T(8,128)(2,1)S(1)}, u32[]{:S(2)}) copy-start(bf16[368,1152]{1,0:T(8,128)(2,1)S(1)} %collective-permute-done) | copy-start | bytes 2543620
  73.0 51.8 %copy-start.32 = (f32[1152]{0:T(1024)S(1)}, f32[1152]{0:T(1024)}, u32[]{:S(2)}) copy-start(f32[1152]{0:T(1024)} %param.21) | copy-start | bytes 13828
  73.0 51.8 %copy-start.36 = (f32[1152]{0:T(1024)S(1)}, f32[1152]{0:T(1024)}, u32[]{:S(2)}) copy-start(f32[1152]{0:T(1024)} %param.22) | copy-start | bytes 13828
  136.4 15.3 %copy-start.35 = (f32[1152]{0:T(1024)S(1)}, f32[1152]{0:T(1024)}, u32[]{:S(2)}) copy-start(f32[1152]{0:T(1024)} %param.29) | copy-start | bytes 13828
  151.6 6.0 copy-start.4
  151.6 6.0 copy-start.6
  157.6 0.7 copy-start.25
  157.6 0.7 copy-start.28
  370.2 271.5 %reduce-scatter.12.cloned.1.call-start = ((), (), s32[]{:S(2)}) async-start(), calls=%async_computation.14 | async-start | bytes 10340352
  370.8 417.8 %reduce-scatter.8.cloned.1.call-start = ((), (), s32[]{:S(2)}) async-start(), calls=%async_computation.12 | async-start | bytes 10948608 | tf_op jit(solution)/shard_map/reduce_scatter | solution.py:217
  371.3 4.1 copy-start.11
  371.3 4.1 copy-start.19
  371.3 4.1 copy-start.29
  380.9 1.7 copy-start.8
  389.4 1.0 copy-start.3
  390.4 0.8 copy-start.7
  418.2 2.7 copy-start.5
  418.2 3.8 copy-start.9
  421.9 2.5 copy-start.13
  421.9 2.5 copy-start.16
  421.9 2.5 copy-start.33
  421.9 2.5 copy-start.37
  449.7 14.6 %copy-start.10 = (f32[736,1152]{1,0:T(8,128)S(1)}, f32[736,1152]{1,0:T(8,128)}, u32[]{:S(2)}) copy-start(f32[736,1152]{1,0:T(8,128)} %copy-done.8) | copy-start | bytes 10174468
  449.7 14.6 %copy-start.14 = (bf16[368,1152]{1,0:T(8,128)(2,1)S(1)}, bf16[368,1152]{1,0:T(8,128)(2,1)}, u32[]{:S(2)}) copy-start(bf16[368,1152]{1,0:T(8,128)(2,1)} %copy-done.12) | copy-start | bytes 2543620
  449.7 14.6 %copy-start.17 = (bf16[368,1152]{1,0:T(8,128)(2,1)S(1)}, bf16[368,1152]{1,0:T(8,128)(2,1)}, u32[]{:S(2)}) copy-start(bf16[368,1152]{1,0:T(8,128)(2,1)} %copy-done.15) | copy-start | bytes 2543620
  449.7 14.6 %copy-start.34 = (f32[1152]{0:T(1024)S(1)}, f32[1152]{0:T(1024)}, u32[]{:S(2)}) copy-start(f32[1152]{0:T(1024)} %param.21) | copy-start | bytes 13828
  470.0 63.1 %collective-permute-start.3 = (bf16[368,1152]{1,0:T(8,128)(2,1)}, bf16[368,1152]{1,0:T(8,128)(2,1)}, u32[]{:S(2)}, u32[]{:S(2)}) collective-permute-start(bf16[368,1152]{1,0:T(8,128)(2,1)} %slice.158), channel_id=1, source_target_pairs={{0,1},{1,0},{2,3},{3,2},{4,5},{5,4},{6,7},{7,6},{8,9},{9,8},{10,11... | collective-permute-start | bytes 2543624 | tf_op jit(solution)/shard_map/ppermute | solution.py:257
  474.3 11.3 %copy-start.20 = (bf16[736,1152]{1,0:T(8,128)(2,1)S(1)}, bf16[736,1152]{1,0:T(8,128)(2,1)}, u32[]{:S(2)}) copy-start(bf16[736,1152]{1,0:T(8,128)(2,1)} %get-tuple-element.132) | copy-start | bytes 5087236
  477.1 8.7 %copy-start.24 = (f32[4352]{0:T(1024)S(1)}, f32[4352]{0:T(1024)}, u32[]{:S(2)}) copy-start(f32[4352]{0:T(1024)} %reduce.1) | copy-start | bytes 52228
  485.7 0.8 copy-start.26
  529.1 23.4 %collective-permute-start.2 = (bf16[368,1152]{1,0:T(8,128)(2,1)S(1)}, bf16[368,1152]{1,0:T(8,128)(2,1)}, u32[]{:S(2)}, u32[]{:S(2)}) collective-permute-start(bf16[368,1152]{1,0:T(8,128)(2,1)S(1)} %get-tuple-element.135), channel_id=1, source_target_pairs={{0,1},{1,0},{2,3},{3,2},{4,5},{5,4},{6,7},{7,6},{8,9},{9,8},{10,11... | collective-permute-start | bytes 2543624 | tf_op jit(solution)/shard_map/ppermute | solution.py:257
  548.9 104.8 %all-to-all-start.4 = ((bf16[4,2,19584]{2,1,0:T(2,128)(2,1)}), bf16[4,2,19584]{2,1,0:T(2,128)(2,1)S(1)}, u32[]{:S(2)}, u32[]{:S(2)}) async-start(bf16[4,2,19584]{2,1,0:T(2,128)(2,1)} %reshape.183), calls=%async_computation.5 | async-start | bytes 626688 | tf_op jit(solution)/shard_map/all_to_all | solution.py:219
  653.7 10.0 %all-to-all-start.5 = ((bf16[4,2,19584]{2,1,0:T(2,128)(2,1)}), bf16[4,2,19584]{2,1,0:T(2,128)(2,1)S(1)}, u32[]{:S(2)}, u32[]{:S(2)}) async-start(bf16[4,2,19584]{2,1,0:T(2,128)(2,1)} %reshape.185), calls=%async_computation.6 | async-start | bytes 626688 | tf_op jit(solution)/shard_map/all_to_all | solution.py:219
  800.4 10.2 %all-to-all-start.3 = ((bf16[4,2,20736]{2,1,0:T(2,128)(2,1)}), bf16[4,2,20736]{2,1,0:T(2,128)(2,1)S(1)}, u32[]{:S(2)}, u32[]{:S(2)}) async-start(bf16[4,2,20736]{2,1,0:T(2,128)(2,1)} %reshape.181), calls=%async_computation.4 | async-start | bytes 663552 | tf_op jit(solution)/shard_map/all_to_all | solution.py:219
  803.8 10.3 %copy-start.1 = (s32[2,4,736]{2,1,0:T(4,128)S(1)}, s32[2,4,736]{2,1,0:T(4,128)}, u32[]{:S(2)}) copy-start(s32[2,4,736]{2,1,0:T(4,128)} %param.19) | copy-start | bytes 70660
Sparse Core Ops, SparseCore 0:
  21.8 102.9 all-gather.3
  127.6 83.1 all-gather.5
  213.7 83.0 all-gather.7
  370.4 133.1 reduce-scatter.9
  509.6 132.1 reduce-scatter.11
  647.7 140.9 reduce-scatter.7

commit v2 on v1

--- a/solution.py
+++ b/solution.py
@@ -62,9 +62,7 @@
     out_ref,
     total_ref,
     grad_ref,
-    grad_query_ref,
-    grad_key_ref,
-    grad_value_ref,
+    grads_ref,
 ):
     for head in range(heads):
         rows = slice(head * HEAD_DIM, (head + 1) * HEAD_DIM)
@@ -81,9 +79,9 @@
             grad.astype(wide) * out_ref[rows, :].astype(wide), axis=0, keepdims=True
         )
         grad_raw = (probs * (grad_probs - along)).astype(low)
-        grad_value_ref[rows, :] = product(grad, probs.astype(low), 1, 1).astype(low)
-        grad_query_ref[rows, :] = (product(key, grad_raw, 1, 0) * score_scale).astype(low)
-        grad_key_ref[rows, :] = (product(query, grad_raw, 1, 1) * score_scale).astype(low)
+        grads_ref[2, rows, :] = product(grad, probs.astype(low), 1, 1).astype(low)
+        grads_ref[0, rows, :] = (product(key, grad_raw, 1, 0) * score_scale).astype(low)
+        grads_ref[1, rows, :] = (product(query, grad_raw, 1, 1) * score_scale).astype(low)
 
 
 def attend(projected, bias, heads, step_heads):
@@ -127,8 +125,8 @@
             pl.BlockSpec((step_heads, 1, tokens), lambda i: (i, 0, 0)),
             part(0),
         ],
-        out_specs=[part(0)] * 3,
-        out_shape=[jax.ShapeDtypeStruct((heads * HEAD_DIM, tokens), low)] * 3,
+        out_specs=pl.BlockSpec((3, HEAD_DIM * step_heads, tokens), lambda i: (0, i, 0)),
+        out_shape=jax.ShapeDtypeStruct((3, heads * HEAD_DIM, tokens), low),
         compiler_params=pltpu.CompilerParams(vmem_limit_bytes=48 * 2**20),
         cost_estimate=pl.CostEstimate(
             flops=heads * tokens * tokens * 2048, bytes_accessed=16 * 2**20, transcendentals=0
@@ -138,17 +136,23 @@
 
 
 def mlp_kernel(
+    joined,
+    carried,
     normed_ref,
     grad_ref,
     up_ref,
     down_ref,
     bias_ref,
-    out_ref,
-    grad_normed_ref,
-    grad_up_ref,
-    grad_down_ref,
-    grad_bias_ref,
+    *refs,
 ):
+    if carried:
+        out_before, normed_before = refs[:2]
+        refs = refs[2:]
+    if joined:
+        out_ref, grad_normed_ref, grad_rows_ref, grad_bias_ref = refs
+        grad_up_ref, grad_down_ref = grad_rows_ref.at[0], grad_rows_ref.at[1]
+    else:
+        out_ref, grad_normed_ref, grad_up_ref, grad_down_ref, grad_bias_ref = refs
     step = pl.program_id(0)
     normed, grad = normed_ref[...], grad_ref[...]
     up, down = up_ref[...], down_ref[...]
@@ -170,8 +174,12 @@
 
     @pl.when(step == 0)
     def first():
-        out_ref[...] = out_term
-        grad_normed_ref[...] = normed_term
+        if carried:
+            out_ref[...] = out_before[...] + out_term
+            grad_normed_ref[...] = normed_before[...] + normed_term
+        else:
+            out_ref[...] = out_term
+            grad_normed_ref[...] = normed_term
 
     @pl.when(step > 0)
     def later():
@@ -179,45 +187,244 @@
         grad_normed_ref[...] += normed_term
 
 
-def mlp(normed, grad, up, down, bias, block):
+def mlp(normed, grad, up, down, bias, block, before=None):
     tokens, width = normed.shape
-    units = up.shape[0]
+    joined = down is None
+    units = up.shape[0] // 2 if joined else up.shape[0]
+    steps = units // block
     whole = pl.BlockSpec((tokens, width), lambda i: (0, 0))
     rows = pl.BlockSpec((block, width), lambda i: (i, 0))
+    lower = pl.BlockSpec((block, width), lambda i: (steps + i, 0)) if joined else rows
     column = pl.BlockSpec((block, 1), lambda i: (i, 0))
+    sums = [jax.ShapeDtypeStruct((tokens, width), wide)] * 2
+    if joined:
+        grad_specs = [pl.BlockSpec((2, block, width), lambda i: (0, i, 0))]
+        grad_shapes = [jax.ShapeDtypeStruct((2, units, width), low)]
+    else:
+        grad_specs = [rows, rows]
+        grad_shapes = [jax.ShapeDtypeStruct((units, width), low)] * 2
+    earlier = [] if before is None else list(before)
     return pl.pallas_call(
-        mlp_kernel,
-        grid=(units // block,),
-        in_specs=[whole, whole, rows, rows, column],
-        out_specs=[whole, whole, rows, rows, column],
-        out_shape=[
-            jax.ShapeDtypeStruct((tokens, width), wide),
-            jax.ShapeDtypeStruct((tokens, width), wide),
-            jax.ShapeDtypeStruct((units, width), low),
-            jax.ShapeDtypeStruct((units, width), low),
-            jax.ShapeDtypeStruct((units, 1), wide),
-        ],
+        partial(mlp_kernel, joined, before is not None),
+        grid=(steps,),
+        in_specs=[whole, whole, rows, lower, column] + [whole] * len(earlier),
+        out_specs=[whole, whole] + grad_specs + [column],
+        out_shape=sums + grad_shapes + [jax.ShapeDtypeStruct((units, 1), wide)],
+        input_output_aliases={5: 0, 6: 1} if earlier else {},
         compiler_params=pltpu.CompilerParams(vmem_limit_bytes=60 * 2**20),
         cost_estimate=pl.CostEstimate(
             flops=16 * tokens * width * units, bytes_accessed=64 * 2**20, transcendentals=0
         ),
         name="mlp",
-    )(normed, grad, up, down, bias)
-
-
-def gather_slab(pieces, dp_count):
+    )(normed, grad, up, up if joined else down, bias, *earlier)
+
+
+def place_kernel(kind_ref, *refs):
+    pieces, out_ref, sems = refs[:8], refs[8], refs[9]
+    kind = kind_ref[0]
+    quarter = out_ref.shape[1] // 4
+    copies = []
+    for core in range(2):
+        near, near_y, far, far_x = pieces[4 * core : 4 * core + 4]
+        same, across = kind ^ core, kind ^ (core + 2)
+        moves = (
+            (near.at[pl.ds(0, quarter)], same, 0),
+            (near.at[pl.ds(quarter, quarter)], across, 0),
+            (near_y.at[pl.ds(0, quarter)], same, 1),
+            (near_y.at[pl.ds(quarter, quarter)], across, 1),
+            (far, same, 2),
+            (far_x, across, 2),
+        )
+        for source, target, start in moves:
+            copies.append(
+                pltpu.make_async_copy(
+                    source,
+                    out_ref.at[target, pl.ds(start * quarter, source.shape[0])],
+                    sems.at[len(copies)],
+                )
+            )
+    for copy in copies:
+        copy.start()
+    for copy in copies:
+        copy.wait()
+
+
+def place(kind, pieces):
+    rows, width = pieces[0].shape
+    anywhere = pl.BlockSpec(memory_space=pl.ANY)
+    return pl.pallas_call(
+        place_kernel,
+        in_specs=[pl.BlockSpec(memory_space=pltpu.SMEM)] + [anywhere] * 8,
+        out_specs=anywhere,
+        out_shape=jax.ShapeDtypeStruct((4, 2 * rows, width), low),
+        scratch_shapes=[pltpu.SemaphoreType.DMA((12,))],
+        cost_estimate=pl.CostEstimate(
+            flops=0, bytes_accessed=32 * rows * width, transcendentals=0
+        ),
+        name="place",
+    )(kind, *pieces)
+
+
+def kinds_kernel(kind_ref, grads_ref, attended_ref, normed_ref, branch_ref, out_ref):
+    kind = pl.program_id(0)
+
+    @pl.when(kind < 3)
+    def projections():
+        out_ref[0] = product(grads_ref[0], normed_ref[...], 1, 0).astype(low)
+
+    @pl.when(kind == 3)
+    def output():
+        out_ref[0] = product(attended_ref[...], branch_ref[...], 1, 0).astype(low)
+
+
+def kinds_grad(kind, grads, attended, normed, branch, block):
+    _, rows, tokens = grads.shape
+    width = normed.shape[1]
+    whole = pl.BlockSpec((tokens, width), lambda k, i, ref: (0, 0))
+
+    def spot(k, i, ref):
+        other = k ^ ref[0]
+        return ((other & 1) * 2 + (other >> 1), i, 0)
+
+    return pl.pallas_call(
+        kinds_kernel,
+        grid_spec=pltpu.PrefetchScalarGridSpec(
+            num_scalar_prefetch=1,
+            grid=(4, rows // block),
+            in_specs=[
+                pl.BlockSpec((1, block, tokens), lambda k, i, ref: (jnp.minimum(k, 2), i, 0)),
+                pl.BlockSpec((block, tokens), lambda k, i, ref: (i, 0)),
+                whole,
+                whole,
+            ],
+            out_specs=pl.BlockSpec((1, block, width), spot),
+        ),
+        out_shape=jax.ShapeDtypeStruct((4, rows, width), low),
+        compiler_params=pltpu.CompilerParams(vmem_limit_bytes=40 * 2**20),
+        cost_estimate=pl.CostEstimate(
+            flops=12 * rows * width * tokens, bytes_accessed=24 * 2**20, transcendentals=0
+        ),
+        name="kinds_grad",
+    )(kind, grads, attended, normed, branch)
+
+
+def gather_rows(owned):
+    return lax.all_gather(owned, everyone, axis=0, tiled=True)
+
+
+def scatter_rows(terms):
+    return lax.psum_scatter(terms, everyone, scatter_dimension=0, tiled=True)
+
+
+def to_rows(pieces, dp_count):
     rows, part = pieces.shape
-    owned = lax.all_to_all(
+    return lax.all_to_all(
         pieces.reshape(dp_count, rows // dp_count, part), "dp", 0, 2, tiled=True
-    )
-    return lax.all_gather(owned[0], everyone, axis=0, tiled=True)
-
-
-def scatter_slab(terms, dp_count):
-    owned = lax.psum_scatter(terms, everyone, scatter_dimension=0, tiled=True)
+    )[0]
+
+
+def to_columns(owned, dp_count):
     rows, width = owned.shape
     back = lax.all_to_all(owned[None], "dp", 2, 0, tiled=True)
     return back.reshape(dp_count * rows, width // dp_count).astype(wide)
+
+
+class Hops:
+    def __init__(self, dp_count, tensor_count):
+        self.count = dp_count * tensor_count
+        self.y, self.z = 1, (2, 4, 6)
+        self.core, self.x = tensor_count, 2 * tensor_count
+        z1, z2, z3 = self.z
+        self.near = (0, z1)
+        self.far = (z2, z3)
+
+    def send(self, values, distance):
+        pairs = [(place, place ^ distance) for place in range(self.count)]
+        return lax.ppermute(values, everyone, pairs)
+
+    def order(self):
+        x, y = self.x, self.y
+        near = [n ^ p ^ q for q in (0, y) for p in (0, x) for n in self.near]
+        far = [n ^ p ^ q for q in (0, x) for p in (0, y) for n in self.far]
+        return near + far
+
+    def gather_kinds(self, block):
+        z1, z2, z3 = [self.send(block, z) for z in self.z]
+        near = jnp.concatenate([block, z1], axis=0)
+        far = jnp.concatenate([z2, z3], axis=0)
+        near = jnp.concatenate([near, self.send(near, self.x)], axis=0)
+        far = jnp.concatenate([far, self.send(far, self.y)], axis=0)
+        near_y, far_x = self.send(near, self.y), self.send(far, self.x)
+        pieces = [near, near_y, far, far_x]
+        return pieces + [self.send(piece, self.core) for piece in pieces]
+
+    def gather_units(self, block):
+        half = block.shape[0] // 2
+
+        def join(*blocks):
+            return jnp.concatenate(
+                [b[: b.shape[0] // 2] for b in blocks] + [b[b.shape[0] // 2 :] for b in blocks],
+                axis=0,
+            )
+
+        z1, z2, z3 = [self.send(block, z) for z in self.z]
+        near, far = join(block, z1), join(z2, z3)
+        near, far = join(near, self.send(near, self.x)), join(far, self.send(far, self.y))
+        own = join(near, self.send(near, self.y), far, self.send(far, self.x))
+        return own, self.send(own, self.core)
+
+    def add(self, *terms):
+        total = terms[0].astype(wide)
+        for term in terms[1:]:
+            total = total + term.astype(wide)
+        return total.astype(low)
+
+    def reduce_last(self, near, far, axis):
+        take = lambda values, place: lax.index_in_dim(values, place, axis, keepdims=False)
+        near = self.add(take(near, 0), self.send(take(near, 1), self.x))
+        far = self.add(take(far, 0), self.send(take(far, 1), self.y))
+        return self.add(
+            take(near, 0),
+            self.send(take(near, 1), self.z[0]),
+            self.send(take(far, 0), self.z[1]),
+            self.send(take(far, 1), self.z[2]),
+        )
+
+    def reduce_kinds(self, terms):
+        rows = terms.shape[1] // 8
+        width = terms.shape[2]
+        terms = terms.reshape(2, 2, 8, rows, width)
+        sent = self.send(terms[1], self.core)
+        near_y = self.add(terms[0, :, 2:4], sent[:, 2:4])
+        far_x = self.add(terms[0, 1, 4:8], sent[1, 4:8])
+        near_y, far_x = self.send(near_y, self.y), self.send(far_x, self.x)
+        near = self.add(terms[0, :, 0:2], sent[:, 0:2], near_y)
+        far = self.add(terms[0, 0, 4:8], sent[0, 4:8], far_x)
+        near = near.reshape(2, 2, rows, width)
+        far = far.reshape(2, 2, rows, width)
+        return self.reduce_last(near, far, 0)
+
+    def reduce_units(self, own, sibling):
+        width = own.shape[2]
+        sent = self.send(sibling, self.core).reshape(2, 4, -1, width)
+        own = own.reshape(2, 4, -1, width)
+        near_y = self.send(self.add(own[:, 1], sent[:, 1]), self.y)
+        far_x = self.send(self.add(own[:, 3], sent[:, 3]), self.x)
+        near = self.add(own[:, 0], sent[:, 0], near_y).reshape(2, 2, 2, -1, width)
+        far = self.add(own[:, 2], sent[:, 2], far_x).reshape(2, 2, 2, -1, width)
+        near = self.add(near[:, 0], self.send(near[:, 1], self.x))
+        far = self.add(far[:, 0], self.send(far[:, 1], self.y))
+        return self.add(
+            near[:, 0],
+            self.send(near[:, 1], self.z[0]),
+            self.send(far[:, 0], self.z[1]),
+            self.send(far[:, 1], self.z[2]),
+        )
+
+    def sum_all(self, values):
+        for distance in (self.core, self.x, self.y, self.z[0], self.z[1]):
+            values = values + self.send(values, distance)
+        return values
 
 
 def shards(
@@ -248,10 +455,17 @@
     heads = head_cols * tensor_count // HEAD_DIM
     quantum = 8 * dp_count
     slab_units = -(-unit_cols // quantum) * quantum
-    tensor_place = lax.axis_index("tensor")
+    by_hops = (dp_count, tensor_count) == (4, 8)
+    hop_units = 4 * 56 if by_hops else 0
+    bulk_units = slab_units - hop_units
+    dp_place, tensor_place = lax.axis_index("dp"), lax.axis_index("tensor")
+    here = dp_place * tensor_count + tensor_place
+    devices = dp_count * tensor_count
     col_start = tensor_place * head_cols
     side = tensor_place % 2
     pairs = [(place, place ^ 1) for place in range(tensor_count)]
+    hops = Hops(dp_count, tensor_count)
+    kind = dp_place.reshape(1).astype(jnp.int32)
 
     def swap(values):
         return lax.ppermute(values, "tensor", pairs)
@@ -266,17 +480,39 @@
         other = swap(values[half_rows:].astype(low)).astype(values.dtype)
         return jnp.where(side == 0, jnp.stack([kept, other]), jnp.stack([other, kept]))
 
-    def slab_order(values):
-        padded = jnp.pad(
-            values.reshape(tensor_count, unit_cols), ((0, 0), (0, slab_units - unit_cols))
-        )
-        return padded.reshape(tensor_count, dp_count, -1).transpose(1, 0, 2).reshape(-1)
-
-    def unit_order(values):
-        slabs = values.reshape(dp_count, tensor_count, -1).transpose(1, 0, 2)
-        return slabs.reshape(tensor_count, slab_units)[:, :unit_cols].reshape(-1)
+    if by_hops:
+        head_places = tensor_place ^ jnp.array(
+            [n ^ q for group in (hops.near, hops.far) for q in (0, hops.y) for n in group]
+        )
+        hop_order = hops.order()
+        hop_order = hop_order + [place ^ hops.core for place in hop_order]
+        hop_places = here ^ jnp.array(hop_order)
+        hop_find = [hop_order.index(place) for place in range(devices)]
+
+    def to_heads(values):
+        if not by_hops:
+            return values
+        return values.reshape(tensor_count, head_cols)[head_places].reshape(-1)
+
+    def from_heads(values):
+        if not by_hops:
+            return values
+        blocks = values.reshape(tensor_count, head_cols)
+        return jnp.zeros_like(blocks).at[head_places].set(blocks).reshape(-1)
+
+    def in_slabs(values, start, stop):
+        part = values[:, start:stop].reshape(tensor_count, dp_count, -1)
+        return part.transpose(1, 0, 2)
+
+    def from_slabs(values):
+        return (
+            values.reshape(dp_count, tensor_count, -1).transpose(1, 0, 2).reshape(tensor_count, -1)
+        )
 
     x_slot = one_slot(inputs).astype(wide)
+    attn_block = to_rows(
+        jnp.concatenate([w_query.T, w_key.T, w_value.T, w_out], axis=0), dp_count
+    )
     grad_out = one_slot(cotangent)
     mask_row = lax.dynamic_slice(
         pad_mask, (side, tensor_place // 2, 0), (1, 1, 2 * half_rows)
@@ -284,36 +520,72 @@
     mask_row = jnp.where(side == 0, mask_row, mask_row[::-1]).reshape(2 * half_rows, 1)
     bias_col = jnp.where(mask_row > 0, 0.0, masked_score).astype(wide)
 
-    attn_rows = gather_slab(
-        jnp.concatenate([w_query.T, w_key.T, w_value.T, w_out], axis=0), dp_count
-    )
-    kinds = attn_rows.reshape(4, dp_count // 4, tensor_count, -1, width)
-    kinds = kinds.transpose(0, 2, 1, 3, 4).reshape(4, -1, width)
+    unit_pad = ((0, slab_units - unit_cols), (0, 0))
+    up_cols, down_cols = jnp.pad(w_up.T, unit_pad), jnp.pad(w_down, unit_pad)
+    bulk_rows = bulk_units // dp_count
+    hop_rows = hop_units // dp_count
+    split = lambda values: (
+        values[:bulk_units].reshape(dp_count, bulk_rows, values.shape[1]),
+        values[bulk_units:].reshape(dp_count, hop_rows, values.shape[1]),
+    )
+    (up_bulk, up_hop), (down_bulk, down_hop) = split(up_cols), split(down_cols)
+    mlp_owned = to_rows(
+        jnp.concatenate([up_bulk, down_bulk, up_hop, down_hop], axis=1).reshape(
+            2 * slab_units, -1
+        ),
+        dp_count,
+    )
+    if by_hops:
+        kinds = place(kind, hops.gather_kinds(attn_block))
+        up_rows = gather_rows(mlp_owned[:bulk_rows])
+        down_rows = gather_rows(mlp_owned[bulk_rows : 2 * bulk_rows])
+        hop_own, hop_sibling = hops.gather_units(mlp_owned[2 * bulk_rows :])
+    else:
+        attn_rows = gather_rows(attn_block)
+        kinds = attn_rows.reshape(4, dp_count // 4, tensor_count, -1, width)
+        kinds = kinds.transpose(0, 2, 1, 3, 4).reshape(4, -1, width)
+        up_rows = gather_rows(mlp_owned[:bulk_rows])
+        down_rows = gather_rows(mlp_owned[bulk_rows:])
     qkv_rows = kinds[:3].reshape(-1, width)
     out_rows = kinds[3]
-    unit_pad = ((0, slab_units - unit_cols), (0, 0))
-    up_rows = gather_slab(jnp.pad(w_up.T, unit_pad), dp_count)
-    down_rows = gather_slab(jnp.pad(w_down, unit_pad), dp_count)
+    slab_bias = jnp.pad(
+        b_up.reshape(tensor_count, unit_cols), ((0, 0), (0, slab_units - unit_cols))
+    )
 
     unit_first, scale_first = norm_stats(x_slot)
     normed_first = (unit_first * attn_norm_gain + attn_norm_shift).astype(low)
-    qkv_bias = jnp.concatenate([b_query, jnp.zeros_like(b_query), b_value])
+    qkv_bias = jnp.concatenate([to_heads(b_query), jnp.zeros_like(b_query), to_heads(b_value)])
     projected = (product(qkv_rows, normed_first, 1, 1) + qkv_bias[:, None]).astype(low)
     attended, total = attend(projected, bias_col, heads, 4)
     middle = x_slot + (product(attended, out_rows, 0, 0) + b_out)
     unit_second, scale_second = norm_stats(middle)
     normed_second = (unit_second * mlp_norm_gain + mlp_norm_shift).astype(low)
-    down_out, grad_normed_second, grad_up, grad_down, grad_up_bias = mlp(
-        normed_second,
-        grad_out,
-        up_rows,
-        down_rows,
-        slab_order(b_up)[:, None],
-        8 * (slab_units // 8),
-    )
+    bulk_bias = in_slabs(slab_bias, 0, bulk_units).reshape(-1, 1)
+    bulk_block = 512 if by_hops else bulk_units
+    *sums, grad_up, grad_down, bulk_grad = mlp(
+        normed_second, grad_out, up_rows, down_rows, bulk_bias, bulk_block
+    )
+    up_owned, down_owned = scatter_rows(grad_up), scatter_rows(grad_down)
+    bulk_grad = bulk_grad[:, 0]
+    if by_hops:
+        hop_bias = in_slabs(slab_bias, bulk_units, slab_units).reshape(devices, hop_rows)
+        hop_bias = hop_bias[hop_places].reshape(2, -1, 1)
+        *sums, grad_sibling, sibling_bias = mlp(
+            normed_second, grad_out, hop_sibling, None, hop_bias[1], 448, sums
+        )
+        *sums, grad_own, own_bias = mlp(
+            normed_second, grad_out, hop_own, None, hop_bias[0], 448, sums
+        )
+        hop_owned = hops.reduce_units(grad_own, grad_sibling)
+        hop_grad = jnp.concatenate([own_bias[:, 0], sibling_bias[:, 0]]).reshape(devices, -1)
+        hop_grad = hop_grad[jnp.array(hop_find)][here ^ jnp.arange(devices)].reshape(-1)
+        up_grad = jnp.concatenate([bulk_grad, hop_grad])
+        mlp_grads = jnp.concatenate([up_owned, down_owned, hop_owned[0], hop_owned[1]], axis=0)
+    else:
+        up_grad = bulk_grad
+        mlp_grads = jnp.concatenate([up_owned, down_owned], axis=0)
+    down_out, grad_normed_second = sums
     layer_out = both_micros((middle + (down_out + b_down)).astype(low))
-    grad_w_up = scatter_slab(grad_up, dp_count)[:unit_cols].T
-    grad_w_down = scatter_slab(grad_down, dp_count)[:unit_cols]
 
     grad_mid_norm, gain_second, shift_second = norm_backward(
         grad_normed_second, unit_second, scale_second, mlp_norm_gain
@@ -322,53 +594,82 @@
     grad_middle = grad_wide + grad_mid_norm
     grad_branch = grad_middle.astype(low)
     grad_attended = product(out_rows, grad_branch, 1, 1).astype(low)
-    grad_out_rows = product(attended, grad_branch, 1, 0).astype(low)
-    grad_query, grad_key, grad_value = attend_back(
+    grad_projected = attend_back(
         projected, bias_col, attended, total, grad_attended, heads, 4
     )
-    grad_projected = jnp.concatenate([grad_query, grad_key, grad_value], axis=0)
-    grad_qkv_rows = product(grad_projected, normed_first, 1, 0).astype(low)
-    grad_normed_first = product(grad_projected, qkv_rows, 0, 0)
+    grad_flat = grad_projected.reshape(-1, 2 * half_rows)
+    grad_normed_first = product(grad_flat, qkv_rows, 0, 0)
+    if by_hops:
+        grad_kinds = kinds_grad(
+            kind, grad_projected, attended, normed_first, grad_branch, heads * HEAD_DIM // 4
+        )
+        attn_owned = hops.reduce_kinds(grad_kinds)
+    else:
+        grad_qkv_rows = product(grad_flat, normed_first, 1, 0).astype(low)
+        grad_out_rows = product(attended, grad_branch, 1, 0).astype(low)
+        grad_kinds = jnp.concatenate([grad_qkv_rows, grad_out_rows], axis=0)
+        grad_kinds = grad_kinds.reshape(4, tensor_count, dp_count // 4, -1, width)
+        attn_owned = scatter_rows(grad_kinds.transpose(0, 2, 1, 3, 4).reshape(-1, width))
     grad_in_norm, gain_first, shift_first = norm_backward(
         grad_normed_first, unit_first, scale_first, attn_norm_gain
     )
     input_grad = both_micros(grad_middle + grad_in_norm)
-    grad_kinds = jnp.concatenate([grad_qkv_rows, grad_out_rows], axis=0)
-    grad_kinds = grad_kinds.reshape(4, tensor_count, dp_count // 4, -1, width)
-    grad_kinds = grad_kinds.transpose(0, 2, 1, 3, 4).reshape(-1, width)
-    attn_owned = scatter_slab(grad_kinds, dp_count).reshape(4, head_cols, -1)
-
-    vectors = [
-        gain_first,
-        shift_first,
-        jnp.sum(grad_query, axis=1, dtype=wide),
-        jnp.sum(grad_value, axis=1, dtype=wide),
+
+    mlp_cols = to_columns(mlp_grads, dp_count).reshape(dp_count, 2 * slab_units // dp_count, -1)
+    cuts = (0, bulk_rows, 2 * bulk_rows, 2 * bulk_rows + hop_rows, 2 * bulk_rows + 2 * hop_rows)
+    parts = [
+        mlp_cols[:, cuts[i] : cuts[i + 1]].reshape(-1, mlp_cols.shape[2]) for i in range(4)
+    ]
+    grad_w_up = jnp.concatenate([parts[0], parts[2]], axis=0)[:unit_cols].T
+    grad_w_down = jnp.concatenate([parts[1], parts[3]], axis=0)[:unit_cols]
+    attn_cols = to_columns(attn_owned, dp_count).reshape(4, head_cols, -1)
+
+    early = [
         jnp.sum(grad_branch, axis=0, dtype=wide),
         gain_second,
         shift_second,
         jnp.sum(grad_wide, axis=0),
-        grad_up_bias[:, 0],
+        up_grad,
     ]
-    summed = lax.psum(jnp.concatenate(vectors), everyone)
-    small = [summed[i * width : (i + 1) * width] for i in range(8)]
+    late = [
+        gain_first,
+        shift_first,
+        from_heads(jnp.sum(grad_projected[0], axis=1, dtype=wide)),
+        from_heads(jnp.sum(grad_projected[2], axis=1, dtype=wide)),
+    ]
+    if by_hops:
+        early = hops.sum_all(jnp.concatenate(early).reshape(-1, 128)).reshape(-1)
+        late = hops.sum_all(jnp.concatenate(late).reshape(-1, 128)).reshape(-1)
+    else:
+        early = lax.psum(jnp.concatenate(early), everyone)
+        late = lax.psum(jnp.concatenate(late), everyone)
+    early_part = lambda place: early[place * width : (place + 1) * width]
+    late_part = lambda place: late[place * width : (place + 1) * width]
+    up_all = early[4 * width :]
+    bulk_count = tensor_count * bulk_units
+    up_all = jnp.concatenate(
+        [from_slabs(up_all[:bulk_count])]
+        + ([from_slabs(up_all[bulk_count:])] if by_hops else []),
+        axis=1,
+    )
     return (
         layer_out,
         input_grad,
-        small[0],
-        small[1],
-        attn_owned[0].T,
-        lax.dynamic_slice_in_dim(small[2], col_start, head_cols),
-        attn_owned[1].T,
-        attn_owned[2].T,
-        lax.dynamic_slice_in_dim(small[3], col_start, head_cols),
-        attn_owned[3],
-        small[4],
-        small[5],
-        small[6],
+        late_part(0),
+        late_part(1),
+        attn_cols[0].T,
+        lax.dynamic_slice_in_dim(late_part(2), col_start, head_cols),
+        attn_cols[1].T,
+        attn_cols[2].T,
+        lax.dynamic_slice_in_dim(late_part(3), col_start, head_cols),
+        attn_cols[3],
+        early_part(0),
+        early_part(1),
+        early_part(2),
         grad_w_up,
-        unit_order(summed[8 * width :]),
+        up_all[:, :unit_cols].reshape(-1),
         grad_w_down,
-        small[7],
+        early_part(3),
     )
 
 

time: 825 us -> 1030 us (1.25)
  Pallas kernels: 114 us -> 466 us
  waiting for transfers between devices: 417 us -> 246 us
  blocking collectives: 72.1 us -> 16.3 us
  starting transfers between devices: 17.2 us -> 71.6 us
  local copies, waits for them, and re-layouts: 71.2 us -> 102 us
  matrix products: 48.6 us -> 33.2 us
    pallas_call x1 -> x5, Pallas kernels: 73.5 us -> 424 us  [the longest x1 323 us: place(): pl.pallas_call(place_kernel, in_specs=[pl.BlockSpec(memory_space=pltpu.SM...]
    ppermute x0 -> x45, waiting for transfers between devices: none -> 246 us  [send(): return lax.ppermute(values, everyone, pairs)]
    all_gather x3 -> x2, waiting for transfers between devices: 154 us -> 0.01 us  [gather_rows(): return lax.all_gather(owned, everyone, axis=0, tiled=True)]
    reduce_scatter x1 -> x2, waiting for transfers between devices: 120 us -> 0.04 us  [scatter_rows(): return lax.psum_scatter(terms, everyone, scatter_dimension=0, tiled=True)]
    unnamed x8 -> x4, waiting for transfers between devices: 86.8 us -> 0.07 us
    ppermute x0 -> x45, starting transfers between devices: none -> 56.2 us  [send(): return lax.ppermute(values, everyone, pairs)]
    ppermute x4, waiting for transfers between devices: 50.5 us -> 0.01 us  [swap(): return lax.ppermute(values, 'tensor', pairs)]
    psum x1 -> x0, blocking collectives: 39.8 us -> none  [shards(): summed = lax.psum(jnp.concatenate(vectors), everyone)]
  transfers between devices with their start and end apart: 13 -> 56, of which waited for: 9 -> 24; matrix products, arithmetic and copies ran while one was open for 20% -> 18% of each run, Pallas kernels for 5% -> 44%
where the time goes in v2:
time: 1030 us; the launch traced here: 1020 us
  Pallas kernels  466 us (45%)
  waiting for transfers between devices  246 us (24%)
  local copies, waits for them, and re-layouts  102 us (10%)
  starting transfers between devices  71.6 us (7%)
  other arithmetic  68.5 us (7%)
  matrix products  33.2 us (3%)
  blocking collectives  16.3 us (2%)
  between operations  15.6 us (2%)
    pallas_call x1, Pallas kernels, place(): pl.pallas_call(place_kernel, in_specs=[pl.BlockSpec(memory_space=pltpu.SM...  323 us
    ppermute x45, waiting for transfers between devices, send(): return lax.ppermute(values, everyone, pairs)  246 us
    pallas_call x3, Pallas kernels, mlp(): pl.pallas_call(partial(mlp_kernel, joined, before is not None), grid=(ste...  87 us
    ppermute x45, starting transfers between devices, send(): return lax.ppermute(values, everyone, pairs)  56.2 us
    unnamed x171, local copies, waits for them, and re-layouts  40.1 us
    dot_general x4, matrix products, product(): lax.dot_general(left, right, (((left_dim,), (right_dim,)), ((), ())), pre...  33.2 us
    pallas_call x1, Pallas kernels, attend_back(): pl.pallas_call(partial(attend_back_kernel, step_heads), grid=(steps,), in...  26.7 us
  transfers between devices with their start and end apart: 56, of which 24 were waited for; matrix products, arithmetic and copies ran while one was open for 18% of the time, Pallas kernels for 44%

profile of v2, /device:TPU:0, one launch (start us, length us, event | category | flops | bytes accessed | tf_op | source)
XLA Modules:
  0.0 1019.0 jit_solution(116937933861801358)
XLA Ops:
  10.0 16.3 %all_to_all.48 = bf16[4,272,288]{2,1,0:T(8,128)(2,1)S(1)} all-to-all(bf16[4,272,288]{2,1,0:T(8,128)(2,1)S(1)} %pad_maximum_fusion.4), channel_id=1, replica_groups=mesh['dp'=4,'tensor'=8] {'dp'}, dimensions={0} | all-to-all | bytes 1253376 | tf_op jit(solution)/shard_map/all_to_all | solution.py:321
  29.0 2.4 dynamic-slice_bitcast_fusion.3
  33.9 3.5 all-to-all-start
  37.4 2.8 dynamic-slice_bitcast_fusion.1
  49.4 2.7 collective-permute-start.4
  62.5 20.8 %collective-permute-done.4 = bf16[144,1152]{1,0:T(8,128)(2,1)} collective-permute-done((bf16[144,1152]{1,0:T(8,128)(2,1)S(1)}, bf16[144,1152]{1,0:T(8,128)(2,1)}, u32[]{:S(2)}, u32[]{:S(2)}) %collective-permute-start.4) | collective-permute-done | bytes 331808 | tf_op jit(solution)/shard_map/ppermute | solution.py:343
  84.3 7.9 collective-permute-start.16
  95.7 27.4 %collective-permute-done.16 = bf16[112,1152]{1,0:T(8,128)(2,1)S(1)} collective-permute-done((bf16[112,1152]{1,0:T(8,128)(2,1)}, bf16[112,1152]{1,0:T(8,128)(2,1)S(1)}, u32[]{:S(2)}, u32[]{:S(2)}) %collective-permute-start.16) | collective-permute-done | bytes 258080 | tf_op jit(solution)/shard_map/ppermute | solution.py:343
  127.9 25.9 %collective-permute-done.14 = bf16[224,1152]{1,0:T(8,128)(2,1)S(1)} collective-permute-done((bf16[224,1152]{1,0:T(8,128)(2,1)S(1)}, bf16[224,1152]{1,0:T(8,128)(2,1)S(1)}, u32[]{:S(2)}, u32[]{:S(2)}) %collective-permute-start.14) | collective-permute-done | bytes 516128 | tf_op jit(solution)/shard_map/ppermute | solution.py:343
  159.9 24.1 %collective-permute-done.15 = bf16[448,1152]{1,0:T(8,128)(2,1)S(1)} collective-permute-done((bf16[448,1152]{1,0:T(8,128)(2,1)S(1)}, bf16[448,1152]{1,0:T(8,128)(2,1)S(1)}, u32[]{:S(2)}, u32[]{:S(2)}) %collective-permute-start.15) | collective-permute-done | bytes 1032224 | tf_op jit(solution)/shard_map/ppermute | solution.py:343
  188.6 2.5 pad_maximum_fusion.1.grad_ref
  192.5 11.7 %collective-permute-done.7.refs_3_ = bf16[576,1152]{1,0:T(8,128)(2,1)S(1)} collective-permute-done((bf16[576,1152]{1,0:T(8,128)(2,1)S(1)}, bf16[576,1152]{1,0:T(8,128)(2,1)S(1)}, u32[]{:S(2)}, u32[]{:S(2)}) %collective-permute-start.7) | collective-permute-done | bytes 1327136 | tf_op jit(solution)/shard_map/ppermute | solution.py:343
  204.1 16.6 %collective-permute-done.3.refs_1_ = bf16[576,1152]{1,0:T(8,128)(2,1)S(1)} collective-permute-done((bf16[576,1152]{1,0:T(8,128)(2,1)S(1)}, bf16[576,1152]{1,0:T(8,128)(2,1)S(1)}, u32[]{:S(2)}, u32[]{:S(2)}) %collective-permute-start.3) | collective-permute-done | bytes 1327136 | tf_op jit(solution)/shard_map/ppermute | solution.py:343
  220.8 3.6 collective-permute-done.19
  234.1 322.8 %place.1 = bf16[4,1152,1152]{2,1,0:T(8,128)(2,1)} custom-call(s32[1]{0:T(128)} %bitcast.2.kind_ref, bf16[576,1152]{1,0:T(8,128)(2,1)} %copy-done.22, bf16[576,1152]{1,0:T(8,128)(2,1)} %copy-done.25, bf16[576,1152]{1,0:T(8,128)(2,1)} %copy-done.23, bf16[576,1152]{1,0:T(8,128)(2,1)} %copy-done.24, bf16[576,1152]{1,0:T(8,128)(2,1)} %copy-done.27, ...), custom_call_target="tpu_custom_call" | custom-call | bytes 21233664 | tf_op jit(solution)/shard_map/place/pallas_call | solution.py:255
  556.9 7.1 slice.479
  564.0 12.3 %add_convert_fusion.query_ref.key_ref.value_ref = bf16[3456,736]{1,0:T(8,128)(2,1)} fusion(bf16[3456,1152]{1,0:T(8,128)(2,1)} %bitcast.253, bf16[736,1152]{1,0:T(8,128)(2,1)S(1)} %fusion.7.normed_ref, f32[3456]{0:T(1024)S(1)} %copy-done.47), kind=kOutput, calls=%fused_computation.7 | convolution fusion | flops 5865578496 | bytes 14759424 | tf_op jit(solution)/shard_map/dot_general | solution.py:23
  576.4 15.3 %attend.1 = (bf16[1152,736]{1,0:T(8,128)(2,1)S(1)}, f32[16,1,736]{2,1,0:T(1,128)S(1)}) custom-call(bf16[3456,736]{1,0:T(8,128)(2,1)} %add_convert_fusion.query_ref.key_ref.value_ref, bf16[3456,736]{1,0:T(8,128)(2,1)} %add_convert_fusion.query_ref.key_ref.value_ref, bf16[3456,736]{1,0:T(8,128)(2,1)} %add_convert_fusion.query_ref.key_ref.value_ref, ...), custom_call_target="tpu_custom_call" | custom-call | flops 8875147264 | bytes 16777216 | tf_op jit(solution)/shard_map/attend/pallas_call | solution.py:93
  591.7 5.3 fusion.49
  599.6 43.1 %mlp.3 = (f32[736,1152]{1,0:T(8,128)}, f32[736,1152]{1,0:T(8,128)}, bf16[2560,1152]{1,0:T(8,128)(2,1)}, bf16[2560,1152]{1,0:T(8,128)(2,1)}, f32[2560,1]{1,0:T(8,128)}) custom-call(bf16[736,1152]{1,0:T(8,128)(2,1)} %add_convert_fusion.2.normed_ref, bf16[736,1152]{1,0:T(8,128)(2,1)} %pad_maximum_fusion.1.grad_ref, ...), custom_call_target="tpu_custom_call" | custom-call | flops 34728837120 | bytes 67108864 | tf_op jit(solution)/shard_map/mlp/pallas_call | solution.py:207
  642.7 21.8 %mlp.4 = (f32[736,1152]{1,0:T(8,128)}, f32[736,1152]{1,0:T(8,128)}, bf16[2,896,1152]{2,1,0:T(8,128)(2,1)}, f32[896,1]{1,0:T(8,128)}) custom-call(bf16[736,1152]{1,0:T(8,128)(2,1)} %add_convert_fusion.2.normed_ref, bf16[736,1152]{1,0:T(8,128)(2,1)} %pad_maximum_fusion.1.grad_ref, ...), custom_call_target="tpu_custom_call", output_to_operand_aliasing={{0}: (5, {}), {1}: (6, {})} | custom-call | flops 12155092992 | bytes 67108864 | tf_op jit(solution)/shard_map/mlp/pallas_call | solution.py:207
  665.1 22.1 %mlp.5 = (f32[736,1152]{1,0:T(8,128)}, f32[736,1152]{1,0:T(8,128)}, bf16[2,896,1152]{2,1,0:T(8,128)(2,1)}, f32[896,1]{1,0:T(8,128)}) custom-call(bf16[736,1152]{1,0:T(8,128)(2,1)} %add_convert_fusion.2.normed_ref, bf16[736,1152]{1,0:T(8,128)(2,1)} %pad_maximum_fusion.1.grad_ref, ...), custom_call_target="tpu_custom_call", output_to_operand_aliasing={{0}: (5, {}), {1}: (6, {})} | custom-call | flops 12155092992 | bytes 67108864 | tf_op jit(solution)/shard_map/mlp/pallas_call | solution.py:207
  692.0 4.0 multiply_reduce_fusion
  697.8 7.5 convert_reduce_fusion.4
  705.5 5.6 convolution_convert_fusion
  711.1 2.7 copy.242.grad_ref
  716.3 26.7 %attend_back.1.grads_ref = bf16[3,1152,736]{2,1,0:T(8,128)(2,1)} custom-call(bf16[3456,736]{1,0:T(8,128)(2,1)} %add_convert_fusion.query_ref.key_ref.value_ref, bf16[3456,736]{1,0:T(8,128)(2,1)} %add_convert_fusion.query_ref.key_ref.value_ref, bf16[3456,736]{1,0:T(8,128)(2,1)} %add_convert_fusion.query_ref.key_ref.value_ref, f32[736,1]{1,0:T(8,128)S(1)} %copy-done.6, ...), custom_call_target="tpu_custom_call" | custom-call | flops 17750294528 | bytes 16777216 | tf_op jit(solution)/shard_map/attend_back/pallas_call | solution.py:116
  742.9 2.5 copy-done.2
  745.4 14.1 %kinds_grad.1 = bf16[4,1152,1152]{2,1,0:T(8,128)(2,1)} custom-call(s32[1]{0:T(128)} %bitcast.2.kind_ref, bf16[3,1152,736]{2,1,0:T(8,128)(2,1)S(1)} %copy-done.2, bf16[1152,736]{1,0:T(8,128)(2,1)S(1)} %copy-done.8, bf16[736,1152]{1,0:T(8,128)(2,1)S(1)} %copy-done.4, bf16[736,1152]{1,0:T(8,128)(2,1)S(1)} %get-tuple-element.143.branch_ref), custom_call_target="tpu_custom_call" | custom-call | flops 11720982528 | bytes 25165824 | tf_op jit(solution)/shard_map/kinds_grad/pallas_call | solution.py:289
  759.6 5.3 slice.514
  765.5 10.0 fusion.12
  784.4 4.0 fusion.11
  793.9 1.9 collective-permute-start.39
  804.5 4.1 fusion.23
  809.7 2.0 collective-permute-start.45
  814.0 2.0 maximum_select_fusion
  816.0 39.6 %collective-permute-done.42 = bf16[2,224,1152]{2,1,0:T(8,128)(2,1)} collective-permute-done((bf16[2,224,1152]{2,1,0:T(8,128)(2,1)}, bf16[2,224,1152]{2,1,0:T(8,128)(2,1)}, u32[]{:S(2)}, u32[]{:S(2)}) %collective-permute-start.42) | collective-permute-done | bytes 1032224 | tf_op jit(solution)/shard_map/ppermute | solution.py:343
  855.5 2.9 fusion.21
  858.6 2.3 collective-permute-start.43
  861.0 2.5 collective-permute-start.46
  865.3 3.4 collective-permute-done.43
  870.6 5.7 collective-permute-done.46
  876.5 4.7 collective-permute-start.48
  883.0 16.8 %collective-permute-done.47 = bf16[2,56,1152]{2,1,0:T(8,128)(2,1)S(1)} collective-permute-done((bf16[2,56,1152]{2,1,0:T(8,128)(2,1)S(1)}, bf16[2,56,1152]{2,1,0:T(8,128)(2,1)S(1)}, u32[]{:S(2)}, u32[]{:S(2)}) %collective-permute-start.47) | collective-permute-done | bytes 258080 | tf_op jit(solution)/shard_map/ppermute | solution.py:343
  899.9 5.7 collective-permute-done.29
  909.2 9.8 collective-permute-done.32
  920.8 2.0 collective-permute-start.33
  922.8 6.2 collective-permute-done.30
  929.3 2.3 collective-permute-done.33
  931.8 4.3 collective-permute-start.34
  938.6 2.7 collective-permute-done.31
  941.3 17.7 %collective-permute-done.34 = bf16[144,1152]{1,0:T(8,128)(2,1)S(1)} collective-permute-done((bf16[144,1152]{1,0:T(8,128)(2,1)S(1)}, bf16[144,1152]{1,0:T(8,128)(2,1)S(1)}, u32[]{:S(2)}, u32[]{:S(2)}) %collective-permute-start.34) | collective-permute-done | bytes 331808 | tf_op jit(solution)/shard_map/ppermute | solution.py:343
  959.2 2.6 copy.244
  962.4 7.0 reduce.7
  971.1 4.1 all-to-all-start.2
  976.4 4.1 copy.258
  980.5 6.4 reduce.8
  986.9 2.1 reshape.460
  989.0 3.5 all-to-all-start.3
  992.5 2.9 maximum_select_fusion.1
  995.4 3.1 reshape.459
  998.5 2.4 copy.245
  1005.0 2.2 reshape.461
  1007.1 2.5 copy.259
  (402 shorter events, 121.5 us)
Async XLA Ops:
  7.2 592.4 %all-gather.3.cloned.1.call-start = ((), (), s32[]{:S(2)}) async-start(), calls=%async_computation.6 | async-start | bytes 6082560 | tf_op jit(solution)/shard_map/all_gather | solution.py:312
  31.4 159.7 %copy-start.10 = (bf16[368,1152]{1,0:T(8,128)(2,1)}, bf16[368,1152]{1,0:T(8,128)(2,1)S(1)}, u32[]{:S(2)}) copy-start(bf16[368,1152]{1,0:T(8,128)(2,1)S(1)} %get-tuple-element.155) | copy-start | bytes 2543620
  31.5 95.5 %collective-permute-start = (bf16[368,1152]{1,0:T(8,128)(2,1)}, bf16[368,1152]{1,0:T(8,128)(2,1)S(1)}, u32[]{:S(2)}, u32[]{:S(2)}) collective-permute-start(bf16[368,1152]{1,0:T(8,128)(2,1)} %get-tuple-element.156), channel_id=1, source_target_pairs={{0,1},{1,0},{2,3},{3,2},{4,5},{5,4},{6,7},{7,6},{8,9},{9,8},{10,11... | collective-permute-start | bytes 2543624 | tf_op jit(solution)/shard_map/ppermute | solution.py:471
  33.9 15.1 %all-to-all-start = ((bf16[4,144,288]{2,1,0:T(8,128)(2,1)}), bf16[4,144,288]{2,1,0:T(8,128)(2,1)S(1)}, u32[]{:S(2)}, u32[]{:S(2)}) async-start(bf16[4,144,288]{2,1,0:T(8,128)(2,1)} %bitcast.6), calls=%async_computation | async-start | bytes 884736 | tf_op jit(solution)/shard_map/all_to_all | solution.py:321
  37.4 562.2 %all-gather.5.cloned.1.call-start = ((), (), s32[]{:S(2)}) async-start(), calls=%async_computation.7 | async-start | bytes 6082560 | tf_op jit(solution)/shard_map/all_gather | solution.py:312
  40.2 148.4 %collective-permute-start.12 = (bf16[368,1152]{1,0:T(8,128)(2,1)}, bf16[368,1152]{1,0:T(8,128)(2,1)}, u32[]{:S(2)}, u32[]{:S(2)}) collective-permute-start(bf16[368,1152]{1,0:T(8,128)(2,1)} %get-tuple-element.154), channel_id=1, source_target_pairs={{0,1},{1,0},{2,3},{3,2},{4,5},{5,4},{6,7},{7,6},{8,9},{9,8},{10,11... | collective-permute-start | bytes 2543624 | tf_op jit(solution)/shard_map/ppermute | solution.py:471
  44.0 532.3 %copy-start.5 = (f32[736,1]{1,0:T(8,128)}, f32[736,1]{1,0:T(8,128)S(1)}, u32[]{:S(2)}) copy-start(f32[736,1]{1,0:T(8,128)S(1)} %select_n.95.bias_ref) | copy-start | bytes 8836
  49.4 33.8 %collective-permute-start.4 = (bf16[144,1152]{1,0:T(8,128)(2,1)S(1)}, bf16[144,1152]{1,0:T(8,128)(2,1)}, u32[]{:S(2)}, u32[]{:S(2)}) collective-permute-start(bf16[144,1152]{1,0:T(8,128)(2,1)S(1)} %squeeze.96), channel_id=1, source_target_pairs={{0,4},{1,5},{2,6},{3,7},{4,0},{5,1},{6,2},{7,3},{8,12},{9,13},{10,... | collective-permute-start | bytes 995336 | tf_op jit(solution)/shard_map/ppermute | solution.py:343
  52.1 32.2 %collective-permute-start.5 = (bf16[144,1152]{1,0:T(8,128)(2,1)S(1)}, bf16[144,1152]{1,0:T(8,128)(2,1)}, u32[]{:S(2)}, u32[]{:S(2)}) collective-permute-start(bf16[144,1152]{1,0:T(8,128)(2,1)S(1)} %squeeze.96), channel_id=1, source_target_pairs={{0,6},{1,7},{2,4},{3,5},{4,2},{5,3},{6,0},{7,1},{8,14},{9,15},{10,... | collective-permute-start | bytes 995336 | tf_op jit(solution)/shard_map/ppermute | solution.py:343
  53.5 40.9 %collective-permute-start.1 = (bf16[144,1152]{1,0:T(8,128)(2,1)S(1)}, bf16[144,1152]{1,0:T(8,128)(2,1)S(1)}, u32[]{:S(2)}, u32[]{:S(2)}) collective-permute-start(bf16[144,1152]{1,0:T(8,128)(2,1)S(1)} %squeeze.96), channel_id=1, source_target_pairs={{0,2},{1,3},{2,0},{3,1},{4,6},{5,7},{6,4},{7,5},{8,10},{9,11},{10,... | collective-permute-start | bytes 995336 | tf_op jit(solution)/shard_map/ppermute | solution.py:343
  62.4 912.8 %reduce-scatter.3.cloned.1.call-start = ((), (), s32[]{:S(2)}) async-start(), calls=%async_computation.8 | async-start | bytes 6082560 | tf_op jit(solution)/shard_map/reduce_scatter | solution.py:316
  62.4 63.8 %copy-start.48 = (bf16[448,1152]{1,0:T(8,128)(2,1)S(1)}, bf16[448,1152]{1,0:T(8,128)(2,1)}, u32[]{:S(2)}) copy-start(bf16[448,1152]{1,0:T(8,128)(2,1)} %get-tuple-element.198) | copy-start | bytes 3096580
  83.3 41.4 %collective-permute-start.13 = (bf16[112,1152]{1,0:T(8,128)(2,1)}, bf16[112,1152]{1,0:T(8,128)(2,1)S(1)}, u32[]{:S(2)}, u32[]{:S(2)}) collective-permute-start(bf16[112,1152]{1,0:T(8,128)(2,1)} %copy.230), channel_id=1, source_target_pairs={{0,2},{1,3},{2,0},{3,1},{4,6},{5,7},{6,4},{7,5},{8,10},{9,11},{10,... | collective-permute-start | bytes 774152 | tf_op jit(solution)/shard_map/ppermute | solution.py:343
  84.3 38.8 %collective-permute-start.16 = (bf16[112,1152]{1,0:T(8,128)(2,1)}, bf16[112,1152]{1,0:T(8,128)(2,1)S(1)}, u32[]{:S(2)}, u32[]{:S(2)}) collective-permute-start(bf16[112,1152]{1,0:T(8,128)(2,1)} %copy.230), channel_id=1, source_target_pairs={{0,4},{1,5},{2,6},{3,7},{4,0},{5,1},{6,2},{7,3},{8,12},{9,13},{10,... | collective-permute-start | bytes 774152 | tf_op jit(solution)/shard_map/ppermute | solution.py:343
  94.4 32.0 %collective-permute-start.17 = (bf16[112,1152]{1,0:T(8,128)(2,1)}, bf16[112,1152]{1,0:T(8,128)(2,1)S(1)}, u32[]{:S(2)}, u32[]{:S(2)}) collective-permute-start(bf16[112,1152]{1,0:T(8,128)(2,1)} %copy.230), channel_id=1, source_target_pairs={{0,6},{1,7},{2,4},{3,5},{4,2},{5,3},{6,0},{7,1},{8,14},{9,15},{10,... | collective-permute-start | bytes 774152 | tf_op jit(solution)/shard_map/ppermute | solution.py:343
  123.1 33.3 %collective-permute-start.6 = (bf16[288,1152]{1,0:T(8,128)(2,1)S(1)}, bf16[288,1152]{1,0:T(8,128)(2,1)S(1)}, u32[]{:S(2)}, u32[]{:S(2)}) collective-permute-start(bf16[288,1152]{1,0:T(8,128)(2,1)S(1)} %pad_maximum_fusion.6), channel_id=1, source_target_pairs={{0,1},{1,0},{2,3},{3,2},{4,5},{5,4},{6,7},{7,6},{8,9},{9,8},{10,11... | collective-permute-start | bytes 1990664 | tf_op jit(solution)/shard_map/ppermute | solution.py:343
  124.7 33.6 %collective-permute-start.2 = (bf16[288,1152]{1,0:T(8,128)(2,1)S(1)}, bf16[288,1152]{1,0:T(8,128)(2,1)S(1)}, u32[]{:S(2)}, u32[]{:S(2)}) collective-permute-start(bf16[288,1152]{1,0:T(8,128)(2,1)S(1)} %pad_maximum_fusion.5), channel_id=1, source_target_pairs={{0,16},{1,17},{2,18},{3,19},{4,20},{5,21},{6,22},{7,23},{8,24},{9,... | collective-permute-start | bytes 1990664 | tf_op jit(solution)/shard_map/ppermute | solution.py:343
  126.4 27.5 %collective-permute-start.14 = (bf16[224,1152]{1,0:T(8,128)(2,1)S(1)}, bf16[224,1152]{1,0:T(8,128)(2,1)S(1)}, u32[]{:S(2)}, u32[]{:S(2)}) collective-permute-start(bf16[224,1152]{1,0:T(8,128)(2,1)S(1)} %pad_maximum_fusion.7), channel_id=1, source_target_pairs={{0,16},{1,17},{2,18},{3,19},{4,20},{5,21},{6,22},{7,23},{8,24},{9,... | collective-permute-start | bytes 1548296 | tf_op jit(solution)/shard_map/ppermute | solution.py:343
  127.0 32.8 %collective-permute-start.18 = (bf16[224,1152]{1,0:T(8,128)(2,1)S(1)}, bf16[224,1152]{1,0:T(8,128)(2,1)S(1)}, u32[]{:S(2)}, u32[]{:S(2)}) collective-permute-start(bf16[224,1152]{1,0:T(8,128)(2,1)S(1)} %pad_maximum_fusion.8), channel_id=1, source_target_pairs={{0,1},{1,0},{2,3},{3,2},{4,5},{5,4},{6,7},{7,6},{8,9},{9,8},{10,11... | collective-permute-start | bytes 1548296 | tf_op jit(solution)/shard_map/ppermute | solution.py:343
  127.9 63.2 %copy-start.36 = (f32[736]{0:T(1024)}, f32[736]{0:T(1024)S(1)}, u32[]{:S(2)}) copy-start(f32[736]{0:T(1024)S(1)} %broadcast_multiply_fusion.5) | copy-start | bytes 8836
  155.3 28.7 %collective-permute-start.15 = (bf16[448,1152]{1,0:T(8,128)(2,1)S(1)}, bf16[448,1152]{1,0:T(8,128)(2,1)S(1)}, u32[]{:S(2)}, u32[]{:S(2)}) collective-permute-start(bf16[448,1152]{1,0:T(8,128)(2,1)S(1)} %get-tuple-element.179), channel_id=1, source_target_pairs={{0,1},{1,0},{2,3},{3,2},{4,5},{5,4},{6,7},{7,6},{8,9},{9,8},{10,11... | collective-permute-start | bytes 3096584 | tf_op jit(solution)/shard_map/ppermute | solution.py:343
  156.6 47.6 %collective-permute-start.7 = (bf16[576,1152]{1,0:T(8,128)(2,1)S(1)}, bf16[576,1152]{1,0:T(8,128)(2,1)S(1)}, u32[]{:S(2)}, u32[]{:S(2)}) collective-permute-start(bf16[576,1152]{1,0:T(8,128)(2,1)S(1)} %constant_dynamic-update-slice_fusion.3.refs_2_), channel_id=1, source_target_pairs={{0,16},{1,17},{2,18},{3,19},{4,20},{5,21},{6,22},{7,23},{8,24},{9,... | collective-permute-start | bytes 3981320 | tf_op jit(solution)/shard_map/ppermute | solution.py:343
  158.3 62.5 %collective-permute-start.3 = (bf16[576,1152]{1,0:T(8,128)(2,1)S(1)}, bf16[576,1152]{1,0:T(8,128)(2,1)S(1)}, u32[]{:S(2)}, u32[]{:S(2)}) collective-permute-start(bf16[576,1152]{1,0:T(8,128)(2,1)S(1)} %constant_dynamic-update-slice_fusion.refs_0_), channel_id=1, source_target_pairs={{0,1},{1,0},{2,3},{3,2},{4,5},{5,4},{6,7},{7,6},{8,9},{9,8},{10,11... | collective-permute-start | bytes 3981320 | tf_op jit(solution)/shard_map/ppermute | solution.py:343
  187.0 37.5 %collective-permute-start.19 = (bf16[448,1152]{1,0:T(8,128)(2,1)S(1)}, bf16[448,1152]{1,0:T(8,128)(2,1)S(1)}, u32[]{:S(2)}, u32[]{:S(2)}) collective-permute-start(bf16[448,1152]{1,0:T(8,128)(2,1)S(1)} %get-tuple-element.177), channel_id=1, source_target_pairs={{0,16},{1,17},{2,18},{3,19},{4,20},{5,21},{6,22},{7,23},{8,24},{9,... | collective-permute-start | bytes 3096584 | tf_op jit(solution)/shard_map/ppermute | solution.py:343
  191.9 372.1 %copy-start.3 = (bf16[736,1152]{1,0:T(8,128)(2,1)}, bf16[736,1152]{1,0:T(8,128)(2,1)S(1)}, u32[]{:S(2)}) copy-start(bf16[736,1152]{1,0:T(8,128)(2,1)S(1)} %fusion.7.normed_ref) | copy-start | bytes 5087236
  191.9 39.2 %collective-permute-start.10 = (bf16[576,1152]{1,0:T(8,128)(2,1)S(1)}, bf16[576,1152]{1,0:T(8,128)(2,1)S(1)}, u32[]{:S(2)}, u32[]{:S(2)}) collective-permute-start(bf16[576,1152]{1,0:T(8,128)(2,1)S(1)} %constant_dynamic-update-slice_fusion.3.refs_2_), channel_id=1, source_target_pairs={{0,8},{1,9},{2,10},{3,11},{4,12},{5,13},{6,14},{7,15},{8,0},{9,1},... | collective-permute-start | bytes 3981320 | tf_op jit(solution)/shard_map/ppermute | solution.py:343
  192.0 39.1 %collective-permute-start.8 = (bf16[576,1152]{1,0:T(8,128)(2,1)S(1)}, bf16[576,1152]{1,0:T(8,128)(2,1)S(1)}, u32[]{:S(2)}, u32[]{:S(2)}) collective-permute-start(bf16[576,1152]{1,0:T(8,128)(2,1)S(1)} %constant_dynamic-update-slice_fusion.refs_0_), channel_id=1, source_target_pairs={{0,8},{1,9},{2,10},{3,11},{4,12},{5,13},{6,14},{7,15},{8,0},{9,1},... | collective-permute-start | bytes 3981320 | tf_op jit(solution)/shard_map/ppermute | solution.py:343
  204.1 27.0 %collective-permute-start.11 = (bf16[576,1152]{1,0:T(8,128)(2,1)S(1)}, bf16[576,1152]{1,0:T(8,128)(2,1)S(1)}, u32[]{:S(2)}, u32[]{:S(2)}) collective-permute-start(bf16[576,1152]{1,0:T(8,128)(2,1)S(1)} %collective-permute-done.7.refs_3_), channel_id=1, source_target_pairs={{0,8},{1,9},{2,10},{3,11},{4,12},{5,13},{6,14},{7,15},{8,0},{9,1},... | collective-permute-start | bytes 3981320 | tf_op jit(solution)/shard_map/ppermute | solution.py:343
  220.8 10.4 %collective-permute-start.9 = (bf16[576,1152]{1,0:T(8,128)(2,1)S(1)}, bf16[576,1152]{1,0:T(8,128)(2,1)S(1)}, u32[]{:S(2)}, u32[]{:S(2)}) collective-permute-start(bf16[576,1152]{1,0:T(8,128)(2,1)S(1)} %collective-permute-done.3.refs_1_), channel_id=1, source_target_pairs={{0,8},{1,9},{2,10},{3,11},{4,12},{5,13},{6,14},{7,15},{8,0},{9,1},... | collective-permute-start | bytes 3981320 | tf_op jit(solution)/shard_map/ppermute | solution.py:343
  231.1 411.6 %collective-permute-start.20 = (bf16[1792,1152]{1,0:T(8,128)(2,1)}, bf16[1792,1152]{1,0:T(8,128)(2,1)}, u32[]{:S(2)}, u32[]{:S(2)}) collective-permute-start(bf16[1792,1152]{1,0:T(8,128)(2,1)} %slice_dynamic-update-slice_fusion.up_ref.down_ref), channel_id=1, source_target_pairs={{0,8},{1,9},{2,10},{3,11},{4,12},{5,13},{6,14},{7,15},{8,0},{9,1},... | collective-permute-start | bytes 12386312 | tf_op jit(solution)/shard_map/ppermute | solution.py:343
  597.0 95.0 %copy-start.9 = (f32[736,1152]{1,0:T(8,128)}, f32[736,1152]{1,0:T(8,128)S(1)}, u32[]{:S(2)}) copy-start(f32[736,1152]{1,0:T(8,128)S(1)} %get-tuple-element.211) | copy-start | bytes 10174468
  597.8 94.2 %copy-start.38 = (f32[736]{0:T(1024)}, f32[736]{0:T(1024)S(1)}, u32[]{:S(2)}) copy-start(f32[736]{0:T(1024)S(1)} %add_rsqrt_fusion) | copy-start | bytes 8836
  664.5 140.0 %collective-permute-start.41 = (bf16[2,896,1152]{2,1,0:T(8,128)(2,1)}, bf16[2,896,1152]{2,1,0:T(8,128)(2,1)}, u32[]{:S(2)}, u32[]{:S(2)}) collective-permute-start(bf16[2,896,1152]{2,1,0:T(8,128)(2,1)} %get-tuple-element.46), channel_id=1, source_target_pairs={{0,8},{1,9},{2,10},{3,11},{4,12},{5,13},{6,14},{7,15},{8,0},{9,1},... | collective-permute-start | bytes 12386312 | tf_op jit(solution)/shard_map/ppermute | solution.py:343
  665.1 310.2 %reduce-scatter.5.cloned.1.call-start = ((), (), s32[]{:S(2)}) async-start(), calls=%async_computation.9 | async-start | bytes 6082560 | tf_op jit(solution)/shard_map/reduce_scatter | solution.py:316
  705.4 75.5 %collective-permute-start.36 = (f32[70,128]{1,0:T(8,128)S(1)}, f32[70,128]{1,0:T(8,128)}, u32[]{:S(2)}, u32[]{:S(2)}) collective-permute-start(f32[70,128]{1,0:T(8,128)S(1)} %bitcast.288), channel_id=1, source_target_pairs={{0,8},{1,9},{2,10},{3,11},{4,12},{5,13},{6,14},{7,15},{8,0},{9,1},... | collective-permute-start | bytes 107528 | tf_op jit(solution)/shard_map/ppermute | solution.py:343
  764.9 98.7 %collective-permute-start.28 = (bf16[2,8,144,1152]{3,2,1,0:T(8,128)(2,1)}, bf16[2,8,144,1152]{3,2,1,0:T(8,128)(2,1)}, u32[]{:S(2)}, u32[]{:S(2)}) collective-permute-start(bf16[2,8,144,1152]{3,2,1,0:T(8,128)(2,1)} %bitcast.258), channel_id=1, source_target_pairs={{0,8},{1,9},{2,10},{3,11},{4,12},{5,13},{6,14},{7,15},{8,0},{9,1},... | collective-permute-start | bytes 15925256 | tf_op jit(solution)/shard_map/ppermute | solution.py:343
  777.9 1.3 collective-permute-start.23
  779.2 3.8 collective-permute-start.24
  781.6 6.9 collective-permute-start.37
  783.0 5.4 collective-permute-start.25
  788.5 3.8 collective-permute-start.26
  789.4 4.4 collective-permute-start.38
  790.3 22.2 %collective-permute-start.22 = (bf16[368,1152]{1,0:T(8,128)(2,1)S(1)}, bf16[368,1152]{1,0:T(8,128)(2,1)}, u32[]{:S(2)}, u32[]{:S(2)}) collective-permute-start(bf16[368,1152]{1,0:T(8,128)(2,1)S(1)} %slice.672), channel_id=1, source_target_pairs={{0,1},{1,0},{2,3},{3,2},{4,5},{5,4},{6,7},{7,6},{8,9},{9,8},{10,11... | collective-permute-start | bytes 2543624 | tf_op jit(solution)/shard_map/ppermute | solution.py:471
  792.3 4.7 collective-permute-start.27
  793.9 4.1 collective-permute-start.39
  797.0 195.5 %collective-permute-start.21 = (bf16[368,1152]{1,0:T(8,128)(2,1)}, bf16[368,1152]{1,0:T(8,128)(2,1)}, u32[]{:S(2)}, u32[]{:S(2)}) collective-permute-start(bf16[368,1152]{1,0:T(8,128)(2,1)} %get-tuple-element.152), channel_id=1, source_target_pairs={{0,1},{1,0},{2,3},{3,2},{4,5},{5,4},{6,7},{7,6},{8,9},{9,8},{10,11... | collective-permute-start | bytes 2543624 | tf_op jit(solution)/shard_map/ppermute | solution.py:471
  798.7 4.9 collective-permute-start.40
  808.6 46.9 %collective-permute-start.42 = (bf16[2,224,1152]{2,1,0:T(8,128)(2,1)}, bf16[2,224,1152]{2,1,0:T(8,128)(2,1)}, u32[]{:S(2)}, u32[]{:S(2)}) collective-permute-start(bf16[2,224,1152]{2,1,0:T(8,128)(2,1)} %get-tuple-element.147), channel_id=1, source_target_pairs={{0,1},{1,0},{2,3},{3,2},{4,5},{5,4},{6,7},{7,6},{8,9},{9,8},{10,11... | collective-permute-start | bytes 3096584 | tf_op jit(solution)/shard_map/ppermute | solution.py:343
  809.7 45.8 %collective-permute-start.45 = (bf16[2,224,1152]{2,1,0:T(8,128)(2,1)}, bf16[2,224,1152]{2,1,0:T(8,128)(2,1)}, u32[]{:S(2)}, u32[]{:S(2)}) collective-permute-start(bf16[2,224,1152]{2,1,0:T(8,128)(2,1)} %get-tuple-element.148), channel_id=1, source_target_pairs={{0,16},{1,17},{2,18},{3,19},{4,20},{5,21},{6,22},{7,23},{8,24},{9,... | collective-permute-start | bytes 3096584 | tf_op jit(solution)/shard_map/ppermute | solution.py:343
  812.5 51.1 %slice-start.3 = ((s8[10616832]{0:T(1024)(128)(4,1)}), s8[2228224]{0:T(1024)(128)(4,1)S(1)}, s32[]{:S(2)}) async-start(s8[10616832]{0:T(1024)(128)(4,1)} %bitcast.247), calls=%async_computation.13 | async-start | bytes 4456448
  858.6 10.2 collective-permute-start.43
  861.0 15.2 %collective-permute-start.46 = (bf16[2,2,56,1152]{3,2,0,1:T(8,128)(2,1)S(1)}, bf16[2,2,56,1152]{3,2,0,1:T(8,128)(2,1)S(1)}, u32[]{:S(2)}, u32[]{:S(2)}) collective-permute-start(bf16[2,2,56,1152]{3,2,0,1:T(8,128)(2,1)S(1)} %bitcast.282), channel_id=1, source_target_pairs={{0,1},{1,0},{2,3},{3,2},{4,5},{5,4},{6,7},{7,6},{8,9},{9,8},{10,11... | collective-permute-start | bytes 1548296 | tf_op jit(solution)/shard_map/ppermute | solution.py:343
  865.2 40.3 %collective-permute-start.29 = (bf16[2,2,144,1152]{3,2,1,0:T(8,128)(2,1)S(1)}, bf16[2,2,144,1152]{3,2,1,0:T(8,128)(2,1)S(1)}, u32[]{:S(2)}, u32[]{:S(2)}) collective-permute-start(bf16[2,2,144,1152]{3,2,1,0:T(8,128)(2,1)S(1)} %fusion.17), channel_id=1, source_target_pairs={{0,1},{1,0},{2,3},{3,2},{4,5},{5,4},{6,7},{7,6},{8,9},{9,8},{10,11... | collective-permute-start | bytes 3981320 | tf_op jit(solution)/shard_map/ppermute | solution.py:343
  868.9 14.0 %collective-permute-start.44 = (bf16[2,56,1152]{2,1,0:T(8,128)(2,1)S(1)}, bf16[2,56,1152]{2,1,0:T(8,128)(2,1)S(1)}, u32[]{:S(2)}, u32[]{:S(2)}) collective-permute-start(bf16[2,56,1152]{2,1,0:T(8,128)(2,1)S(1)} %slice_bitcast_fusion.27), channel_id=1, source_target_pairs={{0,2},{1,3},{2,0},{3,1},{4,6},{5,7},{6,4},{7,5},{8,10},{9,11},{10,... | collective-permute-start | bytes 774152 | tf_op jit(solution)/shard_map/ppermute | solution.py:343
  876.4 23.3 %collective-permute-start.47 = (bf16[2,56,1152]{2,1,0:T(8,128)(2,1)S(1)}, bf16[2,56,1152]{2,1,0:T(8,128)(2,1)S(1)}, u32[]{:S(2)}, u32[]{:S(2)}) collective-permute-start(bf16[2,56,1152]{2,1,0:T(8,128)(2,1)S(1)} %get-tuple-element.175), channel_id=1, source_target_pairs={{0,4},{1,5},{2,6},{3,7},{4,0},{5,1},{6,2},{7,3},{8,12},{9,13},{10,... | collective-permute-start | bytes 774152 | tf_op jit(solution)/shard_map/ppermute | solution.py:343
  876.5 23.2 %collective-permute-start.48 = (bf16[2,56,1152]{2,1,0:T(8,128)(2,1)S(1)}, bf16[2,56,1152]{2,1,0:T(8,128)(2,1)S(1)}, u32[]{:S(2)}, u32[]{:S(2)}) collective-permute-start(bf16[2,56,1152]{2,1,0:T(8,128)(2,1)S(1)} %get-tuple-element.176), channel_id=1, source_target_pairs={{0,6},{1,7},{2,4},{3,5},{4,2},{5,3},{6,0},{7,1},{8,14},{9,15},{10,... | collective-permute-start | bytes 774152 | tf_op jit(solution)/shard_map/ppermute | solution.py:343
  882.9 36.1 %collective-permute-start.32 = (bf16[4,144,1152]{2,1,0:T(8,128)(2,1)S(1)}, bf16[4,144,1152]{2,1,0:T(8,128)(2,1)S(1)}, u32[]{:S(2)}, u32[]{:S(2)}) collective-permute-start(bf16[4,144,1152]{2,1,0:T(8,128)(2,1)S(1)} %fusion.14), channel_id=1, source_target_pairs={{0,16},{1,17},{2,18},{3,19},{4,20},{5,21},{6,22},{7,23},{8,24},{9,... | collective-permute-start | bytes 3981320 | tf_op jit(solution)/shard_map/ppermute | solution.py:343
  907.5 21.5 %collective-permute-start.30 = (bf16[2,144,1152]{2,1,0:T(8,128)(2,1)S(1)}, bf16[2,144,1152]{2,1,0:T(8,128)(2,1)S(1)}, u32[]{:S(2)}, u32[]{:S(2)}) collective-permute-start(bf16[2,144,1152]{2,1,0:T(8,128)(2,1)S(1)} %slice_bitcast_fusion.19), channel_id=1, source_target_pairs={{0,16},{1,17},{2,18},{3,19},{4,20},{5,21},{6,22},{7,23},{8,24},{9,... | collective-permute-start | bytes 1990664 | tf_op jit(solution)/shard_map/ppermute | solution.py:343
  920.8 10.7 %collective-permute-start.33 = (bf16[2,144,1152]{2,1,0:T(8,128)(2,1)S(1)}, bf16[2,144,1152]{2,1,0:T(8,128)(2,1)S(1)}, u32[]{:S(2)}, u32[]{:S(2)}) collective-permute-start(bf16[2,144,1152]{2,1,0:T(8,128)(2,1)S(1)} %slice.527), channel_id=1, source_target_pairs={{0,1},{1,0},{2,3},{3,2},{4,5},{5,4},{6,7},{7,6},{8,9},{9,8},{10,11... | collective-permute-start | bytes 1990664 | tf_op jit(solution)/shard_map/ppermute | solution.py:343
  929.2 12.1 %collective-permute-start.31 = (bf16[144,1152]{1,0:T(8,128)(2,1)S(1)}, bf16[144,1152]{1,0:T(8,128)(2,1)S(1)}, u32[]{:S(2)}, u32[]{:S(2)}) collective-permute-start(bf16[144,1152]{1,0:T(8,128)(2,1)S(1)} %slice_bitcast_fusion.23), channel_id=1, source_target_pairs={{0,2},{1,3},{2,0},{3,1},{4,6},{5,7},{6,4},{7,5},{8,10},{9,11},{10,... | collective-permute-start | bytes 995336 | tf_op jit(solution)/shard_map/ppermute | solution.py:343
  931.8 27.3 %collective-permute-start.34 = (bf16[144,1152]{1,0:T(8,128)(2,1)S(1)}, bf16[144,1152]{1,0:T(8,128)(2,1)S(1)}, u32[]{:S(2)}, u32[]{:S(2)}) collective-permute-start(bf16[144,1152]{1,0:T(8,128)(2,1)S(1)} %get-tuple-element.173), channel_id=1, source_target_pairs={{0,4},{1,5},{2,6},{3,7},{4,0},{5,1},{6,2},{7,3},{8,12},{9,13},{10,... | collective-permute-start | bytes 995336 | tf_op jit(solution)/shard_map/ppermute | solution.py:343
  936.1 22.9 %collective-permute-start.35 = (bf16[144,1152]{1,0:T(8,128)(2,1)S(1)}, bf16[144,1152]{1,0:T(8,128)(2,1)S(1)}, u32[]{:S(2)}, u32[]{:S(2)}) collective-permute-start(bf16[144,1152]{1,0:T(8,128)(2,1)S(1)} %get-tuple-element.174), channel_id=1, source_target_pairs={{0,6},{1,7},{2,4},{3,5},{4,2},{5,3},{6,0},{7,1},{8,14},{9,15},{10,... | collective-permute-start | bytes 995336 | tf_op jit(solution)/shard_map/ppermute | solution.py:343
  971.1 17.9 %all-to-all-start.2 = ((bf16[4,2,20736]{2,1,0:T(2,128)(2,1)}), bf16[4,2,20736]{2,1,0:T(2,128)(2,1)}, u32[]{:S(2)}, u32[]{:S(2)}) async-start(bf16[4,2,20736]{2,1,0:T(2,128)(2,1)} %reshape.458), calls=%async_computation.2 | async-start | bytes 663552 | tf_op jit(solution)/shard_map/all_to_all | solution.py:328
  989.0 16.0 %all-to-all-start.3 = ((bf16[4,2,39168]{2,1,0:T(2,128)(2,1)}), bf16[4,2,39168]{2,1,0:T(2,128)(2,1)S(1)}, u32[]{:S(2)}, u32[]{:S(2)}) async-start(bf16[4,2,39168]{2,1,0:T(2,128)(2,1)} %reshape.460), calls=%async_computation.5 | async-start | bytes 1253376 | tf_op jit(solution)/shard_map/all_to_all | solution.py:328
  (56 other events, 910.8 us)
Sparse Core Ops, SparseCore 0:
  29.1 100.4 all-gather.2
  133.1 81.8 all-gather.4
  665.2 110.9 reduce-scatter.2
  797.0 128.8 reduce-scatter.4

commit v3 on v1

v3 whole, which is shorter than its diff:
```python
from functools import partial

import jax
import jax.numpy as jnp
from jax import lax
from jax.experimental import pallas as pl
from jax.experimental.pallas import tpu as pltpu
from jax.sharding import PartitionSpec as P

HEAD_DIM = 72
norm_eps = 1e-06
masked_score = -1000000000.0
low = jnp.bfloat16
wide = jnp.float32
score_scale = HEAD_DIM**-0.5
log2_e = 1.4426950408889634
gelu_scale = 0.7978845608028654
gelu_cube = 0.044715
everyone = ("dp", "tensor")


def product(left, right, left_dim, right_dim):
    return lax.dot_general(
        left, right, (((left_dim,), (right_dim,)), ((), ())), preferred_element_type=wide
    )


def attend_kernel(heads, query_ref, key_ref, value_ref, bias_ref, out_ref, total_ref):
    for head in range(heads):
        rows = slice(head * HEAD_DIM, (head + 1) * HEAD_DIM)
        scores = product(key_ref[rows, :], query_ref[rows, :], 0, 0) * (score_scale * log2_e)
        scores = scores + bias_ref[...]
        top = jnp.max(scores, axis=0, keepdims=True)
        weights = jnp.exp2(scores - top)
        total = jnp.sum(weights, axis=0, keepdims=True)
        mixed = product(value_ref[rows, :], weights.astype(low), 1, 0)
        out_ref[rows, :] = (mixed * (1.0 / total)).astype(low)
        total_ref[head] = top + jnp.log2(total)


def attend_back_kernel(
    heads,
    query_ref,
    key_ref,
    value_ref,
    bias_ref,
    out_ref,
    total_ref,
    grad_ref,
    grads_ref,
):
    for head in range(heads):
        rows = slice(head * HEAD_DIM, (head + 1) * HEAD_DIM)
        query, key, value, grad = (
            query_ref[rows, :],
            key_ref[rows, :],
            value_ref[rows, :],
            grad_ref[rows, :],
        )
        scores = product(key, query, 0, 0) * (score_scale * log2_e) + bias_ref[...]
        probs = jnp.exp2(scores - total_ref[head])
        grad_probs = product(value, grad, 0, 0)
        along = jnp.sum(
            grad.astype(wide) * out_ref[rows, :].astype(wide), axis=0, keepdims=True
        )
        grad_raw = (probs * (grad_probs - along)).astype(low)
        grads_ref[2, rows, :] = product(grad, probs.astype(low), 1, 1).astype(low)
        grads_ref[0, rows, :] = (product(key, grad_raw, 1, 0) * score_scale).astype(low)
        grads_ref[1, rows, :] = (product(query, grad_raw, 1, 1) * score_scale).astype(low)


def attend(projected, bias, heads, step_heads):
    tokens = projected.shape[1]
    steps = heads // step_heads
    part = lambda place: pl.BlockSpec(
        (HEAD_DIM * step_heads, tokens), lambda i, place=place: (place * steps + i, 0)
    )
    return pl.pallas_call(
        partial(attend_kernel, step_heads),
        grid=(steps,),
        in_specs=[part(0), part(1), part(2), pl.BlockSpec((tokens, 1), lambda i: (0, 0))],
        out_specs=[part(0), pl.BlockSpec((step_heads, 1, tokens), lambda i: (i, 0, 0))],
        out_shape=[
            jax.ShapeDtypeStruct((heads * HEAD_DIM, tokens), low),
            jax.ShapeDtypeStruct((heads, 1, tokens), wide),
        ],
        compiler_params=pltpu.CompilerParams(vmem_limit_bytes=48 * 2**20),
        cost_estimate=pl.CostEstimate(
            flops=heads * tokens * tokens * 1024, bytes_accessed=16 * 2**20, transcendentals=0
        ),
        name="attend",
    )(projected, projected, projected, bias)


def attend_back(projected, bias, attended, total, grad, heads, step_heads):
    tokens = projected.shape[1]
    steps = heads // step_heads
    part = lambda place: pl.BlockSpec(
        (HEAD_DIM * step_heads, tokens), lambda i, place=place: (place * steps + i, 0)
    )
    return pl.pallas_call(
        partial(attend_back_kernel, step_heads),
        grid=(steps,),
        in_specs=[
            part(0),
            part(1),
            part(2),
            pl.BlockSpec((tokens, 1), lambda i: (0, 0)),
            part(0),
            pl.BlockSpec((step_heads, 1, tokens), lambda i: (i, 0, 0)),
            part(0),
        ],
        out_specs=pl.BlockSpec((3, HEAD_DIM * step_heads, tokens), lambda i: (0, i, 0)),
        out_shape=jax.ShapeDtypeStruct((3, heads * HEAD_DIM, tokens), low),
        compiler_params=pltpu.CompilerParams(vmem_limit_bytes=48 * 2**20),
        cost_estimate=pl.CostEstimate(
            flops=heads * tokens * tokens * 2048, bytes_accessed=16 * 2**20, transcendentals=0
        ),
        name="attend_back",
    )(projected, projected, projected, bias, attended, total, grad)


def kinds_kernel(kind_ref, grads_ref, attended_ref, normed_ref, branch_ref, out_ref):
    kind = pl.program_id(0)

    @pl.when(kind < 3)
    def projections():
        out_ref[0] = product(grads_ref[0], normed_ref[...], 1, 0).astype(low)

    @pl.when(kind == 3)
    def output():
        out_ref[0] = product(attended_ref[...], branch_ref[...], 1, 0).astype(low)


def kinds_grad(kind, grads, attended, normed, branch, block):
    _, rows, tokens = grads.shape
    width = normed.shape[1]
    whole = pl.BlockSpec((tokens, width), lambda k, i, ref: (0, 0))

    def spot(k, i, ref):
        other = k ^ ref[0]
        return ((other & 1) * 2 + (other >> 1), i, 0)

    return pl.pallas_call(
        kinds_kernel,
        grid_spec=pltpu.PrefetchScalarGridSpec(
            num_scalar_prefetch=1,
            grid=(4, rows // block),
            in_specs=[
                pl.BlockSpec((1, block, tokens), lambda k, i, ref: (jnp.minimum(k, 2), i, 0)),
                pl.BlockSpec((block, tokens), lambda k, i, ref: (i, 0)),
                whole,
                whole,
            ],
            out_specs=pl.BlockSpec((1, block, width), spot),
        ),
        out_shape=jax.ShapeDtypeStruct((4, rows, width), low),
        compiler_params=pltpu.CompilerParams(vmem_limit_bytes=40 * 2**20),
        cost_estimate=pl.CostEstimate(
            flops=12 * rows * width * tokens, bytes_accessed=24 * 2**20, transcendentals=0
        ),
        name="kinds_grad",
    )(kind, grads, attended, normed, branch)


def norm_forward(values, gain, shift):
    row_mean = jnp.mean(values, axis=-1, keepdims=True)
    centred = values - row_mean
    inv_scale = lax.rsqrt(jnp.mean(centred * centred, axis=-1, keepdims=True) + norm_eps)
    return (centred * inv_scale * gain + shift).astype(low)


def norm_back_kernel(values_ref, grad_ref, gain_ref, base_ref, full_ref, low_ref, sums_ref):
    values = values_ref[...].astype(wide)
    centred = values - jnp.mean(values, axis=-1, keepdims=True)
    inv_scale = lax.rsqrt(jnp.mean(centred * centred, axis=-1, keepdims=True) + norm_eps)
    unit = centred * inv_scale
    grad = grad_ref[...]
    scaled = grad * gain_ref[...]
    mean_grad = jnp.mean(scaled, axis=-1, keepdims=True)
    mean_along = jnp.mean(scaled * unit, axis=-1, keepdims=True)
    base = base_ref[...].astype(wide)
    full = base + inv_scale * (scaled - mean_grad - unit * mean_along)
    rounded = full.astype(low)
    full_ref[...] = full
    low_ref[...] = rounded
    total = lambda rows: jnp.sum(rows, axis=0, keepdims=True)
    sums = jnp.concatenate(
        [total(grad * unit), total(grad), total(rounded.astype(wide)), total(base)], axis=0
    )

    @pl.when(pl.program_id(0) == 0)
    def first():
        sums_ref[...] = sums

    @pl.when(pl.program_id(0) > 0)
    def later():
        sums_ref[...] += sums


def norm_back(values, grad, gain, base):
    tokens, width = values.shape
    block = tokens // 4
    rows = pl.BlockSpec((block, width), lambda i: (i, 0))
    return pl.pallas_call(
        norm_back_kernel,
        grid=(4,),
        in_specs=[rows, rows, pl.BlockSpec((1, width), lambda i: (0, 0)), rows],
        out_specs=[rows, rows, pl.BlockSpec((4, width), lambda i: (0, 0))],
        out_shape=[
            jax.ShapeDtypeStruct((tokens, width), wide),
            jax.ShapeDtypeStruct((tokens, width), low),
            jax.ShapeDtypeStruct((4, width), wide),
        ],
        compiler_params=pltpu.CompilerParams(vmem_limit_bytes=40 * 2**20),
        cost_estimate=pl.CostEstimate(
            flops=32 * tokens * width, bytes_accessed=16 * tokens * width, transcendentals=0
        ),
        name="norm_back",
    )(values, grad, gain.reshape(1, width), base)


def mlp_kernel(carried, normed_ref, grad_ref, bias_ref, *refs):
    pieces, refs = refs[:8], refs[8:]
    if carried:
        out_before, normed_before = refs[:2]
        refs = refs[2:]
    out_ref, grad_normed_ref, first_ref, last_ref, grad_bias_ref, ups, downs, sems = refs
    step = pl.program_id(0)
    slot = step % 2
    rows = ups.shape[1] // 2

    def copies(at):
        moves = []
        for half in range(2):
            piece = pieces[2 * at + half]
            for kind, target in enumerate((ups, downs)):
                moves.append(
                    pltpu.make_async_copy(
                        piece.at[pl.ds(kind * rows, rows)],
                        target.at[at % 2, pl.ds(half * rows, rows)],
                        sems.at[at % 2, 2 * half + kind],
                    )
                )
        return moves

    for at in range(4):

        @pl.when(step + 1 == at if at else step == 0)
        def fetch():
            for move in copies(at):
                move.start()

    for at in range(4):

        @pl.when(step == at)
        def arrive():
            for move in copies(at):
                move.wait()

    normed, grad = normed_ref[...], grad_ref[...]
    up, down = ups[slot], downs[slot]
    pre_act = product(up, normed, 1, 1) + bias_ref[...]
    square = pre_act * pre_act
    bent = jnp.tanh(gelu_scale * (pre_act + gelu_cube * square * pre_act))
    half = 0.5 * (1.0 + bent)
    active = (pre_act * half).astype(low)
    slope = half + 0.5 * pre_act * (1.0 - bent * bent) * (
        gelu_scale * (1.0 + 3.0 * gelu_cube * square)
    )
    grad_wide = product(down, grad, 1, 1) * slope
    grad_pre = grad_wide.astype(low)
    grad_bias_ref[...] = jnp.sum(grad_wide, axis=1, keepdims=True)
    grad_down = product(active, grad, 1, 0).astype(low)
    grad_up = product(grad_pre, normed, 1, 0).astype(low)

    def keep(ref):
        for place in range(2):
            ref[place, 0] = grad_up[place * rows : (place + 1) * rows]
            ref[place, 1] = grad_down[place * rows : (place + 1) * rows]

    pl.when(step < 2)(lambda: keep(first_ref))
    pl.when(step >= 2)(lambda: keep(last_ref))
    out_term = product(active, down, 0, 0)
    normed_term = product(grad_pre, up, 0, 0)

    @pl.when(step == 0)
    def first():
        if carried:
            out_ref[...] = out_before[...] + out_term
            grad_normed_ref[...] = normed_before[...] + normed_term
        else:
            out_ref[...] = out_term
            grad_normed_ref[...] = normed_term

    @pl.when(step > 0)
    def later():
        out_ref[...] += out_term
        grad_normed_ref[...] += normed_term


def mlp(normed, grad, bias, pieces, before=None):
    tokens, width = normed.shape
    rows = pieces[0].shape[0] // 2
    whole = pl.BlockSpec((tokens, width), lambda i: (0, 0))
    column = pl.BlockSpec((2 * rows, 1), lambda i: (i, 0))
    grads = jax.ShapeDtypeStruct((4, 2, rows, width), low)
    earlier = [] if before is None else list(before)
    return pl.pallas_call(
        partial(mlp_kernel, before is not None),
        grid=(4,),
        in_specs=[whole, whole, column]
        + [pl.BlockSpec(memory_space=pl.ANY)] * 8
        + [whole] * len(earlier),
        out_specs=[
            whole,
            whole,
            pl.BlockSpec((2, 2, rows, width), lambda i: (jnp.minimum(i, 1), 0, 0, 0)),
            pl.BlockSpec((2, 2, rows, width), lambda i: (jnp.maximum(i - 2, 0), 0, 0, 0)),
            column,
        ],
        out_shape=[jax.ShapeDtypeStruct((tokens, width), wide)] * 2
        + [grads, grads, jax.ShapeDtypeStruct((8 * rows, 1), wide)],
        scratch_shapes=[
            pltpu.VMEM((2, 2 * rows, width), low),
            pltpu.VMEM((2, 2 * rows, width), low),
            pltpu.SemaphoreType.DMA((2, 4)),
        ],
        input_output_aliases={11: 0, 12: 1} if earlier else {},
        compiler_params=pltpu.CompilerParams(vmem_limit_bytes=60 * 2**20),
        cost_estimate=pl.CostEstimate(
            flops=16 * tokens * width * 8 * rows, bytes_accessed=40 * 2**20, transcendentals=0
        ),
        name="mlp",
    )(normed, grad, bias, *pieces, *earlier)


def place_kernel(kind_ref, *refs):
    pieces, out_ref = refs[:8], refs[8]
    kind = kind_ref[0]
    quarter = out_ref.shape[1] // 4
    for core in range(2):
        near, near_y, far, far_x = pieces[4 * core : 4 * core + 4]
        same, across = kind ^ core, kind ^ (core + 2)
        out_ref[same, :quarter] = near[:quarter]
        out_ref[across, :quarter] = near[quarter:]
        out_ref[same, quarter : 2 * quarter] = near_y[:quarter]
        out_ref[across, quarter : 2 * quarter] = near_y[quarter:]
        out_ref[same, 2 * quarter :] = far[...]
        out_ref[across, 2 * quarter :] = far_x[...]


def place(kind, pieces):
    rows, width = pieces[0].shape
    local = pl.BlockSpec(memory_space=pltpu.VMEM)
    return pl.pallas_call(
        place_kernel,
        in_specs=[pl.BlockSpec(memory_space=pltpu.SMEM)] + [local] * 8,
        out_specs=local,
        out_shape=jax.ShapeDtypeStruct((4, 2 * rows, width), low),
        compiler_params=pltpu.CompilerParams(vmem_limit_bytes=40 * 2**20),
        cost_estimate=pl.CostEstimate(
            flops=0, bytes_accessed=32 * rows * width, transcendentals=0
        ),
        name="place",
    )(kind, *pieces)


def unite_kernel(kind_ref, *refs):
    outs = refs[4:]
    part = refs[0].shape[1]
    for distance in range(4):
        source = kind_ref[0] ^ distance
        for column in range(4):

            @pl.when(source == column)
            def put():
                start = 0
                for out in outs:
                    rows = out.shape[0]
                    out[:, column * part : (column + 1) * part] = refs[distance][
                        start : start + rows, :
                    ]
                    start += rows


def unite(kind, blocks, cuts):
    part = blocks[0].shape[1]
    local = pl.BlockSpec(memory_space=pltpu.VMEM)
    return pl.pallas_call(
        unite_kernel,
        in_specs=[pl.BlockSpec(memory_space=pltpu.SMEM)] + [local] * 4,
        out_specs=[local] * len(cuts),
        out_shape=[jax.ShapeDtypeStruct((rows, 4 * part), low) for rows in cuts],
        name="unite",
    )(kind, *blocks)


def divide_kernel(kind_ref, *refs):
    ins, outs = refs[:-4], refs[-4:]
    part = outs[0].shape[1]
    for distance in range(4):
        target = kind_ref[0] ^ distance
        for column in range(4):

            @pl.when(target == column)
            def put():
                start = 0
                for ref in ins:
                    rows = ref.shape[0]
                    outs[distance][start : start + rows, :] = ref[
                        :, column * part : (column + 1) * part
                    ]
                    start += rows


def divide(kind, owned):
    rows = sum(values.shape[0] for values in owned)
    part = owned[0].shape[1] // 4
    local = pl.BlockSpec(memory_space=pltpu.VMEM)
    return pl.pallas_call(
        divide_kernel,
        in_specs=[pl.BlockSpec(memory_space=pltpu.SMEM)] + [local] * len(owned),
        out_specs=[local] * 4,
        out_shape=[jax.ShapeDtypeStruct((rows, part), low)] * 4,
        name="divide",
    )(kind, *owned)


def settle_kernel(kind_ref, *refs):
    for distance in range(4):
        refs[4][kind_ref[0] ^ distance] = refs[distance][...].astype(wide)


def settle(kind, blocks):
    rows, part = blocks[0].shape
    local = pl.BlockSpec(memory_space=pltpu.VMEM)
    return pl.pallas_call(
        settle_kernel,
        in_specs=[pl.BlockSpec(memory_space=pltpu.SMEM)] + [local] * 4,
        out_specs=local,
        out_shape=jax.ShapeDtypeStruct((4, rows, part), wide),
        name="settle",
    )(kind, *blocks)


def after(values, *earlier):
    return lax.optimization_barrier((values, earlier))[0]


def add_low(*terms):
    total = terms[0].astype(wide)
    for term in terms[1:]:
        total = total + term.astype(wide)
    return total.astype(low)


def join(kinds, *blocks):
    width = blocks[0].shape[-1]
    parts = [block.reshape(kinds, -1, width) for block in blocks]
    return jnp.concatenate(parts, axis=1).reshape(-1, width)


class Hops:
    def __init__(self, dp_count, tensor_count):
        self.count = dp_count * tensor_count
        self.y, self.z = 1, (2, 4, 6)
        self.core, self.x = tensor_count, 2 * tensor_count
        self.near, self.far = (0, 2), (4, 6)

    def send(self, values, distance):
        pairs = [(place, place ^ distance) for place in range(self.count)]
        return lax.ppermute(values, everyone, pairs)

    def order(self):
        x, y = self.x, self.y
        near = [n ^ p ^ q for q in (0, y) for p in (0, x) for n in self.near]
        far = [n ^ p ^ q for q in (0, x) for p in (0, y) for n in self.far]
        return near + far

    def along_z(self, block):
        return [self.send(block, z) for z in self.z]

    def second(self, kinds, block, arrived):
        z1, z2, z3 = arrived
        near, far = join(kinds, block, z1), join(kinds, z2, z3)
        return near, far, self.send(near, self.x), self.send(far, self.y)

    def third(self, kinds, near, far, near_x, far_y):
        near, far = join(kinds, near, near_x), join(kinds, far, far_y)
        return near, self.send(near, self.y), far, self.send(far, self.x)

    def sibling(self, *pieces):
        return [self.send(piece, self.core) for piece in pieces]

    def sum_all(self, values):
        for distance in (self.core, self.x, self.y, self.z[0], self.z[1]):
            values = values + self.send(values, distance)
        return values

    def across_dp(self, blocks):
        return [blocks[0]] + [self.send(blocks[j], j * self.core) for j in (1, 2, 3)]


class Reduction:
    def __init__(self, hops, own, sibling, joined):
        self.hops, self.own, self.joined = hops, own, joined
        self.arrived = hops.send(sibling, hops.core)
        self.width = own.shape[-1]

    def part(self, place):
        terms = (self.own, self.arrived)
        if self.joined:
            return tuple(term[place] for term in terms)
        cuts = (
            lambda term: term[:, 0:2],
            lambda term: term[:, 2:4],
            lambda term: term[0, 4:8],
            lambda term: term[1, 4:8],
        )
        return tuple(cuts[place](term) for term in terms)

    def halves(self, values):
        axis = 1 if self.joined else 0
        shape = (2, 2, 2, -1, self.width) if self.joined else (2, 2, -1, self.width)
        values = values.reshape(shape)
        return [lax.index_in_dim(values, place, axis, keepdims=False) for place in (0, 1)]

    def blocks(self, values):
        axis = 1 if self.joined else 0
        return [lax.index_in_dim(values, place, axis, keepdims=False) for place in (0, 1)]

    def ready_third(self):
        self.operands = add_low(*self.part(1)), add_low(*self.part(3))
        return self.operands

    def third(self, *earlier):
        near, far = after(self.operands, *earlier)
        near, far = self.hops.send(near, self.hops.y), self.hops.send(far, self.hops.x)
        near, far = add_low(*self.part(0), near), add_low(*self.part(2), far)
        self.near, self.far = self.halves(near), self.halves(far)
        self.operands = self.near[1], self.far[1]
        return self.operands

    def second(self, *earlier):
        near, far = after(self.operands, *earlier)
        near, far = self.hops.send(near, self.hops.x), self.hops.send(far, self.hops.y)
        near, far = add_low(self.near[0], near), add_low(self.far[0], far)
        self.near, self.far = self.blocks(near), self.blocks(far)
        self.operands = self.near[1], self.far[0], self.far[1]
        return self.operands

    def along_z(self, *earlier):
        operands = after(self.operands, *earlier)
        arrived = [self.hops.send(v, z) for v, z in zip(operands, self.hops.z, strict=True)]
        return add_low(self.near[0], *arrived)


def shards(
    dp_count,
    tensor_count,
    inputs,
    pad_mask,
    cotangent,
    attn_norm_gain,
    attn_norm_shift,
    w_query,
    b_query,
    w_key,
    w_value,
    b_value,
    w_out,
    b_out,
    mlp_norm_gain,
    mlp_norm_shift,
    w_up,
    b_up,
    w_down,
    b_down,
):
    half_rows, width = inputs.shape[1:]
    tokens = 2 * half_rows
    head_cols = w_query.shape[1]
    unit_cols = w_up.shape[1]
    quantum = 8 * dp_count
    slab_units = -(-unit_cols // quantum) * quantum
    by_hops = (dp_count, tensor_count) == (4, 8)
    dp_place, tensor_place = lax.axis_index("dp"), lax.axis_index("tensor")
    devices = dp_count * tensor_count
    here = dp_place * tensor_count + tensor_place
    col_start = tensor_place * head_cols
    side = tensor_place % 2
    pairs = [(place, place ^ 1) for place in range(tensor_count)]
    hops = Hops(dp_count, tensor_count)
    kind = dp_place.reshape(1).astype(jnp.int32)
    heads = head_cols * tensor_count // HEAD_DIM // 2
    piece_rows = heads * HEAD_DIM

    def swap(values):
        return lax.ppermute(values, "tensor", pairs)

    def one_slot(values, *earlier):
        kept = lax.dynamic_index_in_dim(values, side, 0, keepdims=False)
        sent = lax.dynamic_index_in_dim(values, 1 - side, 0, keepdims=False)
        if earlier:
            sent = after(sent, *earlier)
        return jnp.concatenate([kept, swap(sent)], axis=0)

    def both_micros(kept, other):
        return jnp.where(side == 0, jnp.stack([kept, other]), jnp.stack([other, kept]))

    unit_pad = ((0, slab_units - unit_cols), (0, 0))
    up_cols, down_cols = jnp.pad(w_up.T, unit_pad), jnp.pad(w_down, unit_pad)
    attn_cols = jnp.concatenate([w_query.T, w_key.T, w_value.T, w_out], axis=0)
    if by_hops:
        unit_cuts = (72, slab_units // 4 - 72)
        first_units = 4 * unit_cuts[0]
        share = lambda values, low_end, high_end: values[low_end:high_end].reshape(
            4, -1, values.shape[1]
        )
        mlp_cols = jnp.concatenate(
            [
                share(up_cols, 0, first_units),
                share(down_cols, 0, first_units),
                share(up_cols, first_units, slab_units),
                share(down_cols, first_units, slab_units),
            ],
            axis=1,
        )
        attn_cols = attn_cols.reshape(4, head_cols, -1)
        pick = lambda values, j: lax.dynamic_index_in_dim(
            values, dp_place ^ j, 0, keepdims=False
        )
        attn_blocks = hops.across_dp([pick(attn_cols, j) for j in range(4)])
        a_one, a_two = unite(kind, attn_blocks, (HEAD_DIM, HEAD_DIM))
        x_slot = one_slot(inputs)
        mlp_cols = after(mlp_cols, *attn_blocks[1:])
        mlp_blocks = hops.across_dp([pick(mlp_cols, j) for j in range(4)])
        m_one, m_two = unite(kind, mlp_blocks, [2 * rows for rows in unit_cuts])

        a_one_z = hops.along_z(a_one)
        a_one_two = hops.second(1, a_one, a_one_z)
        a_two_z = hops.along_z(after(a_two, *a_one_z))
        a_one_three = hops.third(1, *a_one_two)
        m_one_z = hops.along_z(after(m_one, *a_two_z))
        a_two, a_two_z = after((a_two, a_two_z), *a_one_three)
        kinds_one = place(kind, list(a_one_three) + hops.sibling(*a_one_three))
        a_two_two = hops.second(1, a_two, a_two_z)
        a_two_three = hops.third(1, *a_two_two)
        grad_out = one_slot(cotangent, *a_two_two[2:])
        m_two_z = hops.along_z(after(m_two, *m_one_z))
        m_one, m_one_z = after((m_one, m_one_z), *a_two_three)
        kinds_two = place(kind, list(a_two_three) + hops.sibling(*a_two_three))
        m_one_two = hops.second(2, m_one, m_one_z)
        m_one_three = hops.third(2, *m_one_two)
        m_one_sibling = hops.sibling(*m_one_three)
        m_two, m_two_z = after((m_two, m_two_z), *m_one_three)
        m_two_two = hops.second(2, m_two, m_two_z)
        m_two_three = hops.third(2, *m_two_two)
        m_two_sibling = hops.sibling(*m_two_three)
        kinds = [kinds_one, kinds_two]
        unit_pieces = [
            m_one_sibling + list(m_one_three),
            m_two_sibling + list(m_two_three),
        ]
        order = hops.order()
        order = [place ^ hops.core for place in order] + order
        unit_places = here ^ jnp.array(order)
        unit_find = jnp.array([order.index(place) for place in range(devices)])
        head_places = tensor_place ^ jnp.array(
            [n ^ q for group in (hops.near, hops.far) for q in (0, hops.y) for n in group]
        )
    else:
        x_slot, grad_out = one_slot(inputs), one_slot(cotangent)
        unit_cuts = (slab_units // dp_count,)

        def gathered(values):
            owned = lax.all_to_all(
                values.reshape(dp_count, -1, values.shape[1]), "dp", 0, 2, tiled=True
            )
            return lax.all_gather(owned[0], everyone, axis=0, tiled=True)

        attn_rows = gathered(attn_cols)
        attn_rows = attn_rows.reshape(4, dp_count // 4, tensor_count, -1, width)
        attn_rows = attn_rows.transpose(0, 2, 1, 3, 4).reshape(4, -1, width)
        kinds = [attn_rows[:, :piece_rows], attn_rows[:, piece_rows:]]
        up_rows = gathered(up_cols).reshape(4, 8, -1, width)
        down_rows = gathered(down_cols).reshape(4, 8, -1, width)
        unit_pieces = [
            [jnp.concatenate([up_rows[part, i], down_rows[part, i]]) for i in range(8)]
            for part in range(4)
        ]

    def head_bias(values, part):
        if by_hops:
            blocks = values.reshape(tensor_count, 2, HEAD_DIM)[:, part]
            return blocks[head_places].reshape(-1)
        return values[part * piece_rows : (part + 1) * piece_rows]

    def head_grads(one, two):
        if by_hops:
            blocks = jnp.stack([one.reshape(-1, HEAD_DIM), two.reshape(-1, HEAD_DIM)], axis=1)
            return jnp.zeros_like(blocks).at[head_places].set(blocks).reshape(-1)
        return jnp.concatenate([one, two])

    slab_bias = jnp.pad(
        b_up.reshape(tensor_count, unit_cols), ((0, 0), (0, slab_units - unit_cols))
    )
    unit_starts = [dp_count * sum(unit_cuts[:i]) for i in range(len(unit_cuts) + 1)]

    def unit_bias(part):
        if not by_hops:
            values = slab_bias.reshape(tensor_count, dp_count, -1).transpose(1, 0, 2)
            return values.reshape(4, -1, 1)[part]
        values = slab_bias[:, unit_starts[part] : unit_starts[part + 1]]
        values = values.reshape(tensor_count, dp_count, -1).transpose(1, 0, 2)
        return values.reshape(devices, -1)[unit_places].reshape(-1, 1)

    def unit_grads(values):
        slabs = []
        for part in values if by_hops else [jnp.concatenate(values)]:
            part = part.reshape(devices, -1)
            if by_hops:
                part = part[unit_find][here ^ jnp.arange(devices)]
            part = part.reshape(dp_count, tensor_count, -1).transpose(1, 0, 2)
            slabs.append(part.reshape(tensor_count, -1))
        return jnp.concatenate(slabs, axis=1)

    mask_row = lax.dynamic_slice(pad_mask, (side, tensor_place // 2, 0), (1, 1, tokens))
    mask_row = mask_row.reshape(2, half_rows)
    mask_row = jnp.where(side == 0, mask_row, mask_row[::-1]).reshape(tokens, 1)
    bias_col = jnp.where(mask_row > 0, 0.0, masked_score).astype(wide)

    normed_first = norm_forward(x_slot.astype(wide), attn_norm_gain, attn_norm_shift)
    projected, attended, totals = [], [], []
    branch = b_out
    for part in range(2):
        zeros = jnp.zeros((piece_rows,), wide)
        bias = jnp.concatenate([head_bias(b_query, part), zeros, head_bias(b_value, part)])
        rows = kinds[part][:3].reshape(-1, width)
        projected.append((product(rows, normed_first, 1, 1) + bias[:, None]).astype(low))
        mixed, total = attend(projected[part], bias_col, heads, 4)
        attended.append(mixed)
        totals.append(total)
        branch = product(mixed, kinds[part][3], 0, 0) + branch
    middle = x_slot.astype(wide) + branch
    normed_second = norm_forward(middle, mlp_norm_gain, mlp_norm_shift)
    sums, grad_siblings, grad_owns, up_sums = None, [], [], []
    for part, pieces in enumerate(unit_pieces):
        *sums, grad_sibling, grad_own, up_sum = mlp(
            normed_second, grad_out, unit_bias(part), pieces, sums
        )
        grad_siblings.append(grad_sibling)
        grad_owns.append(grad_own)
        up_sums.append(up_sum[:, 0])
    down_out, grad_normed_second = sums
    out_low = (middle + (down_out + b_down)).astype(low)

    if by_hops:
        m_one, m_two = [
            Reduction(hops, own, sibling, True)
            for own, sibling in zip(grad_owns, grad_siblings, strict=True)
        ]
        grad_normed_second = after(grad_normed_second, *m_one.ready_third())
    grad_middle, grad_branch, second_sums = norm_back(
        middle, grad_normed_second, mlp_norm_gain, grad_out
    )
    grad_attended = [product(kinds[part][3], grad_branch, 1, 1).astype(low) for part in range(2)]
    first_terms, projection_grads, kind_grads = 0.0, [], []
    for part in range(2):
        grads = attend_back(
            projected[part],
            bias_col,
            attended[part],
            totals[part],
            grad_attended[part],
            heads,
            4,
        )
        if by_hops:
            if part == 0:
                grads = after(grads, *m_one.third(), *m_two.ready_third())
            else:
                m_one_second = m_one.second()
                grads = after(grads, *m_one_second)
        projection_grads.append(grads)
        kind_grads.append(
            kinds_grad(kind, grads, attended[part], normed_first, grad_branch, piece_rows // 2)
        )
        if by_hops and part == 0:
            terms = kind_grads[0].reshape(2, 2, 8, HEAD_DIM, width)
            a_one = Reduction(hops, terms[0], terms[1], False)
    if by_hops:
        m_two_third = m_two.third(*m_one_second)
        terms = kind_grads[1].reshape(2, 2, 8, HEAD_DIM, width)
        a_two = Reduction(hops, terms[0], terms[1], False)
    for part in range(2):
        rows = kinds[part][:3].reshape(-1, width)
        terms = projection_grads[part].reshape(-1, tokens)
        if by_hops and part == 1:
            terms = after(terms, *a_one.ready_third())
        first_terms = product(terms, rows, 0, 0) + first_terms
    input_full, input_low, first_sums = norm_back(
        x_slot, first_terms, attn_norm_gain, grad_middle
    )
    layer_out = both_micros(out_low[:half_rows], swap(out_low[half_rows:]))
    input_grad = both_micros(
        input_full[:half_rows], swap(input_low[half_rows:]).astype(wide)
    )

    if by_hops:
        m_one_owned = m_one.along_z()
        m_two_second = m_two.second(m_two_third, input_low)
        a_two.ready_third()
        a_one_third = a_one.third(*m_two_third)
        m_two_owned = m_two.along_z(m_one_owned)
        a_one_second = a_one.second(*a_one_third)
        a_two_third = a_two.third(*a_one_third)
        a_one_owned = a_one.along_z(m_two_owned)
        a_two.second(*a_two_third)
        a_two_owned = a_two.along_z()
        mlp_owned = [m_one_owned[0], m_one_owned[1], m_two_owned[0], m_two_owned[1]]
        attn_owned = [a_one_owned, a_two_owned]
        mlp_back = settle(kind, hops.across_dp(divide(kind, mlp_owned)))
        attn_back = settle(kind, hops.across_dp(divide(kind, attn_owned)))
        bounds = [0]
        for rows in (unit_cuts[0], unit_cuts[0], unit_cuts[1], unit_cuts[1]):
            bounds.append(bounds[-1] + rows)
        parts = [
            mlp_back[:, bounds[i] : bounds[i + 1]].reshape(-1, mlp_back.shape[2])
            for i in range(4)
        ]
        grad_w_up = jnp.concatenate([parts[0], parts[2]], axis=0)
        grad_w_down = jnp.concatenate([parts[1], parts[3]], axis=0)
    else:

        def scattered(values):
            owned = lax.psum_scatter(values, everyone, scatter_dimension=0, tiled=True)
            back = lax.all_to_all(owned[None], "dp", 2, 0, tiled=True)
            return back.reshape(-1, width // dp_count).astype(wide)

        both = jnp.concatenate(
            [half for pair in zip(grad_siblings, grad_owns, strict=True) for half in pair], axis=0
        )
        grad_w_up = scattered(both[:, 0].reshape(-1, width))
        grad_w_down = scattered(both[:, 1].reshape(-1, width))
        terms = jnp.concatenate(kind_grads, axis=1)
        terms = terms.reshape(4, tensor_count, dp_count // 4, -1, width)
        terms = terms.transpose(0, 2, 1, 3, 4).reshape(-1, width)
        attn_back = scattered(terms).reshape(4, head_cols, -1)

    total_over = lambda i: jnp.concatenate(
        [jnp.sum(grads[i], axis=1, dtype=wide) for grads in projection_grads]
    )
    split_heads = lambda values: head_grads(values[:piece_rows], values[piece_rows:])
    early = jnp.concatenate([second_sums.reshape(-1), unit_grads(up_sums).reshape(-1)])
    late = jnp.concatenate(
        [
            first_sums[:2].reshape(-1),
            split_heads(total_over(0)),
            split_heads(total_over(2)),
        ]
    )
    if by_hops:
        early = hops.sum_all(early.reshape(-1, 128)).reshape(-1)
        late = hops.sum_all(late.reshape(-1, 128)).reshape(-1)
    else:
        early, late = lax.psum(early, everyone), lax.psum(late, everyone)
    early_part = lambda i: early[i * width : (i + 1) * width]
    late_part = lambda i: late[i * width : (i + 1) * width]
    up_all = early[4 * width :].reshape(tensor_count, slab_units)
    return (
        layer_out,
        input_grad,
        late_part(0),
        late_part(1),
        attn_back[0].T,
        lax.dynamic_slice_in_dim(late_part(2), col_start, head_cols),
        attn_back[1].T,
        attn_back[2].T,
        lax.dynamic_slice_in_dim(late_part(3), col_start, head_cols),
        attn_back[3],
        early_part(2),
        early_part(0),
        early_part(1),
        grad_w_up[:unit_cols].T,
        up_all[:, :unit_cols].reshape(-1),
        grad_w_down[:unit_cols],
        early_part(3),
    )


def solution(mesh):
    tokens = P(None, ("dp", "tensor"), None)
    columns = P("dp", "tensor")
    rows = P("tensor", "dp")
    return jax.shard_map(
        partial(shards, mesh.shape["dp"], mesh.shape["tensor"]),
        mesh=mesh,
        in_specs=(
            tokens,
            P(None, "dp", None),
            tokens,
            P(),
            P(),
            columns,
            P(),
            columns,
            columns,
            P(),
            rows,
            P(),
            P(),
            P(),
            columns,
            P(),
            rows,
            P(),
        ),
        out_specs=(
            tokens,
            tokens,
            P(),
            P(),
            columns,
            P("tensor"),
            columns,
            columns,
            P("tensor"),
            rows,
            P(),
            P(),
            P(),
            columns,
            P(),
            rows,
            P(),
        ),
        check_vma=False,
    )
```

time: 825 us -> 649 us (0.79)
  waiting for transfers between devices: 417 us -> 172 us
  starting transfers between devices: 17.2 us -> 105 us
  blocking collectives: 72.1 us -> 0 us
  Pallas kernels: 114 us -> 161 us
  other arithmetic: 65.5 us -> 90.4 us
  between operations: 15.1 us -> 2.6 us
  matrix products: 48.6 us -> 36.9 us
    ppermute x0 -> x98, waiting for transfers between devices: none -> 158 us  [send(): return lax.ppermute(values, everyone, pairs)]
    all_gather x3 -> x0, waiting for transfers between devices: 154 us -> none  [gather_slab(): return lax.all_gather(owned[0], everyone, axis=0, tiled=True)]
    reduce_scatter x1 -> x0, waiting for transfers between devices: 120 us -> none  [scatter_slab(): owned = lax.psum_scatter(terms, everyone, scatter_dimension=0, tiled=True)]
    ppermute x0 -> x98, starting transfers between devices: none -> 102 us  [send(): return lax.ppermute(values, everyone, pairs)]
    unnamed x8 -> x0, waiting for transfers between devices: 86.8 us -> none
    convert_element_type x1 -> x27, other arithmetic: 1.79 us -> 49.1 us  [the longest x24 43 us: add_low(): return total.astype(low)]
    pallas_call x1 -> x14, Pallas kernels: 73.5 us -> 119 us  [the longest x2 84.1 us: mlp(): pl.pallas_call(partial(mlp_kernel, before is not None), grid=(4,), in_spe...]
    psum x1 -> x0, blocking collectives: 39.8 us -> none  [shards(): summed = lax.psum(jnp.concatenate(vectors), everyone)]
  transfers between devices with their start and end apart: 13 -> 102, of which waited for: 9 -> 36; matrix products, arithmetic and copies ran while one was open for 20% -> 27% of each run, Pallas kernels for 5% -> 23%
where the time goes in v3:
time: 649 us; the launch traced here: 640 us
  waiting for transfers between devices  172 us (27%)
  Pallas kernels  161 us (25%)
  starting transfers between devices  105 us (16%)
  other arithmetic  90.4 us (14%)
  local copies, waits for them, and re-layouts  71.6 us (11%)
  matrix products  36.9 us (6%)
    ppermute x98, waiting for transfers between devices, send(): return lax.ppermute(values, everyone, pairs)  158 us
    ppermute x98, starting transfers between devices, send(): return lax.ppermute(values, everyone, pairs)  102 us
    pallas_call x2, Pallas kernels, mlp(): pl.pallas_call(partial(mlp_kernel, before is not None), grid=(4,), in_spe...  84.1 us
    convert_element_type x24, other arithmetic, add_low(): return total.astype(low)  43 us
    dot_general x8, matrix products, product(): lax.dot_general(left, right, (((left_dim,), (right_dim,)), ((), ())), pre...  36.9 us
    pallas_call x2, Pallas kernels, attend_back(): pl.pallas_call(partial(attend_back_kernel, step_heads), grid=(steps,), in...  27.6 us
    unnamed x190, local copies, waits for them, and re-layouts  18.5 us
    pallas_call x2, Pallas kernels, attend(): pl.pallas_call(partial(attend_kernel, step_heads), grid=(steps,), in_spec...  14.6 us
  transfers between devices with their start and end apart: 102, of which 36 were waited for; matrix products, arithmetic and copies ran while one was open for 27% of the time, Pallas kernels for 23%

profile of v3, /device:TPU:0, one launch (start us, length us, event | category | flops | bytes accessed | tf_op | source)
XLA Modules:
  0.0 640.2 jit_solution(10184576027901467057)
XLA Ops:
  3.1 2.5 collective-permute-start.2
  16.1 2.6 collective-permute-start.5
  21.4 2.7 collective-permute-done.4
  24.6 6.9 %collective-permute-done.5 = bf16[72,1152]{1,0:T(8,128)(2,1)S(1)} collective-permute-done((bf16[72,1152]{1,0:T(8,128)(2,1)}, bf16[72,1152]{1,0:T(8,128)(2,1)S(1)}, u32[]{:S(2)}, u32[]{:S(2)}) %collective-permute-start.5) | collective-permute-done | bytes 165920 | tf_op jit(solution)/shard_map/ppermute | solution.py:473
  31.5 3.3 collective-permute-start.7
  43.3 2.6 unite.3
  45.8 5.6 collective-permute-done.8
  51.4 3.5 collective-permute-start.30
  61.0 8.2 %collective-permute-done.30 = bf16[144,1152]{1,0:T(8,128)(2,1)} collective-permute-done((bf16[144,1152]{1,0:T(8,128)(2,1)}, bf16[144,1152]{1,0:T(8,128)(2,1)}, u32[]{:S(2)}, u32[]{:S(2)}) %collective-permute-start.30) | collective-permute-done | bytes 331808 | tf_op jit(solution)/shard_map/ppermute | solution.py:473
  87.8 7.0 %collective-permute-done.16 = bf16[144,1152]{1,0:T(8,128)(2,1)S(1)} collective-permute-done((bf16[144,1152]{1,0:T(8,128)(2,1)S(1)}, bf16[144,1152]{1,0:T(8,128)(2,1)S(1)}, u32[]{:S(2)}, u32[]{:S(2)}) %collective-permute-start.16) | collective-permute-done | bytes 331808 | tf_op jit(solution)/shard_map/ppermute | solution.py:473
  101.5 4.2 add_convert_fusion.query_ref.key_ref.value_ref
  105.6 8.5 %collective-permute-done.17.refs_3_ = bf16[288,1152]{1,0:T(8,128)(2,1)S(1)} collective-permute-done((bf16[288,1152]{1,0:T(8,128)(2,1)S(1)}, bf16[288,1152]{1,0:T(8,128)(2,1)S(1)}, u32[]{:S(2)}, u32[]{:S(2)}) %collective-permute-start.17) | collective-permute-done | bytes 663584 | tf_op jit(solution)/shard_map/ppermute | solution.py:473
  114.1 2.3 collective-permute-done.15.refs_1_
  120.4 7.0 %attend.3 = (bf16[576,736]{1,0:T(8,128)(2,1)S(1)}, f32[8,1,736]{2,1,0:T(1,128)S(1)}) custom-call(bf16[1728,736]{1,0:T(8,128)(2,1)S(1)} %add_convert_fusion.query_ref.key_ref.value_ref, bf16[1728,736]{1,0:T(8,128)(2,1)S(1)} %add_convert_fusion.query_ref.key_ref.value_ref, bf16[1728,736]{1,0:T(8,128)(2,1)S(1)} %add_convert_fusion.query_ref.key_ref.value_ref, ...), custom_call_target="tpu_custom_call" | custom-call | flops 4437573632 | bytes 16777216 | tf_op jit(solution)/shard_map/attend/pallas_call | solution.py:78
  130.8 3.4 convolution_add_fusion
  134.6 13.7 %collective-permute-done.38 = bf16[288,1152]{1,0:T(8,128)(2,1)} collective-permute-done((bf16[288,1152]{1,0:T(8,128)(2,1)}, bf16[288,1152]{1,0:T(8,128)(2,1)}, u32[]{:S(2)}, u32[]{:S(2)}) %collective-permute-start.38) | collective-permute-done | bytes 663584 | tf_op jit(solution)/shard_map/ppermute | solution.py:473
  149.7 2.5 pad_maximum_fusion.3
  152.1 6.0 collective-permute-start.33
  168.9 3.9 add_convert_fusion.1.query_ref.key_ref.value_ref
  172.8 7.6 %attend.2 = (bf16[576,736]{1,0:T(8,128)(2,1)S(1)}, f32[8,1,736]{2,1,0:T(1,128)S(1)}) custom-call(bf16[1728,736]{1,0:T(8,128)(2,1)S(1)} %add_convert_fusion.1.query_ref.key_ref.value_ref, bf16[1728,736]{1,0:T(8,128)(2,1)S(1)} %add_convert_fusion.1.query_ref.key_ref.value_ref, bf16[1728,736]{1,0:T(8,128)(2,1)S(1)} %add_convert_fusion.1.query_ref.key_ref.value_ref, ...), custom_call_target="tpu_custom_call" | custom-call | flops 4437573632 | bytes 16777216 | tf_op jit(solution)/shard_map/attend/pallas_call | solution.py:78
  180.4 4.6 fusion.50
  185.7 8.8 %collective-permute-done.39.refs_7_ = bf16[576,1152]{1,0:T(8,128)(2,1)} collective-permute-done((bf16[576,1152]{1,0:T(8,128)(2,1)}, bf16[576,1152]{1,0:T(8,128)(2,1)}, u32[]{:S(2)}, u32[]{:S(2)}) %collective-permute-start.39) | collective-permute-done | bytes 1327136 | tf_op jit(solution)/shard_map/ppermute | solution.py:473
  199.2 10.7 %collective-permute-done.44 = bf16[256,1152]{1,0:T(8,128)(2,1)S(1)} collective-permute-done((bf16[256,1152]{1,0:T(8,128)(2,1)S(1)}, bf16[256,1152]{1,0:T(8,128)(2,1)S(1)}, u32[]{:S(2)}, u32[]{:S(2)}) %collective-permute-start.44) | collective-permute-done | bytes 589856 | tf_op jit(solution)/shard_map/ppermute | solution.py:473
  215.4 7.9 %collective-permute-done.40 = bf16[256,1152]{1,0:T(8,128)(2,1)S(1)} collective-permute-done((bf16[256,1152]{1,0:T(8,128)(2,1)S(1)}, bf16[256,1152]{1,0:T(8,128)(2,1)S(1)}, u32[]{:S(2)}, u32[]{:S(2)}) %collective-permute-start.40) | collective-permute-done | bytes 589856 | tf_op jit(solution)/shard_map/ppermute | solution.py:473
  229.1 43.9 %mlp.2 = (f32[736,1152]{1,0:T(8,128)}, f32[736,1152]{1,0:T(8,128)}, bf16[4,2,288,1152]{3,2,1,0:T(8,128)(2,1)}, bf16[4,2,288,1152]{3,2,1,0:T(8,128)(2,1)}, f32[2304,1]{1,0:T(8,128)}) custom-call(bf16[736,1152]{1,0:T(8,128)(2,1)} %add_convert_fusion.3.normed_ref, bf16[736,1152]{1,0:T(8,128)(2,1)} %pad_maximum_fusion.1.grad_ref.base_ref, ...), custom_call_target="tpu_custom_call" | custom-call | flops 31255953408 | bytes 41943040 | tf_op jit(solution)/shard_map/mlp/pallas_call | solution.py:309
  277.0 2.7 pad_maximum_fusion.values_ref
  288.9 40.2 %mlp.3 = (f32[736,1152]{1,0:T(8,128)}, f32[736,1152]{1,0:T(8,128)}, bf16[4,2,256,1152]{3,2,1,0:T(8,128)(2,1)}, bf16[4,2,256,1152]{3,2,1,0:T(8,128)(2,1)}, f32[2048,1]{1,0:T(8,128)}) custom-call(bf16[736,1152]{1,0:T(8,128)(2,1)} %add_convert_fusion.3.normed_ref, ...), custom_call_target="tpu_custom_call", output_to_operand_aliasing={{0}: (11, {}), {1}: (12, {})} | custom-call | flops 27783069696 | bytes 41943040 | tf_op jit(solution)/shard_map/mlp/pallas_call | solution.py:309
  332.2 2.5 add_convert_fusion.2
  337.0 4.8 fusion.11
  341.8 3.3 norm_back.2
  348.4 9.1 %collective-permute-done.52 = bf16[368,1152]{1,0:T(8,128)(2,1)} collective-permute-done((bf16[368,1152]{1,0:T(8,128)(2,1)}, bf16[368,1152]{1,0:T(8,128)(2,1)}, u32[]{:S(2)}, u32[]{:S(2)}) %collective-permute-start.52) | collective-permute-done | bytes 847904 | tf_op jit(solution)/shard_map/ppermute | solution.py:600
  357.5 3.5 maximum_select_fusion.1
  361.7 2.7 convolution_convert_fusion.grad_ref
  366.0 2.7 convolution_convert_fusion.1.grad_ref
  371.3 13.9 %attend_back.3.grads_ref = bf16[3,576,736]{2,1,0:T(8,128)(2,1)S(1)} custom-call(bf16[1728,736]{1,0:T(8,128)(2,1)} %copy-done.31, bf16[1728,736]{1,0:T(8,128)(2,1)} %copy-done.31, bf16[1728,736]{1,0:T(8,128)(2,1)} %copy-done.31, f32[736,1]{1,0:T(8,128)S(1)} %copy-done.23, bf16[576,736]{1,0:T(8,128)(2,1)S(1)} %copy-done.29, ...), custom_call_target="tpu_custom_call" | custom-call | flops 8875147264 | bytes 16777216 | tf_op jit(solution)/shard_map/attend_back/pallas_call | solution.py:101
  386.8 2.4 collective-permute-start.98
  389.1 13.7 %attend_back.2.grads_ref = bf16[3,576,736]{2,1,0:T(8,128)(2,1)S(1)} custom-call(bf16[1728,736]{1,0:T(8,128)(2,1)} %copy-done.32, bf16[1728,736]{1,0:T(8,128)(2,1)} %copy-done.32, bf16[1728,736]{1,0:T(8,128)(2,1)} %copy-done.32, f32[736,1]{1,0:T(8,128)S(1)} %copy-done.23, bf16[576,736]{1,0:T(8,128)(2,1)S(1)} %copy-done.17, ...), custom_call_target="tpu_custom_call" | custom-call | flops 8875147264 | bytes 16777216 | tf_op jit(solution)/shard_map/attend_back/pallas_call | solution.py:101
  405.8 4.3 fusion.17
  410.0 4.3 fusion.6
  418.2 6.1 kinds_grad.2
  426.8 2.7 fusion.41
  429.7 8.3 %convolution_bitcast_fusion = f32[736,1152]{1,0:T(8,128)} fusion(bf16[3,576,736]{2,1,0:T(8,128)(2,1)} %copy-done.14, bf16[4,576,1152]{2,1,0:T(8,128)(2,1)} %copy-done.3), kind=kOutput, calls=%fused_computation.22 | convolution fusion | flops 2930245632 | bytes 10027008 | tf_op jit(solution)/shard_map/dot_general | solution.py:23
  446.3 2.3 collective-permute-start.76
  449.6 6.0 kinds_grad.3
  455.7 2.8 fusion.40
  461.6 9.4 %collective-permute-done.75 = bf16[2,72,1152]{2,1,0:T(8,128)(2,1)} collective-permute-done((bf16[2,72,1152]{2,1,0:T(8,128)(2,1)}, bf16[2,72,1152]{2,1,0:T(8,128)(2,1)}, u32[]{:S(2)}, u32[]{:S(2)}) %collective-permute-start.75) | collective-permute-done | bytes 331808 | tf_op jit(solution)/shard_map/ppermute | solution.py:473
  477.4 7.2 %convolution_add_fusion.2.grad_ref = f32[736,1152]{1,0:T(8,128)S(1)} fusion(f32[736,1152]{1,0:T(8,128)} %convolution_bitcast_fusion, bf16[1728,736]{1,0:T(8,128)(2,1)S(1)} %bitcast.335, bf16[1728,1152]{1,0:T(8,128)(2,1)} %bitcast.349), kind=kOutput, calls=%fused_computation.21 | convolution fusion | flops 2931093504 | bytes 13307904 | tf_op jit(solution)/shard_map/dot_general | solution.py:23
  484.7 3.3 norm_back.3
  492.2 3.9 fusion.8
  497.3 2.7 collective-permute-done.63
  500.0 4.8 collective-permute-start.64
  508.8 4.3 collective-permute-done.65
  516.0 5.4 collective-permute-done.73
  523.1 11.2 %collective-permute-done.69 = bf16[4,72,1152]{2,1,0:T(8,128)(2,1)S(1)} collective-permute-done((bf16[4,72,1152]{2,1,0:T(8,128)(2,1)S(1)}, bf16[4,72,1152]{2,1,0:T(8,128)(2,1)S(1)}, u32[]{:S(2)}, u32[]{:S(2)}) %collective-permute-start.69) | collective-permute-done | bytes 663584 | tf_op jit(solution)/shard_map/ppermute | solution.py:473
  536.8 2.3 collective-permute-start.79
  546.7 4.8 collective-permute-done.60
  557.8 2.8 divide.3
  561.3 12.3 %collective-permute-done.71 = bf16[2,72,1152]{2,1,0:T(8,128)(2,1)} collective-permute-done((bf16[2,72,1152]{2,1,0:T(8,128)(2,1)}, bf16[2,72,1152]{2,1,0:T(8,128)(2,1)}, u32[]{:S(2)}, u32[]{:S(2)}) %collective-permute-start.71) | collective-permute-done | bytes 331808 | tf_op jit(solution)/shard_map/ppermute | solution.py:473
  581.8 2.4 collective-permute-start.82
  584.2 2.6 settle.3
  605.0 4.9 collective-permute-done.86
  612.1 2.4 collective-permute-start.90
  617.7 6.7 %collective-permute-done.89 = bf16[72,1152]{1,0:T(8,128)(2,1)S(1)} collective-permute-done((bf16[72,1152]{1,0:T(8,128)(2,1)S(1)}, bf16[72,1152]{1,0:T(8,128)(2,1)S(1)}, u32[]{:S(2)}, u32[]{:S(2)}) %collective-permute-start.89) | collective-permute-done | bytes 165920 | tf_op jit(solution)/shard_map/ppermute | solution.py:473
  630.2 3.2 collective-permute-done.92.refs_2_
  (546 shorter events, 223.4 us)
Async XLA Ops:
  16.1 15.4 %collective-permute-start.5 = (bf16[72,1152]{1,0:T(8,128)(2,1)}, bf16[72,1152]{1,0:T(8,128)(2,1)S(1)}, u32[]{:S(2)}, u32[]{:S(2)}) collective-permute-start(bf16[72,1152]{1,0:T(8,128)(2,1)} %get-tuple-element.99), channel_id=1, source_target_pairs={{0,4},{1,5},{2,6},{3,7},{4,0},{5,1},{6,2},{7,3},{8,12},{9,13},{10,... | collective-permute-start | bytes 497672 | tf_op jit(solution)/shard_map/ppermute | solution.py:473
  19.6 17.8 %collective-permute-start.27 = (bf16[272,288]{1,0:T(8,128)(2,1)S(1)}, bf16[272,288]{1,0:T(8,128)(2,1)S(1)}, u32[]{:S(2)}, u32[]{:S(2)}) collective-permute-start(bf16[272,288]{1,0:T(8,128)(2,1)S(1)} %get-tuple-element.219), channel_id=1, source_target_pairs={{0,8},{1,9},{2,10},{3,11},{4,12},{5,13},{6,14},{7,15},{8,0},{9,1},... | collective-permute-start | bytes 470024 | tf_op jit(solution)/shard_map/ppermute | solution.py:473
  19.7 18.5 %collective-permute-start.28 = (bf16[272,288]{1,0:T(8,128)(2,1)S(1)}, bf16[272,288]{1,0:T(8,128)(2,1)S(1)}, u32[]{:S(2)}, u32[]{:S(2)}) collective-permute-start(bf16[272,288]{1,0:T(8,128)(2,1)S(1)} %get-tuple-element.218), channel_id=1, source_target_pairs={{0,16},{1,17},{2,18},{3,19},{4,20},{5,21},{6,22},{7,23},{8,24},{9,... | collective-permute-start | bytes 470024 | tf_op jit(solution)/shard_map/ppermute | solution.py:473
  35.7 20.0 %collective-permute-start.12 = (bf16[144,1152]{1,0:T(8,128)(2,1)S(1)}, bf16[144,1152]{1,0:T(8,128)(2,1)}, u32[]{:S(2)}, u32[]{:S(2)}) collective-permute-start(bf16[144,1152]{1,0:T(8,128)(2,1)S(1)} %maximum_bitcast_fusion.5), channel_id=1, source_target_pairs={{0,1},{1,0},{2,3},{3,2},{4,5},{5,4},{6,7},{7,6},{8,9},{9,8},{10,11... | collective-permute-start | bytes 995336 | tf_op jit(solution)/shard_map/ppermute | solution.py:473
  37.4 44.2 %collective-permute-start = (bf16[368,1152]{1,0:T(8,128)(2,1)}, bf16[368,1152]{1,0:T(8,128)(2,1)}, u32[]{:S(2)}, u32[]{:S(2)}) collective-permute-start(bf16[368,1152]{1,0:T(8,128)(2,1)} %get-tuple-element.200), channel_id=1, source_target_pairs={{0,1},{1,0},{2,3},{3,2},{4,5},{5,4},{6,7},{7,6},{8,9},{9,8},{10,11... | collective-permute-start | bytes 2543624 | tf_op jit(solution)/shard_map/ppermute | solution.py:600
  41.3 17.1 %collective-permute-start.10 = (bf16[144,1152]{1,0:T(8,128)(2,1)S(1)}, bf16[144,1152]{1,0:T(8,128)(2,1)}, u32[]{:S(2)}, u32[]{:S(2)}) collective-permute-start(bf16[144,1152]{1,0:T(8,128)(2,1)S(1)} %maximum_bitcast_fusion.4), channel_id=1, source_target_pairs={{0,16},{1,17},{2,18},{3,19},{4,20},{5,21},{6,22},{7,23},{8,24},{9,... | collective-permute-start | bytes 995336 | tf_op jit(solution)/shard_map/ppermute | solution.py:473
  51.4 17.8 %collective-permute-start.30 = (bf16[144,1152]{1,0:T(8,128)(2,1)}, bf16[144,1152]{1,0:T(8,128)(2,1)}, u32[]{:S(2)}, u32[]{:S(2)}) collective-permute-start(bf16[144,1152]{1,0:T(8,128)(2,1)} %get-tuple-element.113), channel_id=1, source_target_pairs={{0,2},{1,3},{2,0},{3,1},{4,6},{5,7},{6,4},{7,5},{8,10},{9,11},{10,... | collective-permute-start | bytes 995336 | tf_op jit(solution)/shard_map/ppermute | solution.py:473
  55.0 26.2 %collective-permute-start.31 = (bf16[144,1152]{1,0:T(8,128)(2,1)}, bf16[144,1152]{1,0:T(8,128)(2,1)}, u32[]{:S(2)}, u32[]{:S(2)}) collective-permute-start(bf16[144,1152]{1,0:T(8,128)(2,1)} %get-tuple-element.113), channel_id=1, source_target_pairs={{0,4},{1,5},{2,6},{3,7},{4,0},{5,1},{6,2},{7,3},{8,12},{9,13},{10,... | collective-permute-start | bytes 995336 | tf_op jit(solution)/shard_map/ppermute | solution.py:473
  55.7 25.4 %collective-permute-start.32 = (bf16[144,1152]{1,0:T(8,128)(2,1)}, bf16[144,1152]{1,0:T(8,128)(2,1)}, u32[]{:S(2)}, u32[]{:S(2)}) collective-permute-start(bf16[144,1152]{1,0:T(8,128)(2,1)} %get-tuple-element.113), channel_id=1, source_target_pairs={{0,6},{1,7},{2,4},{3,5},{4,2},{5,3},{6,0},{7,1},{8,14},{9,15},{10,... | collective-permute-start | bytes 995336 | tf_op jit(solution)/shard_map/ppermute | solution.py:473
  58.4 26.5 %collective-permute-start.13 = (bf16[288,1152]{1,0:T(8,128)(2,1)S(1)}, bf16[288,1152]{1,0:T(8,128)(2,1)S(1)}, u32[]{:S(2)}, u32[]{:S(2)}) collective-permute-start(bf16[288,1152]{1,0:T(8,128)(2,1)S(1)} %maximum_bitcast_fusion.1.refs_2_), channel_id=1, source_target_pairs={{0,16},{1,17},{2,18},{3,19},{4,20},{5,21},{6,22},{7,23},{8,24},{9,... | collective-permute-start | bytes 1990664 | tf_op jit(solution)/shard_map/ppermute | solution.py:473
  69.2 15.9 %collective-permute-start.11 = (bf16[288,1152]{1,0:T(8,128)(2,1)S(1)}, bf16[288,1152]{1,0:T(8,128)(2,1)S(1)}, u32[]{:S(2)}, u32[]{:S(2)}) collective-permute-start(bf16[288,1152]{1,0:T(8,128)(2,1)S(1)} %maximum_bitcast_fusion.refs_0_), channel_id=1, source_target_pairs={{0,1},{1,0},{2,3},{3,2},{4,5},{5,4},{6,7},{7,6},{8,9},{9,8},{10,11... | collective-permute-start | bytes 1990664 | tf_op jit(solution)/shard_map/ppermute | solution.py:473
  81.1 17.2 %collective-permute-start.24 = (bf16[288,1152]{1,0:T(8,128)(2,1)S(1)}, bf16[288,1152]{1,0:T(8,128)(2,1)S(1)}, u32[]{:S(2)}, u32[]{:S(2)}) collective-permute-start(bf16[288,1152]{1,0:T(8,128)(2,1)S(1)} %maximum_bitcast_fusion.1.refs_2_), channel_id=1, source_target_pairs={{0,8},{1,9},{2,10},{3,11},{4,12},{5,13},{6,14},{7,15},{8,0},{9,1},... | collective-permute-start | bytes 1990664 | tf_op jit(solution)/shard_map/ppermute | solution.py:473
  81.1 17.5 %collective-permute-start.22 = (bf16[288,1152]{1,0:T(8,128)(2,1)S(1)}, bf16[288,1152]{1,0:T(8,128)(2,1)S(1)}, u32[]{:S(2)}, u32[]{:S(2)}) collective-permute-start(bf16[288,1152]{1,0:T(8,128)(2,1)S(1)} %maximum_bitcast_fusion.refs_0_), channel_id=1, source_target_pairs={{0,8},{1,9},{2,10},{3,11},{4,12},{5,13},{6,14},{7,15},{8,0},{9,1},... | collective-permute-start | bytes 1990664 | tf_op jit(solution)/shard_map/ppermute | solution.py:473
  96.7 17.4 %collective-permute-start.17 = (bf16[288,1152]{1,0:T(8,128)(2,1)S(1)}, bf16[288,1152]{1,0:T(8,128)(2,1)S(1)}, u32[]{:S(2)}, u32[]{:S(2)}) collective-permute-start(bf16[288,1152]{1,0:T(8,128)(2,1)S(1)} %maximum_bitcast_fusion.3.refs_2_), channel_id=1, source_target_pairs={{0,16},{1,17},{2,18},{3,19},{4,20},{5,21},{6,22},{7,23},{8,24},{9,... | collective-permute-start | bytes 1990664 | tf_op jit(solution)/shard_map/ppermute | solution.py:473
  98.4 62.0 %collective-permute-start.20 = (bf16[288,1152]{1,0:T(8,128)(2,1)S(1)}, bf16[288,1152]{1,0:T(8,128)(2,1)S(1)}, u32[]{:S(2)}, u32[]{:S(2)}) collective-permute-start(bf16[288,1152]{1,0:T(8,128)(2,1)S(1)} %maximum_bitcast_fusion.3.refs_2_), channel_id=1, source_target_pairs={{0,8},{1,9},{2,10},{3,11},{4,12},{5,13},{6,14},{7,15},{8,0},{9,1},... | collective-permute-start | bytes 1990664 | tf_op jit(solution)/shard_map/ppermute | solution.py:473
  98.6 17.7 %collective-permute-start.15 = (bf16[288,1152]{1,0:T(8,128)(2,1)S(1)}, bf16[288,1152]{1,0:T(8,128)(2,1)S(1)}, u32[]{:S(2)}, u32[]{:S(2)}) collective-permute-start(bf16[288,1152]{1,0:T(8,128)(2,1)S(1)} %maximum_bitcast_fusion.2.refs_0_), channel_id=1, source_target_pairs={{0,1},{1,0},{2,3},{3,2},{4,5},{5,4},{6,7},{7,6},{8,9},{9,8},{10,11... | collective-permute-start | bytes 1990664 | tf_op jit(solution)/shard_map/ppermute | solution.py:473
  99.8 61.8 %collective-permute-start.18 = (bf16[288,1152]{1,0:T(8,128)(2,1)S(1)}, bf16[288,1152]{1,0:T(8,128)(2,1)}, u32[]{:S(2)}, u32[]{:S(2)}) collective-permute-start(bf16[288,1152]{1,0:T(8,128)(2,1)S(1)} %maximum_bitcast_fusion.2.refs_0_), channel_id=1, source_target_pairs={{0,8},{1,9},{2,10},{3,11},{4,12},{5,13},{6,14},{7,15},{8,0},{9,1},... | collective-permute-start | bytes 1990664 | tf_op jit(solution)/shard_map/ppermute | solution.py:473
  99.8 34.7 %collective-permute-start.26 = (bf16[368,1152]{1,0:T(8,128)(2,1)S(1)}, bf16[368,1152]{1,0:T(8,128)(2,1)S(1)}, u32[]{:S(2)}, u32[]{:S(2)}) collective-permute-start(bf16[368,1152]{1,0:T(8,128)(2,1)S(1)} %copy-done.53), channel_id=1, source_target_pairs={{0,1},{1,0},{2,3},{3,2},{4,5},{5,4},{6,7},{7,6},{8,9},{9,8},{10,11... | collective-permute-start | bytes 2543624 | tf_op jit(solution)/shard_map/ppermute | solution.py:600
  119.2 29.1 %collective-permute-start.38 = (bf16[288,1152]{1,0:T(8,128)(2,1)}, bf16[288,1152]{1,0:T(8,128)(2,1)}, u32[]{:S(2)}, u32[]{:S(2)}) collective-permute-start(bf16[288,1152]{1,0:T(8,128)(2,1)} %bitcast.59), channel_id=1, source_target_pairs={{0,1},{1,0},{2,3},{3,2},{4,5},{5,4},{6,7},{7,6},{8,9},{9,8},{10,11... | collective-permute-start | bytes 1990664 | tf_op jit(solution)/shard_map/ppermute | solution.py:473
  130.1 22.0 %collective-permute-start.36 = (bf16[288,1152]{1,0:T(8,128)(2,1)S(1)}, bf16[288,1152]{1,0:T(8,128)(2,1)S(1)}, u32[]{:S(2)}, u32[]{:S(2)}) collective-permute-start(bf16[288,1152]{1,0:T(8,128)(2,1)S(1)} %bitcast.367), channel_id=1, source_target_pairs={{0,16},{1,17},{2,18},{3,19},{4,20},{5,21},{6,22},{7,23},{8,24},{9,... | collective-permute-start | bytes 1990664 | tf_op jit(solution)/shard_map/ppermute | solution.py:473
  134.5 28.6 %collective-permute-start.21 = (bf16[288,1152]{1,0:T(8,128)(2,1)S(1)}, bf16[288,1152]{1,0:T(8,128)(2,1)S(1)}, u32[]{:S(2)}, u32[]{:S(2)}) collective-permute-start(bf16[288,1152]{1,0:T(8,128)(2,1)S(1)} %collective-permute-done.17.refs_3_), channel_id=1, source_target_pairs={{0,8},{1,9},{2,10},{3,11},{4,12},{5,13},{6,14},{7,15},{8,0},{9,1},... | collective-permute-start | bytes 1990664 | tf_op jit(solution)/shard_map/ppermute | solution.py:473
  148.3 15.4 %collective-permute-start.19 = (bf16[288,1152]{1,0:T(8,128)(2,1)S(1)}, bf16[288,1152]{1,0:T(8,128)(2,1)S(1)}, u32[]{:S(2)}, u32[]{:S(2)}) collective-permute-start(bf16[288,1152]{1,0:T(8,128)(2,1)S(1)} %copy-done.19), channel_id=1, source_target_pairs={{0,8},{1,9},{2,10},{3,11},{4,12},{5,13},{6,14},{7,15},{8,0},{9,1},... | collective-permute-start | bytes 1990664 | tf_op jit(solution)/shard_map/ppermute | solution.py:473
  152.1 32.9 %collective-permute-start.33 = (bf16[128,1152]{1,0:T(8,128)(2,1)}, bf16[128,1152]{1,0:T(8,128)(2,1)}, u32[]{:S(2)}, u32[]{:S(2)}) collective-permute-start(bf16[128,1152]{1,0:T(8,128)(2,1)} %get-tuple-element.117), channel_id=1, source_target_pairs={{0,2},{1,3},{2,0},{3,1},{4,6},{5,7},{6,4},{7,5},{8,10},{9,11},{10,... | collective-permute-start | bytes 884744 | tf_op jit(solution)/shard_map/ppermute | solution.py:473
  160.4 24.8 %collective-permute-start.34 = (bf16[128,1152]{1,0:T(8,128)(2,1)}, bf16[128,1152]{1,0:T(8,128)(2,1)}, u32[]{:S(2)}, u32[]{:S(2)}) collective-permute-start(bf16[128,1152]{1,0:T(8,128)(2,1)} %get-tuple-element.117), channel_id=1, source_target_pairs={{0,4},{1,5},{2,6},{3,7},{4,0},{5,1},{6,2},{7,3},{8,12},{9,13},{10,... | collective-permute-start | bytes 884744 | tf_op jit(solution)/shard_map/ppermute | solution.py:473
  161.6 24.0 %collective-permute-start.35 = (bf16[128,1152]{1,0:T(8,128)(2,1)}, bf16[128,1152]{1,0:T(8,128)(2,1)}, u32[]{:S(2)}, u32[]{:S(2)}) collective-permute-start(bf16[128,1152]{1,0:T(8,128)(2,1)} %get-tuple-element.117), channel_id=1, source_target_pairs={{0,6},{1,7},{2,4},{3,5},{4,2},{5,3},{6,0},{7,1},{8,14},{9,15},{10,... | collective-permute-start | bytes 884744 | tf_op jit(solution)/shard_map/ppermute | solution.py:473
  163.1 31.3 %collective-permute-start.39 = (bf16[576,1152]{1,0:T(8,128)(2,1)}, bf16[576,1152]{1,0:T(8,128)(2,1)}, u32[]{:S(2)}, u32[]{:S(2)}) collective-permute-start(bf16[576,1152]{1,0:T(8,128)(2,1)} %bitcast.61.refs_6_), channel_id=1, source_target_pairs={{0,16},{1,17},{2,18},{3,19},{4,20},{5,21},{6,22},{7,23},{8,24},{9,... | collective-permute-start | bytes 3981320 | tf_op jit(solution)/shard_map/ppermute | solution.py:473
  163.7 31.0 %collective-permute-start.37 = (bf16[576,1152]{1,0:T(8,128)(2,1)}, bf16[576,1152]{1,0:T(8,128)(2,1)}, u32[]{:S(2)}, u32[]{:S(2)}) collective-permute-start(bf16[576,1152]{1,0:T(8,128)(2,1)} %bitcast.56.refs_4_), channel_id=1, source_target_pairs={{0,1},{1,0},{2,3},{3,2},{4,5},{5,4},{6,7},{7,6},{8,9},{9,8},{10,11... | collective-permute-start | bytes 3981320 | tf_op jit(solution)/shard_map/ppermute | solution.py:473
  185.1 41.7 %collective-permute-start.50 = (bf16[576,1152]{1,0:T(8,128)(2,1)}, bf16[576,1152]{1,0:T(8,128)(2,1)S(1)}, u32[]{:S(2)}, u32[]{:S(2)}) collective-permute-start(bf16[576,1152]{1,0:T(8,128)(2,1)} %bitcast.61.refs_6_), channel_id=1, source_target_pairs={{0,8},{1,9},{2,10},{3,11},{4,12},{5,13},{6,14},{7,15},{8,0},{9,1},... | collective-permute-start | bytes 3981320 | tf_op jit(solution)/shard_map/ppermute | solution.py:473
  185.2 43.9 %collective-permute-start.48 = (bf16[576,1152]{1,0:T(8,128)(2,1)}, bf16[576,1152]{1,0:T(8,128)(2,1)}, u32[]{:S(2)}, u32[]{:S(2)}) collective-permute-start(bf16[576,1152]{1,0:T(8,128)(2,1)} %bitcast.56.refs_4_), channel_id=1, source_target_pairs={{0,8},{1,9},{2,10},{3,11},{4,12},{5,13},{6,14},{7,15},{8,0},{9,1},... | collective-permute-start | bytes 3981320 | tf_op jit(solution)/shard_map/ppermute | solution.py:473
  197.6 31.5 %collective-permute-start.51 = (bf16[576,1152]{1,0:T(8,128)(2,1)}, bf16[576,1152]{1,0:T(8,128)(2,1)}, u32[]{:S(2)}, u32[]{:S(2)}) collective-permute-start(bf16[576,1152]{1,0:T(8,128)(2,1)} %collective-permute-done.39.refs_7_), channel_id=1, source_target_pairs={{0,8},{1,9},{2,10},{3,11},{4,12},{5,13},{6,14},{7,15},{8,0},{9,1},... | collective-permute-start | bytes 3981320 | tf_op jit(solution)/shard_map/ppermute | solution.py:473
  197.6 31.4 %collective-permute-start.49 = (bf16[576,1152]{1,0:T(8,128)(2,1)}, bf16[576,1152]{1,0:T(8,128)(2,1)}, u32[]{:S(2)}, u32[]{:S(2)}) collective-permute-start(bf16[576,1152]{1,0:T(8,128)(2,1)} %collective-permute-done.37.refs_5_), channel_id=1, source_target_pairs={{0,8},{1,9},{2,10},{3,11},{4,12},{5,13},{6,14},{7,15},{8,0},{9,1},... | collective-permute-start | bytes 3981320 | tf_op jit(solution)/shard_map/ppermute | solution.py:473
  223.2 50.4 %collective-permute-start.46 = (bf16[512,1152]{1,0:T(8,128)(2,1)}, bf16[512,1152]{1,0:T(8,128)(2,1)}, u32[]{:S(2)}, u32[]{:S(2)}) collective-permute-start(bf16[512,1152]{1,0:T(8,128)(2,1)} %bitcast.71.refs_6_), channel_id=1, source_target_pairs={{0,16},{1,17},{2,18},{3,19},{4,20},{5,21},{6,22},{7,23},{8,24},{9,... | collective-permute-start | bytes 3538952 | tf_op jit(solution)/shard_map/ppermute | solution.py:473
  227.9 46.2 %collective-permute-start.42 = (bf16[512,1152]{1,0:T(8,128)(2,1)}, bf16[512,1152]{1,0:T(8,128)(2,1)}, u32[]{:S(2)}, u32[]{:S(2)}) collective-permute-start(bf16[512,1152]{1,0:T(8,128)(2,1)} %bitcast.66.refs_4_), channel_id=1, source_target_pairs={{0,1},{1,0},{2,3},{3,2},{4,5},{5,4},{6,7},{7,6},{8,9},{9,8},{10,11... | collective-permute-start | bytes 3538952 | tf_op jit(solution)/shard_map/ppermute | solution.py:473
  273.0 64.0 %collective-permute-start.53 = (bf16[4,2,288,1152]{3,2,1,0:T(8,128)(2,1)}, bf16[4,2,288,1152]{3,2,1,0:T(8,128)(2,1)}, u32[]{:S(2)}, u32[]{:S(2)}) collective-permute-start(bf16[4,2,288,1152]{3,2,1,0:T(8,128)(2,1)} %get-tuple-element.127), channel_id=1, source_target_pairs={{0,8},{1,9},{2,10},{3,11},{4,12},{5,13},{6,14},{7,15},{8,0},{9,1},... | collective-permute-start | bytes 15925256 | tf_op jit(solution)/shard_map/ppermute | solution.py:473
  329.1 76.6 %collective-permute-start.58 = (bf16[4,2,256,1152]{3,2,1,0:T(8,128)(2,1)}, bf16[4,2,256,1152]{3,2,1,0:T(8,128)(2,1)}, u32[]{:S(2)}, u32[]{:S(2)}) collective-permute-start(bf16[4,2,256,1152]{3,2,1,0:T(8,128)(2,1)} %get-tuple-element.137), channel_id=1, source_target_pairs={{0,8},{1,9},{2,10},{3,11},{4,12},{5,13},{6,14},{7,15},{8,0},{9,1},... | collective-permute-start | bytes 14155784 | tf_op jit(solution)/shard_map/ppermute | solution.py:473
  336.0 21.5 %collective-permute-start.52 = (bf16[368,1152]{1,0:T(8,128)(2,1)}, bf16[368,1152]{1,0:T(8,128)(2,1)}, u32[]{:S(2)}, u32[]{:S(2)}) collective-permute-start(bf16[368,1152]{1,0:T(8,128)(2,1)} %get-tuple-element.196), channel_id=1, source_target_pairs={{0,1},{1,0},{2,3},{3,2},{4,5},{5,4},{6,7},{7,6},{8,9},{9,8},{10,11... | collective-permute-start | bytes 2543624 | tf_op jit(solution)/shard_map/ppermute | solution.py:600
  368.7 41.4 %collective-permute-start.54 = (bf16[2,288,1152]{2,1,0:T(8,128)(2,1)}, bf16[2,288,1152]{2,1,0:T(8,128)(2,1)}, u32[]{:S(2)}, u32[]{:S(2)}) collective-permute-start(bf16[2,288,1152]{2,1,0:T(8,128)(2,1)} %get-tuple-element.130), channel_id=1, source_target_pairs={{0,1},{1,0},{2,3},{3,2},{4,5},{5,4},{6,7},{7,6},{8,9},{9,8},{10,11... | collective-permute-start | bytes 3981320 | tf_op jit(solution)/shard_map/ppermute | solution.py:473
  369.9 40.1 %collective-permute-start.55 = (bf16[2,288,1152]{2,1,0:T(8,128)(2,1)S(1)}, bf16[2,288,1152]{2,1,0:T(8,128)(2,1)}, u32[]{:S(2)}, u32[]{:S(2)}) collective-permute-start(bf16[2,288,1152]{2,1,0:T(8,128)(2,1)S(1)} %copy-done.51), channel_id=1, source_target_pairs={{0,16},{1,17},{2,18},{3,19},{4,20},{5,21},{6,22},{7,23},{8,24},{9,... | collective-permute-start | bytes 3981320 | tf_op jit(solution)/shard_map/ppermute | solution.py:473
  370.7 16.1 %collective-permute-start.97 = (f32[70,128]{1,0:T(8,128)S(1)}, f32[70,128]{1,0:T(8,128)S(1)}, u32[]{:S(2)}, u32[]{:S(2)}) collective-permute-start(f32[70,128]{1,0:T(8,128)S(1)} %add.428), channel_id=1, source_target_pairs={{0,2},{1,3},{2,0},{3,1},{4,6},{5,7},{6,4},{7,5},{8,10},{9,11},{10,... | collective-permute-start | bytes 107528 | tf_op jit(solution)/shard_map/ppermute | solution.py:473
  386.8 17.6 %collective-permute-start.98 = (f32[70,128]{1,0:T(8,128)S(1)}, f32[70,128]{1,0:T(8,128)S(1)}, u32[]{:S(2)}, u32[]{:S(2)}) collective-permute-start(f32[70,128]{1,0:T(8,128)S(1)} %add.429), channel_id=1, source_target_pairs={{0,4},{1,5},{2,6},{3,7},{4,0},{5,1},{6,2},{7,3},{8,12},{9,13},{10,... | collective-permute-start | bytes 107528 | tf_op jit(solution)/shard_map/ppermute | solution.py:473
  425.5 16.6 %collective-permute-start.56 = (bf16[2,2,72,1152]{3,2,0,1:T(8,128)(2,1)}, bf16[2,2,72,1152]{3,2,0,1:T(8,128)(2,1)}, u32[]{:S(2)}, u32[]{:S(2)}) collective-permute-start(bf16[2,2,72,1152]{3,2,0,1:T(8,128)(2,1)} %get-tuple-element.132), channel_id=1, source_target_pairs={{0,16},{1,17},{2,18},{3,19},{4,20},{5,21},{6,22},{7,23},{8,24},{9,... | collective-permute-start | bytes 1990664 | tf_op jit(solution)/shard_map/ppermute | solution.py:473
  429.5 43.5 %collective-permute-start.59 = (bf16[2,8,72,1152]{3,2,1,0:T(8,128)(2,1)}, bf16[2,8,72,1152]{3,2,1,0:T(8,128)(2,1)}, u32[]{:S(2)}, u32[]{:S(2)}) collective-permute-start(bf16[2,8,72,1152]{3,2,1,0:T(8,128)(2,1)} %bitcast.93), channel_id=1, source_target_pairs={{0,8},{1,9},{2,10},{3,11},{4,12},{5,13},{6,14},{7,15},{8,0},{9,1},... | collective-permute-start | bytes 7962632 | tf_op jit(solution)/shard_map/ppermute | solution.py:473
  444.2 16.7 %collective-permute-start.74 = (bf16[2,72,1152]{2,1,0:T(8,128)(2,1)}, bf16[2,72,1152]{2,1,0:T(8,128)(2,1)}, u32[]{:S(2)}, u32[]{:S(2)}) collective-permute-start(bf16[2,72,1152]{2,1,0:T(8,128)(2,1)} %slice_bitcast_fusion.15), channel_id=1, source_target_pairs={{0,2},{1,3},{2,0},{3,1},{4,6},{5,7},{6,4},{7,5},{8,10},{9,11},{10,... | collective-permute-start | bytes 995336 | tf_op jit(solution)/shard_map/ppermute | solution.py:473
  444.8 26.2 %collective-permute-start.75 = (bf16[2,72,1152]{2,1,0:T(8,128)(2,1)}, bf16[2,72,1152]{2,1,0:T(8,128)(2,1)}, u32[]{:S(2)}, u32[]{:S(2)}) collective-permute-start(bf16[2,72,1152]{2,1,0:T(8,128)(2,1)} %get-tuple-element.153), channel_id=1, source_target_pairs={{0,4},{1,5},{2,6},{3,7},{4,0},{5,1},{6,2},{7,3},{8,12},{9,13},{10,... | collective-permute-start | bytes 995336 | tf_op jit(solution)/shard_map/ppermute | solution.py:473
  446.3 24.6 %collective-permute-start.76 = (bf16[2,72,1152]{2,1,0:T(8,128)(2,1)}, bf16[2,72,1152]{2,1,0:T(8,128)(2,1)}, u32[]{:S(2)}, u32[]{:S(2)}) collective-permute-start(bf16[2,72,1152]{2,1,0:T(8,128)(2,1)} %get-tuple-element.154), channel_id=1, source_target_pairs={{0,6},{1,7},{2,4},{3,5},{4,2},{5,3},{6,0},{7,1},{8,14},{9,15},{10,... | collective-permute-start | bytes 995336 | tf_op jit(solution)/shard_map/ppermute | solution.py:473
  448.6 43.6 %collective-permute-start.66 = (bf16[2,256,1152]{2,1,0:T(8,128)(2,1)}, bf16[2,256,1152]{2,1,0:T(8,128)(2,1)}, u32[]{:S(2)}, u32[]{:S(2)}) collective-permute-start(bf16[2,256,1152]{2,1,0:T(8,128)(2,1)} %get-tuple-element.144), channel_id=1, source_target_pairs={{0,1},{1,0},{2,3},{3,2},{4,5},{5,4},{6,7},{7,6},{8,9},{9,8},{10,11... | collective-permute-start | bytes 3538952 | tf_op jit(solution)/shard_map/ppermute | solution.py:473
  460.9 31.3 %collective-permute-start.67 = (bf16[2,256,1152]{2,1,0:T(8,128)(2,1)}, bf16[2,256,1152]{2,1,0:T(8,128)(2,1)}, u32[]{:S(2)}, u32[]{:S(2)}) collective-permute-start(bf16[2,256,1152]{2,1,0:T(8,128)(2,1)} %get-tuple-element.145), channel_id=1, source_target_pairs={{0,16},{1,17},{2,18},{3,19},{4,20},{5,21},{6,22},{7,23},{8,24},{9,... | collective-permute-start | bytes 3538952 | tf_op jit(solution)/shard_map/ppermute | solution.py:473
  471.0 70.3 %collective-permute-start.83 = (bf16[2,8,72,1152]{3,2,1,0:T(8,128)(2,1)}, bf16[2,8,72,1152]{3,2,1,0:T(8,128)(2,1)}, u32[]{:S(2)}, u32[]{:S(2)}) collective-permute-start(bf16[2,8,72,1152]{3,2,1,0:T(8,128)(2,1)} %bitcast.353), channel_id=1, source_target_pairs={{0,8},{1,9},{2,10},{3,11},{4,12},{5,13},{6,14},{7,15},{8,0},{9,1},... | collective-permute-start | bytes 7962632 | tf_op jit(solution)/shard_map/ppermute | solution.py:473
  505.0 16.3 %collective-permute-start.73 = (bf16[2,2,64,1152]{3,2,0,1:T(8,128)(2,1)S(1)}, bf16[2,2,64,1152]{3,2,0,1:T(8,128)(2,1)S(1)}, u32[]{:S(2)}, u32[]{:S(2)}) collective-permute-start(bf16[2,2,64,1152]{3,2,0,1:T(8,128)(2,1)S(1)} %bitcast.384), channel_id=1, source_target_pairs={{0,1},{1,0},{2,3},{3,2},{4,5},{5,4},{6,7},{7,6},{8,9},{9,8},{10,11... | collective-permute-start | bytes 1769480 | tf_op jit(solution)/shard_map/ppermute | solution.py:473
  506.3 16.4 %collective-permute-start.72 = (bf16[2,2,64,1152]{3,2,0,1:T(8,128)(2,1)S(1)}, bf16[2,2,64,1152]{3,2,0,1:T(8,128)(2,1)S(1)}, u32[]{:S(2)}, u32[]{:S(2)}) collective-permute-start(bf16[2,2,64,1152]{3,2,0,1:T(8,128)(2,1)S(1)} %bitcast.383), channel_id=1, source_target_pairs={{0,16},{1,17},{2,18},{3,19},{4,20},{5,21},{6,22},{7,23},{8,24},{9,... | collective-permute-start | bytes 1769480 | tf_op jit(solution)/shard_map/ppermute | solution.py:473
  507.6 26.7 %collective-permute-start.69 = (bf16[4,72,1152]{2,1,0:T(8,128)(2,1)S(1)}, bf16[4,72,1152]{2,1,0:T(8,128)(2,1)S(1)}, u32[]{:S(2)}, u32[]{:S(2)}) collective-permute-start(bf16[4,72,1152]{2,1,0:T(8,128)(2,1)S(1)} %copy-done.56), channel_id=1, source_target_pairs={{0,16},{1,17},{2,18},{3,19},{4,20},{5,21},{6,22},{7,23},{8,24},{9,... | collective-permute-start | bytes 1990664 | tf_op jit(solution)/shard_map/ppermute | solution.py:473
  513.1 23.7 %collective-permute-start.68 = (bf16[2,2,72,1152]{3,2,1,0:T(8,128)(2,1)S(1)}, bf16[2,2,72,1152]{3,2,1,0:T(8,128)(2,1)S(1)}, u32[]{:S(2)}, u32[]{:S(2)}) collective-permute-start(bf16[2,2,72,1152]{3,2,1,0:T(8,128)(2,1)S(1)} %copy-done.55), channel_id=1, source_target_pairs={{0,1},{1,0},{2,3},{3,2},{4,5},{5,4},{6,7},{7,6},{8,9},{9,8},{10,11... | collective-permute-start | bytes 1990664 | tf_op jit(solution)/shard_map/ppermute | solution.py:473
  521.4 30.1 %collective-permute-start.60 = (bf16[368,1152]{1,0:T(8,128)(2,1)S(1)}, bf16[368,1152]{1,0:T(8,128)(2,1)S(1)}, u32[]{:S(2)}, u32[]{:S(2)}) collective-permute-start(bf16[368,1152]{1,0:T(8,128)(2,1)S(1)} %slice.427), channel_id=1, source_target_pairs={{0,1},{1,0},{2,3},{3,2},{4,5},{5,4},{6,7},{7,6},{8,9},{9,8},{10,11... | collective-permute-start | bytes 2543624 | tf_op jit(solution)/shard_map/ppermute | solution.py:600
  523.0 31.8 %collective-permute-start.77 = (bf16[2,64,1152]{2,1,0:T(8,128)(2,1)S(1)}, bf16[2,64,1152]{2,1,0:T(8,128)(2,1)S(1)}, u32[]{:S(2)}, u32[]{:S(2)}) collective-permute-start(bf16[2,64,1152]{2,1,0:T(8,128)(2,1)S(1)} %slice_bitcast_fusion.18), channel_id=1, source_target_pairs={{0,2},{1,3},{2,0},{3,1},{4,6},{5,7},{6,4},{7,5},{8,10},{9,11},{10,... | collective-permute-start | bytes 884744 | tf_op jit(solution)/shard_map/ppermute | solution.py:473
  534.3 21.4 %collective-permute-start.78 = (bf16[2,64,1152]{2,1,0:T(8,128)(2,1)S(1)}, bf16[2,64,1152]{2,1,0:T(8,128)(2,1)S(1)}, u32[]{:S(2)}, u32[]{:S(2)}) collective-permute-start(bf16[2,64,1152]{2,1,0:T(8,128)(2,1)S(1)} %get-tuple-element.156), channel_id=1, source_target_pairs={{0,4},{1,5},{2,6},{3,7},{4,0},{5,1},{6,2},{7,3},{8,12},{9,13},{10,... | collective-permute-start | bytes 884744 | tf_op jit(solution)/shard_map/ppermute | solution.py:473
  536.8 20.1 %collective-permute-start.79 = (bf16[2,64,1152]{2,1,0:T(8,128)(2,1)S(1)}, bf16[2,64,1152]{2,1,0:T(8,128)(2,1)S(1)}, u32[]{:S(2)}, u32[]{:S(2)}) collective-permute-start(bf16[2,64,1152]{2,1,0:T(8,128)(2,1)S(1)} %get-tuple-element.157), channel_id=1, source_target_pairs={{0,6},{1,7},{2,4},{3,5},{4,2},{5,3},{6,0},{7,1},{8,14},{9,15},{10,... | collective-permute-start | bytes 884744 | tf_op jit(solution)/shard_map/ppermute | solution.py:473
  545.5 44.3 %collective-permute-start.85 = (bf16[4,72,1152]{2,1,0:T(8,128)(2,1)}, bf16[4,72,1152]{2,1,0:T(8,128)(2,1)}, u32[]{:S(2)}, u32[]{:S(2)}) collective-permute-start(bf16[4,72,1152]{2,1,0:T(8,128)(2,1)} %fusion.22), channel_id=1, source_target_pairs={{0,16},{1,17},{2,18},{3,19},{4,20},{5,21},{6,22},{7,23},{8,24},{9,... | collective-permute-start | bytes 1990664 | tf_op jit(solution)/shard_map/ppermute | solution.py:473
  551.5 40.6 %collective-permute-start.84 = (bf16[2,2,72,1152]{3,2,1,0:T(8,128)(2,1)}, bf16[2,2,72,1152]{3,2,1,0:T(8,128)(2,1)}, u32[]{:S(2)}, u32[]{:S(2)}) collective-permute-start(bf16[2,2,72,1152]{3,2,1,0:T(8,128)(2,1)} %add_convert_fusion.10), channel_id=1, source_target_pairs={{0,1},{1,0},{2,3},{3,2},{4,5},{5,4},{6,7},{7,6},{8,9},{9,8},{10,11... | collective-permute-start | bytes 1990664 | tf_op jit(solution)/shard_map/ppermute | solution.py:473
  554.8 18.8 %collective-permute-start.71 = (bf16[2,72,1152]{2,1,0:T(8,128)(2,1)}, bf16[2,72,1152]{2,1,0:T(8,128)(2,1)}, u32[]{:S(2)}, u32[]{:S(2)}) collective-permute-start(bf16[2,72,1152]{2,1,0:T(8,128)(2,1)} %slice.572), channel_id=1, source_target_pairs={{0,1},{1,0},{2,3},{3,2},{4,5},{5,4},{6,7},{7,6},{8,9},{9,8},{10,11... | collective-permute-start | bytes 995336 | tf_op jit(solution)/shard_map/ppermute | solution.py:473
  555.6 19.9 %collective-permute-start.70 = (bf16[2,72,1152]{2,1,0:T(8,128)(2,1)}, bf16[2,72,1152]{2,1,0:T(8,128)(2,1)}, u32[]{:S(2)}, u32[]{:S(2)}) collective-permute-start(bf16[2,72,1152]{2,1,0:T(8,128)(2,1)} %slice_bitcast_fusion.11), channel_id=1, source_target_pairs={{0,16},{1,17},{2,18},{3,19},{4,20},{5,21},{6,22},{7,23},{8,24},{9,... | collective-permute-start | bytes 995336 | tf_op jit(solution)/shard_map/ppermute | solution.py:473
  560.6 18.8 %collective-permute-start.100 = (bf16[272,288]{1,0:T(8,128)(2,1)}, bf16[272,288]{1,0:T(8,128)(2,1)S(1)}, u32[]{:S(2)}, u32[]{:S(2)}) collective-permute-start(bf16[272,288]{1,0:T(8,128)(2,1)} %get-tuple-element.177), channel_id=1, source_target_pairs={{0,16},{1,17},{2,18},{3,19},{4,20},{5,21},{6,22},{7,23},{8,24},{9,... | collective-permute-start | bytes 470024 | tf_op jit(solution)/shard_map/ppermute | solution.py:473
  579.4 32.6 %collective-permute-start.80 = (bf16[72,1152]{1,0:T(8,128)(2,1)}, bf16[72,1152]{1,0:T(8,128)(2,1)}, u32[]{:S(2)}, u32[]{:S(2)}) collective-permute-start(bf16[72,1152]{1,0:T(8,128)(2,1)} %slice_bitcast_fusion.32), channel_id=1, source_target_pairs={{0,2},{1,3},{2,0},{3,1},{4,6},{5,7},{6,4},{7,5},{8,10},{9,11},{10,... | collective-permute-start | bytes 497672 | tf_op jit(solution)/shard_map/ppermute | solution.py:473
  581.2 33.2 %collective-permute-start.81 = (bf16[72,1152]{1,0:T(8,128)(2,1)}, bf16[72,1152]{1,0:T(8,128)(2,1)}, u32[]{:S(2)}, u32[]{:S(2)}) collective-permute-start(bf16[72,1152]{1,0:T(8,128)(2,1)} %get-tuple-element.159), channel_id=1, source_target_pairs={{0,4},{1,5},{2,6},{3,7},{4,0},{5,1},{6,2},{7,3},{8,12},{9,13},{10,... | collective-permute-start | bytes 497672 | tf_op jit(solution)/shard_map/ppermute | solution.py:473
  581.8 32.7 %collective-permute-start.82 = (bf16[72,1152]{1,0:T(8,128)(2,1)}, bf16[72,1152]{1,0:T(8,128)(2,1)}, u32[]{:S(2)}, u32[]{:S(2)}) collective-permute-start(bf16[72,1152]{1,0:T(8,128)(2,1)} %get-tuple-element.160), channel_id=1, source_target_pairs={{0,6},{1,7},{2,4},{3,5},{4,2},{5,3},{6,0},{7,1},{8,14},{9,15},{10,... | collective-permute-start | bytes 497672 | tf_op jit(solution)/shard_map/ppermute | solution.py:473
  (131 other events, 1344.5 us)

commit v4 on v3

v4 whole, which is shorter than its diff:
```python
from functools import partial

import jax
import jax.numpy as jnp
from jax import lax
from jax.experimental import pallas as pl
from jax.experimental.pallas import tpu as pltpu
from jax.sharding import PartitionSpec as P

HEAD_DIM = 72
norm_eps = 1e-06
masked_score = -1000000000.0
low = jnp.bfloat16
wide = jnp.float32
score_scale = HEAD_DIM**-0.5
log2_e = 1.4426950408889634
gelu_scale = 0.7978845608028654
gelu_cube = 0.044715
everyone = ("dp", "tensor")


def product(left, right, left_dim, right_dim):
    return lax.dot_general(
        left, right, (((left_dim,), (right_dim,)), ((), ())), preferred_element_type=wide
    )


def attend_kernel(heads, query_ref, key_ref, value_ref, bias_ref, out_ref, total_ref):
    for head in range(heads):
        rows = slice(head * HEAD_DIM, (head + 1) * HEAD_DIM)
        scores = product(key_ref[rows, :], query_ref[rows, :], 0, 0) * (score_scale * log2_e)
        scores = scores + bias_ref[...]
        top = jnp.max(scores, axis=0, keepdims=True)
        weights = jnp.exp2(scores - top)
        total = jnp.sum(weights, axis=0, keepdims=True)
        mixed = product(value_ref[rows, :], weights.astype(low), 1, 0)
        out_ref[rows, :] = (mixed * (1.0 / total)).astype(low)
        total_ref[head] = top + jnp.log2(total)


def attend_back_kernel(
    heads,
    query_ref,
    key_ref,
    value_ref,
    bias_ref,
    out_ref,
    total_ref,
    weights_ref,
    branch_ref,
    grads_ref,
):
    grad_rows = product(weights_ref[...], branch_ref[...], 1, 1).astype(low)
    for head in range(heads):
        rows = slice(head * HEAD_DIM, (head + 1) * HEAD_DIM)
        query, key, value, grad = (
            query_ref[rows, :],
            key_ref[rows, :],
            value_ref[rows, :],
            grad_rows[rows, :],
        )
        scores = product(key, query, 0, 0) * (score_scale * log2_e) + bias_ref[...]
        probs = jnp.exp2(scores - total_ref[head])
        grad_probs = product(value, grad, 0, 0)
        along = jnp.sum(
            grad.astype(wide) * out_ref[rows, :].astype(wide), axis=0, keepdims=True
        )
        grad_raw = (probs * (grad_probs - along)).astype(low)
        grads_ref[2, rows, :] = product(grad, probs.astype(low), 1, 1).astype(low)
        grads_ref[0, rows, :] = (product(key, grad_raw, 1, 0) * score_scale).astype(low)
        grads_ref[1, rows, :] = (product(query, grad_raw, 1, 1) * score_scale).astype(low)


def attend(projected, bias, heads, step_heads):
    tokens = projected.shape[1]
    steps = heads // step_heads
    part = lambda place: pl.BlockSpec(
        (HEAD_DIM * step_heads, tokens), lambda i, place=place: (place * steps + i, 0)
    )
    return pl.pallas_call(
        partial(attend_kernel, step_heads),
        grid=(steps,),
        in_specs=[part(0), part(1), part(2), pl.BlockSpec((tokens, 1), lambda i: (0, 0))],
        out_specs=[part(0), pl.BlockSpec((step_heads, 1, tokens), lambda i: (i, 0, 0))],
        out_shape=[
            jax.ShapeDtypeStruct((heads * HEAD_DIM, tokens), low),
            jax.ShapeDtypeStruct((heads, 1, tokens), wide),
        ],
        compiler_params=pltpu.CompilerParams(vmem_limit_bytes=48 * 2**20),
        cost_estimate=pl.CostEstimate(
            flops=heads * tokens * tokens * 128, bytes_accessed=2**20, transcendentals=0
        ),
        name="attend",
    )(projected, projected, projected, bias)


def attend_back(projected, bias, attended, total, weights, branch, heads, step_heads):
    tokens = projected.shape[1]
    steps = heads // step_heads
    part = lambda place: pl.BlockSpec(
        (HEAD_DIM * step_heads, tokens), lambda i, place=place: (place * steps + i, 0)
    )
    return pl.pallas_call(
        partial(attend_back_kernel, step_heads),
        grid=(steps,),
        in_specs=[
            part(0),
            part(1),
            part(2),
            pl.BlockSpec((tokens, 1), lambda i: (0, 0)),
            part(0),
            pl.BlockSpec((step_heads, 1, tokens), lambda i: (i, 0, 0)),
            pl.BlockSpec((HEAD_DIM * step_heads, branch.shape[1]), lambda i: (3 * steps + i, 0)),
            pl.BlockSpec(branch.shape, lambda i: (0, 0)),
        ],
        out_specs=pl.BlockSpec((3, HEAD_DIM * step_heads, tokens), lambda i: (0, i, 0)),
        out_shape=jax.ShapeDtypeStruct((3, heads * HEAD_DIM, tokens), low),
        compiler_params=pltpu.CompilerParams(vmem_limit_bytes=48 * 2**20),
        cost_estimate=pl.CostEstimate(
            flops=heads * tokens * tokens * 128, bytes_accessed=2**20, transcendentals=0
        ),
        name="attend_back",
    )(projected, projected, projected, bias, attended, total, weights, branch)


def norm_forward(values, gain, shift):
    row_mean = jnp.mean(values, axis=-1, keepdims=True)
    centred = values - row_mean
    inv_scale = lax.rsqrt(jnp.mean(centred * centred, axis=-1, keepdims=True) + norm_eps)
    return (centred * inv_scale * gain + shift).astype(low)


def norm_back_kernel(values_ref, grad_ref, gain_ref, base_ref, full_ref, low_ref, sums_ref):
    values = values_ref[...].astype(wide)
    centred = values - jnp.mean(values, axis=-1, keepdims=True)
    inv_scale = lax.rsqrt(jnp.mean(centred * centred, axis=-1, keepdims=True) + norm_eps)
    unit = centred * inv_scale
    grad = grad_ref[...]
    scaled = grad * gain_ref[...]
    mean_grad = jnp.mean(scaled, axis=-1, keepdims=True)
    mean_along = jnp.mean(scaled * unit, axis=-1, keepdims=True)
    base = base_ref[...].astype(wide)
    full = base + inv_scale * (scaled - mean_grad - unit * mean_along)
    rounded = full.astype(low)
    full_ref[...] = full
    low_ref[...] = rounded
    total = lambda rows: jnp.sum(rows, axis=0, keepdims=True)
    sums = jnp.concatenate(
        [total(grad * unit), total(grad), total(rounded.astype(wide)), total(base)], axis=0
    )

    @pl.when(pl.program_id(0) == 0)
    def first():
        sums_ref[...] = sums

    @pl.when(pl.program_id(0) > 0)
    def later():
        sums_ref[...] += sums


def norm_back(values, grad, gain, base):
    tokens, width = values.shape
    block = tokens // 4
    rows = pl.BlockSpec((block, width), lambda i: (i, 0))
    return pl.pallas_call(
        norm_back_kernel,
        grid=(4,),
        in_specs=[rows, rows, pl.BlockSpec((1, width), lambda i: (0, 0)), rows],
        out_specs=[rows, rows, pl.BlockSpec((4, width), lambda i: (0, 0))],
        out_shape=[
            jax.ShapeDtypeStruct((tokens, width), wide),
            jax.ShapeDtypeStruct((tokens, width), low),
            jax.ShapeDtypeStruct((4, width), wide),
        ],
        compiler_params=pltpu.CompilerParams(vmem_limit_bytes=40 * 2**20),
        cost_estimate=pl.CostEstimate(
            flops=tokens * width, bytes_accessed=tokens * width, transcendentals=0
        ),
        name="norm_back",
    )(values, grad, gain.reshape(1, width), base)


def mlp_kernel(carried, plan, normed_ref, grad_ref, bias_ref, *refs):
    starts, rows, group, pieces = plan
    weights, refs = refs[:pieces], refs[pieces:]
    steps = 32 // group
    if carried:
        out_before, normed_before = refs[:2]
        refs = refs[2:]
    out_ref, grad_normed_ref, *grad_refs, grad_bias_ref, ups, downs, sems = refs
    step = pl.program_id(0)
    slot = step % 2

    def copies(at):
        moves = []
        many = group if pieces == 1 else 2
        size = group // many * rows
        for place in range(many):
            block = weights[0].at[at * many + place] if pieces == 1 else weights[2 * at + place]
            for kind, target in enumerate((ups, downs)):
                moves.append(
                    pltpu.make_async_copy(
                        block.at[pl.ds(starts[kind], size)],
                        target.at[at % 2, pl.ds(place * size, size)],
                        sems.at[at % 2, 2 * place + kind],
                    )
                )
        return moves

    for at in range(steps):

        @pl.when(step + 1 == at if at else step == 0)
        def fetch():
            for move in copies(at):
                move.start()

    for at in range(steps):

        @pl.when(step == at)
        def arrive():
            for move in copies(at):
                move.wait()

    normed, grad = normed_ref[...], grad_ref[...]
    up, down = ups[slot], downs[slot]
    pre_act = product(up, normed, 1, 1) + bias_ref[...]
    square = pre_act * pre_act
    bent = jnp.tanh(gelu_scale * (pre_act + gelu_cube * square * pre_act))
    half = 0.5 * (1.0 + bent)
    active = (pre_act * half).astype(low)
    slope = half + 0.5 * pre_act * (1.0 - bent * bent) * (
        gelu_scale * (1.0 + 3.0 * gelu_cube * square)
    )
    grad_wide = product(down, grad, 1, 1) * slope
    grad_pre = grad_wide.astype(low)
    grad_bias_ref[...] = jnp.sum(grad_wide, axis=1, keepdims=True)
    grad_down = product(active, grad, 1, 0).astype(low)
    grad_up = product(grad_pre, normed, 1, 0).astype(low)

    def keep(ref):
        many = ref.shape[2]
        for place in range(ref.shape[0]):
            ref[place, 0] = grad_up[place * many : (place + 1) * many]
            ref[place, 1] = grad_down[place * many : (place + 1) * many]

    if pieces == 1:
        keep(grad_refs[0])
    else:
        pl.when(step < 2)(lambda: keep(grad_refs[0]))
        pl.when(step >= 2)(lambda: keep(grad_refs[1]))
    out_term = product(active, down, 0, 0)
    normed_term = product(grad_pre, up, 0, 0)

    @pl.when(step == 0)
    def first():
        if carried:
            out_ref[...] = out_before[...] + out_term
            grad_normed_ref[...] = normed_before[...] + normed_term
        else:
            out_ref[...] = out_term
            grad_normed_ref[...] = normed_term

    @pl.when(step > 0)
    def later():
        out_ref[...] += out_term
        grad_normed_ref[...] += normed_term


def mlp(normed, grad, bias, weights, starts, rows, group=8, before=None):
    tokens, width = normed.shape
    steps = 32 // group
    whole = pl.BlockSpec((tokens, width), lambda i: (0, 0))
    column = pl.BlockSpec((group * rows, 1), lambda i: (i, 0))
    if len(weights) == 1:
        grad_specs = [pl.BlockSpec((group, 2, rows, width), lambda i: (i, 0, 0, 0))]
        grad_shapes = [jax.ShapeDtypeStruct((32, 2, rows, width), low)]
    else:
        part = (2, 2, 4 * rows, width)
        grad_specs = [
            pl.BlockSpec(part, lambda i: (jnp.minimum(i, 1), 0, 0, 0)),
            pl.BlockSpec(part, lambda i: (jnp.maximum(i - 2, 0), 0, 0, 0)),
        ]
        grad_shapes = [jax.ShapeDtypeStruct((4, 2, 4 * rows, width), low)] * 2
    earlier = [] if before is None else list(before)
    return pl.pallas_call(
        partial(mlp_kernel, before is not None, (starts, rows, group, len(weights))),
        grid=(steps,),
        in_specs=[whole, whole, column]
        + [pl.BlockSpec(memory_space=pl.ANY)] * len(weights)
        + [whole] * len(earlier),
        out_specs=[whole, whole] + grad_specs + [column],
        out_shape=[jax.ShapeDtypeStruct((tokens, width), wide)] * 2
        + grad_shapes
        + [jax.ShapeDtypeStruct((32 * rows, 1), wide)],
        scratch_shapes=[
            pltpu.VMEM((2, group * rows, width), low),
            pltpu.VMEM((2, group * rows, width), low),
            pltpu.SemaphoreType.DMA((2, 2 * group)),
        ],
        input_output_aliases=(
            {3 + len(weights): 0, 4 + len(weights): 1} if earlier else {}
        ),
        compiler_params=pltpu.CompilerParams(vmem_limit_bytes=60 * 2**20),
        cost_estimate=pl.CostEstimate(
            flops=2 * tokens * width * 32 * rows, bytes_accessed=2**20, transcendentals=0
        ),
        name="mlp",
    )(normed, grad, bias, *weights, *earlier)


def kinds_kernel(slabs, kind_ref, grads_ref, attended_ref, normed_ref, branch_ref, *outs):
    kind = pl.program_id(0)
    held = outs[8]
    rows = held.shape[0] // slabs

    own = ((kind ^ kind_ref[0]) & 1) == 0

    def keep(terms):
        def block(spot):
            slab = spot
            if slabs == 8:
                away = (spot >> 2) * 4 + (spot & 1) * 2 + ((spot >> 1) & 1)
                slab = away ^ kind_ref[1]
            start = pl.multiple_of(slab * rows, 16)
            return held[pl.ds(start, rows), :]

        held[...] = terms
        across = (kind ^ kind_ref[0]) >> 1
        many = slabs // 4 if slabs > 1 else 1

        def put(near, near_y, far, far_x):
            for place in range(many):
                near[0, place] = block(place)
                near_y[0, place] = block(many + place)
            for place in range(2 * many):

                @pl.when(across == 0)
                def same():
                    far[place] = block(2 * many + place)

                @pl.when(across == 1)
                def other():
                    far_x[place] = block(2 * many + place)

        pl.when(own)(lambda: put(*outs[:4]))
        pl.when(jnp.logical_not(own))(lambda: put(*outs[4:8]))

    @pl.when(kind < 3)
    def projections():
        keep(product(grads_ref[0], normed_ref[...], 1, 0).astype(low))

    @pl.when(kind == 3)
    def output():
        keep(product(attended_ref[...], branch_ref[...], 1, 0).astype(low))


def kinds_grad(places, grads, attended, normed, branch, slabs):
    _, rows, tokens = grads.shape
    width = normed.shape[1]
    whole = pl.BlockSpec((tokens, width), lambda k, ref: (0, 0))
    many, each = slabs // 4, rows // slabs
    near = pl.BlockSpec((1, many, each, width), lambda k, ref: ((k ^ ref[0]) >> 1, 0, 0, 0))
    far = pl.BlockSpec((2 * many, each, width), lambda k, ref: (0, 0, 0))
    near_shape = jax.ShapeDtypeStruct((2, many, each, width), low)
    far_shape = jax.ShapeDtypeStruct((2 * many, each, width), low)
    return pl.pallas_call(
        partial(kinds_kernel, slabs),
        grid_spec=pltpu.PrefetchScalarGridSpec(
            num_scalar_prefetch=1,
            grid=(4,),
            in_specs=[
                pl.BlockSpec((1, rows, tokens), lambda k, ref: (jnp.minimum(k, 2), 0, 0)),
                pl.BlockSpec((rows, tokens), lambda k, ref: (0, 0)),
                whole,
                whole,
            ],
            out_specs=[near, near, far, far] * 2,
            scratch_shapes=[pltpu.VMEM((rows, width), low)],
        ),
        out_shape=[near_shape, near_shape, far_shape, far_shape] * 2,
        compiler_params=pltpu.CompilerParams(vmem_limit_bytes=48 * 2**20),
        cost_estimate=pl.CostEstimate(
            flops=rows * width * tokens, bytes_accessed=2**20, transcendentals=0
        ),
        name="kinds_grad",
    )(places, grads, attended, normed, branch)


def unite_kernel(kind_ref, *refs):
    outs = refs[4:]
    part = refs[0].shape[1]
    for distance in range(4):
        source = kind_ref[0] ^ distance
        for column in range(4):

            @pl.when(source == column)
            def put():
                start = 0
                for out in outs:
                    rows = out.shape[0]
                    out[:, column * part : (column + 1) * part] = refs[distance][
                        start : start + rows, :
                    ]
                    start += rows


def unite(kind, blocks, cuts):
    part = blocks[0].shape[1]
    local = pl.BlockSpec(memory_space=pltpu.VMEM)
    return pl.pallas_call(
        unite_kernel,
        in_specs=[pl.BlockSpec(memory_space=pltpu.SMEM)] + [local] * 4,
        out_specs=[local] * len(cuts),
        out_shape=[jax.ShapeDtypeStruct((rows, 4 * part), low) for rows in cuts],
        name="unite",
    )(kind, *blocks)


def divide_kernel(kind_ref, *refs):
    ins, outs = refs[:-4], refs[-4:]
    part = outs[0].shape[1]
    for distance in range(4):
        target = kind_ref[0] ^ distance
        for column in range(4):

            @pl.when(target == column)
            def put():
                start = 0
                for ref in ins:
                    rows = ref.shape[0]
                    outs[distance][start : start + rows, :] = ref[
                        :, column * part : (column + 1) * part
                    ]
                    start += rows


def divide(kind, owned):
    rows = sum(values.shape[0] for values in owned)
    part = owned[0].shape[1] // 4
    local = pl.BlockSpec(memory_space=pltpu.VMEM)
    return pl.pallas_call(
        divide_kernel,
        in_specs=[pl.BlockSpec(memory_space=pltpu.SMEM)] + [local] * len(owned),
        out_specs=[local] * 4,
        out_shape=[jax.ShapeDtypeStruct((rows, part), low)] * 4,
        name="divide",
    )(kind, *owned)


def settle_kernel(kind_ref, *refs):
    for distance in range(4):
        refs[4][kind_ref[0] ^ distance] = refs[distance][...].astype(wide)


def settle(kind, blocks):
    rows, part = blocks[0].shape
    local = pl.BlockSpec(memory_space=pltpu.VMEM)
    return pl.pallas_call(
        settle_kernel,
        in_specs=[pl.BlockSpec(memory_space=pltpu.SMEM)] + [local] * 4,
        out_specs=local,
        out_shape=jax.ShapeDtypeStruct((4, rows, part), wide),
        name="settle",
    )(kind, *blocks)


def after(values, *earlier):
    return lax.optimization_barrier((values, earlier))[0]


def add_low(*terms):
    total = terms[0].astype(wide)
    for term in terms[1:]:
        total = total + term.astype(wide)
    return total.astype(low)


def join(kinds, *blocks):
    width = blocks[0].shape[-1]
    parts = [block.reshape(kinds, -1, width) for block in blocks]
    return jnp.concatenate(parts, axis=1).reshape(-1, width)


class Hops:
    def __init__(self, dp_count, tensor_count):
        self.count = dp_count * tensor_count
        self.y, self.z = 1, (2, 4, 6)
        self.core, self.x = tensor_count, 2 * tensor_count
        self.near, self.far = (0, 2), (4, 6)

    def send(self, values, distance):
        pairs = [(place, place ^ distance) for place in range(self.count)]
        return lax.ppermute(values, everyone, pairs)

    def order(self):
        x, y = self.x, self.y
        near = [n ^ p ^ q for q in (0, y) for p in (0, x) for n in self.near]
        far = [n ^ p ^ q for q in (0, x) for p in (0, y) for n in self.far]
        return near + far

    def along_z(self, block):
        return [self.send(block, z) for z in self.z]

    def second_operands(self, kinds, block, arrived):
        z1, z2, z3 = arrived
        return join(kinds, block, z1), join(kinds, z2, z3)

    def sibling(self, *pieces):
        return [self.send(piece, self.core) for piece in pieces]

    def across_dp(self, blocks):
        return [blocks[0]] + [self.send(blocks[j], j * self.core) for j in (1, 2, 3)]


class Reduction:
    def __init__(self, hops, own, sibling, joined):
        self.hops, self.own, self.joined = hops, own, joined
        if joined:
            self.arrived = hops.send(sibling, hops.core)
        else:
            self.arrived = [hops.send(piece, hops.core) for piece in sibling]
        self.width = own[0].shape[-1]

    def part(self, place):
        return self.own[place], self.arrived[place]

    def halves(self, values):
        axis = 1 if self.joined else 0
        shape = (2, 2, 2, -1, self.width) if self.joined else (2, 2, -1, self.width)
        values = values.reshape(shape)
        return [lax.index_in_dim(values, place, axis, keepdims=False) for place in (0, 1)]

    def blocks(self, values):
        axis = 1 if self.joined else 0
        return [lax.index_in_dim(values, place, axis, keepdims=False) for place in (0, 1)]

    def ready_third(self):
        self.operands = add_low(*self.part(1)), add_low(*self.part(3))
        return self.operands

    def send_third(self):
        near, far = self.operands
        self.moved = self.hops.send(near, self.hops.y), self.hops.send(far, self.hops.x)

    def third(self):
        near, far = self.moved
        near, far = add_low(*self.part(0), near), add_low(*self.part(2), far)
        self.near, self.far = self.halves(near), self.halves(far)
        self.operands = self.near[1], self.far[1]
        return self.operands

    def send_second(self):
        near, far = self.operands
        self.moved = self.hops.send(near, self.hops.x), self.hops.send(far, self.hops.y)

    def second(self):
        near, far = self.moved
        near, far = add_low(self.near[0], near), add_low(self.far[0], far)
        self.near, self.far = self.blocks(near), self.blocks(far)
        self.operands = self.near[1], self.far[0], self.far[1]
        return self.operands

    def send_along_z(self):
        self.moved = [
            self.hops.send(v, z) for v, z in zip(self.operands, self.hops.z, strict=True)
        ]

    def along_z(self):
        return add_low(self.near[0], *self.moved)


def shards(
    dp_count,
    tensor_count,
    inputs,
    pad_mask,
    cotangent,
    attn_norm_gain,
    attn_norm_shift,
    w_query,
    b_query,
    w_key,
    w_value,
    b_value,
    w_out,
    b_out,
    mlp_norm_gain,
    mlp_norm_shift,
    w_up,
    b_up,
    w_down,
    b_down,
):
    half_rows, width = inputs.shape[1:]
    tokens = 2 * half_rows
    head_cols = w_query.shape[1]
    unit_cols = w_up.shape[1]
    quantum = 8 * dp_count
    slab_units = -(-unit_cols // quantum) * quantum
    by_hops = (dp_count, tensor_count) == (4, 8)
    dp_place, tensor_place = lax.axis_index("dp"), lax.axis_index("tensor")
    devices = dp_count * tensor_count
    here = (dp_place * tensor_count + tensor_place).astype(jnp.int32)
    col_start = tensor_place * head_cols
    side = tensor_place % 2
    pairs = [(place, place ^ 1) for place in range(tensor_count)]
    hops = Hops(dp_count, tensor_count)
    places = jnp.stack([dp_place, tensor_place]).astype(jnp.int32)
    places = places if by_hops else places * 0
    kind = places[:1]
    heads = head_cols * tensor_count // HEAD_DIM

    def swap(values):
        return lax.ppermute(values, "tensor", pairs)

    def one_slot(values, *earlier):
        kept = lax.dynamic_index_in_dim(values, side, 0, keepdims=False)
        sent = lax.dynamic_index_in_dim(values, 1 - side, 0, keepdims=False)
        if earlier:
            sent = after(sent, *earlier)
        return jnp.concatenate([kept, swap(sent)], axis=0)

    def both_micros(kept, other):
        return jnp.where(side == 0, jnp.stack([kept, other]), jnp.stack([other, kept]))

    unit_pad = ((0, slab_units - unit_cols), (0, 0))
    up_cols, down_cols = jnp.pad(w_up.T, unit_pad), jnp.pad(w_down, unit_pad)
    attn_cols = jnp.concatenate([w_query.T, w_key.T, w_value.T, w_out], axis=0)
    if by_hops:
        unit_cuts = (48, slab_units // 4 - 48)
        first_units = 4 * unit_cuts[0]
        share = lambda values, low_end, high_end: values[low_end:high_end].reshape(
            4, -1, values.shape[1]
        )
        mlp_cols = jnp.concatenate(
            [
                share(up_cols, 0, first_units),
                share(down_cols, 0, first_units),
                share(up_cols, first_units, slab_units),
                share(down_cols, first_units, slab_units),
            ],
            axis=1,
        )
        attn_cols = attn_cols.reshape(4, head_cols, -1)
        pick = lambda values, j: lax.dynamic_index_in_dim(
            values, dp_place ^ j, 0, keepdims=False
        )
        attn_blocks = hops.across_dp([pick(attn_cols, j) for j in range(4)])
        (attn_block,) = unite(kind, attn_blocks, (head_cols,))
        mlp_blocks = hops.across_dp([pick(mlp_cols, j) for j in range(4)])
        bulk_block, hop_block = unite(kind, mlp_blocks, [2 * rows for rows in unit_cuts])
        attn_rows = lax.all_gather(attn_block, everyone).reshape(4, -1, width)
        x_slot = one_slot(inputs)
        grad_out = one_slot(cotangent, x_slot)
        bulk_weights = lax.all_gather(bulk_block, everyone)
        hop_z = hops.along_z(hop_block)
        order = hops.order()
        order = [place ^ hops.core for place in order] + order
        unit_places = here ^ jnp.array(order)
        unit_here = (unit_places[:, None] == jnp.arange(devices)[None, :]).astype(wide)
        shuffled = partial(jnp.dot, precision=lax.Precision.HIGHEST)
    else:
        x_slot, grad_out = one_slot(inputs), one_slot(cotangent)
        unit_cuts = (slab_units // dp_count,)

        def gathered(values):
            owned = lax.all_to_all(
                values.reshape(dp_count, -1, values.shape[1]), "dp", 0, 2, tiled=True
            )
            return lax.all_gather(owned[0], everyone, axis=0, tiled=True)

        attn_rows = gathered(attn_cols)
        attn_rows = attn_rows.reshape(4, dp_count // 4, tensor_count, -1, width)
        attn_rows = attn_rows.transpose(0, 2, 1, 3, 4).reshape(4, -1, width)
        columns = [values.reshape(dp_count, -1, values.shape[1]) for values in (up_cols, down_cols)]
        unit_weights = gathered(jnp.concatenate(columns, axis=1).reshape(2 * slab_units, -1))
        unit_weights = unit_weights.reshape(32, devices // 32, 2, -1, width)
        bulk_weights = unit_weights.transpose(0, 2, 1, 3, 4).reshape(32, -1, width)

    slab_bias = jnp.pad(
        b_up.reshape(tensor_count, unit_cols), ((0, 0), (0, slab_units - unit_cols))
    )
    unit_starts = [dp_count * sum(unit_cuts[:i]) for i in range(len(unit_cuts) + 1)]

    def unit_bias(part):
        values = slab_bias[:, unit_starts[part] : unit_starts[part + 1]]
        values = values.reshape(tensor_count, dp_count, -1).transpose(1, 0, 2)
        if part == 1:
            values = shuffled(unit_here, values.reshape(devices, -1))
        return values.reshape(-1, 1)

    def unit_grads(values):
        slabs = []
        for place, part in enumerate(values):
            if place == 1:
                part = shuffled(unit_here.T, part.reshape(devices, -1))
            part = part.reshape(dp_count, tensor_count, -1).transpose(1, 0, 2)
            slabs.append(part.reshape(tensor_count, -1))
        return jnp.concatenate(slabs, axis=1)

    mask_row = lax.dynamic_slice(pad_mask, (side, tensor_place // 2, 0), (1, 1, tokens))
    mask_row = mask_row.reshape(2, half_rows)
    mask_row = jnp.where(side == 0, mask_row, mask_row[::-1]).reshape(tokens, 1)
    bias_col = jnp.where(mask_row > 0, 0.0, masked_score).astype(wide)

    normed_first = norm_forward(x_slot.astype(wide), attn_norm_gain, attn_norm_shift)
    qkv_rows, out_rows = attn_rows[:3].reshape(-1, width), attn_rows[3]
    qkv_bias = jnp.concatenate([b_query, jnp.zeros_like(b_query), b_value])
    projected = (product(qkv_rows, normed_first, 1, 1) + qkv_bias[:, None]).astype(low)
    if by_hops:
        hop_z = after(hop_z, grad_out, normed_first)
    if by_hops:
        hop_near, hop_far = hops.second_operands(2, hop_block, hop_z)
        near_x, far_y = hops.send(hop_near, hops.x), hops.send(hop_far, hops.y)
        near_x, far_y = after((near_x, far_y))
        hop_near, hop_far = join(2, hop_near, near_x), join(2, hop_far, far_y)
        attended, totals = attend(projected, bias_col, heads, 4)
        near_y, far_x = hops.send(hop_near, hops.y), hops.send(hop_far, hops.x)
        near_y, far_x = after((near_y, far_x), attended)
        hop_three = [hop_near, near_y, hop_far, far_x]
        hop_weights = hops.sibling(*hop_three) + list(hop_three)
    else:
        attended, totals = attend(projected, bias_col, heads, 4)
    branch = product(attended, out_rows, 0, 0) + b_out
    middle = x_slot.astype(wide) + branch
    normed_second = norm_forward(middle, mlp_norm_gain, mlp_norm_shift)
    rows = unit_cuts[0] * devices // 32
    sums, up_sums = None, []
    if by_hops:
        *sums, grad_sibling, grad_own, up_sum = mlp(
            normed_second,
            grad_out,
            unit_bias(1),
            hop_weights,
            (0, 4 * unit_cuts[1]),
            unit_cuts[1],
        )
        up_sums.append(up_sum[:, 0])
    bulk = partial(
        mlp,
        normed_second,
        grad_out,
        unit_bias(0),
        [bulk_weights],
        (0, rows),
        rows,
        16 if by_hops else 4,
    )
    if by_hops:
        units = Reduction(hops, grad_own, grad_sibling, True)
        sums = after(sums, units.ready_third())
        units.send_third()
        *sums, bulk_grads, up_sum = bulk(sums)
    else:
        *sums, bulk_grads, up_sum = bulk()
    up_sums = [up_sum[:, 0]] + up_sums
    bulk_grads = bulk_grads.reshape(32, 2, devices // 32, -1, width).transpose(0, 2, 1, 3, 4)
    bulk_owned = lax.psum_scatter(
        bulk_grads.reshape(2 * 32 * rows, width), everyone, scatter_dimension=0, tiled=True
    )
    down_out, grad_normed_second = sums
    if by_hops:
        units_third = units.third()
        grad_normed_second = after(grad_normed_second, units_third)
    grad_middle, grad_branch, second_sums = norm_back(
        middle, grad_normed_second, mlp_norm_gain, grad_out
    )
    out_low = (middle + (down_out + b_down)).astype(low)
    back = partial(
        attend_back, projected, bias_col, attended, totals, attn_rows.reshape(-1, width)
    )
    if by_hops:
        units.send_second()
        out_other = swap(after(out_low[half_rows:], units_third))
        grads = back(grad_branch, heads, 4)
        grads, out_other = after((grads, out_other), units.second())
        layer_out = both_micros(out_low[:half_rows], out_other)
        units.send_along_z()
        kind_grads = kinds_grad(
            places, grads, attended, normed_first, grad_branch, tensor_count
        )
        attns = Reduction(hops, kind_grads[:4], kind_grads[4:], False)
        grads = after(grads, kind_grads)
        first_terms = product(grads.reshape(-1, tokens), qkv_rows, 0, 0)
        units.moved = after(units.moved, first_terms)
        first_terms = after(first_terms, attns.ready_third())
        attns.send_third()
        input_full, input_low, first_sums = norm_back(
            x_slot, first_terms, attn_norm_gain, grad_middle
        )
        units_owned = units.along_z()
        attns.moved = after(attns.moved, units_owned)
        attns_third = attns.third()
    else:
        grads = back(grad_branch, heads, 4)
        first_terms = product(grads.reshape(-1, tokens), qkv_rows, 0, 0)
        input_full, input_low, first_sums = norm_back(
            x_slot, first_terms, attn_norm_gain, grad_middle
        )
        out_other = swap(out_low[half_rows:])
        layer_out = both_micros(out_low[:half_rows], out_other)

    total_over = lambda i: jnp.sum(grads[i], axis=1, dtype=wide)
    small = jnp.concatenate(
        [
            second_sums.reshape(-1),
            first_sums[:2].reshape(-1),
            total_over(0),
            total_over(2),
            unit_grads(up_sums).reshape(-1),
        ]
    )
    if by_hops:
        small, mlp_owned = after(
            (small.reshape(-1, 128), [bulk_owned, units_owned[0], units_owned[1]]), attns_third
        )
        attns.send_second()
        small = small + sum(hops.send(small, z) for z in hops.z)
        mlp_parts = divide(kind, mlp_owned)
        attns.moved = after(attns.moved, small, mlp_parts)
        attns_second = attns.second()
        attns.send_along_z()
        small, input_low, mlp_parts = after((small, input_low, mlp_parts), attns_second)
        input_other = swap(input_low[half_rows:])
        mlp_blocks = hops.across_dp(mlp_parts)
        mlp_back = settle(kind, mlp_blocks)
        attns.moved = after(attns.moved, mlp_back, input_other)
        small = after(small, attns.moved)
        small = small + hops.send(small, hops.y)
        small = small + sum(hops.send(small, j * hops.core) for j in (1, 2, 3))
        attn_parts = divide(kind, [attns.along_z()])
        attn_back = settle(kind, hops.across_dp(attn_parts))
        small = small.reshape(-1)
    else:
        small = lax.psum(small, everyone)
        input_other = swap(input_low[half_rows:])
    input_grad = both_micros(input_full[:half_rows], input_other.astype(wide))

    if by_hops:
        bounds = [0]
        for rows in (unit_cuts[0], unit_cuts[0], unit_cuts[1], unit_cuts[1]):
            bounds.append(bounds[-1] + rows)
        parts = [
            mlp_back[:, bounds[i] : bounds[i + 1]].reshape(-1, mlp_back.shape[2])
            for i in range(4)
        ]
        grad_w_up = jnp.concatenate([parts[0], parts[2]], axis=0)
        grad_w_down = jnp.concatenate([parts[1], parts[3]], axis=0)
    else:

        def to_columns(owned):
            back = lax.all_to_all(owned[None], "dp", 2, 0, tiled=True)
            return back.reshape(-1, width // dp_count).astype(wide)

        columns = to_columns(bulk_owned)
        columns = columns.reshape(dp_count, 2, -1, columns.shape[1])
        grad_w_up = columns[:, 0].reshape(-1, columns.shape[3])
        grad_w_down = columns[:, 1].reshape(-1, columns.shape[3])
        flat = grads.reshape(-1, tokens)
        terms = [product(flat, normed_first, 1, 0), product(attended, grad_branch, 1, 0)]
        terms = jnp.concatenate(terms, axis=0).astype(low)
        terms = terms.reshape(4, tensor_count, dp_count // 4, -1, width)
        terms = terms.transpose(0, 2, 1, 3, 4).reshape(-1, width)
        owned = lax.psum_scatter(terms, everyone, scatter_dimension=0, tiled=True)
        attn_back = to_columns(owned).reshape(4, head_cols, -1)

    part = lambda i: small[i * width : (i + 1) * width]
    up_all = small[8 * width :].reshape(tensor_count, slab_units)
    return (
        layer_out,
        input_grad,
        part(4),
        part(5),
        attn_back[0].T,
        lax.dynamic_slice_in_dim(part(6), col_start, head_cols),
        attn_back[1].T,
        attn_back[2].T,
        lax.dynamic_slice_in_dim(part(7), col_start, head_cols),
        attn_back[3],
        part(2),
        part(0),
        part(1),
        grad_w_up[:unit_cols].T,
        up_all[:, :unit_cols].reshape(-1),
        grad_w_down[:unit_cols],
        part(3),
    )


def solution(mesh):
    tokens = P(None, ("dp", "tensor"), None)
    columns = P("dp", "tensor")
    rows = P("tensor", "dp")
    return jax.shard_map(
        partial(shards, mesh.shape["dp"], mesh.shape["tensor"]),
        mesh=mesh,
        in_specs=(
            tokens,
            P(None, "dp", None),
            tokens,
            P(),
            P(),
            columns,
            P(),
            columns,
            columns,
            P(),
            rows,
            P(),
            P(),
            P(),
            columns,
            P(),
            rows,
            P(),
        ),
        out_specs=(
            tokens,
            tokens,
            P(),
            P(),
            columns,
            P("tensor"),
            columns,
            columns,
            P("tensor"),
            rows,
            P(),
            P(),
            P(),
            columns,
            P(),
            rows,
            P(),
        ),
        check_vma=False,
    )
```

time: 649 us -> 532 us (0.82)
  starting transfers between devices: 105 us -> 49.4 us
  other arithmetic: 90.4 us -> 62.8 us
  waiting for transfers between devices: 172 us -> 148 us
  local copies, waits for them, and re-layouts: 71.6 us -> 55.7 us
  between operations: 2.6 us -> 14.9 us
  matrix products: 36.9 us -> 26.9 us
    ppermute x98 -> x49, starting transfers between devices: 102 us -> 43.7 us  [send(): return lax.ppermute(values, everyone, pairs)]
    ppermute x98 -> x49, waiting for transfers between devices: 158 us -> 118 us  [send(): return lax.ppermute(values, everyone, pairs)]
    convert_element_type x24 -> x12, other arithmetic: 43 us -> 28.8 us  [add_low(): return total.astype(low)]
    dot_general x8 -> x3, matrix products: 36.9 us -> 26.5 us  [product(): lax.dot_general(left, right, (((left_dim,), (right_dim,)), ((), ())), pre...]
    ppermute x4, waiting for transfers between devices: 14.2 us -> 23 us  [swap(): return lax.ppermute(values, 'tensor', pairs)]
    concatenate x8 -> x4, other arithmetic: 14.4 us -> 6.97 us  [join(): return jnp.concatenate(parts, axis=1).reshape(-1, width)]
    all_gather x0 -> x2, waiting for transfers between devices: none -> 6.84 us  [the longest x1 6.83 us: shards(): attn_rows = lax.all_gather(attn_block, everyone).reshape(4, -1, width)]
    gather x10 -> x0, local copies, waits for them, and re-layouts: 6.63 us -> none  [the longest x4 2.47 us: head_bias(): return blocks[head_places].reshape(-1)]
  transfers between devices with their start and end apart: 102 -> 56, of which waited for: 36 -> 19; matrix products, arithmetic and copies ran while one was open for 27% -> 23% of each run, Pallas kernels for 23% -> 31%
where the time goes in v4:
time: 532 us; the launch traced here: 521 us
  Pallas kernels  163 us (31%)
  waiting for transfers between devices  148 us (28%)
  other arithmetic  62.8 us (12%)
  local copies, waits for them, and re-layouts  55.7 us (10%)
  starting transfers between devices  49.4 us (9%)
  matrix products  26.9 us (5%)
  between operations  14.9 us (3%)
    ppermute x49, waiting for transfers between devices, send(): return lax.ppermute(values, everyone, pairs)  118 us
    pallas_call x2, Pallas kernels, mlp(): pl.pallas_call(partial(mlp_kernel, before is not None, (starts, rows, gro...  81.1 us
    ppermute x49, starting transfers between devices, send(): return lax.ppermute(values, everyone, pairs)  43.7 us
    convert_element_type x12, other arithmetic, add_low(): return total.astype(low)  28.8 us
    pallas_call x1, Pallas kernels, attend_back(): pl.pallas_call(partial(attend_back_kernel, step_heads), grid=(steps,), in...  28.6 us
    dot_general x3, matrix products, product(): lax.dot_general(left, right, (((left_dim,), (right_dim,)), ((), ())), pre...  26.5 us
    ppermute x4, waiting for transfers between devices, swap(): return lax.ppermute(values, 'tensor', pairs)  23 us
    unnamed x136, local copies, waits for them, and re-layouts  20.8 us
  transfers between devices with their start and end apart: 56, of which 19 were waited for; matrix products, arithmetic and copies ran while one was open for 23% of the time, Pallas kernels for 31%

profile of v4, /device:TPU:0, one launch (start us, length us, event | category | flops | bytes accessed | tf_op | source)
XLA Modules:
  0.0 521.3 jit_solution(9250339061879657761)
XLA Ops:
  9.7 2.5 collective-permute-start.2
  12.3 3.8 collective-permute-done.2.refs_2_
  16.1 2.0 collective-permute-done.3.refs_3_
  18.7 2.2 unite.2
  28.9 4.8 collective-permute-done.6.refs_2_
  33.6 6.1 %collective-permute-done.7.refs_3_ = bf16[272,288]{1,0:T(8,128)(2,1)} collective-permute-done((bf16[272,288]{1,0:T(8,128)(2,1)}, bf16[272,288]{1,0:T(8,128)(2,1)}, u32[]{:S(2)}, u32[]{:S(2)}) %collective-permute-start.7) | collective-permute-done | bytes 156704 | tf_op jit(solution)/shard_map/ppermute | solution.py:493
  39.7 2.6 unite.3
  42.3 3.6 collective-permute-start.10
  50.3 23.0 %collective-permute-done.4 = bf16[368,1152]{1,0:T(8,128)(2,1)S(1)} collective-permute-done((bf16[368,1152]{1,0:T(8,128)(2,1)S(1)}, bf16[368,1152]{1,0:T(8,128)(2,1)S(1)}, u32[]{:S(2)}, u32[]{:S(2)}) %collective-permute-start.4) | collective-permute-done | bytes 847904 | tf_op jit(solution)/shard_map/ppermute | solution.py:614
  74.7 21.0 %collective-permute-done.9 = bf16[176,1152]{1,0:T(8,128)(2,1)S(1)} collective-permute-done((bf16[176,1152]{1,0:T(8,128)(2,1)}, bf16[176,1152]{1,0:T(8,128)(2,1)S(1)}, u32[]{:S(2)}, u32[]{:S(2)}) %collective-permute-start.9) | collective-permute-done | bytes 405536 | tf_op jit(solution)/shard_map/ppermute | solution.py:493
  102.5 32.4 %collective-permute-done.12 = bf16[352,1152]{1,0:T(8,128)(2,1)} collective-permute-done((bf16[352,1152]{1,0:T(8,128)(2,1)}, bf16[352,1152]{1,0:T(8,128)(2,1)}, u32[]{:S(2)}, u32[]{:S(2)}) %collective-permute-start.12) | collective-permute-done | bytes 811040 | tf_op jit(solution)/shard_map/ppermute | solution.py:493
  135.4 2.5 pad_maximum_fusion.3
  138.9 2.4 pad_maximum_fusion.2
  142.7 6.8 %all-gather.5.cloned.1.call-done.weights_ref = bf16[4608,1152]{1,0:T(8,128)(2,1)} async-done(((bf16[144,1152]{1,0:T(8,128)(2,1)}), bf16[4608,1152]{1,0:T(8,128)(2,1)}) %all-gather.5.cloned.1.call-update) | async-done | bytes 10616848 | tf_op jit(solution)/shard_map/all_gather | solution.py:652
  149.5 11.2 %add_convert_fusion.query_ref.key_ref.value_ref = bf16[3456,736]{1,0:T(8,128)(2,1)} fusion(bf16[736,1152]{1,0:T(8,128)(2,1)S(1)} %fusion.11.normed_ref, bf16[4608,1152]{1,0:T(8,128)(2,1)} %all-gather.5.cloned.1.call-done.weights_ref, f32[3456]{0:T(1024)S(1)} %pad_maximum_fusion.11), kind=kOutput, calls=%fused_computation | convolution fusion | flops 5865578496 | bytes 14759424 | tf_op jit(solution)/shard_map/dot_general | solution.py:23
  160.7 15.3 %attend.1 = (bf16[1152,736]{1,0:T(8,128)(2,1)S(1)}, f32[16,1,736]{2,1,0:T(1,128)S(1)}) custom-call(bf16[3456,736]{1,0:T(8,128)(2,1)} %add_convert_fusion.query_ref.key_ref.value_ref, bf16[3456,736]{1,0:T(8,128)(2,1)} %add_convert_fusion.query_ref.key_ref.value_ref, bf16[3456,736]{1,0:T(8,128)(2,1)} %add_convert_fusion.query_ref.key_ref.value_ref, ...), custom_call_target="tpu_custom_call" | custom-call | flops 1109393408 | bytes 1048576 | tf_op jit(solution)/shard_map/attend/pallas_call | solution.py:80
  176.9 4.2 collective-permute-done.14.refs_5_
  181.6 4.8 fusion.39
  187.1 1.8 add_convert_fusion.2.normed_ref
  188.9 49.4 %mlp.2 = (f32[736,1152]{1,0:T(8,128)}, f32[736,1152]{1,0:T(8,128)}, bf16[4,2,352,1152]{3,2,1,0:T(8,128)(2,1)}, bf16[4,2,352,1152]{3,2,1,0:T(8,128)(2,1)}, f32[2816,1]{1,0:T(8,128)}) custom-call(bf16[736,1152]{1,0:T(8,128)(2,1)} %add_convert_fusion.2.normed_ref, bf16[736,1152]{1,0:T(8,128)(2,1)} %pad_maximum_fusion.1.grad_ref.base_ref, ...), custom_call_target="tpu_custom_call" | custom-call | flops 4775215104 | bytes 1048576 | tf_op jit(solution)/shard_map/mlp/pallas_call | solution.py:285
  238.4 10.6 %collective-permute-done.19 = bf16[4,2,352,1152]{3,2,1,0:T(8,128)(2,1)S(1)} collective-permute-done((bf16[4,2,352,1152]{3,2,1,0:T(8,128)(2,1)}, bf16[4,2,352,1152]{3,2,1,0:T(8,128)(2,1)S(1)}, u32[]{:S(2)}, u32[]{:S(2)}) %collective-permute-start.19) | collective-permute-done | bytes 6488096 | tf_op jit(solution)/shard_map/ppermute | solution.py:493
  249.0 6.7 %fusion.16 = (bf16[2,352,1152]{2,1,0:T(8,128)(2,1)}, bf16[2,352,1152]{2,1,0:T(8,128)(2,1)}) fusion(bf16[4,2,352,1152]{3,2,1,0:T(8,128)(2,1)S(1)} %collective-permute-done.19, bf16[4,2,352,1152]{3,2,1,0:T(8,128)(2,1)} %get-tuple-element.102), kind=kLoop, calls=%fused_computation.37 | loop fusion | flops 6488064 | bytes 9732096 | tf_op jit(solution)/shard_map/convert_element_type | solution.py:475
  259.9 1.8 reduce.4
  262.1 31.6 %mlp.3 = (f32[736,1152]{1,0:T(8,128)}, f32[736,1152]{1,0:T(8,128)}, bf16[32,2,48,1152]{3,2,1,0:T(8,128)(2,1)}, f32[1536,1]{1,0:T(8,128)}) custom-call(bf16[736,1152]{1,0:T(8,128)(2,1)} %add_convert_fusion.2.normed_ref, bf16[736,1152]{1,0:T(8,128)(2,1)} %pad_maximum_fusion.1.grad_ref.base_ref, ...), custom_call_target="tpu_custom_call", output_to_operand_aliasing={{0}: (4, {}), {1}: (5, {})} | custom-call | flops 2604662784 | bytes 1048576 | tf_op jit(solution)/shard_map/mlp/pallas_call | solution.py:285
  296.1 3.6 add_convert_fusion.1
  299.7 5.3 %fusion.12 = (bf16[2,352,1152]{2,1,0:T(8,128)(2,1)S(1)}, bf16[2,352,1152]{2,1,0:T(8,128)(2,1)S(1)}) fusion(bf16[2,352,1152]{2,1,0:T(8,128)(2,1)} %collective-permute-done.21, bf16[4,2,352,1152]{3,2,1,0:T(8,128)(2,1)} %copy-done.22, bf16[4,2,352,1152]{3,2,1,0:T(8,128)(2,1)} %get-tuple-element.102, bf16[2,352,1152]{2,1,0:T(8,128)(2,1)} %collective-permute-done.20), kind=kLoop, calls=%fused_computation.22 | loop fusion | flops 9732096 | bytes 12976128 | tf_op jit(solution)/shard_map/convert_element_type | solution.py:475
  308.9 3.0 slice_bitcast_fusion.1
  313.9 2.1 copy-done.3
  316.0 3.8 norm_back.2
  321.0 1.7 copy-done.11
  326.8 28.6 %attend_back.1.grads_ref = bf16[3,1152,736]{2,1,0:T(8,128)(2,1)} custom-call(bf16[3456,736]{1,0:T(8,128)(2,1)} %add_convert_fusion.query_ref.key_ref.value_ref, bf16[3456,736]{1,0:T(8,128)(2,1)} %add_convert_fusion.query_ref.key_ref.value_ref, bf16[3456,736]{1,0:T(8,128)(2,1)} %add_convert_fusion.query_ref.key_ref.value_ref, f32[736,1]{1,0:T(8,128)S(1)} %copy-done.10, ...), custom_call_target="tpu_custom_call" | custom-call | flops 1109393408 | bytes 1048576 | tf_op jit(solution)/shard_map/attend_back/pallas_call | solution.py:103
  359.5 2.4 collective-permute-start.29
  363.8 17.3 %kinds_grad.1 = (bf16[2,2,144,1152]{3,2,1,0:T(8,128)(2,1)S(1)}, bf16[2,2,144,1152]{3,2,1,0:T(8,128)(2,1)S(1)}, bf16[4,144,1152]{2,1,0:T(8,128)(2,1)S(1)}, bf16[4...) custom-call(s32[2]{0:T(128)S(1)} %pad_add_fusion.kind_ref, ...), custom_call_target="tpu_custom_call" | custom-call | flops 976748544 | bytes 1048576 | tf_op jit(solution)/shard_map/kinds_grad/pallas_call | solution.py:366
  381.6 10.6 %fusion.2.grad_ref = f32[736,1152]{1,0:T(8,128)S(1)} fusion(bf16[3456,736]{1,0:T(8,128)(2,1)S(1)} %bitcast.169, bf16[4608,1152]{1,0:T(8,128)(2,1)} %all-gather.5.cloned.1.call-done.weights_ref), kind=kOutput, calls=%fused_computation.3 | convolution fusion | flops 5860491264 | bytes 16441344 | tf_op jit(solution)/shard_map/dot_general | solution.py:23
  398.6 1.8 fusion.22
  401.2 3.3 norm_back.3
  404.4 1.7 copy-done.13
  410.0 20.2 %collective-permute-done.32 = bf16[4,144,1152]{2,1,0:T(8,128)(2,1)} collective-permute-done((bf16[4,144,1152]{2,1,0:T(8,128)(2,1)}, bf16[4,144,1152]{2,1,0:T(8,128)(2,1)}, u32[]{:S(2)}, u32[]{:S(2)}) %collective-permute-start.32) | collective-permute-done | bytes 1327136 | tf_op jit(solution)/shard_map/ppermute | solution.py:493
  430.2 5.2 collective-permute-done.31
  435.4 2.3 add_convert_fusion.5
  439.0 2.2 add_convert_fusion.6
  442.2 1.7 collective-permute-start.37
  446.8 1.8 collective-permute-start.35
  450.2 3.1 maximum_select_fusion.1
  453.2 2.7 divide.2
  456.9 1.7 collective-permute-done.37
  463.1 1.8 collective-permute-start.44
  466.0 1.7 collective-permute-start.39
  467.8 2.1 collective-permute-start.41
  469.9 2.2 collective-permute-start.42
  475.4 2.5 settle.2
  477.9 2.1 fusion.36
  480.0 1.8 fusion.35
  481.8 2.0 copy.85
  483.8 1.8 copy.84
  487.4 2.2 pad_maximum_fusion.7
  489.6 2.0 fusion.23
  491.7 2.3 collective-permute-done.41
  494.5 2.1 fusion.26.refs_0_
  496.5 2.1 divide.3
  502.9 2.0 maximum_select_fusion
  505.0 1.8 collective-permute-start.48
  507.5 2.0 settle.3
  509.6 2.2 slice_bitcast_fusion.12
  (314 shorter events, 90.7 us)
Async XLA Ops:
  7.2 142.3 %all-gather.5.cloned.1.call-start = ((), (), s32[]{:S(2)}) async-start(), calls=%async_computation.2 | async-start | bytes 10948608 | tf_op jit(solution)/shard_map/all_gather | solution.py:652
  9.2 3.1 collective-permute-start.1
  9.7 6.4 %collective-permute-start.2 = (bf16[144,288]{1,0:T(8,128)(2,1)S(1)}, bf16[144,288]{1,0:T(8,128)(2,1)S(1)}, u32[]{:S(2)}, u32[]{:S(2)}) collective-permute-start(bf16[144,288]{1,0:T(8,128)(2,1)S(1)} %get-tuple-element.194), channel_id=1, source_target_pairs={{0,16},{1,17},{2,18},{3,19},{4,20},{5,21},{6,22},{7,23},{8,24},{9,... | collective-permute-start | bytes 248840 | tf_op jit(solution)/shard_map/ppermute | solution.py:493
  12.2 5.9 %collective-permute-start.3 = (bf16[144,288]{1,0:T(8,128)(2,1)S(1)}, bf16[144,288]{1,0:T(8,128)(2,1)S(1)}, u32[]{:S(2)}, u32[]{:S(2)}) collective-permute-start(bf16[144,288]{1,0:T(8,128)(2,1)S(1)} %get-tuple-element.193), channel_id=1, source_target_pairs={{0,24},{1,25},{2,26},{3,27},{4,28},{5,29},{6,30},{7,31},{8,16},{9,... | collective-permute-start | bytes 248840 | tf_op jit(solution)/shard_map/ppermute | solution.py:493
  20.9 241.2 %all-gather.7.cloned.1.call-start = ((), (), s32[]{:S(2)}) async-start(), calls=%async_computation.3 | async-start | bytes 7299072 | tf_op jit(solution)/shard_map/all_gather | solution.py:655
  22.1 27.5 %copy-start.17 = (bf16[368,1152]{1,0:T(8,128)(2,1)}, bf16[368,1152]{1,0:T(8,128)(2,1)S(1)}, u32[]{:S(2)}) copy-start(bf16[368,1152]{1,0:T(8,128)(2,1)S(1)} %get-tuple-element.171) | copy-start | bytes 2543620
  22.1 24.6 %collective-permute-start = (bf16[368,1152]{1,0:T(8,128)(2,1)}, bf16[368,1152]{1,0:T(8,128)(2,1)S(1)}, u32[]{:S(2)}, u32[]{:S(2)}) collective-permute-start(bf16[368,1152]{1,0:T(8,128)(2,1)} %get-tuple-element.172), channel_id=1, source_target_pairs={{0,1},{1,0},{2,3},{3,2},{4,5},{5,4},{6,7},{7,6},{8,9},{9,8},{10,11... | collective-permute-start | bytes 2543624 | tf_op jit(solution)/shard_map/ppermute | solution.py:614
  25.4 3.5 collective-permute-start.5
  25.4 8.3 %collective-permute-start.6 = (bf16[272,288]{1,0:T(8,128)(2,1)}, bf16[272,288]{1,0:T(8,128)(2,1)}, u32[]{:S(2)}, u32[]{:S(2)}) collective-permute-start(bf16[272,288]{1,0:T(8,128)(2,1)} %get-tuple-element.186), channel_id=1, source_target_pairs={{0,16},{1,17},{2,18},{3,19},{4,20},{5,21},{6,22},{7,23},{8,24},{9,... | collective-permute-start | bytes 470024 | tf_op jit(solution)/shard_map/ppermute | solution.py:493
  26.8 12.9 %collective-permute-start.7 = (bf16[272,288]{1,0:T(8,128)(2,1)}, bf16[272,288]{1,0:T(8,128)(2,1)}, u32[]{:S(2)}, u32[]{:S(2)}) collective-permute-start(bf16[272,288]{1,0:T(8,128)(2,1)} %get-tuple-element.185), channel_id=1, source_target_pairs={{0,24},{1,25},{2,26},{3,27},{4,28},{5,29},{6,30},{7,31},{8,16},{9,... | collective-permute-start | bytes 470024 | tf_op jit(solution)/shard_map/ppermute | solution.py:493
  42.3 32.4 %collective-permute-start.10 = (bf16[176,1152]{1,0:T(8,128)(2,1)}, bf16[176,1152]{1,0:T(8,128)(2,1)S(1)}, u32[]{:S(2)}, u32[]{:S(2)}) collective-permute-start(bf16[176,1152]{1,0:T(8,128)(2,1)} %get-tuple-element.92), channel_id=1, source_target_pairs={{0,6},{1,7},{2,4},{3,5},{4,2},{5,3},{6,0},{7,1},{8,14},{9,15},{10,... | collective-permute-start | bytes 1216520 | tf_op jit(solution)/shard_map/ppermute | solution.py:493
  45.9 28.8 %collective-permute-start.8 = (bf16[176,1152]{1,0:T(8,128)(2,1)}, bf16[176,1152]{1,0:T(8,128)(2,1)S(1)}, u32[]{:S(2)}, u32[]{:S(2)}) collective-permute-start(bf16[176,1152]{1,0:T(8,128)(2,1)} %get-tuple-element.92), channel_id=1, source_target_pairs={{0,2},{1,3},{2,0},{3,1},{4,6},{5,7},{6,4},{7,5},{8,10},{9,11},{10,... | collective-permute-start | bytes 1216520 | tf_op jit(solution)/shard_map/ppermute | solution.py:493
  45.9 49.9 %collective-permute-start.9 = (bf16[176,1152]{1,0:T(8,128)(2,1)}, bf16[176,1152]{1,0:T(8,128)(2,1)S(1)}, u32[]{:S(2)}, u32[]{:S(2)}) collective-permute-start(bf16[176,1152]{1,0:T(8,128)(2,1)} %get-tuple-element.92), channel_id=1, source_target_pairs={{0,4},{1,5},{2,6},{3,7},{4,0},{5,1},{6,2},{7,3},{8,12},{9,13},{10,... | collective-permute-start | bytes 1216520 | tf_op jit(solution)/shard_map/ppermute | solution.py:493
  48.1 25.2 %collective-permute-start.4 = (bf16[368,1152]{1,0:T(8,128)(2,1)S(1)}, bf16[368,1152]{1,0:T(8,128)(2,1)S(1)}, u32[]{:S(2)}, u32[]{:S(2)}) collective-permute-start(bf16[368,1152]{1,0:T(8,128)(2,1)S(1)} %copy-done.38), channel_id=1, source_target_pairs={{0,1},{1,0},{2,3},{3,2},{4,5},{5,4},{6,7},{7,6},{8,9},{9,8},{10,11... | collective-permute-start | bytes 2543624 | tf_op jit(solution)/shard_map/ppermute | solution.py:614
  50.3 99.2 %copy-start.21 = (bf16[736,1152]{1,0:T(8,128)(2,1)}, bf16[736,1152]{1,0:T(8,128)(2,1)S(1)}, u32[]{:S(2)}) copy-start(bf16[736,1152]{1,0:T(8,128)(2,1)S(1)} %fusion.11.normed_ref) | copy-start | bytes 5087236
  73.3 24.3 %copy-start.32 = (bf16[176,1152]{1,0:T(8,128)(2,1)S(1)}, bf16[176,1152]{1,0:T(8,128)(2,1)}, u32[]{:S(2)}) copy-start(bf16[176,1152]{1,0:T(8,128)(2,1)} %get-tuple-element.92) | copy-start | bytes 1216516
  74.7 23.9 %copy-start.35 = (bf16[176,1152]{1,0:T(8,128)(2,1)}, bf16[176,1152]{1,0:T(8,128)(2,1)S(1)}, u32[]{:S(2)}) copy-start(bf16[176,1152]{1,0:T(8,128)(2,1)S(1)} %collective-permute-done.10) | copy-start | bytes 1216516
  96.8 38.0 %collective-permute-start.12 = (bf16[352,1152]{1,0:T(8,128)(2,1)}, bf16[352,1152]{1,0:T(8,128)(2,1)}, u32[]{:S(2)}, u32[]{:S(2)}) collective-permute-start(bf16[352,1152]{1,0:T(8,128)(2,1)} %bitcast.31), channel_id=1, source_target_pairs={{0,1},{1,0},{2,3},{3,2},{4,5},{5,4},{6,7},{7,6},{8,9},{9,8},{10,11... | collective-permute-start | bytes 2433032 | tf_op jit(solution)/shard_map/ppermute | solution.py:493
  98.6 36.9 %copy-start.36 = (bf16[176,1152]{1,0:T(8,128)(2,1)S(1)}, bf16[176,1152]{1,0:T(8,128)(2,1)}, u32[]{:S(2)}) copy-start(bf16[176,1152]{1,0:T(8,128)(2,1)} %copy-done.35) | copy-start | bytes 1216516
  98.6 36.9 %collective-permute-start.11 = (bf16[352,1152]{1,0:T(8,128)(2,1)}, bf16[352,1152]{1,0:T(8,128)(2,1)}, u32[]{:S(2)}, u32[]{:S(2)}) collective-permute-start(bf16[352,1152]{1,0:T(8,128)(2,1)} %bitcast.28), channel_id=1, source_target_pairs={{0,16},{1,17},{2,18},{3,19},{4,20},{5,21},{6,22},{7,23},{8,24},{9,... | collective-permute-start | bytes 2433032 | tf_op jit(solution)/shard_map/ppermute | solution.py:493
  99.8 346.0 %reduce-scatter.2.cloned.1.call-start = ((), (), s32[]{:S(2)}) async-start(), calls=%async_computation.1 | async-start | bytes 7299072 | tf_op jit(solution)/shard_map/reduce_scatter | solution.py:758
  100.6 60.0 %copy-start.9 = (f32[736,1]{1,0:T(8,128)}, f32[736,1]{1,0:T(8,128)S(1)}, u32[]{:S(2)}) copy-start(f32[736,1]{1,0:T(8,128)S(1)} %select_n.91.bias_ref) | copy-start | bytes 8836
  102.5 36.4 %copy-start.34 = (bf16[176,1152]{1,0:T(8,128)(2,1)S(1)}, bf16[176,1152]{1,0:T(8,128)(2,1)}, u32[]{:S(2)}) copy-start(bf16[176,1152]{1,0:T(8,128)(2,1)} %copy-done.33) | copy-start | bytes 1216516
  138.0 38.9 %collective-permute-start.15 = (bf16[704,1152]{1,0:T(8,128)(2,1)}, bf16[704,1152]{1,0:T(8,128)(2,1)}, u32[]{:S(2)}, u32[]{:S(2)}) collective-permute-start(bf16[704,1152]{1,0:T(8,128)(2,1)} %bitcast.35.refs_6_), channel_id=1, source_target_pairs={{0,16},{1,17},{2,18},{3,19},{4,20},{5,21},{6,22},{7,23},{8,24},{9,... | collective-permute-start | bytes 4866056 | tf_op jit(solution)/shard_map/ppermute | solution.py:493
  138.9 50.0 %collective-permute-start.17 = (bf16[704,1152]{1,0:T(8,128)(2,1)}, bf16[704,1152]{1,0:T(8,128)(2,1)}, u32[]{:S(2)}, u32[]{:S(2)}) collective-permute-start(bf16[704,1152]{1,0:T(8,128)(2,1)} %bitcast.35.refs_6_), channel_id=1, source_target_pairs={{0,8},{1,9},{2,10},{3,11},{4,12},{5,13},{6,14},{7,15},{8,0},{9,1},... | collective-permute-start | bytes 4866056 | tf_op jit(solution)/shard_map/ppermute | solution.py:493
  141.3 39.8 %collective-permute-start.14 = (bf16[704,1152]{1,0:T(8,128)(2,1)}, bf16[704,1152]{1,0:T(8,128)(2,1)}, u32[]{:S(2)}, u32[]{:S(2)}) collective-permute-start(bf16[704,1152]{1,0:T(8,128)(2,1)} %bitcast.33.refs_4_), channel_id=1, source_target_pairs={{0,1},{1,0},{2,3},{3,2},{4,5},{5,4},{6,7},{7,6},{8,9},{9,8},{10,11... | collective-permute-start | bytes 4866056 | tf_op jit(solution)/shard_map/ppermute | solution.py:493
  142.4 46.4 %collective-permute-start.13 = (bf16[704,1152]{1,0:T(8,128)(2,1)}, bf16[704,1152]{1,0:T(8,128)(2,1)}, u32[]{:S(2)}, u32[]{:S(2)}) collective-permute-start(bf16[704,1152]{1,0:T(8,128)(2,1)} %bitcast.33.refs_4_), channel_id=1, source_target_pairs={{0,8},{1,9},{2,10},{3,11},{4,12},{5,13},{6,14},{7,15},{8,0},{9,1},... | collective-permute-start | bytes 4866056 | tf_op jit(solution)/shard_map/ppermute | solution.py:493
  181.1 7.8 %collective-permute-start.16 = (bf16[704,1152]{1,0:T(8,128)(2,1)}, bf16[704,1152]{1,0:T(8,128)(2,1)}, u32[]{:S(2)}, u32[]{:S(2)}) collective-permute-start(bf16[704,1152]{1,0:T(8,128)(2,1)} %collective-permute-done.14.refs_5_), channel_id=1, source_target_pairs={{0,8},{1,9},{2,10},{3,11},{4,12},{5,13},{6,14},{7,15},{8,0},{9,1},... | collective-permute-start | bytes 4866056 | tf_op jit(solution)/shard_map/ppermute | solution.py:493
  181.1 7.8 %collective-permute-start.18 = (bf16[704,1152]{1,0:T(8,128)(2,1)}, bf16[704,1152]{1,0:T(8,128)(2,1)}, u32[]{:S(2)}, u32[]{:S(2)}) collective-permute-start(bf16[704,1152]{1,0:T(8,128)(2,1)} %collective-permute-done.15.refs_7_), channel_id=1, source_target_pairs={{0,8},{1,9},{2,10},{3,11},{4,12},{5,13},{6,14},{7,15},{8,0},{9,1},... | collective-permute-start | bytes 4866056 | tf_op jit(solution)/shard_map/ppermute | solution.py:493
  238.3 10.7 %collective-permute-start.19 = (bf16[4,2,352,1152]{3,2,1,0:T(8,128)(2,1)}, bf16[4,2,352,1152]{3,2,1,0:T(8,128)(2,1)S(1)}, u32[]{:S(2)}, u32[]{:S(2)}) collective-permute-start(bf16[4,2,352,1152]{3,2,1,0:T(8,128)(2,1)} %get-tuple-element.103), channel_id=1, source_target_pairs={{0,8},{1,9},{2,10},{3,11},{4,12},{5,13},{6,14},{7,15},{8,0},{9,1},... | collective-permute-start | bytes 19464200 | tf_op jit(solution)/shard_map/ppermute | solution.py:493
  255.7 44.0 %collective-permute-start.20 = (bf16[2,352,1152]{2,1,0:T(8,128)(2,1)}, bf16[2,352,1152]{2,1,0:T(8,128)(2,1)}, u32[]{:S(2)}, u32[]{:S(2)}) collective-permute-start(bf16[2,352,1152]{2,1,0:T(8,128)(2,1)} %get-tuple-element.166), channel_id=1, source_target_pairs={{0,1},{1,0},{2,3},{3,2},{4,5},{5,4},{6,7},{7,6},{8,9},{9,8},{10,11... | collective-permute-start | bytes 4866056 | tf_op jit(solution)/shard_map/ppermute | solution.py:493
  256.9 42.8 %collective-permute-start.21 = (bf16[2,352,1152]{2,1,0:T(8,128)(2,1)}, bf16[2,352,1152]{2,1,0:T(8,128)(2,1)}, u32[]{:S(2)}, u32[]{:S(2)}) collective-permute-start(bf16[2,352,1152]{2,1,0:T(8,128)(2,1)} %get-tuple-element.165), channel_id=1, source_target_pairs={{0,16},{1,17},{2,18},{3,19},{4,20},{5,21},{6,22},{7,23},{8,24},{9,... | collective-permute-start | bytes 4866056 | tf_op jit(solution)/shard_map/ppermute | solution.py:493
  308.3 48.4 %collective-permute-start.24 = (bf16[2,2,88,1152]{3,2,0,1:T(8,128)(2,1)}, bf16[2,2,88,1152]{3,2,0,1:T(8,128)(2,1)}, u32[]{:S(2)}, u32[]{:S(2)}) collective-permute-start(bf16[2,2,88,1152]{3,2,0,1:T(8,128)(2,1)} %get-tuple-element.209), channel_id=1, source_target_pairs={{0,1},{1,0},{2,3},{3,2},{4,5},{5,4},{6,7},{7,6},{8,9},{9,8},{10,11... | collective-permute-start | bytes 2433032 | tf_op jit(solution)/shard_map/ppermute | solution.py:493
  311.9 50.0 %collective-permute-start.23 = (bf16[2,2,88,1152]{3,2,0,1:T(8,128)(2,1)}, bf16[2,2,88,1152]{3,2,0,1:T(8,128)(2,1)}, u32[]{:S(2)}, u32[]{:S(2)}) collective-permute-start(bf16[2,2,88,1152]{3,2,0,1:T(8,128)(2,1)} %get-tuple-element.210), channel_id=1, source_target_pairs={{0,16},{1,17},{2,18},{3,19},{4,20},{5,21},{6,22},{7,23},{8,24},{9,... | collective-permute-start | bytes 2433032 | tf_op jit(solution)/shard_map/ppermute | solution.py:493
  312.7 51.1 %collective-permute-start.22 = (bf16[368,1152]{1,0:T(8,128)(2,1)}, bf16[368,1152]{1,0:T(8,128)(2,1)}, u32[]{:S(2)}, u32[]{:S(2)}) collective-permute-start(bf16[368,1152]{1,0:T(8,128)(2,1)} %get-tuple-element.111), channel_id=1, source_target_pairs={{0,1},{1,0},{2,3},{3,2},{4,5},{5,4},{6,7},{7,6},{8,9},{9,8},{10,11... | collective-permute-start | bytes 2543624 | tf_op jit(solution)/shard_map/ppermute | solution.py:614
  326.8 30.0 %copy-start.28 = (bf16[2,1,2,88,1152]{4,3,2,1,0:T(8,128)(2,1)S(1)}, bf16[2,1,2,88,1152]{4,3,2,1,0:T(8,128)(2,1)}, u32[]{:S(2)}) copy-start(bf16[2,1,2,88,1152]{4,3,2,1,0:T(8,128)(2,1)} %get-tuple-element.177) | copy-start | bytes 2433028
  358.2 38.7 %collective-permute-start.28 = (bf16[2,88,1152]{2,1,0:T(8,128)(2,1)S(1)}, bf16[2,88,1152]{2,1,0:T(8,128)(2,1)}, u32[]{:S(2)}, u32[]{:S(2)}) collective-permute-start(bf16[2,88,1152]{2,1,0:T(8,128)(2,1)S(1)} %get-tuple-element.190), channel_id=1, source_target_pairs={{0,4},{1,5},{2,6},{3,7},{4,0},{5,1},{6,2},{7,3},{8,12},{9,13},{10,... | collective-permute-start | bytes 1216520 | tf_op jit(solution)/shard_map/ppermute | solution.py:493
  359.5 39.0 %collective-permute-start.29 = (bf16[2,88,1152]{2,1,0:T(8,128)(2,1)S(1)}, bf16[2,88,1152]{2,1,0:T(8,128)(2,1)}, u32[]{:S(2)}, u32[]{:S(2)}) collective-permute-start(bf16[2,88,1152]{2,1,0:T(8,128)(2,1)S(1)} %get-tuple-element.189), channel_id=1, source_target_pairs={{0,6},{1,7},{2,4},{3,5},{4,2},{5,3},{6,0},{7,1},{8,14},{9,15},{10,... | collective-permute-start | bytes 1216520 | tf_op jit(solution)/shard_map/ppermute | solution.py:493
  363.3 35.3 %collective-permute-start.27 = (bf16[2,88,1152]{2,1,0:T(8,128)(2,1)S(1)}, bf16[2,88,1152]{2,1,0:T(8,128)(2,1)}, u32[]{:S(2)}, u32[]{:S(2)}) collective-permute-start(bf16[2,88,1152]{2,1,0:T(8,128)(2,1)S(1)} %slice_bitcast_fusion.7), channel_id=1, source_target_pairs={{0,2},{1,3},{2,0},{3,1},{4,6},{5,7},{6,4},{7,5},{8,10},{9,11},{10,... | collective-permute-start | bytes 1216520 | tf_op jit(solution)/shard_map/ppermute | solution.py:493
  381.1 11.2 %collective-permute-start.26 = (bf16[4,144,1152]{2,1,0:T(8,128)(2,1)}, bf16[4,144,1152]{2,1,0:T(8,128)(2,1)S(1)}, u32[]{:S(2)}, u32[]{:S(2)}) collective-permute-start(bf16[4,144,1152]{2,1,0:T(8,128)(2,1)} %get-tuple-element.121), channel_id=1, source_target_pairs={{0,8},{1,9},{2,10},{3,11},{4,12},{5,13},{6,14},{7,15},{8,0},{9,1},... | collective-permute-start | bytes 3981320 | tf_op jit(solution)/shard_map/ppermute | solution.py:493
  381.1 12.7 %collective-permute-start.25 = (bf16[2,2,144,1152]{3,2,1,0:T(8,128)(2,1)}, bf16[2,2,144,1152]{3,2,1,0:T(8,128)(2,1)S(1)}, u32[]{:S(2)}, u32[]{:S(2)}) collective-permute-start(bf16[2,2,144,1152]{3,2,1,0:T(8,128)(2,1)} %get-tuple-element.119), channel_id=1, source_target_pairs={{0,8},{1,9},{2,10},{3,11},{4,12},{5,13},{6,14},{7,15},{8,0},{9,1},... | collective-permute-start | bytes 3981320 | tf_op jit(solution)/shard_map/ppermute | solution.py:493
  392.3 43.1 %collective-permute-start.33 = (bf16[4,144,1152]{2,1,0:T(8,128)(2,1)}, bf16[4,144,1152]{2,1,0:T(8,128)(2,1)}, u32[]{:S(2)}, u32[]{:S(2)}) collective-permute-start(bf16[4,144,1152]{2,1,0:T(8,128)(2,1)} %get-tuple-element.120), channel_id=1, source_target_pairs={{0,8},{1,9},{2,10},{3,11},{4,12},{5,13},{6,14},{7,15},{8,0},{9,1},... | collective-permute-start | bytes 3981320 | tf_op jit(solution)/shard_map/ppermute | solution.py:493
  393.9 36.3 %collective-permute-start.32 = (bf16[4,144,1152]{2,1,0:T(8,128)(2,1)}, bf16[4,144,1152]{2,1,0:T(8,128)(2,1)}, u32[]{:S(2)}, u32[]{:S(2)}) collective-permute-start(bf16[4,144,1152]{2,1,0:T(8,128)(2,1)} %add_convert_fusion.7), channel_id=1, source_target_pairs={{0,16},{1,17},{2,18},{3,19},{4,20},{5,21},{6,22},{7,23},{8,24},{9,... | collective-permute-start | bytes 3981320 | tf_op jit(solution)/shard_map/ppermute | solution.py:493
  396.9 38.4 %collective-permute-start.31 = (bf16[2,2,144,1152]{3,2,1,0:T(8,128)(2,1)}, bf16[2,2,144,1152]{3,2,1,0:T(8,128)(2,1)}, u32[]{:S(2)}, u32[]{:S(2)}) collective-permute-start(bf16[2,2,144,1152]{3,2,1,0:T(8,128)(2,1)} %add_convert_fusion.8), channel_id=1, source_target_pairs={{0,1},{1,0},{2,3},{3,2},{4,5},{5,4},{6,7},{7,6},{8,9},{9,8},{10,11... | collective-permute-start | bytes 3981320 | tf_op jit(solution)/shard_map/ppermute | solution.py:493
  398.5 40.6 %collective-permute-start.30 = (bf16[2,2,144,1152]{3,2,1,0:T(8,128)(2,1)}, bf16[2,2,144,1152]{3,2,1,0:T(8,128)(2,1)}, u32[]{:S(2)}, u32[]{:S(2)}) collective-permute-start(bf16[2,2,144,1152]{3,2,1,0:T(8,128)(2,1)} %get-tuple-element.118), channel_id=1, source_target_pairs={{0,8},{1,9},{2,10},{3,11},{4,12},{5,13},{6,14},{7,15},{8,0},{9,1},... | collective-permute-start | bytes 3981320 | tf_op jit(solution)/shard_map/ppermute | solution.py:493
  438.7 18.2 %collective-permute-start.38 = (bf16[2,144,1152]{2,1,0:T(8,128)(2,1)}, bf16[2,144,1152]{2,1,0:T(8,128)(2,1)}, u32[]{:S(2)}, u32[]{:S(2)}) collective-permute-start(bf16[2,144,1152]{2,1,0:T(8,128)(2,1)} %slice.308), channel_id=1, source_target_pairs={{0,1},{1,0},{2,3},{3,2},{4,5},{5,4},{6,7},{7,6},{8,9},{9,8},{10,11... | collective-permute-start | bytes 1990664 | tf_op jit(solution)/shard_map/ppermute | solution.py:493
  442.2 16.4 %collective-permute-start.37 = (bf16[2,144,1152]{2,1,0:T(8,128)(2,1)}, bf16[2,144,1152]{2,1,0:T(8,128)(2,1)}, u32[]{:S(2)}, u32[]{:S(2)}) collective-permute-start(bf16[2,144,1152]{2,1,0:T(8,128)(2,1)} %slice_bitcast_fusion.3), channel_id=1, source_target_pairs={{0,16},{1,17},{2,18},{3,19},{4,20},{5,21},{6,22},{7,23},{8,24},{9,... | collective-permute-start | bytes 1990664 | tf_op jit(solution)/shard_map/ppermute | solution.py:493
  445.8 10.2 %collective-permute-start.34 = (f32[106,128]{1,0:T(8,128)}, f32[106,128]{1,0:T(8,128)}, u32[]{:S(2)}, u32[]{:S(2)}) collective-permute-start(f32[106,128]{1,0:T(8,128)} %bitcast.56), channel_id=1, source_target_pairs={{0,2},{1,3},{2,0},{3,1},{4,6},{5,7},{6,4},{7,5},{8,10},{9,11},{10,... | collective-permute-start | bytes 162824 | tf_op jit(solution)/shard_map/ppermute | solution.py:493
  446.8 9.2 %collective-permute-start.35 = (f32[106,128]{1,0:T(8,128)}, f32[106,128]{1,0:T(8,128)}, u32[]{:S(2)}, u32[]{:S(2)}) collective-permute-start(f32[106,128]{1,0:T(8,128)} %bitcast.56), channel_id=1, source_target_pairs={{0,4},{1,5},{2,6},{3,7},{4,0},{5,1},{6,2},{7,3},{8,12},{9,13},{10,... | collective-permute-start | bytes 162824 | tf_op jit(solution)/shard_map/ppermute | solution.py:493
  448.6 7.4 %collective-permute-start.36 = (f32[106,128]{1,0:T(8,128)}, f32[106,128]{1,0:T(8,128)}, u32[]{:S(2)}, u32[]{:S(2)}) collective-permute-start(f32[106,128]{1,0:T(8,128)} %bitcast.56), channel_id=1, source_target_pairs={{0,6},{1,7},{2,4},{3,5},{4,2},{5,3},{6,0},{7,1},{8,14},{9,15},{10,... | collective-permute-start | bytes 162824 | tf_op jit(solution)/shard_map/ppermute | solution.py:493
  463.1 6.8 %collective-permute-start.43 = (bf16[272,288]{1,0:T(8,128)(2,1)S(1)}, bf16[272,288]{1,0:T(8,128)(2,1)S(1)}, u32[]{:S(2)}, u32[]{:S(2)}) collective-permute-start(bf16[272,288]{1,0:T(8,128)(2,1)S(1)} %copy-done.60), channel_id=1, source_target_pairs={{0,8},{1,9},{2,10},{3,11},{4,12},{5,13},{6,14},{7,15},{8,0},{9,1},... | collective-permute-start | bytes 470024 | tf_op jit(solution)/shard_map/ppermute | solution.py:493
  463.1 8.9 %collective-permute-start.44 = (bf16[272,288]{1,0:T(8,128)(2,1)S(1)}, bf16[272,288]{1,0:T(8,128)(2,1)S(1)}, u32[]{:S(2)}, u32[]{:S(2)}) collective-permute-start(bf16[272,288]{1,0:T(8,128)(2,1)S(1)} %copy-done.59), channel_id=1, source_target_pairs={{0,16},{1,17},{2,18},{3,19},{4,20},{5,21},{6,22},{7,23},{8,24},{9,... | collective-permute-start | bytes 470024 | tf_op jit(solution)/shard_map/ppermute | solution.py:493
  464.9 9.8 %collective-permute-start.45 = (bf16[272,288]{1,0:T(8,128)(2,1)S(1)}, bf16[272,288]{1,0:T(8,128)(2,1)S(1)}, u32[]{:S(2)}, u32[]{:S(2)}) collective-permute-start(bf16[272,288]{1,0:T(8,128)(2,1)S(1)} %copy-done.58), channel_id=1, source_target_pairs={{0,24},{1,25},{2,26},{3,27},{4,28},{5,29},{6,30},{7,31},{8,16},{9,... | collective-permute-start | bytes 470024 | tf_op jit(solution)/shard_map/ppermute | solution.py:493
  466.0 28.5 %collective-permute-start.39 = (bf16[368,1152]{1,0:T(8,128)(2,1)}, bf16[368,1152]{1,0:T(8,128)(2,1)}, u32[]{:S(2)}, u32[]{:S(2)}) collective-permute-start(bf16[368,1152]{1,0:T(8,128)(2,1)} %slice.254), channel_id=1, source_target_pairs={{0,1},{1,0},{2,3},{3,2},{4,5},{5,4},{6,7},{7,6},{8,9},{9,8},{10,11... | collective-permute-start | bytes 2543624 | tf_op jit(solution)/shard_map/ppermute | solution.py:614
  467.8 26.2 %collective-permute-start.41 = (bf16[144,1152]{1,0:T(8,128)(2,1)}, bf16[144,1152]{1,0:T(8,128)(2,1)}, u32[]{:S(2)}, u32[]{:S(2)}) collective-permute-start(bf16[144,1152]{1,0:T(8,128)(2,1)} %get-tuple-element.192), channel_id=1, source_target_pairs={{0,4},{1,5},{2,6},{3,7},{4,0},{5,1},{6,2},{7,3},{8,12},{9,13},{10,... | collective-permute-start | bytes 995336 | tf_op jit(solution)/shard_map/ppermute | solution.py:493
  469.9 24.1 %collective-permute-start.42 = (bf16[144,1152]{1,0:T(8,128)(2,1)}, bf16[144,1152]{1,0:T(8,128)(2,1)}, u32[]{:S(2)}, u32[]{:S(2)}) collective-permute-start(bf16[144,1152]{1,0:T(8,128)(2,1)} %get-tuple-element.191), channel_id=1, source_target_pairs={{0,6},{1,7},{2,4},{3,5},{4,2},{5,3},{6,0},{7,1},{8,14},{9,15},{10,... | collective-permute-start | bytes 995336 | tf_op jit(solution)/shard_map/ppermute | solution.py:493
  472.1 22.4 %collective-permute-start.40 = (bf16[144,1152]{1,0:T(8,128)(2,1)}, bf16[144,1152]{1,0:T(8,128)(2,1)}, u32[]{:S(2)}, u32[]{:S(2)}) collective-permute-start(bf16[144,1152]{1,0:T(8,128)(2,1)} %slice_bitcast_fusion.11), channel_id=1, source_target_pairs={{0,2},{1,3},{2,0},{3,1},{4,6},{5,7},{6,4},{7,5},{8,10},{9,11},{10,... | collective-permute-start | bytes 995336 | tf_op jit(solution)/shard_map/ppermute | solution.py:493
  498.7 8.1 %collective-permute-start.50 = (bf16[144,288]{1,0:T(8,128)(2,1)}, bf16[144,288]{1,0:T(8,128)(2,1)S(1)}, u32[]{:S(2)}, u32[]{:S(2)}) collective-permute-start(bf16[144,288]{1,0:T(8,128)(2,1)} %get-tuple-element.158), channel_id=1, source_target_pairs={{0,8},{1,9},{2,10},{3,11},{4,12},{5,13},{6,14},{7,15},{8,0},{9,1},... | collective-permute-start | bytes 248840 | tf_op jit(solution)/shard_map/ppermute | solution.py:493
  498.7 8.2 %collective-permute-start.51 = (bf16[144,288]{1,0:T(8,128)(2,1)}, bf16[144,288]{1,0:T(8,128)(2,1)S(1)}, u32[]{:S(2)}, u32[]{:S(2)}) collective-permute-start(bf16[144,288]{1,0:T(8,128)(2,1)} %get-tuple-element.159), channel_id=1, source_target_pairs={{0,16},{1,17},{2,18},{3,19},{4,20},{5,21},{6,22},{7,23},{8,24},{9,... | collective-permute-start | bytes 248840 | tf_op jit(solution)/shard_map/ppermute | solution.py:493
  500.2 6.7 %collective-permute-start.52 = (bf16[144,288]{1,0:T(8,128)(2,1)}, bf16[144,288]{1,0:T(8,128)(2,1)S(1)}, u32[]{:S(2)}, u32[]{:S(2)}) collective-permute-start(bf16[144,288]{1,0:T(8,128)(2,1)} %get-tuple-element.160), channel_id=1, source_target_pairs={{0,24},{1,25},{2,26},{3,27},{4,28},{5,29},{6,30},{7,31},{8,16},{9,... | collective-permute-start | bytes 248840 | tf_op jit(solution)/shard_map/ppermute | solution.py:493
  500.5 4.4 collective-permute-start.46
  504.9 6.9 %collective-permute-start.47 = (f32[106,128]{1,0:T(8,128)S(1)}, f32[106,128]{1,0:T(8,128)S(1)}, u32[]{:S(2)}, u32[]{:S(2)}) collective-permute-start(f32[106,128]{1,0:T(8,128)S(1)} %add.260), channel_id=1, source_target_pairs={{0,8},{1,9},{2,10},{3,11},{4,12},{5,13},{6,14},{7,15},{8,0},{9,1},... | collective-permute-start | bytes 162824 | tf_op jit(solution)/shard_map/ppermute | solution.py:493
  505.0 6.8 %collective-permute-start.48 = (f32[106,128]{1,0:T(8,128)S(1)}, f32[106,128]{1,0:T(8,128)S(1)}, u32[]{:S(2)}, u32[]{:S(2)}) collective-permute-start(f32[106,128]{1,0:T(8,128)S(1)} %add.260), channel_id=1, source_target_pairs={{0,16},{1,17},{2,18},{3,19},{4,20},{5,21},{6,22},{7,23},{8,24},{9,... | collective-permute-start | bytes 162824 | tf_op jit(solution)/shard_map/ppermute | solution.py:493
  506.8 5.0 collective-permute-start.49
  (57 other events, 342.8 us)
Sparse Core Ops, SparseCore 0:
  21.0 128.4 all-gather.4
  153.0 73.4 all-gather.6
  295.5 144.5 reduce-scatter.1

commit v5 on v4

--- a/solution.py
+++ b/solution.py
@@ -130,7 +130,22 @@
     return (centred * inv_scale * gain + shift).astype(low)
 
 
-def norm_back_kernel(values_ref, grad_ref, gain_ref, base_ref, full_ref, low_ref, sums_ref):
+def norm_back_kernel(values_ref, grad_ref, gain_ref, base_ref, *refs):
+    if len(refs) > 3:
+        down_ref, shift_ref, full_ref, low_ref, sums_ref, kept_ref, sent_ref = refs
+        total = (values_ref[...] + (down_ref[...] + shift_ref[...])).astype(low)
+        early = pl.program_id(0) < 2
+
+        @pl.when(early)
+        def keep():
+            kept_ref[...] = total
+
+        @pl.when(jnp.logical_not(early))
+        def give():
+            sent_ref[...] = total
+
+    else:
+        full_ref, low_ref, sums_ref = refs
     values = values_ref[...].astype(wide)
     centred = values - jnp.mean(values, axis=-1, keepdims=True)
     inv_scale = lax.rsqrt(jnp.mean(centred * centred, axis=-1, keepdims=True) + norm_eps)
@@ -158,32 +173,41 @@
         sums_ref[...] += sums
 
 
-def norm_back(values, grad, gain, base):
+def norm_back(values, grad, gain, base, down=None, shift=None):
     tokens, width = values.shape
     block = tokens // 4
     rows = pl.BlockSpec((block, width), lambda i: (i, 0))
+    line = pl.BlockSpec((1, width), lambda i: (0, 0))
+    more, halves = [], []
+    if down is not None:
+        more = [down, shift.reshape(1, width)]
+        halves = [
+            pl.BlockSpec((block, width), lambda i: (jnp.minimum(i, 1), 0)),
+            pl.BlockSpec((block, width), lambda i: (jnp.maximum(i - 2, 0), 0)),
+        ]
     return pl.pallas_call(
         norm_back_kernel,
         grid=(4,),
-        in_specs=[rows, rows, pl.BlockSpec((1, width), lambda i: (0, 0)), rows],
-        out_specs=[rows, rows, pl.BlockSpec((4, width), lambda i: (0, 0))],
+        in_specs=[rows, rows, line, rows] + [rows, line][: len(more)],
+        out_specs=[rows, rows, pl.BlockSpec((4, width), lambda i: (0, 0))] + halves,
         out_shape=[
             jax.ShapeDtypeStruct((tokens, width), wide),
             jax.ShapeDtypeStruct((tokens, width), low),
             jax.ShapeDtypeStruct((4, width), wide),
-        ],
+        ]
+        + [jax.ShapeDtypeStruct((tokens // 2, width), low)] * len(halves),
         compiler_params=pltpu.CompilerParams(vmem_limit_bytes=40 * 2**20),
         cost_estimate=pl.CostEstimate(
             flops=tokens * width, bytes_accessed=tokens * width, transcendentals=0
         ),
         name="norm_back",
-    )(values, grad, gain.reshape(1, width), base)
+    )(values, grad, gain.reshape(1, width), base, *more)
 
 
 def mlp_kernel(carried, plan, normed_ref, grad_ref, bias_ref, *refs):
     starts, rows, group, pieces = plan
     weights, refs = refs[:pieces], refs[pieces:]
-    steps = 32 // group
+    steps = 32 // group if pieces == 1 else pieces // 2
     if carried:
         out_before, normed_before = refs[:2]
         refs = refs[2:]
@@ -243,11 +267,7 @@
             ref[place, 0] = grad_up[place * many : (place + 1) * many]
             ref[place, 1] = grad_down[place * many : (place + 1) * many]
 
-    if pieces == 1:
-        keep(grad_refs[0])
-    else:
-        pl.when(step < 2)(lambda: keep(grad_refs[0]))
-        pl.when(step >= 2)(lambda: keep(grad_refs[1]))
+    keep(grad_refs[0])
     out_term = product(active, down, 0, 0)
     normed_term = product(grad_pre, up, 0, 0)
 
@@ -268,19 +288,16 @@
 
 def mlp(normed, grad, bias, weights, starts, rows, group=8, before=None):
     tokens, width = normed.shape
-    steps = 32 // group
+    steps = 32 // group if len(weights) == 1 else len(weights) // 2
+    blocks = 32 if len(weights) == 1 else 4 * len(weights)
     whole = pl.BlockSpec((tokens, width), lambda i: (0, 0))
     column = pl.BlockSpec((group * rows, 1), lambda i: (i, 0))
     if len(weights) == 1:
-        grad_specs = [pl.BlockSpec((group, 2, rows, width), lambda i: (i, 0, 0, 0))]
-        grad_shapes = [jax.ShapeDtypeStruct((32, 2, rows, width), low)]
+        part, many = (group, 2, rows, width), blocks
     else:
-        part = (2, 2, 4 * rows, width)
-        grad_specs = [
-            pl.BlockSpec(part, lambda i: (jnp.minimum(i, 1), 0, 0, 0)),
-            pl.BlockSpec(part, lambda i: (jnp.maximum(i - 2, 0), 0, 0, 0)),
-        ]
-        grad_shapes = [jax.ShapeDtypeStruct((4, 2, 4 * rows, width), low)] * 2
+        part, many = (2, 2, 4 * rows, width), blocks // 4
+    grad_specs = [pl.BlockSpec(part, lambda i: (i, 0, 0, 0))]
+    grad_shapes = [jax.ShapeDtypeStruct((many,) + part[1:], low)]
     earlier = [] if before is None else list(before)
     return pl.pallas_call(
         partial(mlp_kernel, before is not None, (starts, rows, group, len(weights))),
@@ -291,7 +308,7 @@
         out_specs=[whole, whole] + grad_specs + [column],
         out_shape=[jax.ShapeDtypeStruct((tokens, width), wide)] * 2
         + grad_shapes
-        + [jax.ShapeDtypeStruct((32 * rows, 1), wide)],
+        + [jax.ShapeDtypeStruct((blocks * rows, 1), wide)],
         scratch_shapes=[
             pltpu.VMEM((2, group * rows, width), low),
             pltpu.VMEM((2, group * rows, width), low),
@@ -302,7 +319,7 @@
         ),
         compiler_params=pltpu.CompilerParams(vmem_limit_bytes=60 * 2**20),
         cost_estimate=pl.CostEstimate(
-            flops=2 * tokens * width * 32 * rows, bytes_accessed=2**20, transcendentals=0
+            flops=2 * tokens * width * blocks * rows, bytes_accessed=2**20, transcendentals=0
         ),
         name="mlp",
     )(normed, grad, bias, *weights, *earlier)
@@ -519,7 +536,7 @@
             self.arrived = hops.send(sibling, hops.core)
         else:
             self.arrived = [hops.send(piece, hops.core) for piece in sibling]
-        self.width = own[0].shape[-1]
+        self.width = sibling[0].shape[-1]
 
     def part(self, place):
         return self.own[place], self.arrived[place]
@@ -718,7 +735,7 @@
         near_y, far_x = hops.send(hop_near, hops.y), hops.send(hop_far, hops.x)
         near_y, far_x = after((near_y, far_x), attended)
         hop_three = [hop_near, near_y, hop_far, far_x]
-        hop_weights = hops.sibling(*hop_three) + list(hop_three)
+        hop_sibling = hops.sibling(*hop_three)
     else:
         attended, totals = attend(projected, bias_col, heads, 4)
     branch = product(attended, out_rows, 0, 0) + b_out
@@ -727,15 +744,18 @@
     rows = unit_cuts[0] * devices // 32
     sums, up_sums = None, []
     if by_hops:
-        *sums, grad_sibling, grad_own, up_sum = mlp(
-            normed_second,
-            grad_out,
-            unit_bias(1),
-            hop_weights,
-            (0, 4 * unit_cuts[1]),
-            unit_cuts[1],
-        )
-        up_sums.append(up_sum[:, 0])
+        hop_bias = jnp.split(unit_bias(1), 2)
+        hop_rows = unit_cuts[1]
+        hop_mlp = partial(mlp, normed_second, grad_out)
+        *sums, grad_sibling, sibling_sum = hop_mlp(
+            hop_bias[0], hop_sibling, (0, 4 * hop_rows), hop_rows
+        )
+        units = Reduction(hops, None, grad_sibling, True)
+        *sums, units.own, own_sum = hop_mlp(
+            hop_bias[1], hop_three, (0, 4 * hop_rows), hop_rows, 8, sums
+        )
+        up_sums.append(jnp.concatenate([sibling_sum[:, 0], own_sum[:, 0]]))
+        units.arrived = after(units.arrived, sums)
     bulk = partial(
         mlp,
         normed_second,
@@ -747,10 +767,10 @@
         16 if by_hops else 4,
     )
     if by_hops:
-        units = Reduction(hops, grad_own, grad_sibling, True)
         sums = after(sums, units.ready_third())
         units.send_third()
         *sums, bulk_grads, up_sum = bulk(sums)
+        units.moved = after(units.moved, sums)
     else:
         *sums, bulk_grads, up_sum = bulk()
     up_sums = [up_sum[:, 0]] + up_sums
@@ -762,19 +782,19 @@
     if by_hops:
         units_third = units.third()
         grad_normed_second = after(grad_normed_second, units_third)
-    grad_middle, grad_branch, second_sums = norm_back(
-        middle, grad_normed_second, mlp_norm_gain, grad_out
-    )
-    out_low = (middle + (down_out + b_down)).astype(low)
+    grad_middle, grad_branch, second_sums, out_kept, out_sent = norm_back(
+        middle, grad_normed_second, mlp_norm_gain, grad_out, down_out, b_down
+    )
     back = partial(
         attend_back, projected, bias_col, attended, totals, attn_rows.reshape(-1, width)
     )
     if by_hops:
         units.send_second()
-        out_other = swap(after(out_low[half_rows:], units_third))
+        out_other = swap(out_sent)
         grads = back(grad_branch, heads, 4)
-        grads, out_other = after((grads, out_other), units.second())
-        layer_out = both_micros(out_low[:half_rows], out_other)
+        units.moved, out_other = after((units.moved, out_other), grads)
+        grads = after(grads, units.second())
+        layer_out = both_micros(out_kept, out_other)
         units.send_along_z()
         kind_grads = kinds_grad(
             places, grads, attended, normed_first, grad_branch, tensor_count
@@ -797,9 +817,10 @@
         input_full, input_low, first_sums = norm_back(
             x_slot, first_terms, attn_norm_gain, grad_middle
         )
-        out_other = swap(out_low[half_rows:])
-        layer_out = both_micros(out_low[:half_rows], out_other)
-
+        out_other = swap(out_sent)
+        layer_out = both_micros(out_kept, out_other)
+
+    grads, second_sums, up_sums = after((grads, second_sums, up_sums), input_low)
     total_over = lambda i: jnp.sum(grads[i], axis=1, dtype=wide)
     small = jnp.concatenate(
         [

time: 532 us -> 547 us (1.028)
  waiting for transfers between devices: 148 us -> 165 us
  Pallas kernels: 163 us -> 175 us
  local copies, waits for them, and re-layouts: 55.7 us -> 49.9 us
    ppermute x49, waiting for transfers between devices: 118 us -> 139 us  [send(): return lax.ppermute(values, everyone, pairs)]
    pallas_call x2 -> x3, Pallas kernels: 81.1 us -> 89.6 us  [mlp(): pl.pallas_call(partial(mlp_kernel, before is not None, (starts, rows, gro...]
    unnamed x136 -> x150, local copies, waits for them, and re-layouts: 20.8 us -> 18.7 us
  transfers between devices with their start and end apart: 56 -> 56, of which waited for: 19 -> 20; matrix products, arithmetic and copies ran while one was open for 23% -> 19% of each run, Pallas kernels for 31% -> 31%
where the time goes in v5:
time: 547 us; the launch traced here: 540 us
  Pallas kernels  175 us (32%)
  waiting for transfers between devices  165 us (30%)
  other arithmetic  60.5 us (11%)
  local copies, waits for them, and re-layouts  49.9 us (9%)
  starting transfers between devices  47.4 us (9%)
  matrix products  26.9 us (5%)
  between operations  15 us (3%)
    ppermute x49, waiting for transfers between devices, send(): return lax.ppermute(values, everyone, pairs)  139 us
    pallas_call x3, Pallas kernels, mlp(): pl.pallas_call(partial(mlp_kernel, before is not None, (starts, rows, gro...  89.6 us
    ppermute x49, starting transfers between devices, send(): return lax.ppermute(values, everyone, pairs)  42.3 us
    pallas_call x1, Pallas kernels, attend_back(): pl.pallas_call(partial(attend_back_kernel, step_heads), grid=(steps,), in...  28.6 us
    dot_general x3, matrix products, product(): lax.dot_general(left, right, (((left_dim,), (right_dim,)), ((), ())), pre...  26.5 us
    convert_element_type x12, other arithmetic, add_low(): return total.astype(low)  25.4 us
    unnamed x150, local copies, waits for them, and re-layouts  18.7 us
    ppermute x4, waiting for transfers between devices, swap(): return lax.ppermute(values, 'tensor', pairs)  18.1 us
  transfers between devices with their start and end apart: 56, of which 20 were waited for; matrix products, arithmetic and copies ran while one was open for 19% of the time, Pallas kernels for 31%

profile of v5, /device:TPU:0, one launch (start us, length us, event | category | flops | bytes accessed | tf_op | source)
XLA Modules:
  0.0 540.0 jit_solution(8863445904061003516)
XLA Ops:
  9.2 2.4 collective-permute-start.3
  12.3 2.8 collective-permute-done.3.refs_3_
  15.0 2.5 collective-permute-done.2.refs_2_
  18.3 2.2 unite.2
  21.6 2.4 collective-permute-start
  29.2 4.2 collective-permute-done.7.refs_3_
  33.4 6.9 %collective-permute-done.6.refs_2_ = bf16[272,288]{1,0:T(8,128)(2,1)} collective-permute-done((bf16[272,288]{1,0:T(8,128)(2,1)}, bf16[272,288]{1,0:T(8,128)(2,1)}, u32[]{:S(2)}, u32[]{:S(2)}) %collective-permute-start.6) | collective-permute-done | bytes 156704 | tf_op jit(solution)/shard_map/ppermute | solution.py:510
  40.3 2.6 unite.3
  42.9 3.6 collective-permute-start.10
  50.6 18.1 %collective-permute-done.4 = bf16[368,1152]{1,0:T(8,128)(2,1)S(1)} collective-permute-done((bf16[368,1152]{1,0:T(8,128)(2,1)S(1)}, bf16[368,1152]{1,0:T(8,128)(2,1)S(1)}, u32[]{:S(2)}, u32[]{:S(2)}) %collective-permute-start.4) | collective-permute-done | bytes 847904 | tf_op jit(solution)/shard_map/ppermute | solution.py:631
  70.2 25.9 %collective-permute-done.9 = bf16[176,1152]{1,0:T(8,128)(2,1)S(1)} collective-permute-done((bf16[176,1152]{1,0:T(8,128)(2,1)}, bf16[176,1152]{1,0:T(8,128)(2,1)S(1)}, u32[]{:S(2)}, u32[]{:S(2)}) %collective-permute-start.9) | collective-permute-done | bytes 405536 | tf_op jit(solution)/shard_map/ppermute | solution.py:510
  102.8 32.9 %collective-permute-done.11 = bf16[352,1152]{1,0:T(8,128)(2,1)} collective-permute-done((bf16[352,1152]{1,0:T(8,128)(2,1)}, bf16[352,1152]{1,0:T(8,128)(2,1)}, u32[]{:S(2)}, u32[]{:S(2)}) %collective-permute-start.11) | collective-permute-done | bytes 811040 | tf_op jit(solution)/shard_map/ppermute | solution.py:510
  135.8 2.5 pad_maximum_fusion.3
  138.3 1.6 collective-permute-start.14
  139.9 2.4 pad_maximum_fusion.2
  142.9 8.1 %all-gather.5.cloned.1.call-done.weights_ref = bf16[4608,1152]{1,0:T(8,128)(2,1)} async-done(((bf16[144,1152]{1,0:T(8,128)(2,1)}), bf16[4608,1152]{1,0:T(8,128)(2,1)}) %all-gather.5.cloned.1.call-update) | async-done | bytes 10616848 | tf_op jit(solution)/shard_map/all_gather | solution.py:669
  151.1 11.1 %add_convert_fusion.query_ref.key_ref.value_ref = bf16[3456,736]{1,0:T(8,128)(2,1)} fusion(bf16[736,1152]{1,0:T(8,128)(2,1)S(1)} %fusion.11.normed_ref, bf16[4608,1152]{1,0:T(8,128)(2,1)} %all-gather.5.cloned.1.call-done.weights_ref, f32[3456]{0:T(1024)S(1)} %pad_maximum_fusion.11), kind=kOutput, calls=%fused_computation | convolution fusion | flops 5865578496 | bytes 14759424 | tf_op jit(solution)/shard_map/dot_general | solution.py:23
  162.2 15.3 %attend.1 = (bf16[1152,736]{1,0:T(8,128)(2,1)S(1)}, f32[16,1,736]{2,1,0:T(1,128)S(1)}) custom-call(bf16[3456,736]{1,0:T(8,128)(2,1)} %add_convert_fusion.query_ref.key_ref.value_ref, bf16[3456,736]{1,0:T(8,128)(2,1)} %add_convert_fusion.query_ref.key_ref.value_ref, bf16[3456,736]{1,0:T(8,128)(2,1)} %add_convert_fusion.query_ref.key_ref.value_ref, ...), custom_call_target="tpu_custom_call" | custom-call | flops 1109393408 | bytes 1048576 | tf_op jit(solution)/shard_map/attend/pallas_call | solution.py:80
  178.0 4.0 collective-permute-done.13.refs_1_
  182.6 4.8 fusion.40
  188.1 1.8 add_convert_fusion.1.normed_ref
  189.9 27.9 %mlp.3 = (f32[736,1152]{1,0:T(8,128)}, f32[736,1152]{1,0:T(8,128)}, bf16[4,2,352,1152]{3,2,1,0:T(8,128)(2,1)}, f32[1408,1]{1,0:T(8,128)}) custom-call(bf16[736,1152]{1,0:T(8,128)(2,1)} %add_convert_fusion.1.normed_ref, bf16[736,1152]{1,0:T(8,128)(2,1)} %pad_maximum_fusion.1.grad_ref.base_ref, f32[1408,1]{1,0:T(8,128)} %split.15.bias_ref, ...), custom_call_target="tpu_custom_call" | custom-call | flops 2387607552 | bytes 1048576 | tf_op jit(solution)/shard_map/mlp/pallas_call | solution.py:302
  219.0 30.1 %mlp.4 = (f32[736,1152]{1,0:T(8,128)}, f32[736,1152]{1,0:T(8,128)}, bf16[4,2,352,1152]{3,2,1,0:T(8,128)(2,1)}, f32[1408,1]{1,0:T(8,128)}) custom-call(bf16[736,1152]{1,0:T(8,128)(2,1)} %add_convert_fusion.1.normed_ref, bf16[736,1152]{1,0:T(8,128)(2,1)} %pad_maximum_fusion.1.grad_ref.base_ref, ...), custom_call_target="tpu_custom_call", output_to_operand_aliasing={{0}: (7, {}), {1}: (8, {})} | custom-call | flops 2387607552 | bytes 1048576 | tf_op jit(solution)/shard_map/mlp/pallas_call | solution.py:302
  249.1 5.4 fusion.16
  257.1 31.6 %mlp.5 = (f32[736,1152]{1,0:T(8,128)}, f32[736,1152]{1,0:T(8,128)}, bf16[32,2,48,1152]{3,2,1,0:T(8,128)(2,1)}, f32[1536,1]{1,0:T(8,128)}) custom-call(bf16[736,1152]{1,0:T(8,128)(2,1)} %add_convert_fusion.1.normed_ref, bf16[736,1152]{1,0:T(8,128)(2,1)} %pad_maximum_fusion.1.grad_ref.base_ref, ...), custom_call_target="tpu_custom_call", output_to_operand_aliasing={{0}: (4, {}), {1}: (5, {})} | custom-call | flops 2604662784 | bytes 1048576 | tf_op jit(solution)/shard_map/mlp/pallas_call | solution.py:302
  288.7 3.9 collective-permute-done.21
  292.9 5.0 fusion.12
  301.9 7.2 %norm_back.2 = (f32[736,1152]{1,0:T(8,128)S(1)}, bf16[736,1152]{1,0:T(8,128)(2,1)S(1)}, f32[4,1152]{1,0:T(4,128)S(1)}, bf16[368,1152]{1,0:T(8,128)(2,1)S(1)}, bf16[368,1152]{1,0:T(8,128)(2,1)}) custom-call(f32[736,1152]{1,0:T(8,128)S(1)} %get-tuple-element.234.values_ref, f32[736,1152]{1,0:T(8,128)} %get-tuple-element.126.grad_ref, ...), custom_call_target="tpu_custom_call" | custom-call | flops 847872 | bytes 847872 | tf_op jit(solution)/shard_map/norm_back/pallas_call | solution.py:188
  310.3 1.7 copy-done.10
  317.1 1.7 reduce.5
  318.9 2.0 reduce.4
  324.6 28.6 %attend_back.1.grads_ref = bf16[3,1152,736]{2,1,0:T(8,128)(2,1)} custom-call(bf16[3456,736]{1,0:T(8,128)(2,1)} %add_convert_fusion.query_ref.key_ref.value_ref, bf16[3456,736]{1,0:T(8,128)(2,1)} %add_convert_fusion.query_ref.key_ref.value_ref, bf16[3456,736]{1,0:T(8,128)(2,1)} %add_convert_fusion.query_ref.key_ref.value_ref, f32[736,1]{1,0:T(8,128)S(1)} %copy-done.9, ...), custom_call_target="tpu_custom_call" | custom-call | flops 1109393408 | bytes 1048576 | tf_op jit(solution)/shard_map/attend_back/pallas_call | solution.py:103
  357.1 2.5 collective-permute-start.29
  360.2 17.0 %kinds_grad.1 = (bf16[2,2,144,1152]{3,2,1,0:T(8,128)(2,1)S(1)}, bf16[2,2,144,1152]{3,2,1,0:T(8,128)(2,1)S(1)}, bf16[4,144,1152]{2,1,0:T(8,128)(2,1)S(1)}, bf16[4...) custom-call(s32[2]{0:T(128)S(1)} %pad_add_fusion.kind_ref, ...), custom_call_target="tpu_custom_call" | custom-call | flops 976748544 | bytes 1048576 | tf_op jit(solution)/shard_map/kinds_grad/pallas_call | solution.py:383
  377.9 10.6 %fusion.2.grad_ref = f32[736,1152]{1,0:T(8,128)S(1)} fusion(bf16[3456,736]{1,0:T(8,128)(2,1)S(1)} %bitcast.171, bf16[4608,1152]{1,0:T(8,128)(2,1)} %all-gather.5.cloned.1.call-done.weights_ref), kind=kOutput, calls=%fused_computation.3 | convolution fusion | flops 5860491264 | bytes 16441344 | tf_op jit(solution)/shard_map/dot_general | solution.py:23
  389.1 23.7 %collective-permute-done.28 = bf16[2,88,1152]{2,1,0:T(8,128)(2,1)S(1)} collective-permute-done((bf16[2,88,1152]{2,1,0:T(8,128)(2,1)S(1)}, bf16[2,88,1152]{2,1,0:T(8,128)(2,1)S(1)}, u32[]{:S(2)}, u32[]{:S(2)}) %collective-permute-start.28) | collective-permute-done | bytes 405536 | tf_op jit(solution)/shard_map/ppermute | solution.py:510
  418.2 3.3 norm_back.3
  421.5 1.7 copy-done.12
  427.7 2.6 convert_reduce_fusion.1
  431.7 17.3 %collective-permute-done.31 = bf16[2,2,144,1152]{3,2,1,0:T(8,128)(2,1)} collective-permute-done((bf16[2,2,144,1152]{3,2,1,0:T(8,128)(2,1)}, bf16[2,2,144,1152]{3,2,1,0:T(8,128)(2,1)}, u32[]{:S(2)}, u32[]{:S(2)}) %collective-permute-start.31) | collective-permute-done | bytes 1327136 | tf_op jit(solution)/shard_map/ppermute | solution.py:510
  449.0 2.2 add_convert_fusion.4
  453.6 2.2 add_convert_fusion.5
  458.9 3.3 collective-permute-start.36
  463.3 3.1 maximum_select_fusion.1
  466.3 2.7 divide.2
  469.1 1.5 add_add_fusion.1
  476.1 1.9 collective-permute-start.44
  479.9 2.0 collective-permute-start.42
  481.9 2.2 collective-permute-done.44.refs_2_
  484.1 2.0 collective-permute-start.41
  486.1 1.9 collective-permute-done.45.refs_3_
  488.6 2.5 settle.2
  491.2 2.0 fusion.35
  493.2 1.8 copy.87
  495.0 1.8 copy.85
  500.5 2.6 pad_maximum_fusion.7
  503.0 9.1 %collective-permute-done.41 = bf16[144,1152]{1,0:T(8,128)(2,1)} collective-permute-done((bf16[144,1152]{1,0:T(8,128)(2,1)}, bf16[144,1152]{1,0:T(8,128)(2,1)}, u32[]{:S(2)}, u32[]{:S(2)}) %collective-permute-start.41) | collective-permute-done | bytes 331808 | tf_op jit(solution)/shard_map/ppermute | solution.py:510
  512.1 2.1 fusion.26.refs_0_
  515.6 2.1 divide.3
  517.7 1.9 collective-permute-start.51
  521.1 2.0 maximum_select_fusion
  523.1 1.7 collective-permute-start.49
  526.3 2.0 settle.3
  528.4 2.2 slice_bitcast_fusion.11
  (330 shorter events, 84.3 us)
Async XLA Ops:
  7.2 143.8 %all-gather.5.cloned.1.call-start = ((), (), s32[]{:S(2)}) async-start(), calls=%async_computation.2 | async-start | bytes 10948608 | tf_op jit(solution)/shard_map/all_gather | solution.py:669
  9.2 5.8 %collective-permute-start.3 = (bf16[144,288]{1,0:T(8,128)(2,1)S(1)}, bf16[144,288]{1,0:T(8,128)(2,1)S(1)}, u32[]{:S(2)}, u32[]{:S(2)}) collective-permute-start(bf16[144,288]{1,0:T(8,128)(2,1)S(1)} %get-tuple-element.217), channel_id=1, source_target_pairs={{0,24},{1,25},{2,26},{3,27},{4,28},{5,29},{6,30},{7,31},{8,16},{9,... | collective-permute-start | bytes 248840 | tf_op jit(solution)/shard_map/ppermute | solution.py:510
  11.6 6.0 %collective-permute-start.2 = (bf16[144,288]{1,0:T(8,128)(2,1)S(1)}, bf16[144,288]{1,0:T(8,128)(2,1)S(1)}, u32[]{:S(2)}, u32[]{:S(2)}) collective-permute-start(bf16[144,288]{1,0:T(8,128)(2,1)S(1)} %get-tuple-element.218), channel_id=1, source_target_pairs={{0,16},{1,17},{2,18},{3,19},{4,20},{5,21},{6,22},{7,23},{8,24},{9,... | collective-permute-start | bytes 248840 | tf_op jit(solution)/shard_map/ppermute | solution.py:510
  12.2 5.4 collective-permute-start.1
  20.5 236.6 %all-gather.7.cloned.1.call-start = ((), (), s32[]{:S(2)}) async-start(), calls=%async_computation.3 | async-start | bytes 7299072 | tf_op jit(solution)/shard_map/all_gather | solution.py:672
  21.6 25.7 %collective-permute-start = (bf16[368,1152]{1,0:T(8,128)(2,1)}, bf16[368,1152]{1,0:T(8,128)(2,1)S(1)}, u32[]{:S(2)}, u32[]{:S(2)}) collective-permute-start(bf16[368,1152]{1,0:T(8,128)(2,1)} %get-tuple-element.196), channel_id=1, source_target_pairs={{0,1},{1,0},{2,3},{3,2},{4,5},{5,4},{6,7},{7,6},{8,9},{9,8},{10,11... | collective-permute-start | bytes 2543624 | tf_op jit(solution)/shard_map/ppermute | solution.py:631
  25.7 7.7 %collective-permute-start.7 = (bf16[272,288]{1,0:T(8,128)(2,1)}, bf16[272,288]{1,0:T(8,128)(2,1)}, u32[]{:S(2)}, u32[]{:S(2)}) collective-permute-start(bf16[272,288]{1,0:T(8,128)(2,1)} %get-tuple-element.209), channel_id=1, source_target_pairs={{0,24},{1,25},{2,26},{3,27},{4,28},{5,29},{6,30},{7,31},{8,16},{9,... | collective-permute-start | bytes 470024 | tf_op jit(solution)/shard_map/ppermute | solution.py:510
  26.6 13.7 %collective-permute-start.6 = (bf16[272,288]{1,0:T(8,128)(2,1)}, bf16[272,288]{1,0:T(8,128)(2,1)}, u32[]{:S(2)}, u32[]{:S(2)}) collective-permute-start(bf16[272,288]{1,0:T(8,128)(2,1)} %get-tuple-element.210), channel_id=1, source_target_pairs={{0,16},{1,17},{2,18},{3,19},{4,20},{5,21},{6,22},{7,23},{8,24},{9,... | collective-permute-start | bytes 470024 | tf_op jit(solution)/shard_map/ppermute | solution.py:510
  27.2 13.1 %collective-permute-start.5 = (bf16[272,288]{1,0:T(8,128)(2,1)}, bf16[272,288]{1,0:T(8,128)(2,1)}, u32[]{:S(2)}, u32[]{:S(2)}) collective-permute-start(bf16[272,288]{1,0:T(8,128)(2,1)} %get-tuple-element.211), channel_id=1, source_target_pairs={{0,8},{1,9},{2,10},{3,11},{4,12},{5,13},{6,14},{7,15},{8,0},{9,1},... | collective-permute-start | bytes 470024 | tf_op jit(solution)/shard_map/ppermute | solution.py:510
  42.9 27.3 %collective-permute-start.10 = (bf16[176,1152]{1,0:T(8,128)(2,1)}, bf16[176,1152]{1,0:T(8,128)(2,1)S(1)}, u32[]{:S(2)}, u32[]{:S(2)}) collective-permute-start(bf16[176,1152]{1,0:T(8,128)(2,1)} %get-tuple-element.105), channel_id=1, source_target_pairs={{0,6},{1,7},{2,4},{3,5},{4,2},{5,3},{6,0},{7,1},{8,14},{9,15},{10,... | collective-permute-start | bytes 1216520 | tf_op jit(solution)/shard_map/ppermute | solution.py:510
  46.5 49.6 %collective-permute-start.9 = (bf16[176,1152]{1,0:T(8,128)(2,1)}, bf16[176,1152]{1,0:T(8,128)(2,1)S(1)}, u32[]{:S(2)}, u32[]{:S(2)}) collective-permute-start(bf16[176,1152]{1,0:T(8,128)(2,1)} %get-tuple-element.105), channel_id=1, source_target_pairs={{0,4},{1,5},{2,6},{3,7},{4,0},{5,1},{6,2},{7,3},{8,12},{9,13},{10,... | collective-permute-start | bytes 1216520 | tf_op jit(solution)/shard_map/ppermute | solution.py:510
  46.5 49.6 %collective-permute-start.8 = (bf16[176,1152]{1,0:T(8,128)(2,1)}, bf16[176,1152]{1,0:T(8,128)(2,1)S(1)}, u32[]{:S(2)}, u32[]{:S(2)}) collective-permute-start(bf16[176,1152]{1,0:T(8,128)(2,1)} %get-tuple-element.105), channel_id=1, source_target_pairs={{0,2},{1,3},{2,0},{3,1},{4,6},{5,7},{6,4},{7,5},{8,10},{9,11},{10,... | collective-permute-start | bytes 1216520 | tf_op jit(solution)/shard_map/ppermute | solution.py:510
  48.7 20.1 %collective-permute-start.4 = (bf16[368,1152]{1,0:T(8,128)(2,1)S(1)}, bf16[368,1152]{1,0:T(8,128)(2,1)S(1)}, u32[]{:S(2)}, u32[]{:S(2)}) collective-permute-start(bf16[368,1152]{1,0:T(8,128)(2,1)S(1)} %copy-done.39), channel_id=1, source_target_pairs={{0,1},{1,0},{2,3},{3,2},{4,5},{5,4},{6,7},{7,6},{8,9},{9,8},{10,11... | collective-permute-start | bytes 2543624 | tf_op jit(solution)/shard_map/ppermute | solution.py:631
  50.6 100.5 %copy-start.22 = (bf16[736,1152]{1,0:T(8,128)(2,1)}, bf16[736,1152]{1,0:T(8,128)(2,1)S(1)}, u32[]{:S(2)}) copy-start(bf16[736,1152]{1,0:T(8,128)(2,1)S(1)} %fusion.11.normed_ref) | copy-start | bytes 5087236
  50.6 46.2 %copy-start.33 = (bf16[176,1152]{1,0:T(8,128)(2,1)S(1)}, bf16[176,1152]{1,0:T(8,128)(2,1)}, u32[]{:S(2)}) copy-start(bf16[176,1152]{1,0:T(8,128)(2,1)} %get-tuple-element.105) | copy-start | bytes 1216516
  70.2 29.2 %copy-start.36 = (bf16[176,1152]{1,0:T(8,128)(2,1)}, bf16[176,1152]{1,0:T(8,128)(2,1)S(1)}, u32[]{:S(2)}) copy-start(bf16[176,1152]{1,0:T(8,128)(2,1)S(1)} %collective-permute-done.10) | copy-start | bytes 1216516
  97.8 37.8 %collective-permute-start.11 = (bf16[352,1152]{1,0:T(8,128)(2,1)}, bf16[352,1152]{1,0:T(8,128)(2,1)}, u32[]{:S(2)}, u32[]{:S(2)}) collective-permute-start(bf16[352,1152]{1,0:T(8,128)(2,1)} %bitcast.28), channel_id=1, source_target_pairs={{0,16},{1,17},{2,18},{3,19},{4,20},{5,21},{6,22},{7,23},{8,24},{9,... | collective-permute-start | bytes 2433032 | tf_op jit(solution)/shard_map/ppermute | solution.py:510
  100.3 35.5 %copy-start.37 = (bf16[176,1152]{1,0:T(8,128)(2,1)S(1)}, bf16[176,1152]{1,0:T(8,128)(2,1)}, u32[]{:S(2)}) copy-start(bf16[176,1152]{1,0:T(8,128)(2,1)} %copy-done.36) | copy-start | bytes 1216516
  100.3 35.5 %collective-permute-start.12 = (bf16[352,1152]{1,0:T(8,128)(2,1)}, bf16[352,1152]{1,0:T(8,128)(2,1)}, u32[]{:S(2)}, u32[]{:S(2)}) collective-permute-start(bf16[352,1152]{1,0:T(8,128)(2,1)} %bitcast.31), channel_id=1, source_target_pairs={{0,1},{1,0},{2,3},{3,2},{4,5},{5,4},{6,7},{7,6},{8,9},{9,8},{10,11... | collective-permute-start | bytes 2433032 | tf_op jit(solution)/shard_map/ppermute | solution.py:510
  101.1 61.1 %copy-start.8 = (f32[736,1]{1,0:T(8,128)}, f32[736,1]{1,0:T(8,128)S(1)}, u32[]{:S(2)}) copy-start(f32[736,1]{1,0:T(8,128)S(1)} %select_n.91.bias_ref) | copy-start | bytes 8836
  101.2 37.1 %copy-start.66 = (s32[32]{0:T(128)}, s32[32]{0:T(128)S(1)}, u32[]{:S(2)}) copy-start(s32[32]{0:T(128)S(1)} %broadcast_xor_fusion) | copy-start | bytes 388
  102.5 37.4 %copy-start.35 = (bf16[176,1152]{1,0:T(8,128)(2,1)S(1)}, bf16[176,1152]{1,0:T(8,128)(2,1)}, u32[]{:S(2)}) copy-start(bf16[176,1152]{1,0:T(8,128)(2,1)} %copy-done.34) | copy-start | bytes 1216516
  102.6 356.3 %reduce-scatter.2.cloned.1.call-start = ((), (), s32[]{:S(2)}) async-start(), calls=%async_computation.1 | async-start | bytes 7299072 | tf_op jit(solution)/shard_map/reduce_scatter | solution.py:778
  138.3 51.6 %collective-permute-start.17 = (bf16[704,1152]{1,0:T(8,128)(2,1)}, bf16[704,1152]{1,0:T(8,128)(2,1)}, u32[]{:S(2)}, u32[]{:S(2)}) collective-permute-start(bf16[704,1152]{1,0:T(8,128)(2,1)} %bitcast.35.refs_2_), channel_id=1, source_target_pairs={{0,8},{1,9},{2,10},{3,11},{4,12},{5,13},{6,14},{7,15},{8,0},{9,1},... | collective-permute-start | bytes 4866056 | tf_op jit(solution)/shard_map/ppermute | solution.py:510
  138.3 39.8 %collective-permute-start.14 = (bf16[704,1152]{1,0:T(8,128)(2,1)}, bf16[704,1152]{1,0:T(8,128)(2,1)}, u32[]{:S(2)}, u32[]{:S(2)}) collective-permute-start(bf16[704,1152]{1,0:T(8,128)(2,1)} %bitcast.35.refs_2_), channel_id=1, source_target_pairs={{0,16},{1,17},{2,18},{3,19},{4,20},{5,21},{6,22},{7,23},{8,24},{9,... | collective-permute-start | bytes 4866056 | tf_op jit(solution)/shard_map/ppermute | solution.py:510
  142.3 47.6 %collective-permute-start.15 = (bf16[704,1152]{1,0:T(8,128)(2,1)}, bf16[704,1152]{1,0:T(8,128)(2,1)}, u32[]{:S(2)}, u32[]{:S(2)}) collective-permute-start(bf16[704,1152]{1,0:T(8,128)(2,1)} %bitcast.33.refs_0_), channel_id=1, source_target_pairs={{0,8},{1,9},{2,10},{3,11},{4,12},{5,13},{6,14},{7,15},{8,0},{9,1},... | collective-permute-start | bytes 4866056 | tf_op jit(solution)/shard_map/ppermute | solution.py:510
  142.5 39.5 %collective-permute-start.13 = (bf16[704,1152]{1,0:T(8,128)(2,1)}, bf16[704,1152]{1,0:T(8,128)(2,1)}, u32[]{:S(2)}, u32[]{:S(2)}) collective-permute-start(bf16[704,1152]{1,0:T(8,128)(2,1)} %bitcast.33.refs_0_), channel_id=1, source_target_pairs={{0,1},{1,0},{2,3},{3,2},{4,5},{5,4},{6,7},{7,6},{8,9},{9,8},{10,11... | collective-permute-start | bytes 4866056 | tf_op jit(solution)/shard_map/ppermute | solution.py:510
  182.1 7.8 %collective-permute-start.16 = (bf16[704,1152]{1,0:T(8,128)(2,1)}, bf16[704,1152]{1,0:T(8,128)(2,1)}, u32[]{:S(2)}, u32[]{:S(2)}) collective-permute-start(bf16[704,1152]{1,0:T(8,128)(2,1)} %collective-permute-done.13.refs_1_), channel_id=1, source_target_pairs={{0,8},{1,9},{2,10},{3,11},{4,12},{5,13},{6,14},{7,15},{8,0},{9,1},... | collective-permute-start | bytes 4866056 | tf_op jit(solution)/shard_map/ppermute | solution.py:510
  182.1 7.8 %collective-permute-start.18 = (bf16[704,1152]{1,0:T(8,128)(2,1)}, bf16[704,1152]{1,0:T(8,128)(2,1)}, u32[]{:S(2)}, u32[]{:S(2)}) collective-permute-start(bf16[704,1152]{1,0:T(8,128)(2,1)} %collective-permute-done.14.refs_3_), channel_id=1, source_target_pairs={{0,8},{1,9},{2,10},{3,11},{4,12},{5,13},{6,14},{7,15},{8,0},{9,1},... | collective-permute-start | bytes 4866056 | tf_op jit(solution)/shard_map/ppermute | solution.py:510
  217.8 31.3 %collective-permute-start.19 = (bf16[4,2,352,1152]{3,2,1,0:T(8,128)(2,1)}, bf16[4,2,352,1152]{3,2,1,0:T(8,128)(2,1)}, u32[]{:S(2)}, u32[]{:S(2)}) collective-permute-start(bf16[4,2,352,1152]{3,2,1,0:T(8,128)(2,1)} %get-tuple-element.118), channel_id=1, source_target_pairs={{0,8},{1,9},{2,10},{3,11},{4,12},{5,13},{6,14},{7,15},{8,0},{9,1},... | collective-permute-start | bytes 19464200 | tf_op jit(solution)/shard_map/ppermute | solution.py:510
  254.5 38.2 %collective-permute-start.21 = (bf16[2,352,1152]{2,1,0:T(8,128)(2,1)}, bf16[2,352,1152]{2,1,0:T(8,128)(2,1)}, u32[]{:S(2)}, u32[]{:S(2)}) collective-permute-start(bf16[2,352,1152]{2,1,0:T(8,128)(2,1)} %get-tuple-element.191), channel_id=1, source_target_pairs={{0,16},{1,17},{2,18},{3,19},{4,20},{5,21},{6,22},{7,23},{8,24},{9,... | collective-permute-start | bytes 4866056 | tf_op jit(solution)/shard_map/ppermute | solution.py:510
  254.8 38.2 %collective-permute-start.20 = (bf16[2,352,1152]{2,1,0:T(8,128)(2,1)}, bf16[2,352,1152]{2,1,0:T(8,128)(2,1)}, u32[]{:S(2)}, u32[]{:S(2)}) collective-permute-start(bf16[2,352,1152]{2,1,0:T(8,128)(2,1)} %get-tuple-element.192), channel_id=1, source_target_pairs={{0,1},{1,0},{2,3},{3,2},{4,5},{5,4},{6,7},{7,6},{8,9},{9,8},{10,11... | collective-permute-start | bytes 4866056 | tf_op jit(solution)/shard_map/ppermute | solution.py:510
  313.0 40.3 %collective-permute-start.24 = (bf16[368,1152]{1,0:T(8,128)(2,1)}, bf16[368,1152]{1,0:T(8,128)(2,1)}, u32[]{:S(2)}, u32[]{:S(2)}) collective-permute-start(bf16[368,1152]{1,0:T(8,128)(2,1)} %get-tuple-element.128), channel_id=1, source_target_pairs={{0,1},{1,0},{2,3},{3,2},{4,5},{5,4},{6,7},{7,6},{8,9},{9,8},{10,11... | collective-permute-start | bytes 2543624 | tf_op jit(solution)/shard_map/ppermute | solution.py:631
  313.9 39.4 %collective-permute-start.22 = (bf16[2,2,88,1152]{3,2,0,1:T(8,128)(2,1)}, bf16[2,2,88,1152]{3,2,0,1:T(8,128)(2,1)}, u32[]{:S(2)}, u32[]{:S(2)}) collective-permute-start(bf16[2,2,88,1152]{3,2,0,1:T(8,128)(2,1)} %bitcast.166), channel_id=1, source_target_pairs={{0,16},{1,17},{2,18},{3,19},{4,20},{5,21},{6,22},{7,23},{8,24},{9,... | collective-permute-start | bytes 2433032 | tf_op jit(solution)/shard_map/ppermute | solution.py:510
  315.2 38.0 %collective-permute-start.23 = (bf16[2,2,88,1152]{3,2,0,1:T(8,128)(2,1)}, bf16[2,2,88,1152]{3,2,0,1:T(8,128)(2,1)}, u32[]{:S(2)}, u32[]{:S(2)}) collective-permute-start(bf16[2,2,88,1152]{3,2,0,1:T(8,128)(2,1)} %bitcast.165), channel_id=1, source_target_pairs={{0,1},{1,0},{2,3},{3,2},{4,5},{5,4},{6,7},{7,6},{8,9},{9,8},{10,11... | collective-permute-start | bytes 2433032 | tf_op jit(solution)/shard_map/ppermute | solution.py:510
  324.6 28.7 %copy-start.28 = (bf16[2,1,2,88,1152]{4,3,2,1,0:T(8,128)(2,1)S(1)}, bf16[2,1,2,88,1152]{4,3,2,1,0:T(8,128)(2,1)}, u32[]{:S(2)}) copy-start(bf16[2,1,2,88,1152]{4,3,2,1,0:T(8,128)(2,1)} %get-tuple-element.203) | copy-start | bytes 2433028
  354.8 33.7 %collective-permute-start.27 = (bf16[2,88,1152]{2,1,0:T(8,128)(2,1)S(1)}, bf16[2,88,1152]{2,1,0:T(8,128)(2,1)S(1)}, u32[]{:S(2)}, u32[]{:S(2)}) collective-permute-start(bf16[2,88,1152]{2,1,0:T(8,128)(2,1)S(1)} %slice_bitcast_fusion.6), channel_id=1, source_target_pairs={{0,2},{1,3},{2,0},{3,1},{4,6},{5,7},{6,4},{7,5},{8,10},{9,11},{10,... | collective-permute-start | bytes 1216520 | tf_op jit(solution)/shard_map/ppermute | solution.py:510
  357.1 31.6 %collective-permute-start.29 = (bf16[2,88,1152]{2,1,0:T(8,128)(2,1)S(1)}, bf16[2,88,1152]{2,1,0:T(8,128)(2,1)S(1)}, u32[]{:S(2)}, u32[]{:S(2)}) collective-permute-start(bf16[2,88,1152]{2,1,0:T(8,128)(2,1)S(1)} %get-tuple-element.213), channel_id=1, source_target_pairs={{0,6},{1,7},{2,4},{3,5},{4,2},{5,3},{6,0},{7,1},{8,14},{9,15},{10,... | collective-permute-start | bytes 1216520 | tf_op jit(solution)/shard_map/ppermute | solution.py:510
  359.6 53.2 %collective-permute-start.28 = (bf16[2,88,1152]{2,1,0:T(8,128)(2,1)S(1)}, bf16[2,88,1152]{2,1,0:T(8,128)(2,1)S(1)}, u32[]{:S(2)}, u32[]{:S(2)}) collective-permute-start(bf16[2,88,1152]{2,1,0:T(8,128)(2,1)S(1)} %get-tuple-element.214), channel_id=1, source_target_pairs={{0,4},{1,5},{2,6},{3,7},{4,0},{5,1},{6,2},{7,3},{8,12},{9,13},{10,... | collective-permute-start | bytes 1216520 | tf_op jit(solution)/shard_map/ppermute | solution.py:510
  377.3 35.8 %collective-permute-start.25 = (bf16[2,2,144,1152]{3,2,1,0:T(8,128)(2,1)}, bf16[2,2,144,1152]{3,2,1,0:T(8,128)(2,1)S(1)}, u32[]{:S(2)}, u32[]{:S(2)}) collective-permute-start(bf16[2,2,144,1152]{3,2,1,0:T(8,128)(2,1)} %get-tuple-element.140), channel_id=1, source_target_pairs={{0,8},{1,9},{2,10},{3,11},{4,12},{5,13},{6,14},{7,15},{8,0},{9,1},... | collective-permute-start | bytes 3981320 | tf_op jit(solution)/shard_map/ppermute | solution.py:510
  377.4 37.9 %collective-permute-start.26 = (bf16[4,144,1152]{2,1,0:T(8,128)(2,1)}, bf16[4,144,1152]{2,1,0:T(8,128)(2,1)S(1)}, u32[]{:S(2)}, u32[]{:S(2)}) collective-permute-start(bf16[4,144,1152]{2,1,0:T(8,128)(2,1)} %get-tuple-element.142), channel_id=1, source_target_pairs={{0,8},{1,9},{2,10},{3,11},{4,12},{5,13},{6,14},{7,15},{8,0},{9,1},... | collective-permute-start | bytes 3981320 | tf_op jit(solution)/shard_map/ppermute | solution.py:510
  388.5 65.1 %collective-permute-start.30 = (bf16[2,2,144,1152]{3,2,1,0:T(8,128)(2,1)}, bf16[2,2,144,1152]{3,2,1,0:T(8,128)(2,1)}, u32[]{:S(2)}, u32[]{:S(2)}) collective-permute-start(bf16[2,2,144,1152]{3,2,1,0:T(8,128)(2,1)} %get-tuple-element.139), channel_id=1, source_target_pairs={{0,8},{1,9},{2,10},{3,11},{4,12},{5,13},{6,14},{7,15},{8,0},{9,1},... | collective-permute-start | bytes 3981320 | tf_op jit(solution)/shard_map/ppermute | solution.py:510
  388.7 60.3 %collective-permute-start.33 = (bf16[4,144,1152]{2,1,0:T(8,128)(2,1)}, bf16[4,144,1152]{2,1,0:T(8,128)(2,1)}, u32[]{:S(2)}, u32[]{:S(2)}) collective-permute-start(bf16[4,144,1152]{2,1,0:T(8,128)(2,1)} %get-tuple-element.141), channel_id=1, source_target_pairs={{0,8},{1,9},{2,10},{3,11},{4,12},{5,13},{6,14},{7,15},{8,0},{9,1},... | collective-permute-start | bytes 3981320 | tf_op jit(solution)/shard_map/ppermute | solution.py:510
  414.5 34.5 %collective-permute-start.31 = (bf16[2,2,144,1152]{3,2,1,0:T(8,128)(2,1)}, bf16[2,2,144,1152]{3,2,1,0:T(8,128)(2,1)}, u32[]{:S(2)}, u32[]{:S(2)}) collective-permute-start(bf16[2,2,144,1152]{3,2,1,0:T(8,128)(2,1)} %add_convert_fusion.7), channel_id=1, source_target_pairs={{0,1},{1,0},{2,3},{3,2},{4,5},{5,4},{6,7},{7,6},{8,9},{9,8},{10,11... | collective-permute-start | bytes 3981320 | tf_op jit(solution)/shard_map/ppermute | solution.py:510
  416.7 32.2 %collective-permute-start.32 = (bf16[4,144,1152]{2,1,0:T(8,128)(2,1)}, bf16[4,144,1152]{2,1,0:T(8,128)(2,1)}, u32[]{:S(2)}, u32[]{:S(2)}) collective-permute-start(bf16[4,144,1152]{2,1,0:T(8,128)(2,1)} %add_convert_fusion.6), channel_id=1, source_target_pairs={{0,16},{1,17},{2,18},{3,19},{4,20},{5,21},{6,22},{7,23},{8,24},{9,... | collective-permute-start | bytes 3981320 | tf_op jit(solution)/shard_map/ppermute | solution.py:510
  452.1 18.4 %collective-permute-start.38 = (bf16[2,144,1152]{2,1,0:T(8,128)(2,1)}, bf16[2,144,1152]{2,1,0:T(8,128)(2,1)}, u32[]{:S(2)}, u32[]{:S(2)}) collective-permute-start(bf16[2,144,1152]{2,1,0:T(8,128)(2,1)} %slice.296), channel_id=1, source_target_pairs={{0,1},{1,0},{2,3},{3,2},{4,5},{5,4},{6,7},{7,6},{8,9},{9,8},{10,11... | collective-permute-start | bytes 1990664 | tf_op jit(solution)/shard_map/ppermute | solution.py:510
  456.7 13.9 %collective-permute-start.37 = (bf16[2,144,1152]{2,1,0:T(8,128)(2,1)}, bf16[2,144,1152]{2,1,0:T(8,128)(2,1)}, u32[]{:S(2)}, u32[]{:S(2)}) collective-permute-start(bf16[2,144,1152]{2,1,0:T(8,128)(2,1)} %slice_bitcast_fusion.2), channel_id=1, source_target_pairs={{0,16},{1,17},{2,18},{3,19},{4,20},{5,21},{6,22},{7,23},{8,24},{9,... | collective-permute-start | bytes 1990664 | tf_op jit(solution)/shard_map/ppermute | solution.py:510
  458.9 10.2 %collective-permute-start.36 = (f32[106,128]{1,0:T(8,128)}, f32[106,128]{1,0:T(8,128)}, u32[]{:S(2)}, u32[]{:S(2)}) collective-permute-start(f32[106,128]{1,0:T(8,128)} %bitcast.56), channel_id=1, source_target_pairs={{0,6},{1,7},{2,4},{3,5},{4,2},{5,3},{6,0},{7,1},{8,14},{9,15},{10,... | collective-permute-start | bytes 162824 | tf_op jit(solution)/shard_map/ppermute | solution.py:510
  462.2 6.8 %collective-permute-start.35 = (f32[106,128]{1,0:T(8,128)}, f32[106,128]{1,0:T(8,128)}, u32[]{:S(2)}, u32[]{:S(2)}) collective-permute-start(f32[106,128]{1,0:T(8,128)} %bitcast.56), channel_id=1, source_target_pairs={{0,4},{1,5},{2,6},{3,7},{4,0},{5,1},{6,2},{7,3},{8,12},{9,13},{10,... | collective-permute-start | bytes 162824 | tf_op jit(solution)/shard_map/ppermute | solution.py:510
  462.2 6.8 %collective-permute-start.34 = (f32[106,128]{1,0:T(8,128)}, f32[106,128]{1,0:T(8,128)}, u32[]{:S(2)}, u32[]{:S(2)}) collective-permute-start(f32[106,128]{1,0:T(8,128)} %bitcast.56), channel_id=1, source_target_pairs={{0,2},{1,3},{2,0},{3,1},{4,6},{5,7},{6,4},{7,5},{8,10},{9,11},{10,... | collective-permute-start | bytes 162824 | tf_op jit(solution)/shard_map/ppermute | solution.py:510
  476.1 3.8 collective-permute-start.43
  476.1 8.0 %collective-permute-start.44 = (bf16[272,288]{1,0:T(8,128)(2,1)S(1)}, bf16[272,288]{1,0:T(8,128)(2,1)S(1)}, u32[]{:S(2)}, u32[]{:S(2)}) collective-permute-start(bf16[272,288]{1,0:T(8,128)(2,1)S(1)} %copy-done.63), channel_id=1, source_target_pairs={{0,16},{1,17},{2,18},{3,19},{4,20},{5,21},{6,22},{7,23},{8,24},{9,... | collective-permute-start | bytes 470024 | tf_op jit(solution)/shard_map/ppermute | solution.py:510
  478.0 9.9 %collective-permute-start.45 = (bf16[272,288]{1,0:T(8,128)(2,1)S(1)}, bf16[272,288]{1,0:T(8,128)(2,1)S(1)}, u32[]{:S(2)}, u32[]{:S(2)}) collective-permute-start(bf16[272,288]{1,0:T(8,128)(2,1)S(1)} %copy-done.62), channel_id=1, source_target_pairs={{0,24},{1,25},{2,26},{3,27},{4,28},{5,29},{6,30},{7,31},{8,16},{9,... | collective-permute-start | bytes 470024 | tf_op jit(solution)/shard_map/ppermute | solution.py:510
  478.1 33.9 %collective-permute-start.39 = (bf16[368,1152]{1,0:T(8,128)(2,1)}, bf16[368,1152]{1,0:T(8,128)(2,1)}, u32[]{:S(2)}, u32[]{:S(2)}) collective-permute-start(bf16[368,1152]{1,0:T(8,128)(2,1)} %slice.248), channel_id=1, source_target_pairs={{0,1},{1,0},{2,3},{3,2},{4,5},{5,4},{6,7},{7,6},{8,9},{9,8},{10,11... | collective-permute-start | bytes 2543624 | tf_op jit(solution)/shard_map/ppermute | solution.py:631
  479.4 23.6 %collective-permute-start.40 = (bf16[144,1152]{1,0:T(8,128)(2,1)}, bf16[144,1152]{1,0:T(8,128)(2,1)}, u32[]{:S(2)}, u32[]{:S(2)}) collective-permute-start(bf16[144,1152]{1,0:T(8,128)(2,1)} %slice_bitcast_fusion.10), channel_id=1, source_target_pairs={{0,2},{1,3},{2,0},{3,1},{4,6},{5,7},{6,4},{7,5},{8,10},{9,11},{10,... | collective-permute-start | bytes 995336 | tf_op jit(solution)/shard_map/ppermute | solution.py:510
  479.9 23.1 %collective-permute-start.42 = (bf16[144,1152]{1,0:T(8,128)(2,1)}, bf16[144,1152]{1,0:T(8,128)(2,1)}, u32[]{:S(2)}, u32[]{:S(2)}) collective-permute-start(bf16[144,1152]{1,0:T(8,128)(2,1)} %get-tuple-element.215), channel_id=1, source_target_pairs={{0,6},{1,7},{2,4},{3,5},{4,2},{5,3},{6,0},{7,1},{8,14},{9,15},{10,... | collective-permute-start | bytes 995336 | tf_op jit(solution)/shard_map/ppermute | solution.py:510
  484.1 28.0 %collective-permute-start.41 = (bf16[144,1152]{1,0:T(8,128)(2,1)}, bf16[144,1152]{1,0:T(8,128)(2,1)}, u32[]{:S(2)}, u32[]{:S(2)}) collective-permute-start(bf16[144,1152]{1,0:T(8,128)(2,1)} %get-tuple-element.216), channel_id=1, source_target_pairs={{0,4},{1,5},{2,6},{3,7},{4,0},{5,1},{6,2},{7,3},{8,12},{9,13},{10,... | collective-permute-start | bytes 995336 | tf_op jit(solution)/shard_map/ppermute | solution.py:510
  514.2 8.9 %collective-permute-start.46 = (f32[106,128]{1,0:T(8,128)S(1)}, f32[106,128]{1,0:T(8,128)S(1)}, u32[]{:S(2)}, u32[]{:S(2)}) collective-permute-start(f32[106,128]{1,0:T(8,128)S(1)} %copy-done.42), channel_id=1, source_target_pairs={{0,1},{1,0},{2,3},{3,2},{4,5},{5,4},{6,7},{7,6},{8,9},{9,8},{10,11... | collective-permute-start | bytes 162824 | tf_op jit(solution)/shard_map/ppermute | solution.py:510
  517.7 7.2 %collective-permute-start.50 = (bf16[144,288]{1,0:T(8,128)(2,1)}, bf16[144,288]{1,0:T(8,128)(2,1)S(1)}, u32[]{:S(2)}, u32[]{:S(2)}) collective-permute-start(bf16[144,288]{1,0:T(8,128)(2,1)} %get-tuple-element.184), channel_id=1, source_target_pairs={{0,8},{1,9},{2,10},{3,11},{4,12},{5,13},{6,14},{7,15},{8,0},{9,1},... | collective-permute-start | bytes 248840 | tf_op jit(solution)/shard_map/ppermute | solution.py:510
  517.7 7.3 %collective-permute-start.51 = (bf16[144,288]{1,0:T(8,128)(2,1)}, bf16[144,288]{1,0:T(8,128)(2,1)S(1)}, u32[]{:S(2)}, u32[]{:S(2)}) collective-permute-start(bf16[144,288]{1,0:T(8,128)(2,1)} %get-tuple-element.185), channel_id=1, source_target_pairs={{0,16},{1,17},{2,18},{3,19},{4,20},{5,21},{6,22},{7,23},{8,24},{9,... | collective-permute-start | bytes 248840 | tf_op jit(solution)/shard_map/ppermute | solution.py:510
  519.7 6.0 %collective-permute-start.52 = (bf16[144,288]{1,0:T(8,128)(2,1)}, bf16[144,288]{1,0:T(8,128)(2,1)S(1)}, u32[]{:S(2)}, u32[]{:S(2)}) collective-permute-start(bf16[144,288]{1,0:T(8,128)(2,1)} %get-tuple-element.186), channel_id=1, source_target_pairs={{0,24},{1,25},{2,26},{3,27},{4,28},{5,29},{6,30},{7,31},{8,16},{9,... | collective-permute-start | bytes 248840 | tf_op jit(solution)/shard_map/ppermute | solution.py:510
  523.1 7.5 %collective-permute-start.49 = (f32[106,128]{1,0:T(8,128)S(1)}, f32[106,128]{1,0:T(8,128)S(1)}, u32[]{:S(2)}, u32[]{:S(2)}) collective-permute-start(f32[106,128]{1,0:T(8,128)S(1)} %add.246), channel_id=1, source_target_pairs={{0,24},{1,25},{2,26},{3,27},{4,28},{5,29},{6,30},{7,31},{8,16},{9,... | collective-permute-start | bytes 162824 | tf_op jit(solution)/shard_map/ppermute | solution.py:510
  524.7 5.8 %collective-permute-start.48 = (f32[106,128]{1,0:T(8,128)S(1)}, f32[106,128]{1,0:T(8,128)S(1)}, u32[]{:S(2)}, u32[]{:S(2)}) collective-permute-start(f32[106,128]{1,0:T(8,128)S(1)} %add.246), channel_id=1, source_target_pairs={{0,16},{1,17},{2,18},{3,19},{4,20},{5,21},{6,22},{7,23},{8,24},{9,... | collective-permute-start | bytes 162824 | tf_op jit(solution)/shard_map/ppermute | solution.py:510
  524.9 5.6 %collective-permute-start.47 = (f32[106,128]{1,0:T(8,128)S(1)}, f32[106,128]{1,0:T(8,128)S(1)}, u32[]{:S(2)}, u32[]{:S(2)}) collective-permute-start(f32[106,128]{1,0:T(8,128)S(1)} %add.246), channel_id=1, source_target_pairs={{0,8},{1,9},{2,10},{3,11},{4,12},{5,13},{6,14},{7,15},{8,0},{9,1},... | collective-permute-start | bytes 162824 | tf_op jit(solution)/shard_map/ppermute | solution.py:510
  (63 other events, 397.5 us)
Sparse Core Ops, SparseCore 0:
  20.6 130.4 all-gather.4
  154.5 75.9 all-gather.6
  316.6 142.2 reduce-scatter.1

commit v6 on v5

--- a/solution.py
+++ b/solution.py
@@ -754,7 +754,7 @@
         *sums, units.own, own_sum = hop_mlp(
             hop_bias[1], hop_three, (0, 4 * hop_rows), hop_rows, 8, sums
         )
-        up_sums.append(jnp.concatenate([sibling_sum[:, 0], own_sum[:, 0]]))
+        up_sums.append((sibling_sum, own_sum))
         units.arrived = after(units.arrived, sums)
     bulk = partial(
         mlp,
@@ -773,7 +773,7 @@
         units.moved = after(units.moved, sums)
     else:
         *sums, bulk_grads, up_sum = bulk()
-    up_sums = [up_sum[:, 0]] + up_sums
+    up_sums = [(up_sum,)] + up_sums
     bulk_grads = bulk_grads.reshape(32, 2, devices // 32, -1, width).transpose(0, 2, 1, 3, 4)
     bulk_owned = lax.psum_scatter(
         bulk_grads.reshape(2 * 32 * rows, width), everyone, scatter_dimension=0, tiled=True
@@ -808,9 +808,10 @@
         input_full, input_low, first_sums = norm_back(
             x_slot, first_terms, attn_norm_gain, grad_middle
         )
+        attns.moved = after(attns.moved, input_low)
+        units.moved = after(units.moved, attns.moved)
+        attns_third = attns.third()
         units_owned = units.along_z()
-        attns.moved = after(attns.moved, units_owned)
-        attns_third = attns.third()
     else:
         grads = back(grad_branch, heads, 4)
         first_terms = product(grads.reshape(-1, tokens), qkv_rows, 0, 0)
@@ -821,6 +822,7 @@
         layer_out = both_micros(out_kept, out_other)
 
     grads, second_sums, up_sums = after((grads, second_sums, up_sums), input_low)
+    up_sums = [jnp.concatenate([part[:, 0] for part in parts]) for parts in up_sums]
     total_over = lambda i: jnp.sum(grads[i], axis=1, dtype=wide)
     small = jnp.concatenate(
         [

time: 547 us -> 548 us (level)
    unnamed x150 -> x164, local copies, waits for them, and re-layouts: 18.7 us -> 24.3 us
    ppermute x49, waiting for transfers between devices: 139 us -> 133 us  [send(): return lax.ppermute(values, everyone, pairs)]
  transfers between devices with their start and end apart: 56 -> 56, of which waited for: 20 -> 21; matrix products, arithmetic and copies ran while one was open for 19% -> 19% of each run, Pallas kernels for 31% -> 30%
where the time goes in v6:
time: 548 us; the launch traced here: 539 us
  Pallas kernels  175 us (32%)
  waiting for transfers between devices  163 us (30%)
  other arithmetic  59.8 us (11%)
  local copies, waits for them, and re-layouts  52.6 us (10%)
  starting transfers between devices  46.6 us (9%)
  matrix products  27 us (5%)
  between operations  14.9 us (3%)
    ppermute x49, waiting for transfers between devices, send(): return lax.ppermute(values, everyone, pairs)  133 us
    pallas_call x3, Pallas kernels, mlp(): pl.pallas_call(partial(mlp_kernel, before is not None, (starts, rows, gro...  89.5 us
    ppermute x49, starting transfers between devices, send(): return lax.ppermute(values, everyone, pairs)  42.4 us
    pallas_call x1, Pallas kernels, attend_back(): pl.pallas_call(partial(attend_back_kernel, step_heads), grid=(steps,), in...  28.8 us
    convert_element_type x12, other arithmetic, add_low(): return total.astype(low)  28.6 us
    dot_general x3, matrix products, product(): lax.dot_general(left, right, (((left_dim,), (right_dim,)), ((), ())), pre...  26.6 us
    unnamed x164, local copies, waits for them, and re-layouts  24.3 us
    ppermute x4, waiting for transfers between devices, swap(): return lax.ppermute(values, 'tensor', pairs)  23 us
  transfers between devices with their start and end apart: 56, of which 21 were waited for; matrix products, arithmetic and copies ran while one was open for 19% of the time, Pallas kernels for 30%

profile of v6, /device:TPU:0, one launch (start us, length us, event | category | flops | bytes accessed | tf_op | source)
XLA Modules:
  0.0 538.6 jit_solution(17303421132003540000)
XLA Ops:
  9.7 2.5 collective-permute-start.2
  12.3 3.8 collective-permute-done.2.refs_2_
  16.1 2.0 collective-permute-done.3.refs_3_
  18.7 2.2 unite.2
  22.1 1.6 collective-permute-start
  25.4 1.5 collective-permute-start.6
  28.9 4.7 collective-permute-done.6.refs_2_
  33.6 6.1 %collective-permute-done.7.refs_3_ = bf16[272,288]{1,0:T(8,128)(2,1)} collective-permute-done((bf16[272,288]{1,0:T(8,128)(2,1)}, bf16[272,288]{1,0:T(8,128)(2,1)}, u32[]{:S(2)}, u32[]{:S(2)}) %collective-permute-start.7) | collective-permute-done | bytes 156704 | tf_op jit(solution)/shard_map/ppermute | solution.py:510
  39.7 2.6 unite.3
  42.3 3.6 collective-permute-start.10
  50.3 23.0 %collective-permute-done.4 = bf16[368,1152]{1,0:T(8,128)(2,1)S(1)} collective-permute-done((bf16[368,1152]{1,0:T(8,128)(2,1)S(1)}, bf16[368,1152]{1,0:T(8,128)(2,1)S(1)}, u32[]{:S(2)}, u32[]{:S(2)}) %collective-permute-start.4) | collective-permute-done | bytes 847904 | tf_op jit(solution)/shard_map/ppermute | solution.py:631
  74.6 21.1 %collective-permute-done.9 = bf16[176,1152]{1,0:T(8,128)(2,1)S(1)} collective-permute-done((bf16[176,1152]{1,0:T(8,128)(2,1)}, bf16[176,1152]{1,0:T(8,128)(2,1)S(1)}, u32[]{:S(2)}, u32[]{:S(2)}) %collective-permute-start.9) | collective-permute-done | bytes 405536 | tf_op jit(solution)/shard_map/ppermute | solution.py:510
  101.7 33.1 %collective-permute-done.12 = bf16[352,1152]{1,0:T(8,128)(2,1)} collective-permute-done((bf16[352,1152]{1,0:T(8,128)(2,1)}, bf16[352,1152]{1,0:T(8,128)(2,1)}, u32[]{:S(2)}, u32[]{:S(2)}) %collective-permute-start.12) | collective-permute-done | bytes 811040 | tf_op jit(solution)/shard_map/ppermute | solution.py:510
  135.4 2.5 pad_maximum_fusion.3
  138.9 2.4 pad_maximum_fusion.2
  142.7 6.8 %all-gather.5.cloned.1.call-done.weights_ref = bf16[4608,1152]{1,0:T(8,128)(2,1)} async-done(((bf16[144,1152]{1,0:T(8,128)(2,1)}), bf16[4608,1152]{1,0:T(8,128)(2,1)}) %all-gather.5.cloned.1.call-update) | async-done | bytes 10616848 | tf_op jit(solution)/shard_map/all_gather | solution.py:669
  149.5 11.1 %add_convert_fusion.query_ref.key_ref.value_ref = bf16[3456,736]{1,0:T(8,128)(2,1)} fusion(bf16[736,1152]{1,0:T(8,128)(2,1)S(1)} %fusion.11.normed_ref, bf16[4608,1152]{1,0:T(8,128)(2,1)} %all-gather.5.cloned.1.call-done.weights_ref, f32[3456]{0:T(1024)S(1)} %pad_maximum_fusion.11), kind=kOutput, calls=%fused_computation | convolution fusion | flops 5865578496 | bytes 14759424 | tf_op jit(solution)/shard_map/dot_general | solution.py:23
  160.7 15.3 %attend.1 = (bf16[1152,736]{1,0:T(8,128)(2,1)S(1)}, f32[16,1,736]{2,1,0:T(1,128)S(1)}) custom-call(bf16[3456,736]{1,0:T(8,128)(2,1)} %add_convert_fusion.query_ref.key_ref.value_ref, bf16[3456,736]{1,0:T(8,128)(2,1)} %add_convert_fusion.query_ref.key_ref.value_ref, bf16[3456,736]{1,0:T(8,128)(2,1)} %add_convert_fusion.query_ref.key_ref.value_ref, ...), custom_call_target="tpu_custom_call" | custom-call | flops 1109393408 | bytes 1048576 | tf_op jit(solution)/shard_map/attend/pallas_call | solution.py:80
  176.9 4.2 collective-permute-done.13.refs_1_
  181.6 4.8 fusion.43
  187.0 1.8 add_convert_fusion.1.normed_ref
  188.9 27.7 %mlp.3 = (f32[736,1152]{1,0:T(8,128)}, f32[736,1152]{1,0:T(8,128)}, bf16[4,2,352,1152]{3,2,1,0:T(8,128)(2,1)}, f32[1408,1]{1,0:T(8,128)}) custom-call(bf16[736,1152]{1,0:T(8,128)(2,1)} %add_convert_fusion.1.normed_ref, bf16[736,1152]{1,0:T(8,128)(2,1)} %pad_maximum_fusion.1.grad_ref.base_ref, f32[1408,1]{1,0:T(8,128)} %split.15.bias_ref, ...), custom_call_target="tpu_custom_call" | custom-call | flops 2387607552 | bytes 1048576 | tf_op jit(solution)/shard_map/mlp/pallas_call | solution.py:302
  217.8 30.2 %mlp.4 = (f32[736,1152]{1,0:T(8,128)}, f32[736,1152]{1,0:T(8,128)}, bf16[4,2,352,1152]{3,2,1,0:T(8,128)(2,1)}, f32[1408,1]{1,0:T(8,128)}) custom-call(bf16[736,1152]{1,0:T(8,128)(2,1)} %add_convert_fusion.1.normed_ref, bf16[736,1152]{1,0:T(8,128)(2,1)} %pad_maximum_fusion.1.grad_ref.base_ref, ...), custom_call_target="tpu_custom_call", output_to_operand_aliasing={{0}: (7, {}), {1}: (8, {})} | custom-call | flops 2387607552 | bytes 1048576 | tf_op jit(solution)/shard_map/mlp/pallas_call | solution.py:302
  248.0 5.3 fusion.16
  254.4 1.9 collective-permute-start.21
  257.8 31.6 %mlp.5 = (f32[736,1152]{1,0:T(8,128)}, f32[736,1152]{1,0:T(8,128)}, bf16[32,2,48,1152]{3,2,1,0:T(8,128)(2,1)}, f32[1536,1]{1,0:T(8,128)}) custom-call(bf16[736,1152]{1,0:T(8,128)(2,1)} %add_convert_fusion.1.normed_ref, bf16[736,1152]{1,0:T(8,128)(2,1)} %pad_maximum_fusion.1.grad_ref.base_ref, ...), custom_call_target="tpu_custom_call", output_to_operand_aliasing={{0}: (4, {}), {1}: (5, {})} | custom-call | flops 2604662784 | bytes 1048576 | tf_op jit(solution)/shard_map/mlp/pallas_call | solution.py:302
  289.4 2.4 collective-permute-done.20
  292.6 5.0 fusion.12
  301.6 6.8 %norm_back.2 = (f32[736,1152]{1,0:T(8,128)S(1)}, bf16[736,1152]{1,0:T(8,128)(2,1)S(1)}, f32[4,1152]{1,0:T(4,128)S(1)}, bf16[368,1152]{1,0:T(8,128)(2,1)S(1)}, bf16[368,1152]{1,0:T(8,128)(2,1)}) custom-call(f32[736,1152]{1,0:T(8,128)S(1)} %get-tuple-element.242.values_ref, f32[736,1152]{1,0:T(8,128)} %get-tuple-element.130.grad_ref, ...), custom_call_target="tpu_custom_call" | custom-call | flops 847872 | bytes 847872 | tf_op jit(solution)/shard_map/norm_back/pallas_call | solution.py:188
  309.6 1.7 copy-done.10
  314.3 1.5 collective-permute-start.23
  315.9 1.4 copy-done.4
  318.9 28.8 %attend_back.1.grads_ref = bf16[3,1152,736]{2,1,0:T(8,128)(2,1)} custom-call(bf16[3456,736]{1,0:T(8,128)(2,1)} %add_convert_fusion.query_ref.key_ref.value_ref, bf16[3456,736]{1,0:T(8,128)(2,1)} %add_convert_fusion.query_ref.key_ref.value_ref, bf16[3456,736]{1,0:T(8,128)(2,1)} %add_convert_fusion.query_ref.key_ref.value_ref, f32[736,1]{1,0:T(8,128)S(1)} %copy-done.9, ...), custom_call_target="tpu_custom_call" | custom-call | flops 1109393408 | bytes 1048576 | tf_op jit(solution)/shard_map/attend_back/pallas_call | solution.py:103
  347.6 2.9 collective-permute-done.23
  355.1 16.9 %kinds_grad.1 = (bf16[2,2,144,1152]{3,2,1,0:T(8,128)(2,1)S(1)}, bf16[2,2,144,1152]{3,2,1,0:T(8,128)(2,1)S(1)}, bf16[4,144,1152]{2,1,0:T(8,128)(2,1)S(1)}, bf16[4...) custom-call(s32[2]{0:T(128)S(1)} %pad_add_fusion.kind_ref, ...), custom_call_target="tpu_custom_call" | custom-call | flops 976748544 | bytes 1048576 | tf_op jit(solution)/shard_map/kinds_grad/pallas_call | solution.py:383
  375.9 2.0 collective-permute-start.29
  378.4 3.1 add_convert_fusion.6
  382.6 2.8 add_convert_fusion.7
  385.4 30.5 %collective-permute-done.28 = bf16[2,88,1152]{2,1,0:T(8,128)(2,1)S(1)} collective-permute-done((bf16[2,88,1152]{2,1,0:T(8,128)(2,1)}, bf16[2,88,1152]{2,1,0:T(8,128)(2,1)S(1)}, u32[]{:S(2)}, u32[]{:S(2)}) %collective-permute-start.28) | collective-permute-done | bytes 405536 | tf_op jit(solution)/shard_map/ppermute | solution.py:510
  416.9 10.7 %fusion.2.grad_ref = f32[736,1152]{1,0:T(8,128)S(1)} fusion(bf16[3456,736]{1,0:T(8,128)(2,1)} %bitcast.171, bf16[4608,1152]{1,0:T(8,128)(2,1)} %all-gather.5.cloned.1.call-done.weights_ref), kind=kOutput, calls=%fused_computation.3 | convolution fusion | flops 5860491264 | bytes 16662528 | tf_op jit(solution)/shard_map/dot_general | solution.py:23
  429.2 3.3 norm_back.3
  432.4 1.7 copy-done.15
  435.4 1.5 reduce.4
  442.0 2.6 convert_reduce_fusion.1
  447.9 6.7 %collective-permute-done.30 = bf16[2,2,144,1152]{3,2,1,0:T(8,128)(2,1)} collective-permute-done((bf16[2,2,144,1152]{3,2,1,0:T(8,128)(2,1)}, bf16[2,2,144,1152]{3,2,1,0:T(8,128)(2,1)}, u32[]{:S(2)}, u32[]{:S(2)}) %collective-permute-start.30) | collective-permute-done | bytes 1327136 | tf_op jit(solution)/shard_map/ppermute | solution.py:510
  454.6 2.3 add_convert_fusion.4
  458.9 2.2 add_convert_fusion.5
  465.2 1.6 collective-permute-start.35
  466.8 2.0 collective-permute-start.36
  468.8 3.1 maximum_select_fusion.1
  471.8 2.7 divide.2
  474.5 1.5 add_add_fusion.1
  485.3 2.2 collective-permute-start.42
  488.7 3.5 collective-permute-done.45.refs_3_
  492.9 2.5 settle.2
  497.9 1.8 fusion.38
  501.0 2.5 pad_maximum_fusion.7
  503.6 6.3 %collective-permute-done.41 = bf16[144,1152]{1,0:T(8,128)(2,1)} collective-permute-done((bf16[144,1152]{1,0:T(8,128)(2,1)}, bf16[144,1152]{1,0:T(8,128)(2,1)}, u32[]{:S(2)}, u32[]{:S(2)}) %collective-permute-start.41) | collective-permute-done | bytes 331808 | tf_op jit(solution)/shard_map/ppermute | solution.py:510
  509.8 2.2 collective-permute-done.40
  512.1 2.1 fusion.26.refs_0_
  514.2 2.1 divide.3
  520.3 2.0 maximum_select_fusion
  525.0 2.0 settle.3
  527.0 2.2 slice_bitcast_fusion.11
  (343 shorter events, 91.1 us)
Async XLA Ops:
  7.2 142.3 %all-gather.5.cloned.1.call-start = ((), (), s32[]{:S(2)}) async-start(), calls=%async_computation.2 | async-start | bytes 10948608 | tf_op jit(solution)/shard_map/all_gather | solution.py:669
  9.2 3.1 collective-permute-start.1
  9.7 6.4 %collective-permute-start.2 = (bf16[144,288]{1,0:T(8,128)(2,1)S(1)}, bf16[144,288]{1,0:T(8,128)(2,1)S(1)}, u32[]{:S(2)}, u32[]{:S(2)}) collective-permute-start(bf16[144,288]{1,0:T(8,128)(2,1)S(1)} %get-tuple-element.226), channel_id=1, source_target_pairs={{0,16},{1,17},{2,18},{3,19},{4,20},{5,21},{6,22},{7,23},{8,24},{9,... | collective-permute-start | bytes 248840 | tf_op jit(solution)/shard_map/ppermute | solution.py:510
  12.2 5.9 %collective-permute-start.3 = (bf16[144,288]{1,0:T(8,128)(2,1)S(1)}, bf16[144,288]{1,0:T(8,128)(2,1)S(1)}, u32[]{:S(2)}, u32[]{:S(2)}) collective-permute-start(bf16[144,288]{1,0:T(8,128)(2,1)S(1)} %get-tuple-element.225), channel_id=1, source_target_pairs={{0,24},{1,25},{2,26},{3,27},{4,28},{5,29},{6,30},{7,31},{8,16},{9,... | collective-permute-start | bytes 248840 | tf_op jit(solution)/shard_map/ppermute | solution.py:510
  20.9 236.8 %all-gather.7.cloned.1.call-start = ((), (), s32[]{:S(2)}) async-start(), calls=%async_computation.3 | async-start | bytes 7299072 | tf_op jit(solution)/shard_map/all_gather | solution.py:672
  22.1 27.5 %copy-start.23 = (bf16[368,1152]{1,0:T(8,128)(2,1)}, bf16[368,1152]{1,0:T(8,128)(2,1)S(1)}, u32[]{:S(2)}) copy-start(bf16[368,1152]{1,0:T(8,128)(2,1)S(1)} %get-tuple-element.203) | copy-start | bytes 2543620
  22.1 24.6 %collective-permute-start = (bf16[368,1152]{1,0:T(8,128)(2,1)}, bf16[368,1152]{1,0:T(8,128)(2,1)S(1)}, u32[]{:S(2)}, u32[]{:S(2)}) collective-permute-start(bf16[368,1152]{1,0:T(8,128)(2,1)} %get-tuple-element.204), channel_id=1, source_target_pairs={{0,1},{1,0},{2,3},{3,2},{4,5},{5,4},{6,7},{7,6},{8,9},{9,8},{10,11... | collective-permute-start | bytes 2543624 | tf_op jit(solution)/shard_map/ppermute | solution.py:631
  25.4 3.5 collective-permute-start.5
  25.4 8.3 %collective-permute-start.6 = (bf16[272,288]{1,0:T(8,128)(2,1)}, bf16[272,288]{1,0:T(8,128)(2,1)}, u32[]{:S(2)}, u32[]{:S(2)}) collective-permute-start(bf16[272,288]{1,0:T(8,128)(2,1)} %get-tuple-element.218), channel_id=1, source_target_pairs={{0,16},{1,17},{2,18},{3,19},{4,20},{5,21},{6,22},{7,23},{8,24},{9,... | collective-permute-start | bytes 470024 | tf_op jit(solution)/shard_map/ppermute | solution.py:510
  26.8 12.9 %collective-permute-start.7 = (bf16[272,288]{1,0:T(8,128)(2,1)}, bf16[272,288]{1,0:T(8,128)(2,1)}, u32[]{:S(2)}, u32[]{:S(2)}) collective-permute-start(bf16[272,288]{1,0:T(8,128)(2,1)} %get-tuple-element.217), channel_id=1, source_target_pairs={{0,24},{1,25},{2,26},{3,27},{4,28},{5,29},{6,30},{7,31},{8,16},{9,... | collective-permute-start | bytes 470024 | tf_op jit(solution)/shard_map/ppermute | solution.py:510
  42.3 32.4 %collective-permute-start.10 = (bf16[176,1152]{1,0:T(8,128)(2,1)}, bf16[176,1152]{1,0:T(8,128)(2,1)S(1)}, u32[]{:S(2)}, u32[]{:S(2)}) collective-permute-start(bf16[176,1152]{1,0:T(8,128)(2,1)} %get-tuple-element.109), channel_id=1, source_target_pairs={{0,6},{1,7},{2,4},{3,5},{4,2},{5,3},{6,0},{7,1},{8,14},{9,15},{10,... | collective-permute-start | bytes 1216520 | tf_op jit(solution)/shard_map/ppermute | solution.py:510
  45.9 28.8 %collective-permute-start.8 = (bf16[176,1152]{1,0:T(8,128)(2,1)}, bf16[176,1152]{1,0:T(8,128)(2,1)S(1)}, u32[]{:S(2)}, u32[]{:S(2)}) collective-permute-start(bf16[176,1152]{1,0:T(8,128)(2,1)} %get-tuple-element.109), channel_id=1, source_target_pairs={{0,2},{1,3},{2,0},{3,1},{4,6},{5,7},{6,4},{7,5},{8,10},{9,11},{10,... | collective-permute-start | bytes 1216520 | tf_op jit(solution)/shard_map/ppermute | solution.py:510
  45.9 49.9 %collective-permute-start.9 = (bf16[176,1152]{1,0:T(8,128)(2,1)}, bf16[176,1152]{1,0:T(8,128)(2,1)S(1)}, u32[]{:S(2)}, u32[]{:S(2)}) collective-permute-start(bf16[176,1152]{1,0:T(8,128)(2,1)} %get-tuple-element.109), channel_id=1, source_target_pairs={{0,4},{1,5},{2,6},{3,7},{4,0},{5,1},{6,2},{7,3},{8,12},{9,13},{10,... | collective-permute-start | bytes 1216520 | tf_op jit(solution)/shard_map/ppermute | solution.py:510
  48.1 25.1 %collective-permute-start.4 = (bf16[368,1152]{1,0:T(8,128)(2,1)S(1)}, bf16[368,1152]{1,0:T(8,128)(2,1)S(1)}, u32[]{:S(2)}, u32[]{:S(2)}) collective-permute-start(bf16[368,1152]{1,0:T(8,128)(2,1)S(1)} %copy-done.45), channel_id=1, source_target_pairs={{0,1},{1,0},{2,3},{3,2},{4,5},{5,4},{6,7},{7,6},{8,9},{9,8},{10,11... | collective-permute-start | bytes 2543624 | tf_op jit(solution)/shard_map/ppermute | solution.py:631
  50.3 99.2 %copy-start.27 = (bf16[736,1152]{1,0:T(8,128)(2,1)}, bf16[736,1152]{1,0:T(8,128)(2,1)S(1)}, u32[]{:S(2)}) copy-start(bf16[736,1152]{1,0:T(8,128)(2,1)S(1)} %fusion.11.normed_ref) | copy-start | bytes 5087236
  74.6 25.1 %copy-start.42 = (bf16[176,1152]{1,0:T(8,128)(2,1)}, bf16[176,1152]{1,0:T(8,128)(2,1)S(1)}, u32[]{:S(2)}) copy-start(bf16[176,1152]{1,0:T(8,128)(2,1)S(1)} %collective-permute-done.10) | copy-start | bytes 1216516
  74.6 25.1 %copy-start.40 = (bf16[176,1152]{1,0:T(8,128)(2,1)}, bf16[176,1152]{1,0:T(8,128)(2,1)S(1)}, u32[]{:S(2)}) copy-start(bf16[176,1152]{1,0:T(8,128)(2,1)S(1)} %collective-permute-done.8) | copy-start | bytes 1216516
  96.8 38.0 %collective-permute-start.12 = (bf16[352,1152]{1,0:T(8,128)(2,1)}, bf16[352,1152]{1,0:T(8,128)(2,1)}, u32[]{:S(2)}, u32[]{:S(2)}) collective-permute-start(bf16[352,1152]{1,0:T(8,128)(2,1)} %bitcast.31), channel_id=1, source_target_pairs={{0,1},{1,0},{2,3},{3,2},{4,5},{5,4},{6,7},{7,6},{8,9},{9,8},{10,11... | collective-permute-start | bytes 2433032 | tf_op jit(solution)/shard_map/ppermute | solution.py:510
  98.6 36.9 %collective-permute-start.11 = (bf16[352,1152]{1,0:T(8,128)(2,1)}, bf16[352,1152]{1,0:T(8,128)(2,1)}, u32[]{:S(2)}, u32[]{:S(2)}) collective-permute-start(bf16[352,1152]{1,0:T(8,128)(2,1)} %bitcast.28), channel_id=1, source_target_pairs={{0,16},{1,17},{2,18},{3,19},{4,20},{5,21},{6,22},{7,23},{8,24},{9,... | collective-permute-start | bytes 2433032 | tf_op jit(solution)/shard_map/ppermute | solution.py:510
  99.8 35.6 %copy-start.43 = (bf16[176,1152]{1,0:T(8,128)(2,1)S(1)}, bf16[176,1152]{1,0:T(8,128)(2,1)}, u32[]{:S(2)}) copy-start(bf16[176,1152]{1,0:T(8,128)(2,1)} %copy-done.42) | copy-start | bytes 1216516
  100.0 60.6 %copy-start.8 = (f32[736,1]{1,0:T(8,128)}, f32[736,1]{1,0:T(8,128)S(1)}, u32[]{:S(2)}) copy-start(f32[736,1]{1,0:T(8,128)S(1)} %select_n.91.bias_ref) | copy-start | bytes 8836
  101.4 37.4 %copy-start.41 = (bf16[176,1152]{1,0:T(8,128)(2,1)S(1)}, bf16[176,1152]{1,0:T(8,128)(2,1)}, u32[]{:S(2)}) copy-start(bf16[176,1152]{1,0:T(8,128)(2,1)} %copy-done.40) | copy-start | bytes 1216516
  101.5 362.9 %reduce-scatter.2.cloned.1.call-start = ((), (), s32[]{:S(2)}) async-start(), calls=%async_computation.1 | async-start | bytes 7299072 | tf_op jit(solution)/shard_map/reduce_scatter | solution.py:778
  138.0 38.9 %collective-permute-start.14 = (bf16[704,1152]{1,0:T(8,128)(2,1)}, bf16[704,1152]{1,0:T(8,128)(2,1)}, u32[]{:S(2)}, u32[]{:S(2)}) collective-permute-start(bf16[704,1152]{1,0:T(8,128)(2,1)} %bitcast.35.refs_2_), channel_id=1, source_target_pairs={{0,16},{1,17},{2,18},{3,19},{4,20},{5,21},{6,22},{7,23},{8,24},{9,... | collective-permute-start | bytes 4866056 | tf_op jit(solution)/shard_map/ppermute | solution.py:510
  138.9 50.0 %collective-permute-start.17 = (bf16[704,1152]{1,0:T(8,128)(2,1)}, bf16[704,1152]{1,0:T(8,128)(2,1)}, u32[]{:S(2)}, u32[]{:S(2)}) collective-permute-start(bf16[704,1152]{1,0:T(8,128)(2,1)} %bitcast.35.refs_2_), channel_id=1, source_target_pairs={{0,8},{1,9},{2,10},{3,11},{4,12},{5,13},{6,14},{7,15},{8,0},{9,1},... | collective-permute-start | bytes 4866056 | tf_op jit(solution)/shard_map/ppermute | solution.py:510
  141.3 39.8 %collective-permute-start.13 = (bf16[704,1152]{1,0:T(8,128)(2,1)}, bf16[704,1152]{1,0:T(8,128)(2,1)}, u32[]{:S(2)}, u32[]{:S(2)}) collective-permute-start(bf16[704,1152]{1,0:T(8,128)(2,1)} %bitcast.33.refs_0_), channel_id=1, source_target_pairs={{0,1},{1,0},{2,3},{3,2},{4,5},{5,4},{6,7},{7,6},{8,9},{9,8},{10,11... | collective-permute-start | bytes 4866056 | tf_op jit(solution)/shard_map/ppermute | solution.py:510
  142.4 46.4 %collective-permute-start.15 = (bf16[704,1152]{1,0:T(8,128)(2,1)}, bf16[704,1152]{1,0:T(8,128)(2,1)}, u32[]{:S(2)}, u32[]{:S(2)}) collective-permute-start(bf16[704,1152]{1,0:T(8,128)(2,1)} %bitcast.33.refs_0_), channel_id=1, source_target_pairs={{0,8},{1,9},{2,10},{3,11},{4,12},{5,13},{6,14},{7,15},{8,0},{9,1},... | collective-permute-start | bytes 4866056 | tf_op jit(solution)/shard_map/ppermute | solution.py:510
  181.0 7.8 %collective-permute-start.16 = (bf16[704,1152]{1,0:T(8,128)(2,1)}, bf16[704,1152]{1,0:T(8,128)(2,1)}, u32[]{:S(2)}, u32[]{:S(2)}) collective-permute-start(bf16[704,1152]{1,0:T(8,128)(2,1)} %collective-permute-done.13.refs_1_), channel_id=1, source_target_pairs={{0,8},{1,9},{2,10},{3,11},{4,12},{5,13},{6,14},{7,15},{8,0},{9,1},... | collective-permute-start | bytes 4866056 | tf_op jit(solution)/shard_map/ppermute | solution.py:510
  181.0 7.8 %collective-permute-start.18 = (bf16[704,1152]{1,0:T(8,128)(2,1)}, bf16[704,1152]{1,0:T(8,128)(2,1)}, u32[]{:S(2)}, u32[]{:S(2)}) collective-permute-start(bf16[704,1152]{1,0:T(8,128)(2,1)} %collective-permute-done.14.refs_3_), channel_id=1, source_target_pairs={{0,8},{1,9},{2,10},{3,11},{4,12},{5,13},{6,14},{7,15},{8,0},{9,1},... | collective-permute-start | bytes 4866056 | tf_op jit(solution)/shard_map/ppermute | solution.py:510
  216.6 31.4 %collective-permute-start.19 = (bf16[4,2,352,1152]{3,2,1,0:T(8,128)(2,1)}, bf16[4,2,352,1152]{3,2,1,0:T(8,128)(2,1)}, u32[]{:S(2)}, u32[]{:S(2)}) collective-permute-start(bf16[4,2,352,1152]{3,2,1,0:T(8,128)(2,1)} %get-tuple-element.122), channel_id=1, source_target_pairs={{0,8},{1,9},{2,10},{3,11},{4,12},{5,13},{6,14},{7,15},{8,0},{9,1},... | collective-permute-start | bytes 19464200 | tf_op jit(solution)/shard_map/ppermute | solution.py:510
  253.3 38.4 %collective-permute-start.20 = (bf16[2,352,1152]{2,1,0:T(8,128)(2,1)}, bf16[2,352,1152]{2,1,0:T(8,128)(2,1)}, u32[]{:S(2)}, u32[]{:S(2)}) collective-permute-start(bf16[2,352,1152]{2,1,0:T(8,128)(2,1)} %get-tuple-element.200), channel_id=1, source_target_pairs={{0,1},{1,0},{2,3},{3,2},{4,5},{5,4},{6,7},{7,6},{8,9},{9,8},{10,11... | collective-permute-start | bytes 4866056 | tf_op jit(solution)/shard_map/ppermute | solution.py:510
  254.4 38.2 %collective-permute-start.21 = (bf16[2,352,1152]{2,1,0:T(8,128)(2,1)}, bf16[2,352,1152]{2,1,0:T(8,128)(2,1)}, u32[]{:S(2)}, u32[]{:S(2)}) collective-permute-start(bf16[2,352,1152]{2,1,0:T(8,128)(2,1)} %get-tuple-element.199), channel_id=1, source_target_pairs={{0,16},{1,17},{2,18},{3,19},{4,20},{5,21},{6,22},{7,23},{8,24},{9,... | collective-permute-start | bytes 4866056 | tf_op jit(solution)/shard_map/ppermute | solution.py:510
  312.3 38.3 %collective-permute-start.24 = (bf16[368,1152]{1,0:T(8,128)(2,1)}, bf16[368,1152]{1,0:T(8,128)(2,1)}, u32[]{:S(2)}, u32[]{:S(2)}) collective-permute-start(bf16[368,1152]{1,0:T(8,128)(2,1)} %get-tuple-element.132), channel_id=1, source_target_pairs={{0,1},{1,0},{2,3},{3,2},{4,5},{5,4},{6,7},{7,6},{8,9},{9,8},{10,11... | collective-permute-start | bytes 2543624 | tf_op jit(solution)/shard_map/ppermute | solution.py:631
  313.1 34.5 %collective-permute-start.22 = (bf16[2,2,88,1152]{3,2,0,1:T(8,128)(2,1)}, bf16[2,2,88,1152]{3,2,0,1:T(8,128)(2,1)}, u32[]{:S(2)}, u32[]{:S(2)}) collective-permute-start(bf16[2,2,88,1152]{3,2,0,1:T(8,128)(2,1)} %bitcast.168), channel_id=1, source_target_pairs={{0,16},{1,17},{2,18},{3,19},{4,20},{5,21},{6,22},{7,23},{8,24},{9,... | collective-permute-start | bytes 2433032 | tf_op jit(solution)/shard_map/ppermute | solution.py:510
  314.3 36.2 %collective-permute-start.23 = (bf16[2,2,88,1152]{3,2,0,1:T(8,128)(2,1)}, bf16[2,2,88,1152]{3,2,0,1:T(8,128)(2,1)}, u32[]{:S(2)}, u32[]{:S(2)}) collective-permute-start(bf16[2,2,88,1152]{3,2,0,1:T(8,128)(2,1)} %bitcast.167), channel_id=1, source_target_pairs={{0,1},{1,0},{2,3},{3,2},{4,5},{5,4},{6,7},{7,6},{8,9},{9,8},{10,11... | collective-permute-start | bytes 2433032 | tf_op jit(solution)/shard_map/ppermute | solution.py:510
  318.9 31.7 %copy-start.32 = (bf16[2,1,2,88,1152]{4,3,2,1,0:T(8,128)(2,1)S(1)}, bf16[2,1,2,88,1152]{4,3,2,1,0:T(8,128)(2,1)}, u32[]{:S(2)}) copy-start(bf16[2,1,2,88,1152]{4,3,2,1,0:T(8,128)(2,1)} %get-tuple-element.211) | copy-start | bytes 2433028
  374.2 3.7 collective-permute-start.26
  374.2 7.3 %collective-permute-start.25 = (bf16[2,2,144,1152]{3,2,1,0:T(8,128)(2,1)}, bf16[2,2,144,1152]{3,2,1,0:T(8,128)(2,1)}, u32[]{:S(2)}, u32[]{:S(2)}) collective-permute-start(bf16[2,2,144,1152]{3,2,1,0:T(8,128)(2,1)} %get-tuple-element.144), channel_id=1, source_target_pairs={{0,8},{1,9},{2,10},{3,11},{4,12},{5,13},{6,14},{7,15},{8,0},{9,1},... | collective-permute-start | bytes 3981320 | tf_op jit(solution)/shard_map/ppermute | solution.py:510
  374.7 41.2 %collective-permute-start.28 = (bf16[2,88,1152]{2,1,0:T(8,128)(2,1)}, bf16[2,88,1152]{2,1,0:T(8,128)(2,1)S(1)}, u32[]{:S(2)}, u32[]{:S(2)}) collective-permute-start(bf16[2,88,1152]{2,1,0:T(8,128)(2,1)} %get-tuple-element.222), channel_id=1, source_target_pairs={{0,4},{1,5},{2,6},{3,7},{4,0},{5,1},{6,2},{7,3},{8,12},{9,13},{10,... | collective-permute-start | bytes 1216520 | tf_op jit(solution)/shard_map/ppermute | solution.py:510
  375.9 51.7 %collective-permute-start.29 = (bf16[2,88,1152]{2,1,0:T(8,128)(2,1)S(1)}, bf16[2,88,1152]{2,1,0:T(8,128)(2,1)S(1)}, u32[]{:S(2)}, u32[]{:S(2)}) collective-permute-start(bf16[2,88,1152]{2,1,0:T(8,128)(2,1)S(1)} %get-tuple-element.221), channel_id=1, source_target_pairs={{0,6},{1,7},{2,4},{3,5},{4,2},{5,3},{6,0},{7,1},{8,14},{9,15},{10,... | collective-permute-start | bytes 1216520 | tf_op jit(solution)/shard_map/ppermute | solution.py:510
  377.9 76.7 %collective-permute-start.33 = (bf16[4,144,1152]{2,1,0:T(8,128)(2,1)}, bf16[4,144,1152]{2,1,0:T(8,128)(2,1)}, u32[]{:S(2)}, u32[]{:S(2)}) collective-permute-start(bf16[4,144,1152]{2,1,0:T(8,128)(2,1)} %get-tuple-element.145), channel_id=1, source_target_pairs={{0,8},{1,9},{2,10},{3,11},{4,12},{5,13},{6,14},{7,15},{8,0},{9,1},... | collective-permute-start | bytes 3981320 | tf_op jit(solution)/shard_map/ppermute | solution.py:510
  377.9 49.8 %collective-permute-start.27 = (bf16[2,88,1152]{2,1,0:T(8,128)(2,1)S(1)}, bf16[2,88,1152]{2,1,0:T(8,128)(2,1)S(1)}, u32[]{:S(2)}, u32[]{:S(2)}) collective-permute-start(bf16[2,88,1152]{2,1,0:T(8,128)(2,1)S(1)} %slice_bitcast_fusion.6), channel_id=1, source_target_pairs={{0,2},{1,3},{2,0},{3,1},{4,6},{5,7},{6,4},{7,5},{8,10},{9,11},{10,... | collective-permute-start | bytes 1216520 | tf_op jit(solution)/shard_map/ppermute | solution.py:510
  381.5 66.3 %collective-permute-start.31 = (bf16[4,144,1152]{2,1,0:T(8,128)(2,1)}, bf16[4,144,1152]{2,1,0:T(8,128)(2,1)}, u32[]{:S(2)}, u32[]{:S(2)}) collective-permute-start(bf16[4,144,1152]{2,1,0:T(8,128)(2,1)} %add_convert_fusion.6), channel_id=1, source_target_pairs={{0,16},{1,17},{2,18},{3,19},{4,20},{5,21},{6,22},{7,23},{8,24},{9,... | collective-permute-start | bytes 3981320 | tf_op jit(solution)/shard_map/ppermute | solution.py:510
  416.0 38.6 %collective-permute-start.30 = (bf16[2,2,144,1152]{3,2,1,0:T(8,128)(2,1)}, bf16[2,2,144,1152]{3,2,1,0:T(8,128)(2,1)}, u32[]{:S(2)}, u32[]{:S(2)}) collective-permute-start(bf16[2,2,144,1152]{3,2,1,0:T(8,128)(2,1)} %add_convert_fusion.7), channel_id=1, source_target_pairs={{0,1},{1,0},{2,3},{3,2},{4,5},{5,4},{6,7},{7,6},{8,9},{9,8},{10,11... | collective-permute-start | bytes 3981320 | tf_op jit(solution)/shard_map/ppermute | solution.py:510
  427.6 31.2 %collective-permute-start.32 = (bf16[2,2,144,1152]{3,2,1,0:T(8,128)(2,1)}, bf16[2,2,144,1152]{3,2,1,0:T(8,128)(2,1)}, u32[]{:S(2)}, u32[]{:S(2)}) collective-permute-start(bf16[2,2,144,1152]{3,2,1,0:T(8,128)(2,1)} %get-tuple-element.143), channel_id=1, source_target_pairs={{0,8},{1,9},{2,10},{3,11},{4,12},{5,13},{6,14},{7,15},{8,0},{9,1},... | collective-permute-start | bytes 3981320 | tf_op jit(solution)/shard_map/ppermute | solution.py:510
  457.9 18.2 %collective-permute-start.38 = (bf16[2,144,1152]{2,1,0:T(8,128)(2,1)}, bf16[2,144,1152]{2,1,0:T(8,128)(2,1)}, u32[]{:S(2)}, u32[]{:S(2)}) collective-permute-start(bf16[2,144,1152]{2,1,0:T(8,128)(2,1)} %slice.296), channel_id=1, source_target_pairs={{0,1},{1,0},{2,3},{3,2},{4,5},{5,4},{6,7},{7,6},{8,9},{9,8},{10,11... | collective-permute-start | bytes 1990664 | tf_op jit(solution)/shard_map/ppermute | solution.py:510
  462.0 14.1 %collective-permute-start.37 = (bf16[2,144,1152]{2,1,0:T(8,128)(2,1)}, bf16[2,144,1152]{2,1,0:T(8,128)(2,1)}, u32[]{:S(2)}, u32[]{:S(2)}) collective-permute-start(bf16[2,144,1152]{2,1,0:T(8,128)(2,1)} %slice_bitcast_fusion.2), channel_id=1, source_target_pairs={{0,16},{1,17},{2,18},{3,19},{4,20},{5,21},{6,22},{7,23},{8,24},{9,... | collective-permute-start | bytes 1990664 | tf_op jit(solution)/shard_map/ppermute | solution.py:510
  464.4 10.1 %collective-permute-start.34 = (f32[106,128]{1,0:T(8,128)}, f32[106,128]{1,0:T(8,128)}, u32[]{:S(2)}, u32[]{:S(2)}) collective-permute-start(f32[106,128]{1,0:T(8,128)} %bitcast.57), channel_id=1, source_target_pairs={{0,2},{1,3},{2,0},{3,1},{4,6},{5,7},{6,4},{7,5},{8,10},{9,11},{10,... | collective-permute-start | bytes 162824 | tf_op jit(solution)/shard_map/ppermute | solution.py:510
  465.2 9.3 %collective-permute-start.35 = (f32[106,128]{1,0:T(8,128)}, f32[106,128]{1,0:T(8,128)}, u32[]{:S(2)}, u32[]{:S(2)}) collective-permute-start(f32[106,128]{1,0:T(8,128)} %bitcast.57), channel_id=1, source_target_pairs={{0,4},{1,5},{2,6},{3,7},{4,0},{5,1},{6,2},{7,3},{8,12},{9,13},{10,... | collective-permute-start | bytes 162824 | tf_op jit(solution)/shard_map/ppermute | solution.py:510
  466.8 7.8 %collective-permute-start.36 = (f32[106,128]{1,0:T(8,128)}, f32[106,128]{1,0:T(8,128)}, u32[]{:S(2)}, u32[]{:S(2)}) collective-permute-start(f32[106,128]{1,0:T(8,128)} %bitcast.57), channel_id=1, source_target_pairs={{0,6},{1,7},{2,4},{3,5},{4,2},{5,3},{6,0},{7,1},{8,14},{9,15},{10,... | collective-permute-start | bytes 162824 | tf_op jit(solution)/shard_map/ppermute | solution.py:510
  480.6 4.6 collective-permute-start.43
  480.6 8.0 %collective-permute-start.44 = (bf16[272,288]{1,0:T(8,128)(2,1)S(1)}, bf16[272,288]{1,0:T(8,128)(2,1)S(1)}, u32[]{:S(2)}, u32[]{:S(2)}) collective-permute-start(bf16[272,288]{1,0:T(8,128)(2,1)S(1)} %copy-done.74), channel_id=1, source_target_pairs={{0,16},{1,17},{2,18},{3,19},{4,20},{5,21},{6,22},{7,23},{8,24},{9,... | collective-permute-start | bytes 470024 | tf_op jit(solution)/shard_map/ppermute | solution.py:510
  481.8 10.4 %collective-permute-start.45 = (bf16[272,288]{1,0:T(8,128)(2,1)S(1)}, bf16[272,288]{1,0:T(8,128)(2,1)S(1)}, u32[]{:S(2)}, u32[]{:S(2)}) collective-permute-start(bf16[272,288]{1,0:T(8,128)(2,1)S(1)} %copy-done.73), channel_id=1, source_target_pairs={{0,24},{1,25},{2,26},{3,27},{4,28},{5,29},{6,30},{7,31},{8,16},{9,... | collective-permute-start | bytes 470024 | tf_op jit(solution)/shard_map/ppermute | solution.py:510
  483.4 28.6 %collective-permute-start.39 = (bf16[368,1152]{1,0:T(8,128)(2,1)}, bf16[368,1152]{1,0:T(8,128)(2,1)}, u32[]{:S(2)}, u32[]{:S(2)}) collective-permute-start(bf16[368,1152]{1,0:T(8,128)(2,1)} %slice.248), channel_id=1, source_target_pairs={{0,1},{1,0},{2,3},{3,2},{4,5},{5,4},{6,7},{7,6},{8,9},{9,8},{10,11... | collective-permute-start | bytes 2543624 | tf_op jit(solution)/shard_map/ppermute | solution.py:631
  484.4 25.4 %collective-permute-start.41 = (bf16[144,1152]{1,0:T(8,128)(2,1)}, bf16[144,1152]{1,0:T(8,128)(2,1)}, u32[]{:S(2)}, u32[]{:S(2)}) collective-permute-start(bf16[144,1152]{1,0:T(8,128)(2,1)} %get-tuple-element.224), channel_id=1, source_target_pairs={{0,4},{1,5},{2,6},{3,7},{4,0},{5,1},{6,2},{7,3},{8,12},{9,13},{10,... | collective-permute-start | bytes 995336 | tf_op jit(solution)/shard_map/ppermute | solution.py:510
  485.3 24.6 %collective-permute-start.42 = (bf16[144,1152]{1,0:T(8,128)(2,1)}, bf16[144,1152]{1,0:T(8,128)(2,1)}, u32[]{:S(2)}, u32[]{:S(2)}) collective-permute-start(bf16[144,1152]{1,0:T(8,128)(2,1)} %get-tuple-element.223), channel_id=1, source_target_pairs={{0,6},{1,7},{2,4},{3,5},{4,2},{5,3},{6,0},{7,1},{8,14},{9,15},{10,... | collective-permute-start | bytes 995336 | tf_op jit(solution)/shard_map/ppermute | solution.py:510
  488.7 23.4 %collective-permute-start.40 = (bf16[144,1152]{1,0:T(8,128)(2,1)}, bf16[144,1152]{1,0:T(8,128)(2,1)}, u32[]{:S(2)}, u32[]{:S(2)}) collective-permute-start(bf16[144,1152]{1,0:T(8,128)(2,1)} %slice_bitcast_fusion.10), channel_id=1, source_target_pairs={{0,2},{1,3},{2,0},{3,1},{4,6},{5,7},{6,4},{7,5},{8,10},{9,11},{10,... | collective-permute-start | bytes 995336 | tf_op jit(solution)/shard_map/ppermute | solution.py:510
  516.3 7.4 %collective-permute-start.50 = (bf16[144,288]{1,0:T(8,128)(2,1)}, bf16[144,288]{1,0:T(8,128)(2,1)S(1)}, u32[]{:S(2)}, u32[]{:S(2)}) collective-permute-start(bf16[144,288]{1,0:T(8,128)(2,1)} %get-tuple-element.192), channel_id=1, source_target_pairs={{0,8},{1,9},{2,10},{3,11},{4,12},{5,13},{6,14},{7,15},{8,0},{9,1},... | collective-permute-start | bytes 248840 | tf_op jit(solution)/shard_map/ppermute | solution.py:510
  516.3 8.0 %collective-permute-start.51 = (bf16[144,288]{1,0:T(8,128)(2,1)}, bf16[144,288]{1,0:T(8,128)(2,1)S(1)}, u32[]{:S(2)}, u32[]{:S(2)}) collective-permute-start(bf16[144,288]{1,0:T(8,128)(2,1)} %get-tuple-element.193), channel_id=1, source_target_pairs={{0,16},{1,17},{2,18},{3,19},{4,20},{5,21},{6,22},{7,23},{8,24},{9,... | collective-permute-start | bytes 248840 | tf_op jit(solution)/shard_map/ppermute | solution.py:510
  517.3 7.0 %collective-permute-start.52 = (bf16[144,288]{1,0:T(8,128)(2,1)}, bf16[144,288]{1,0:T(8,128)(2,1)S(1)}, u32[]{:S(2)}, u32[]{:S(2)}) collective-permute-start(bf16[144,288]{1,0:T(8,128)(2,1)} %get-tuple-element.194), channel_id=1, source_target_pairs={{0,24},{1,25},{2,26},{3,27},{4,28},{5,29},{6,30},{7,31},{8,16},{9,... | collective-permute-start | bytes 248840 | tf_op jit(solution)/shard_map/ppermute | solution.py:510
  518.1 4.2 collective-permute-start.46
  522.3 6.9 %collective-permute-start.47 = (f32[106,128]{1,0:T(8,128)S(1)}, f32[106,128]{1,0:T(8,128)S(1)}, u32[]{:S(2)}, u32[]{:S(2)}) collective-permute-start(f32[106,128]{1,0:T(8,128)S(1)} %add.246), channel_id=1, source_target_pairs={{0,8},{1,9},{2,10},{3,11},{4,12},{5,13},{6,14},{7,15},{8,0},{9,1},... | collective-permute-start | bytes 162824 | tf_op jit(solution)/shard_map/ppermute | solution.py:510
  522.4 6.8 %collective-permute-start.48 = (f32[106,128]{1,0:T(8,128)S(1)}, f32[106,128]{1,0:T(8,128)S(1)}, u32[]{:S(2)}, u32[]{:S(2)}) collective-permute-start(f32[106,128]{1,0:T(8,128)S(1)} %add.246), channel_id=1, source_target_pairs={{0,16},{1,17},{2,18},{3,19},{4,20},{5,21},{6,22},{7,23},{8,24},{9,... | collective-permute-start | bytes 162824 | tf_op jit(solution)/shard_map/ppermute | solution.py:510
  523.7 5.5 %collective-permute-start.49 = (f32[106,128]{1,0:T(8,128)S(1)}, f32[106,128]{1,0:T(8,128)S(1)}, u32[]{:S(2)}, u32[]{:S(2)}) collective-permute-start(f32[106,128]{1,0:T(8,128)S(1)} %add.246), channel_id=1, source_target_pairs={{0,24},{1,25},{2,26},{3,27},{4,28},{5,29},{6,30},{7,31},{8,16},{9,... | collective-permute-start | bytes 162824 | tf_op jit(solution)/shard_map/ppermute | solution.py:510
  (70 other events, 398.9 us)
Sparse Core Ops, SparseCore 0:
  21.0 128.4 all-gather.4
  153.0 76.3 all-gather.6
  316.0 147.6 reduce-scatter.1

commit v7 on v5

--- a/solution.py
+++ b/solution.py
@@ -770,7 +770,6 @@
         sums = after(sums, units.ready_third())
         units.send_third()
         *sums, bulk_grads, up_sum = bulk(sums)
-        units.moved = after(units.moved, sums)
     else:
         *sums, bulk_grads, up_sum = bulk()
     up_sums = [up_sum[:, 0]] + up_sums
@@ -792,8 +791,7 @@
         units.send_second()
         out_other = swap(out_sent)
         grads = back(grad_branch, heads, 4)
-        units.moved, out_other = after((units.moved, out_other), grads)
-        grads = after(grads, units.second())
+        grads, out_other = after((grads, out_other), units.second())
         layer_out = both_micros(out_kept, out_other)
         units.send_along_z()
         kind_grads = kinds_grad(
@@ -820,7 +818,6 @@
         out_other = swap(out_sent)
         layer_out = both_micros(out_kept, out_other)
 
-    grads, second_sums, up_sums = after((grads, second_sums, up_sums), input_low)
     total_over = lambda i: jnp.sum(grads[i], axis=1, dtype=wide)
     small = jnp.concatenate(
         [

time: 547 us -> 536 us (0.980)
  waiting for transfers between devices: 165 us -> 138 us
  local copies, waits for them, and re-layouts: 49.9 us -> 62.7 us
    ppermute x49, waiting for transfers between devices: 139 us -> 116 us  [send(): return lax.ppermute(values, everyone, pairs)]
    all_gather x1, waiting for transfers between devices: 8.12 us -> 0.01 us  [shards(): attn_rows = lax.all_gather(attn_block, everyone).reshape(4, -1, width)]
    unnamed x150 -> x144, local copies, waits for them, and re-layouts: 18.7 us -> 23.6 us
  transfers between devices with their start and end apart: 56 -> 56, of which waited for: 20 -> 20; matrix products, arithmetic and copies ran while one was open for 19% -> 23% of each run, Pallas kernels for 31% -> 32%
where the time goes in v7:
time: 536 us; the launch traced here: 525 us
  Pallas kernels  175 us (33%)
  waiting for transfers between devices  138 us (26%)
  local copies, waits for them, and re-layouts  62.7 us (12%)
  other arithmetic  59.2 us (11%)
  starting transfers between devices  48.6 us (9%)
  matrix products  27.7 us (5%)
  between operations  14.8 us (3%)
    ppermute x49, waiting for transfers between devices, send(): return lax.ppermute(values, everyone, pairs)  116 us
    pallas_call x3, Pallas kernels, mlp(): pl.pallas_call(partial(mlp_kernel, before is not None, (starts, rows, gro...  89.1 us
    ppermute x49, starting transfers between devices, send(): return lax.ppermute(values, everyone, pairs)  44.3 us
    pallas_call x1, Pallas kernels, attend_back(): pl.pallas_call(partial(attend_back_kernel, step_heads), grid=(steps,), in...  28.5 us
    dot_general x3, matrix products, product(): lax.dot_general(left, right, (((left_dim,), (right_dim,)), ((), ())), pre...  26.6 us
    convert_element_type x12, other arithmetic, add_low(): return total.astype(low)  25.1 us
    unnamed x144, local copies, waits for them, and re-layouts  23.6 us
    ppermute x4, waiting for transfers between devices, swap(): return lax.ppermute(values, 'tensor', pairs)  22 us
  transfers between devices with their start and end apart: 56, of which 20 were waited for; matrix products, arithmetic and copies ran while one was open for 23% of the time, Pallas kernels for 32%

profile of v7, /device:TPU:0, one launch (start us, length us, event | category | flops | bytes accessed | tf_op | source)
XLA Modules:
  0.0 525.3 jit_solution(1945387699662630238)
XLA Ops:
  9.7 2.5 collective-permute-start.2
  12.3 3.8 collective-permute-done.2.refs_2_
  16.1 2.0 collective-permute-done.3.refs_3_
  18.7 2.2 unite.2
  22.1 1.6 collective-permute-start
  26.2 1.5 collective-permute-start.6
  28.3 2.5 dynamic-slice_bitcast_fusion.1
  30.9 3.8 collective-permute-done.6.refs_2_
  34.7 5.6 %collective-permute-done.7.refs_3_ = bf16[272,288]{1,0:T(8,128)(2,1)} collective-permute-done((bf16[272,288]{1,0:T(8,128)(2,1)S(1)}, bf16[272,288]{1,0:T(8,128)(2,1)}, u32[]{:S(2)}, u32[]{:S(2)}) %collective-permute-start.7) | collective-permute-done | bytes 156704 | tf_op jit(solution)/shard_map/ppermute | solution.py:510
  40.3 2.6 unite.3
  42.9 3.6 collective-permute-start.10
  47.3 1.5 pad_maximum_fusion.values_ref
  50.2 1.9 fusion.11.normed_ref
  52.0 22.0 %collective-permute-done.4 = bf16[368,1152]{1,0:T(8,128)(2,1)S(1)} collective-permute-done((bf16[368,1152]{1,0:T(8,128)(2,1)S(1)}, bf16[368,1152]{1,0:T(8,128)(2,1)S(1)}, u32[]{:S(2)}, u32[]{:S(2)}) %collective-permute-start.4) | collective-permute-done | bytes 847904 | tf_op jit(solution)/shard_map/ppermute | solution.py:631
  75.4 4.3 collective-permute-done.8
  79.7 31.4 %collective-permute-done.9 = bf16[176,1152]{1,0:T(8,128)(2,1)S(1)} collective-permute-done((bf16[176,1152]{1,0:T(8,128)(2,1)}, bf16[176,1152]{1,0:T(8,128)(2,1)S(1)}, u32[]{:S(2)}, u32[]{:S(2)}) %collective-permute-start.9) | collective-permute-done | bytes 405536 | tf_op jit(solution)/shard_map/ppermute | solution.py:510
  117.2 13.1 %collective-permute-done.12 = bf16[352,1152]{1,0:T(8,128)(2,1)} collective-permute-done((bf16[352,1152]{1,0:T(8,128)(2,1)}, bf16[352,1152]{1,0:T(8,128)(2,1)}, u32[]{:S(2)}, u32[]{:S(2)}) %collective-permute-start.12) | collective-permute-done | bytes 811040 | tf_op jit(solution)/shard_map/ppermute | solution.py:510
  132.1 2.4 pad_maximum_fusion.3
  136.0 2.6 pad_maximum_fusion.2
  138.6 1.7 collective-permute-start.13
  140.6 11.2 %add_convert_fusion.query_ref.key_ref.value_ref = bf16[3456,736]{1,0:T(8,128)(2,1)} fusion(bf16[736,1152]{1,0:T(8,128)(2,1)S(1)} %copy-done.22, bf16[4608,1152]{1,0:T(8,128)(2,1)} %all-gather.5.cloned.1.call-done.weights_ref, f32[3456]{0:T(1024)S(1)} %pad_maximum_fusion.11), kind=kOutput, calls=%fused_computation | convolution fusion | flops 5865578496 | bytes 14759424 | tf_op jit(solution)/shard_map/dot_general | solution.py:23
  151.8 15.1 %attend.1 = (bf16[1152,736]{1,0:T(8,128)(2,1)S(1)}, f32[16,1,736]{2,1,0:T(1,128)S(1)}) custom-call(bf16[3456,736]{1,0:T(8,128)(2,1)} %add_convert_fusion.query_ref.key_ref.value_ref, bf16[3456,736]{1,0:T(8,128)(2,1)} %add_convert_fusion.query_ref.key_ref.value_ref, bf16[3456,736]{1,0:T(8,128)(2,1)} %add_convert_fusion.query_ref.key_ref.value_ref, ...), custom_call_target="tpu_custom_call" | custom-call | flops 1109393408 | bytes 1048576 | tf_op jit(solution)/shard_map/attend/pallas_call | solution.py:80
  166.9 10.2 %collective-permute-done.14.refs_3_ = bf16[704,1152]{1,0:T(8,128)(2,1)} collective-permute-done((bf16[704,1152]{1,0:T(8,128)(2,1)}, bf16[704,1152]{1,0:T(8,128)(2,1)}, u32[]{:S(2)}, u32[]{:S(2)}) %collective-permute-start.14) | collective-permute-done | bytes 1622048 | tf_op jit(solution)/shard_map/ppermute | solution.py:510
  177.2 3.4 collective-permute-done.13.refs_1_
  181.1 4.8 fusion.43
  186.6 1.8 add_convert_fusion.1.normed_ref
  188.9 27.9 %mlp.3 = (f32[736,1152]{1,0:T(8,128)}, f32[736,1152]{1,0:T(8,128)}, bf16[4,2,352,1152]{3,2,1,0:T(8,128)(2,1)}, f32[1408,1]{1,0:T(8,128)}) custom-call(bf16[736,1152]{1,0:T(8,128)(2,1)} %add_convert_fusion.1.normed_ref, bf16[736,1152]{1,0:T(8,128)(2,1)} %pad_maximum_fusion.1.grad_ref.base_ref, f32[1408,1]{1,0:T(8,128)} %split.15.bias_ref, ...), custom_call_target="tpu_custom_call" | custom-call | flops 2387607552 | bytes 1048576 | tf_op jit(solution)/shard_map/mlp/pallas_call | solution.py:302
  218.1 29.7 %mlp.4 = (f32[736,1152]{1,0:T(8,128)}, f32[736,1152]{1,0:T(8,128)}, bf16[4,2,352,1152]{3,2,1,0:T(8,128)(2,1)}, f32[1408,1]{1,0:T(8,128)}) custom-call(bf16[736,1152]{1,0:T(8,128)(2,1)} %add_convert_fusion.1.normed_ref, bf16[736,1152]{1,0:T(8,128)(2,1)} %pad_maximum_fusion.1.grad_ref.base_ref, ...), custom_call_target="tpu_custom_call", output_to_operand_aliasing={{0}: (7, {}), {1}: (8, {})} | custom-call | flops 2387607552 | bytes 1048576 | tf_op jit(solution)/shard_map/mlp/pallas_call | solution.py:302
  247.9 5.4 %fusion.16 = (bf16[2,352,1152]{2,1,0:T(8,128)(2,1)}, bf16[2,352,1152]{2,1,0:T(8,128)(2,1)}) fusion(bf16[4,2,352,1152]{3,2,1,0:T(8,128)(2,1)} %collective-permute-done.19, bf16[4,2,352,1152]{3,2,1,0:T(8,128)(2,1)} %get-tuple-element.109), kind=kLoop, calls=%fused_computation.36 | loop fusion | flops 6488064 | bytes 9732096 | tf_op jit(solution)/shard_map/convert_element_type | solution.py:492
  256.1 31.5 %mlp.5 = (f32[736,1152]{1,0:T(8,128)}, f32[736,1152]{1,0:T(8,128)}, bf16[32,2,48,1152]{3,2,1,0:T(8,128)(2,1)}, f32[1536,1]{1,0:T(8,128)}) custom-call(bf16[736,1152]{1,0:T(8,128)(2,1)} %add_convert_fusion.1.normed_ref, bf16[736,1152]{1,0:T(8,128)(2,1)} %pad_maximum_fusion.1.grad_ref.base_ref, ...), custom_call_target="tpu_custom_call", output_to_operand_aliasing={{0}: (4, {}), {1}: (5, {})} | custom-call | flops 2604662784 | bytes 1048576 | tf_op jit(solution)/shard_map/mlp/pallas_call | solution.py:302
  287.7 3.6 collective-permute-done.20
  292.2 4.7 fusion.12
  307.7 2.0 reduce.3
  318.0 2.1 copy-done.4
  320.0 7.3 %norm_back.2 = (f32[736,1152]{1,0:T(8,128)S(1)}, bf16[736,1152]{1,0:T(8,128)(2,1)S(1)}, f32[4,1152]{1,0:T(4,128)S(1)}, bf16[368,1152]{1,0:T(8,128)(2,1)S(1)}, bf16[368,1152]{1,0:T(8,128)(2,1)}) custom-call(f32[736,1152]{1,0:T(8,128)S(1)} %copy-done.4, f32[736,1152]{1,0:T(8,128)} %get-tuple-element.115.grad_ref, f32[1,1152]{1,0:T(1,128)S(1)} %broadcast_in_dim.30.gain_ref, ...), custom_call_target="tpu_custom_call" | custom-call | flops 847872 | bytes 847872 | tf_op jit(solution)/shard_map/norm_back/pallas_call | solution.py:188
  328.5 1.7 copy-done.11
  335.4 28.5 %attend_back.1.grads_ref = bf16[3,1152,736]{2,1,0:T(8,128)(2,1)} custom-call(bf16[3456,736]{1,0:T(8,128)(2,1)} %add_convert_fusion.query_ref.key_ref.value_ref, bf16[3456,736]{1,0:T(8,128)(2,1)} %add_convert_fusion.query_ref.key_ref.value_ref, bf16[3456,736]{1,0:T(8,128)(2,1)} %add_convert_fusion.query_ref.key_ref.value_ref, f32[736,1]{1,0:T(8,128)S(1)} %copy-done.10, ...), custom_call_target="tpu_custom_call" | custom-call | flops 1109393408 | bytes 1048576 | tf_op jit(solution)/shard_map/attend_back/pallas_call | solution.py:103
  366.9 5.4 %collective-permute-start.29 = (bf16[2,88,1152]{2,1,0:T(8,128)(2,1)S(1)}, bf16[2,88,1152]{2,1,0:T(8,128)(2,1)S(1)}, u32[]{:S(2)}, u32[]{:S(2)}) collective-permute-start(bf16[2,88,1152]{2,1,0:T(8,128)(2,1)S(1)} %get-tuple-element.197), channel_id=1, source_target_pairs={{0,6},{1,7},{2,4},{3,5},{4,2},{5,3},{6,0},{7,1},{8,14},{9,15},{10,... | collective-permute-start | bytes 1216520 | tf_op jit(solution)/shard_map/ppermute | solution.py:510
  374.3 17.1 %kinds_grad.1 = (bf16[2,2,144,1152]{3,2,1,0:T(8,128)(2,1)S(1)}, bf16[2,2,144,1152]{3,2,1,0:T(8,128)(2,1)S(1)}, bf16[4,144,1152]{2,1,0:T(8,128)(2,1)S(1)}, bf16[4...) custom-call(s32[2]{0:T(128)S(1)} %pad_add_fusion.kind_ref, ...), custom_call_target="tpu_custom_call" | custom-call | flops 976748544 | bytes 1048576 | tf_op jit(solution)/shard_map/kinds_grad/pallas_call | solution.py:383
  392.0 10.6 %fusion.2.grad_ref = f32[736,1152]{1,0:T(8,128)S(1)} fusion(bf16[3456,736]{1,0:T(8,128)(2,1)S(1)} %bitcast.171, bf16[4608,1152]{1,0:T(8,128)(2,1)} %all-gather.5.cloned.1.call-done.weights_ref), kind=kOutput, calls=%fused_computation.3 | convolution fusion | flops 5860491264 | bytes 16441344 | tf_op jit(solution)/shard_map/dot_general | solution.py:23
  409.9 3.3 norm_back.3
  413.2 1.7 copy-done.13
  418.8 18.8 %collective-permute-done.32 = bf16[4,144,1152]{2,1,0:T(8,128)(2,1)} collective-permute-done((bf16[4,144,1152]{2,1,0:T(8,128)(2,1)}, bf16[4,144,1152]{2,1,0:T(8,128)(2,1)}, u32[]{:S(2)}, u32[]{:S(2)}) %collective-permute-start.32) | collective-permute-done | bytes 1327136 | tf_op jit(solution)/shard_map/ppermute | solution.py:510
  437.6 2.2 collective-permute-done.31
  439.7 2.2 add_convert_fusion.4
  443.4 2.2 add_convert_fusion.5
  450.5 2.4 collective-permute-start.35
  453.7 3.0 maximum_select_fusion.1
  456.7 2.7 divide.2
  459.5 1.5 add_add_fusion.1
  461.0 1.7 collective-permute-done.37
  470.1 1.5 collective-permute-start.39
  471.8 1.7 collective-permute-start.41
  473.4 1.9 collective-permute-start.42
  476.5 2.4 collective-permute-done.45.refs_3_
  479.5 2.5 settle.2
  483.4 1.8 fusion.38
  489.4 2.1 fusion.23
  491.5 6.3 %collective-permute-done.41 = bf16[144,1152]{1,0:T(8,128)(2,1)} collective-permute-done((bf16[144,1152]{1,0:T(8,128)(2,1)}, bf16[144,1152]{1,0:T(8,128)(2,1)}, u32[]{:S(2)}, u32[]{:S(2)}) %collective-permute-start.41) | collective-permute-done | bytes 331808 | tf_op jit(solution)/shard_map/ppermute | solution.py:510
  498.4 2.1 fusion.26.refs_0_
  500.5 2.1 divide.3
  507.0 2.0 maximum_select_fusion
  511.6 2.0 settle.3
  513.7 2.2 slice_bitcast_fusion.11
  (327 shorter events, 101.5 us)
Async XLA Ops:
  7.2 133.4 %all-gather.5.cloned.1.call-start = ((), (), s32[]{:S(2)}) async-start(), calls=%async_computation.2 | async-start | bytes 10948608 | tf_op jit(solution)/shard_map/all_gather | solution.py:669
  9.2 3.1 collective-permute-start.1
  9.7 6.4 %collective-permute-start.2 = (bf16[144,288]{1,0:T(8,128)(2,1)S(1)}, bf16[144,288]{1,0:T(8,128)(2,1)S(1)}, u32[]{:S(2)}, u32[]{:S(2)}) collective-permute-start(bf16[144,288]{1,0:T(8,128)(2,1)S(1)} %get-tuple-element.202), channel_id=1, source_target_pairs={{0,16},{1,17},{2,18},{3,19},{4,20},{5,21},{6,22},{7,23},{8,24},{9,... | collective-permute-start | bytes 248840 | tf_op jit(solution)/shard_map/ppermute | solution.py:510
  12.2 5.9 %collective-permute-start.3 = (bf16[144,288]{1,0:T(8,128)(2,1)S(1)}, bf16[144,288]{1,0:T(8,128)(2,1)S(1)}, u32[]{:S(2)}, u32[]{:S(2)}) collective-permute-start(bf16[144,288]{1,0:T(8,128)(2,1)S(1)} %get-tuple-element.201), channel_id=1, source_target_pairs={{0,24},{1,25},{2,26},{3,27},{4,28},{5,29},{6,30},{7,31},{8,16},{9,... | collective-permute-start | bytes 248840 | tf_op jit(solution)/shard_map/ppermute | solution.py:510
  20.9 235.2 %all-gather.7.cloned.1.call-start = ((), (), s32[]{:S(2)}) async-start(), calls=%async_computation.3 | async-start | bytes 7299072 | tf_op jit(solution)/shard_map/all_gather | solution.py:672
  22.1 25.2 %collective-permute-start = (bf16[368,1152]{1,0:T(8,128)(2,1)}, bf16[368,1152]{1,0:T(8,128)(2,1)S(1)}, u32[]{:S(2)}, u32[]{:S(2)}) collective-permute-start(bf16[368,1152]{1,0:T(8,128)(2,1)} %get-tuple-element.180), channel_id=1, source_target_pairs={{0,1},{1,0},{2,3},{3,2},{4,5},{5,4},{6,7},{7,6},{8,9},{9,8},{10,11... | collective-permute-start | bytes 2543624 | tf_op jit(solution)/shard_map/ppermute | solution.py:631
  26.2 4.7 collective-permute-start.5
  26.2 8.5 %collective-permute-start.6 = (bf16[272,288]{1,0:T(8,128)(2,1)S(1)}, bf16[272,288]{1,0:T(8,128)(2,1)}, u32[]{:S(2)}, u32[]{:S(2)}) collective-permute-start(bf16[272,288]{1,0:T(8,128)(2,1)S(1)} %get-tuple-element.194), channel_id=1, source_target_pairs={{0,16},{1,17},{2,18},{3,19},{4,20},{5,21},{6,22},{7,23},{8,24},{9,... | collective-permute-start | bytes 470024 | tf_op jit(solution)/shard_map/ppermute | solution.py:510
  27.7 12.7 %collective-permute-start.7 = (bf16[272,288]{1,0:T(8,128)(2,1)S(1)}, bf16[272,288]{1,0:T(8,128)(2,1)}, u32[]{:S(2)}, u32[]{:S(2)}) collective-permute-start(bf16[272,288]{1,0:T(8,128)(2,1)S(1)} %get-tuple-element.193), channel_id=1, source_target_pairs={{0,24},{1,25},{2,26},{3,27},{4,28},{5,29},{6,30},{7,31},{8,16},{9,... | collective-permute-start | bytes 470024 | tf_op jit(solution)/shard_map/ppermute | solution.py:510
  28.3 86.3 %copy-start.45 = (f32[8,538]{1,0:T(8,128)}, f32[8,538]{1,0:T(8,128)S(1)}, u32[]{:S(2)}) copy-start(f32[8,538]{1,0:T(8,128)S(1)} %reshape.276) | copy-start | bytes 51652
  42.9 32.5 %collective-permute-start.10 = (bf16[176,1152]{1,0:T(8,128)(2,1)}, bf16[176,1152]{1,0:T(8,128)(2,1)S(1)}, u32[]{:S(2)}, u32[]{:S(2)}) collective-permute-start(bf16[176,1152]{1,0:T(8,128)(2,1)} %get-tuple-element.97), channel_id=1, source_target_pairs={{0,6},{1,7},{2,4},{3,5},{4,2},{5,3},{6,0},{7,1},{8,14},{9,15},{10,... | collective-permute-start | bytes 1216520 | tf_op jit(solution)/shard_map/ppermute | solution.py:510
  46.5 33.2 %collective-permute-start.8 = (bf16[176,1152]{1,0:T(8,128)(2,1)}, bf16[176,1152]{1,0:T(8,128)(2,1)S(1)}, u32[]{:S(2)}, u32[]{:S(2)}) collective-permute-start(bf16[176,1152]{1,0:T(8,128)(2,1)} %get-tuple-element.97), channel_id=1, source_target_pairs={{0,2},{1,3},{2,0},{3,1},{4,6},{5,7},{6,4},{7,5},{8,10},{9,11},{10,... | collective-permute-start | bytes 1216520 | tf_op jit(solution)/shard_map/ppermute | solution.py:510
  46.5 64.6 %collective-permute-start.9 = (bf16[176,1152]{1,0:T(8,128)(2,1)}, bf16[176,1152]{1,0:T(8,128)(2,1)S(1)}, u32[]{:S(2)}, u32[]{:S(2)}) collective-permute-start(bf16[176,1152]{1,0:T(8,128)(2,1)} %get-tuple-element.97), channel_id=1, source_target_pairs={{0,4},{1,5},{2,6},{3,7},{4,0},{5,1},{6,2},{7,3},{8,12},{9,13},{10,... | collective-permute-start | bytes 1216520 | tf_op jit(solution)/shard_map/ppermute | solution.py:510
  48.8 25.3 %collective-permute-start.4 = (bf16[368,1152]{1,0:T(8,128)(2,1)S(1)}, bf16[368,1152]{1,0:T(8,128)(2,1)S(1)}, u32[]{:S(2)}, u32[]{:S(2)}) collective-permute-start(bf16[368,1152]{1,0:T(8,128)(2,1)S(1)} %copy-done.37), channel_id=1, source_target_pairs={{0,1},{1,0},{2,3},{3,2},{4,5},{5,4},{6,7},{7,6},{8,9},{9,8},{10,11... | collective-permute-start | bytes 2543624 | tf_op jit(solution)/shard_map/ppermute | solution.py:631
  74.1 38.1 %copy-start.31 = (bf16[176,1152]{1,0:T(8,128)(2,1)S(1)}, bf16[176,1152]{1,0:T(8,128)(2,1)}, u32[]{:S(2)}) copy-start(bf16[176,1152]{1,0:T(8,128)(2,1)} %get-tuple-element.97) | copy-start | bytes 1216516
  75.4 39.2 %copy-start.33 = (bf16[176,1152]{1,0:T(8,128)(2,1)}, bf16[176,1152]{1,0:T(8,128)(2,1)S(1)}, u32[]{:S(2)}) copy-start(bf16[176,1152]{1,0:T(8,128)(2,1)S(1)} %collective-permute-done.10) | copy-start | bytes 1216516
  79.7 34.9 %copy-start.32 = (bf16[176,1152]{1,0:T(8,128)(2,1)}, bf16[176,1152]{1,0:T(8,128)(2,1)S(1)}, u32[]{:S(2)}) copy-start(bf16[176,1152]{1,0:T(8,128)(2,1)S(1)} %collective-permute-done.8) | copy-start | bytes 1216516
  112.2 18.1 %collective-permute-start.12 = (bf16[352,1152]{1,0:T(8,128)(2,1)}, bf16[352,1152]{1,0:T(8,128)(2,1)}, u32[]{:S(2)}, u32[]{:S(2)}) collective-permute-start(bf16[352,1152]{1,0:T(8,128)(2,1)} %bitcast.31), channel_id=1, source_target_pairs={{0,1},{1,0},{2,3},{3,2},{4,5},{5,4},{6,7},{7,6},{8,9},{9,8},{10,11... | collective-permute-start | bytes 2433032 | tf_op jit(solution)/shard_map/ppermute | solution.py:510
  113.2 18.0 %collective-permute-start.11 = (bf16[352,1152]{1,0:T(8,128)(2,1)}, bf16[352,1152]{1,0:T(8,128)(2,1)S(1)}, u32[]{:S(2)}, u32[]{:S(2)}) collective-permute-start(bf16[352,1152]{1,0:T(8,128)(2,1)} %bitcast.28), channel_id=1, source_target_pairs={{0,16},{1,17},{2,18},{3,19},{4,20},{5,21},{6,22},{7,23},{8,24},{9,... | collective-permute-start | bytes 2433032 | tf_op jit(solution)/shard_map/ppermute | solution.py:510
  114.9 36.8 %copy-start.9 = (f32[736,1]{1,0:T(8,128)}, f32[736,1]{1,0:T(8,128)S(1)}, u32[]{:S(2)}) copy-start(f32[736,1]{1,0:T(8,128)S(1)} %select_n.91.bias_ref) | copy-start | bytes 8836
  116.9 332.4 %reduce-scatter.2.cloned.1.call-start = ((), (), s32[]{:S(2)}) async-start(), calls=%async_computation.1 | async-start | bytes 7299072 | tf_op jit(solution)/shard_map/reduce_scatter | solution.py:777
  134.6 42.6 %collective-permute-start.14 = (bf16[704,1152]{1,0:T(8,128)(2,1)}, bf16[704,1152]{1,0:T(8,128)(2,1)}, u32[]{:S(2)}, u32[]{:S(2)}) collective-permute-start(bf16[704,1152]{1,0:T(8,128)(2,1)} %bitcast.35.refs_2_), channel_id=1, source_target_pairs={{0,16},{1,17},{2,18},{3,19},{4,20},{5,21},{6,22},{7,23},{8,24},{9,... | collective-permute-start | bytes 4866056 | tf_op jit(solution)/shard_map/ppermute | solution.py:510
  136.0 52.4 %collective-permute-start.17 = (bf16[704,1152]{1,0:T(8,128)(2,1)}, bf16[704,1152]{1,0:T(8,128)(2,1)}, u32[]{:S(2)}, u32[]{:S(2)}) collective-permute-start(bf16[704,1152]{1,0:T(8,128)(2,1)} %bitcast.35.refs_2_), channel_id=1, source_target_pairs={{0,8},{1,9},{2,10},{3,11},{4,12},{5,13},{6,14},{7,15},{8,0},{9,1},... | collective-permute-start | bytes 4866056 | tf_op jit(solution)/shard_map/ppermute | solution.py:510
  138.6 42.0 %collective-permute-start.13 = (bf16[704,1152]{1,0:T(8,128)(2,1)}, bf16[704,1152]{1,0:T(8,128)(2,1)}, u32[]{:S(2)}, u32[]{:S(2)}) collective-permute-start(bf16[704,1152]{1,0:T(8,128)(2,1)} %bitcast.33.refs_0_), channel_id=1, source_target_pairs={{0,1},{1,0},{2,3},{3,2},{4,5},{5,4},{6,7},{7,6},{8,9},{9,8},{10,11... | collective-permute-start | bytes 4866056 | tf_op jit(solution)/shard_map/ppermute | solution.py:510
  140.3 48.1 %collective-permute-start.15 = (bf16[704,1152]{1,0:T(8,128)(2,1)}, bf16[704,1152]{1,0:T(8,128)(2,1)}, u32[]{:S(2)}, u32[]{:S(2)}) collective-permute-start(bf16[704,1152]{1,0:T(8,128)(2,1)} %bitcast.33.refs_0_), channel_id=1, source_target_pairs={{0,8},{1,9},{2,10},{3,11},{4,12},{5,13},{6,14},{7,15},{8,0},{9,1},... | collective-permute-start | bytes 4866056 | tf_op jit(solution)/shard_map/ppermute | solution.py:510
  151.8 29.3 %copy-start.64 = (f32[1152]{0:T(1024)S(1)}, f32[1152]{0:T(1024)}, u32[]{:S(2)}) copy-start(f32[1152]{0:T(1024)} %param.30) | copy-start | bytes 13828
  166.9 166.0 %copy-start.5 = (bf16[1152,736]{1,0:T(8,128)(2,1)}, bf16[1152,736]{1,0:T(8,128)(2,1)S(1)}, u32[]{:S(2)}) copy-start(bf16[1152,736]{1,0:T(8,128)(2,1)S(1)} %get-tuple-element.94.out_ref.attended_ref) | copy-start | bytes 5087236
  180.6 7.9 %collective-permute-start.16 = (bf16[704,1152]{1,0:T(8,128)(2,1)}, bf16[704,1152]{1,0:T(8,128)(2,1)}, u32[]{:S(2)}, u32[]{:S(2)}) collective-permute-start(bf16[704,1152]{1,0:T(8,128)(2,1)} %collective-permute-done.13.refs_1_), channel_id=1, source_target_pairs={{0,8},{1,9},{2,10},{3,11},{4,12},{5,13},{6,14},{7,15},{8,0},{9,1},... | collective-permute-start | bytes 4866056 | tf_op jit(solution)/shard_map/ppermute | solution.py:510
  180.6 8.3 %collective-permute-start.18 = (bf16[704,1152]{1,0:T(8,128)(2,1)}, bf16[704,1152]{1,0:T(8,128)(2,1)}, u32[]{:S(2)}, u32[]{:S(2)}) collective-permute-start(bf16[704,1152]{1,0:T(8,128)(2,1)} %collective-permute-done.14.refs_3_), channel_id=1, source_target_pairs={{0,8},{1,9},{2,10},{3,11},{4,12},{5,13},{6,14},{7,15},{8,0},{9,1},... | collective-permute-start | bytes 4866056 | tf_op jit(solution)/shard_map/ppermute | solution.py:510
  216.8 31.0 %collective-permute-start.19 = (bf16[4,2,352,1152]{3,2,1,0:T(8,128)(2,1)}, bf16[4,2,352,1152]{3,2,1,0:T(8,128)(2,1)}, u32[]{:S(2)}, u32[]{:S(2)}) collective-permute-start(bf16[4,2,352,1152]{3,2,1,0:T(8,128)(2,1)} %get-tuple-element.110), channel_id=1, source_target_pairs={{0,8},{1,9},{2,10},{3,11},{4,12},{5,13},{6,14},{7,15},{8,0},{9,1},... | collective-permute-start | bytes 19464200 | tf_op jit(solution)/shard_map/ppermute | solution.py:510
  253.2 38.0 %collective-permute-start.20 = (bf16[2,352,1152]{2,1,0:T(8,128)(2,1)}, bf16[2,352,1152]{2,1,0:T(8,128)(2,1)S(1)}, u32[]{:S(2)}, u32[]{:S(2)}) collective-permute-start(bf16[2,352,1152]{2,1,0:T(8,128)(2,1)} %get-tuple-element.176), channel_id=1, source_target_pairs={{0,1},{1,0},{2,3},{3,2},{4,5},{5,4},{6,7},{7,6},{8,9},{9,8},{10,11... | collective-permute-start | bytes 4866056 | tf_op jit(solution)/shard_map/ppermute | solution.py:510
  254.4 37.8 %collective-permute-start.21 = (bf16[2,352,1152]{2,1,0:T(8,128)(2,1)}, bf16[2,352,1152]{2,1,0:T(8,128)(2,1)}, u32[]{:S(2)}, u32[]{:S(2)}) collective-permute-start(bf16[2,352,1152]{2,1,0:T(8,128)(2,1)} %get-tuple-element.175), channel_id=1, source_target_pairs={{0,16},{1,17},{2,18},{3,19},{4,20},{5,21},{6,22},{7,23},{8,24},{9,... | collective-permute-start | bytes 4866056 | tf_op jit(solution)/shard_map/ppermute | solution.py:510
  300.2 65.0 %collective-permute-start.24 = (bf16[2,2,88,1152]{3,2,0,1:T(8,128)(2,1)}, bf16[2,2,88,1152]{3,2,0,1:T(8,128)(2,1)}, u32[]{:S(2)}, u32[]{:S(2)}) collective-permute-start(bf16[2,2,88,1152]{3,2,0,1:T(8,128)(2,1)} %get-tuple-element.219), channel_id=1, source_target_pairs={{0,1},{1,0},{2,3},{3,2},{4,5},{5,4},{6,7},{7,6},{8,9},{9,8},{10,11... | collective-permute-start | bytes 2433032 | tf_op jit(solution)/shard_map/ppermute | solution.py:510
  316.6 55.7 %collective-permute-start.23 = (bf16[2,2,88,1152]{3,2,0,1:T(8,128)(2,1)}, bf16[2,2,88,1152]{3,2,0,1:T(8,128)(2,1)}, u32[]{:S(2)}, u32[]{:S(2)}) collective-permute-start(bf16[2,2,88,1152]{3,2,0,1:T(8,128)(2,1)} %get-tuple-element.220), channel_id=1, source_target_pairs={{0,16},{1,17},{2,18},{3,19},{4,20},{5,21},{6,22},{7,23},{8,24},{9,... | collective-permute-start | bytes 2433032 | tf_op jit(solution)/shard_map/ppermute | solution.py:510
  331.8 42.5 %collective-permute-start.22 = (bf16[368,1152]{1,0:T(8,128)(2,1)}, bf16[368,1152]{1,0:T(8,128)(2,1)}, u32[]{:S(2)}, u32[]{:S(2)}) collective-permute-start(bf16[368,1152]{1,0:T(8,128)(2,1)} %get-tuple-element.120), channel_id=1, source_target_pairs={{0,1},{1,0},{2,3},{3,2},{4,5},{5,4},{6,7},{7,6},{8,9},{9,8},{10,11... | collective-permute-start | bytes 2543624 | tf_op jit(solution)/shard_map/ppermute | solution.py:631
  335.4 29.8 %copy-start.26 = (bf16[2,1,2,88,1152]{4,3,2,1,0:T(8,128)(2,1)S(1)}, bf16[2,1,2,88,1152]{4,3,2,1,0:T(8,128)(2,1)}, u32[]{:S(2)}) copy-start(bf16[2,1,2,88,1152]{4,3,2,1,0:T(8,128)(2,1)} %get-tuple-element.185) | copy-start | bytes 2433028
  366.8 39.9 %collective-permute-start.28 = (bf16[2,88,1152]{2,1,0:T(8,128)(2,1)S(1)}, bf16[2,88,1152]{2,1,0:T(8,128)(2,1)S(1)}, u32[]{:S(2)}, u32[]{:S(2)}) collective-permute-start(bf16[2,88,1152]{2,1,0:T(8,128)(2,1)S(1)} %get-tuple-element.198), channel_id=1, source_target_pairs={{0,4},{1,5},{2,6},{3,7},{4,0},{5,1},{6,2},{7,3},{8,12},{9,13},{10,... | collective-permute-start | bytes 1216520 | tf_op jit(solution)/shard_map/ppermute | solution.py:510
  366.9 40.8 %collective-permute-start.29 = (bf16[2,88,1152]{2,1,0:T(8,128)(2,1)S(1)}, bf16[2,88,1152]{2,1,0:T(8,128)(2,1)S(1)}, u32[]{:S(2)}, u32[]{:S(2)}) collective-permute-start(bf16[2,88,1152]{2,1,0:T(8,128)(2,1)S(1)} %get-tuple-element.197), channel_id=1, source_target_pairs={{0,6},{1,7},{2,4},{3,5},{4,2},{5,3},{6,0},{7,1},{8,14},{9,15},{10,... | collective-permute-start | bytes 1216520 | tf_op jit(solution)/shard_map/ppermute | solution.py:510
  373.7 34.1 %collective-permute-start.27 = (bf16[2,88,1152]{2,1,0:T(8,128)(2,1)S(1)}, bf16[2,88,1152]{2,1,0:T(8,128)(2,1)S(1)}, u32[]{:S(2)}, u32[]{:S(2)}) collective-permute-start(bf16[2,88,1152]{2,1,0:T(8,128)(2,1)S(1)} %slice_bitcast_fusion.6), channel_id=1, source_target_pairs={{0,2},{1,3},{2,0},{3,1},{4,6},{5,7},{6,4},{7,5},{8,10},{9,11},{10,... | collective-permute-start | bytes 1216520 | tf_op jit(solution)/shard_map/ppermute | solution.py:510
  391.4 11.2 %collective-permute-start.26 = (bf16[4,144,1152]{2,1,0:T(8,128)(2,1)}, bf16[4,144,1152]{2,1,0:T(8,128)(2,1)S(1)}, u32[]{:S(2)}, u32[]{:S(2)}) collective-permute-start(bf16[4,144,1152]{2,1,0:T(8,128)(2,1)} %get-tuple-element.130), channel_id=1, source_target_pairs={{0,8},{1,9},{2,10},{3,11},{4,12},{5,13},{6,14},{7,15},{8,0},{9,1},... | collective-permute-start | bytes 3981320 | tf_op jit(solution)/shard_map/ppermute | solution.py:510
  391.5 12.7 %collective-permute-start.25 = (bf16[2,2,144,1152]{3,2,1,0:T(8,128)(2,1)}, bf16[2,2,144,1152]{3,2,1,0:T(8,128)(2,1)S(1)}, u32[]{:S(2)}, u32[]{:S(2)}) collective-permute-start(bf16[2,2,144,1152]{3,2,1,0:T(8,128)(2,1)} %get-tuple-element.128), channel_id=1, source_target_pairs={{0,8},{1,9},{2,10},{3,11},{4,12},{5,13},{6,14},{7,15},{8,0},{9,1},... | collective-permute-start | bytes 3981320 | tf_op jit(solution)/shard_map/ppermute | solution.py:510
  402.7 37.1 %collective-permute-start.33 = (bf16[4,144,1152]{2,1,0:T(8,128)(2,1)}, bf16[4,144,1152]{2,1,0:T(8,128)(2,1)}, u32[]{:S(2)}, u32[]{:S(2)}) collective-permute-start(bf16[4,144,1152]{2,1,0:T(8,128)(2,1)} %get-tuple-element.129), channel_id=1, source_target_pairs={{0,8},{1,9},{2,10},{3,11},{4,12},{5,13},{6,14},{7,15},{8,0},{9,1},... | collective-permute-start | bytes 3981320 | tf_op jit(solution)/shard_map/ppermute | solution.py:510
  404.2 33.4 %collective-permute-start.32 = (bf16[4,144,1152]{2,1,0:T(8,128)(2,1)}, bf16[4,144,1152]{2,1,0:T(8,128)(2,1)}, u32[]{:S(2)}, u32[]{:S(2)}) collective-permute-start(bf16[4,144,1152]{2,1,0:T(8,128)(2,1)} %add_convert_fusion.6), channel_id=1, source_target_pairs={{0,16},{1,17},{2,18},{3,19},{4,20},{5,21},{6,22},{7,23},{8,24},{9,... | collective-permute-start | bytes 3981320 | tf_op jit(solution)/shard_map/ppermute | solution.py:510
  406.6 33.1 %collective-permute-start.31 = (bf16[2,2,144,1152]{3,2,1,0:T(8,128)(2,1)}, bf16[2,2,144,1152]{3,2,1,0:T(8,128)(2,1)}, u32[]{:S(2)}, u32[]{:S(2)}) collective-permute-start(bf16[2,2,144,1152]{3,2,1,0:T(8,128)(2,1)} %add_convert_fusion.7), channel_id=1, source_target_pairs={{0,1},{1,0},{2,3},{3,2},{4,5},{5,4},{6,7},{7,6},{8,9},{9,8},{10,11... | collective-permute-start | bytes 3981320 | tf_op jit(solution)/shard_map/ppermute | solution.py:510
  407.7 35.7 %collective-permute-start.30 = (bf16[2,2,144,1152]{3,2,1,0:T(8,128)(2,1)}, bf16[2,2,144,1152]{3,2,1,0:T(8,128)(2,1)}, u32[]{:S(2)}, u32[]{:S(2)}) collective-permute-start(bf16[2,2,144,1152]{3,2,1,0:T(8,128)(2,1)} %get-tuple-element.127), channel_id=1, source_target_pairs={{0,8},{1,9},{2,10},{3,11},{4,12},{5,13},{6,14},{7,15},{8,0},{9,1},... | collective-permute-start | bytes 3981320 | tf_op jit(solution)/shard_map/ppermute | solution.py:510
  442.9 18.1 %collective-permute-start.38 = (bf16[2,144,1152]{2,1,0:T(8,128)(2,1)}, bf16[2,144,1152]{2,1,0:T(8,128)(2,1)}, u32[]{:S(2)}, u32[]{:S(2)}) collective-permute-start(bf16[2,144,1152]{2,1,0:T(8,128)(2,1)} %slice.296), channel_id=1, source_target_pairs={{0,1},{1,0},{2,3},{3,2},{4,5},{5,4},{6,7},{7,6},{8,9},{9,8},{10,11... | collective-permute-start | bytes 1990664 | tf_op jit(solution)/shard_map/ppermute | solution.py:510
  446.5 16.2 %collective-permute-start.37 = (bf16[2,144,1152]{2,1,0:T(8,128)(2,1)}, bf16[2,144,1152]{2,1,0:T(8,128)(2,1)}, u32[]{:S(2)}, u32[]{:S(2)}) collective-permute-start(bf16[2,144,1152]{2,1,0:T(8,128)(2,1)} %slice_bitcast_fusion.2), channel_id=1, source_target_pairs={{0,16},{1,17},{2,18},{3,19},{4,20},{5,21},{6,22},{7,23},{8,24},{9,... | collective-permute-start | bytes 1990664 | tf_op jit(solution)/shard_map/ppermute | solution.py:510
  449.3 10.1 %collective-permute-start.34 = (f32[106,128]{1,0:T(8,128)}, f32[106,128]{1,0:T(8,128)}, u32[]{:S(2)}, u32[]{:S(2)}) collective-permute-start(f32[106,128]{1,0:T(8,128)} %bitcast.57), channel_id=1, source_target_pairs={{0,2},{1,3},{2,0},{3,1},{4,6},{5,7},{6,4},{7,5},{8,10},{9,11},{10,... | collective-permute-start | bytes 162824 | tf_op jit(solution)/shard_map/ppermute | solution.py:510
  450.5 9.0 %collective-permute-start.35 = (f32[106,128]{1,0:T(8,128)}, f32[106,128]{1,0:T(8,128)}, u32[]{:S(2)}, u32[]{:S(2)}) collective-permute-start(f32[106,128]{1,0:T(8,128)} %bitcast.57), channel_id=1, source_target_pairs={{0,4},{1,5},{2,6},{3,7},{4,0},{5,1},{6,2},{7,3},{8,12},{9,13},{10,... | collective-permute-start | bytes 162824 | tf_op jit(solution)/shard_map/ppermute | solution.py:510
  452.9 6.6 %collective-permute-start.36 = (f32[106,128]{1,0:T(8,128)}, f32[106,128]{1,0:T(8,128)}, u32[]{:S(2)}, u32[]{:S(2)}) collective-permute-start(f32[106,128]{1,0:T(8,128)} %bitcast.57), channel_id=1, source_target_pairs={{0,6},{1,7},{2,4},{3,5},{4,2},{5,3},{6,0},{7,1},{8,14},{9,15},{10,... | collective-permute-start | bytes 162824 | tf_op jit(solution)/shard_map/ppermute | solution.py:510
  467.3 6.2 %collective-permute-start.43 = (bf16[272,288]{1,0:T(8,128)(2,1)S(1)}, bf16[272,288]{1,0:T(8,128)(2,1)S(1)}, u32[]{:S(2)}, u32[]{:S(2)}) collective-permute-start(bf16[272,288]{1,0:T(8,128)(2,1)S(1)} %copy-done.63), channel_id=1, source_target_pairs={{0,8},{1,9},{2,10},{3,11},{4,12},{5,13},{6,14},{7,15},{8,0},{9,1},... | collective-permute-start | bytes 470024 | tf_op jit(solution)/shard_map/ppermute | solution.py:510
  467.3 8.1 %collective-permute-start.44 = (bf16[272,288]{1,0:T(8,128)(2,1)S(1)}, bf16[272,288]{1,0:T(8,128)(2,1)S(1)}, u32[]{:S(2)}, u32[]{:S(2)}) collective-permute-start(bf16[272,288]{1,0:T(8,128)(2,1)S(1)} %copy-done.62), channel_id=1, source_target_pairs={{0,16},{1,17},{2,18},{3,19},{4,20},{5,21},{6,22},{7,23},{8,24},{9,... | collective-permute-start | bytes 470024 | tf_op jit(solution)/shard_map/ppermute | solution.py:510
  468.2 10.6 %collective-permute-start.45 = (bf16[272,288]{1,0:T(8,128)(2,1)S(1)}, bf16[272,288]{1,0:T(8,128)(2,1)S(1)}, u32[]{:S(2)}, u32[]{:S(2)}) collective-permute-start(bf16[272,288]{1,0:T(8,128)(2,1)S(1)} %copy-done.61), channel_id=1, source_target_pairs={{0,24},{1,25},{2,26},{3,27},{4,28},{5,29},{6,30},{7,31},{8,16},{9,... | collective-permute-start | bytes 470024 | tf_op jit(solution)/shard_map/ppermute | solution.py:510
  470.1 28.3 %collective-permute-start.39 = (bf16[368,1152]{1,0:T(8,128)(2,1)}, bf16[368,1152]{1,0:T(8,128)(2,1)}, u32[]{:S(2)}, u32[]{:S(2)}) collective-permute-start(bf16[368,1152]{1,0:T(8,128)(2,1)} %slice.248), channel_id=1, source_target_pairs={{0,1},{1,0},{2,3},{3,2},{4,5},{5,4},{6,7},{7,6},{8,9},{9,8},{10,11... | collective-permute-start | bytes 2543624 | tf_op jit(solution)/shard_map/ppermute | solution.py:631
  471.8 26.0 %collective-permute-start.41 = (bf16[144,1152]{1,0:T(8,128)(2,1)}, bf16[144,1152]{1,0:T(8,128)(2,1)}, u32[]{:S(2)}, u32[]{:S(2)}) collective-permute-start(bf16[144,1152]{1,0:T(8,128)(2,1)} %get-tuple-element.200), channel_id=1, source_target_pairs={{0,4},{1,5},{2,6},{3,7},{4,0},{5,1},{6,2},{7,3},{8,12},{9,13},{10,... | collective-permute-start | bytes 995336 | tf_op jit(solution)/shard_map/ppermute | solution.py:510
  473.4 24.3 %collective-permute-start.42 = (bf16[144,1152]{1,0:T(8,128)(2,1)}, bf16[144,1152]{1,0:T(8,128)(2,1)}, u32[]{:S(2)}, u32[]{:S(2)}) collective-permute-start(bf16[144,1152]{1,0:T(8,128)(2,1)} %get-tuple-element.199), channel_id=1, source_target_pairs={{0,6},{1,7},{2,4},{3,5},{4,2},{5,3},{6,0},{7,1},{8,14},{9,15},{10,... | collective-permute-start | bytes 995336 | tf_op jit(solution)/shard_map/ppermute | solution.py:510
  475.4 23.1 %collective-permute-start.40 = (bf16[144,1152]{1,0:T(8,128)(2,1)}, bf16[144,1152]{1,0:T(8,128)(2,1)}, u32[]{:S(2)}, u32[]{:S(2)}) collective-permute-start(bf16[144,1152]{1,0:T(8,128)(2,1)} %slice_bitcast_fusion.10), channel_id=1, source_target_pairs={{0,2},{1,3},{2,0},{3,1},{4,6},{5,7},{6,4},{7,5},{8,10},{9,11},{10,... | collective-permute-start | bytes 995336 | tf_op jit(solution)/shard_map/ppermute | solution.py:510
  502.6 7.3 %collective-permute-start.50 = (bf16[144,288]{1,0:T(8,128)(2,1)}, bf16[144,288]{1,0:T(8,128)(2,1)S(1)}, u32[]{:S(2)}, u32[]{:S(2)}) collective-permute-start(bf16[144,288]{1,0:T(8,128)(2,1)} %get-tuple-element.168), channel_id=1, source_target_pairs={{0,8},{1,9},{2,10},{3,11},{4,12},{5,13},{6,14},{7,15},{8,0},{9,1},... | collective-permute-start | bytes 248840 | tf_op jit(solution)/shard_map/ppermute | solution.py:510
  502.6 8.3 %collective-permute-start.51 = (bf16[144,288]{1,0:T(8,128)(2,1)}, bf16[144,288]{1,0:T(8,128)(2,1)S(1)}, u32[]{:S(2)}, u32[]{:S(2)}) collective-permute-start(bf16[144,288]{1,0:T(8,128)(2,1)} %get-tuple-element.169), channel_id=1, source_target_pairs={{0,16},{1,17},{2,18},{3,19},{4,20},{5,21},{6,22},{7,23},{8,24},{9,... | collective-permute-start | bytes 248840 | tf_op jit(solution)/shard_map/ppermute | solution.py:510
  503.6 7.3 %collective-permute-start.52 = (bf16[144,288]{1,0:T(8,128)(2,1)}, bf16[144,288]{1,0:T(8,128)(2,1)S(1)}, u32[]{:S(2)}, u32[]{:S(2)}) collective-permute-start(bf16[144,288]{1,0:T(8,128)(2,1)} %get-tuple-element.170), channel_id=1, source_target_pairs={{0,24},{1,25},{2,26},{3,27},{4,28},{5,29},{6,30},{7,31},{8,16},{9,... | collective-permute-start | bytes 248840 | tf_op jit(solution)/shard_map/ppermute | solution.py:510
  504.5 4.5 collective-permute-start.46
  509.0 6.9 %collective-permute-start.47 = (f32[106,128]{1,0:T(8,128)S(1)}, f32[106,128]{1,0:T(8,128)S(1)}, u32[]{:S(2)}, u32[]{:S(2)}) collective-permute-start(f32[106,128]{1,0:T(8,128)S(1)} %add.246), channel_id=1, source_target_pairs={{0,8},{1,9},{2,10},{3,11},{4,12},{5,13},{6,14},{7,15},{8,0},{9,1},... | collective-permute-start | bytes 162824 | tf_op jit(solution)/shard_map/ppermute | solution.py:510
  509.1 6.8 %collective-permute-start.48 = (f32[106,128]{1,0:T(8,128)S(1)}, f32[106,128]{1,0:T(8,128)S(1)}, u32[]{:S(2)}, u32[]{:S(2)}) collective-permute-start(f32[106,128]{1,0:T(8,128)S(1)} %add.246), channel_id=1, source_target_pairs={{0,16},{1,17},{2,18},{3,19},{4,20},{5,21},{6,22},{7,23},{8,24},{9,... | collective-permute-start | bytes 162824 | tf_op jit(solution)/shard_map/ppermute | solution.py:510
  509.9 5.9 %collective-permute-start.49 = (f32[106,128]{1,0:T(8,128)S(1)}, f32[106,128]{1,0:T(8,128)S(1)}, u32[]{:S(2)}, u32[]{:S(2)}) collective-permute-start(f32[106,128]{1,0:T(8,128)S(1)} %add.246), channel_id=1, source_target_pairs={{0,24},{1,25},{2,26},{3,27},{4,28},{5,29},{6,30},{7,31},{8,16},{9,... | collective-permute-start | bytes 162824 | tf_op jit(solution)/shard_map/ppermute | solution.py:510
  (62 other events, 351.3 us)
Sparse Core Ops, SparseCore 0:
  21.0 105.9 all-gather.4
  130.5 78.4 all-gather.6
  287.8 150.0 reduce-scatter.1
